TPU v7x, 32 devices: a whole 2x2x4 slice. The times are simulated.
32 devices in a mesh: user: 4 (over y, x), item: 8 (over z, core).
Axes of the slice: x: 2, y: 2, z: 4, core: 2. Of those that a mesh axis runs over, the one named last changes fastest.
Arguments:
- user_emb: bfloat16 [8192, 256], P(('user', 'item')), may hold values from -200 to 200
- item_emb: bfloat16 [8192, 256], P(('item', 'user')), may hold values from -6 to 6
- user_hidden: bfloat16 [8192, 2048], P(('user', 'item')), may hold values from -6 to 6
- item_hidden: bfloat16 [8192, 2048], P(('item', 'user')), may hold values from -6 to 6
- user_expert: int32 [8192, 1], P(('user', 'item')), may hold values from 0 to 31; in each aligned block of 256 rows (0 to 255, 256 to 511, ...) at most 16 rows name the same one
- item_expert: int32 [8192, 1], P(('item', 'user')), may hold values from 0 to 31; in each aligned block of 256 rows (0 to 255, 256 to 511, ...) at most 16 rows name the same one
- positive: int32 [8192], P(('user', 'item')), may hold values from 0 to 8191
Outputs:
- row_loss: float32 [8192], P(('user', 'item'))
- user_weight_grad: float32 [32, 2048, 256], P('user', 'item')
- item_weight_grad: float32 [32, 2048, 256], P('user', 'item')
Inputs may be any that keep to these rules, and one draw needn't show every extreme that they name: `user_expert`: among the rows of one device no expert is named more than 16 times; some expert reaches 16 in some device. `item_expert`: among the rows of one device no expert is named more than 16 times; some expert reaches 16 in some device.
All inputs are finite; a program needn't handle non-finite values.
Results may differ from a plain program's by a relative error of at most 0.0031.
Values may be sent and summed in bfloat16 or wider, within the bound.
No kernel may reach another device: no remote copies, remote signals or barrier semaphores. Data moves between devices by JAX's collectives and lax.ppermute only.
A program may use at most 128 MiB of HBM per device.

v0:
```python
import math

import jax
import jax.numpy as jnp
from jax import lax
from jax.sharding import PartitionSpec as P

EMB = 256
EXPERTS = 32
CAP = 16


def score_block(queries, keys):
    raw = lax.dot_general(
        queries, keys, (((1,), (1,)), ((), ())), preferred_element_type=jnp.float32
    )
    return raw * (1.0 / math.sqrt(EMB))


def score_grad(scores, wanted, columns, levels):
    probs = jnp.exp(scores - levels[:, None])
    hits = columns[None, :] == wanted[:, None]
    return (jnp.where(hits, probs - 1.0, probs) * (1.0 / math.sqrt(EMB))).astype(jnp.bfloat16)


def expert_grads(hidden, grad, expert):
    onehot = (expert[:, None] == jnp.arange(EXPERTS, dtype=jnp.int32)[None, :]).astype(jnp.int32)
    slot = jnp.sum(jnp.cumsum(onehot, axis=0) * onehot, axis=1) - 1
    target = expert * CAP + slot
    dispatch = (jnp.arange(EXPERTS * CAP, dtype=jnp.int32)[:, None] == target[None, :]).astype(
        jnp.bfloat16
    )
    sent_hidden = jnp.dot(dispatch, hidden, preferred_element_type=jnp.float32).astype(jnp.bfloat16)
    sent_grad = jnp.dot(
        dispatch, grad.astype(jnp.bfloat16), preferred_element_type=jnp.float32
    ).astype(jnp.bfloat16)
    groups = lax.axis_size("item")
    width = hidden.shape[1] // groups
    spread = jnp.broadcast_to(sent_grad.reshape(EXPERTS, CAP, 1, EMB), (EXPERTS, CAP, groups, EMB))
    packed = jnp.concatenate([sent_hidden.reshape(EXPERTS, CAP, groups, width), spread], axis=3)
    arrived = lax.all_to_all(
        lax.all_to_all(packed, "user", split_axis=0, concat_axis=1, tiled=True),
        "item",
        split_axis=2,
        concat_axis=1,
        tiled=True,
    )
    arrived = arrived[:, :, 0, :]
    return jnp.einsum(
        "hnq,hnm->hqm",
        arrived[:, :, :width],
        arrived[:, :, width:],
        preferred_element_type=jnp.float32,
    )


def shards(user_emb, item_emb, user_hidden, item_hidden, user_expert, item_expert, positive):
    own_rows = user_emb.shape[0]
    users, targets = (
        lax.all_gather(user_emb, "item", axis=0, tiled=True),
        lax.all_gather(positive, "item", axis=0, tiled=True),
    )
    items = lax.all_gather(item_emb, "user", axis=0, tiled=True)
    n_rows = users.shape[0]
    n_cols = items.shape[0]
    step_rows = math.gcd(n_rows, 512)
    first_col = lax.axis_index("item") * n_cols
    columns = first_col + jnp.arange(n_cols, dtype=jnp.int32)

    def block_stats(index):
        begin = index * step_rows
        queries = lax.dynamic_slice_in_dim(users, begin, step_rows)
        wanted = lax.dynamic_slice_in_dim(targets, begin, step_rows)
        scores = score_block(queries, items)
        top = jnp.max(scores, axis=1)
        total = jnp.sum(jnp.exp(scores - top[:, None]), axis=1)
        picked = jnp.sum(jnp.where(columns[None, :] == wanted[:, None], scores, 0.0), axis=1)
        return (top, total, picked)

    top, total, picked = lax.map(block_stats, jnp.arange(n_rows // step_rows, dtype=jnp.int32))
    top = top.reshape(n_rows)
    total = total.reshape(n_rows)
    picked = picked.reshape(n_rows)
    peak = lax.pmax(top, "item")
    total, picked = lax.psum((total * jnp.exp(top - peak), picked), "item")
    log_total = peak + jnp.log(total)
    losses = log_total - picked
    row_loss = lax.dynamic_slice_in_dim(losses, lax.axis_index("item") * own_rows, own_rows)

    def grad_block(carry, index):
        begin = index * step_rows
        queries = lax.dynamic_slice_in_dim(users, begin, step_rows)
        wanted = lax.dynamic_slice_in_dim(targets, begin, step_rows)
        levels = lax.dynamic_slice_in_dim(log_total, begin, step_rows)
        grads = score_grad(score_block(queries, items), wanted, columns, levels)
        user_part = jnp.dot(grads, items, preferred_element_type=jnp.float32)
        carry = carry + lax.dot_general(
            grads, queries, (((0,), (0,)), ((), ())), preferred_element_type=jnp.float32
        )
        return (carry, user_part)

    item_total, user_parts = lax.scan(
        grad_block,
        jnp.zeros((n_cols, users.shape[1]), jnp.float32),
        jnp.arange(n_rows // step_rows, dtype=jnp.int32),
    )
    user_full = user_parts.reshape(n_rows, items.shape[1])
    user_grad = lax.psum_scatter(user_full, "item", scatter_dimension=0, tiled=True)
    item_grad = lax.psum_scatter(item_total, "user", scatter_dimension=0, tiled=True)
    user_weight_grad = expert_grads(user_hidden, user_grad, user_expert[:, 0])
    item_weight_grad = expert_grads(item_hidden, item_grad, item_expert[:, 0])
    return (row_loss, user_weight_grad, item_weight_grad)


def solution(mesh):
    placed = (
        P(("user", "item"), None),
        P(("item", "user"), None),
        P(("user", "item"), None),
        P(("item", "user"), None),
        P(("user", "item"), None),
        P(("item", "user"), None),
        P(("user", "item")),
    )
    return jax.shard_map(
        shards,
        mesh=mesh,
        in_specs=placed,
        out_specs=(P(("user", "item")), P("user", "item", None), P("user", "item", None)),
        check_vma=False,
    )
```

profile of v0, /device:TPU:11, one launch (start us, length us, event | category | flops | bytes accessed | tf_op | source)
XLA Modules:
  0.0 459.7 jit_solution(6002065742389352675)
XLA Ops:
  8.0 9.8 %all-gather = s32[8,1,256]{2,1,0:T(1,128)S(1)} all-gather(s32[1,1,256]{2,1,0:T(1,128)} %bitcast.133), channel_id=1, replica_groups=mesh['user'=4,'item'=8] {'item'}, dimensions={0}, use_global_device_ids=true | all-gather | bytes 9216 | tf_op jit(solution)/shard_map/all_gather | solution.py:61
  17.8 10.5 %all_gather.10 = bf16[1024,256]{1,0:T(8,128)(2,1)} all-gather(bf16[256,256]{1,0:T(8,128)(2,1)} %param.12), channel_id=1, replica_groups=mesh['user'=4,'item'=8] {'user'}, dimensions={0}, use_global_device_ids=true | all-gather | bytes 655360 | tf_op jit(solution)/shard_map/all_gather | solution.py:63
  28.3 5.2 %all-gather.3.cloned.1.call-done = bf16[2048,256]{1,0:T(8,128)(2,1)} async-done(((bf16[256,256]{1,0:T(8,128)(2,1)}), bf16[2048,256]{1,0:T(8,128)(2,1)}) %all-gather.3.cloned.1.call-update) | async-done | bytes 1048592 | tf_op jit(solution)/shard_map/all_gather | solution.py:60
  33.5 16.0 %while.30 = (s32[]{:T(128)}, f32[4,512]{1,0:T(4,128)S(1)}, f32[4,512]{1,0:T(4,128)S(1)}, f32[4,512]{1,0:T(4,128)S(1)}, s32[4]{0:T(128)S(1)}, /*index=5*/bf16[204...) while((s32[]{:T(128)}, f32[4,512]{1,0:T(4,128)S(1)}, ...), condition=%wide.region_4.5_spmd.clone, body=%wide.region_0.4_spmd.clone.sunk | while | flops 272629248 | bytes 5015767 | solution.py:80
  49.6 9.8 %pmax.7 = f32[2048]{0:T(1024)S(1)} all-reduce(f32[2048]{0:T(1024)S(1)} %bitcast.120), channel_id=1, replica_groups=mesh['user'=4,'item'=8] {'item'}, use_global_device_ids=true, to_apply=%region_5.6 | all-reduce | flops 2048 | bytes 16384 | tf_op jit(solution)/shard_map/pmax | solution.py:84
  59.4 25.6 %all-reduce = (f32[2048]{0:T(1024)S(1)}, f32[2048]{0:T(1024)S(1)}) all-reduce(f32[2048]{0:T(1024)S(1)} %bitcast.122, f32[2048]{0:T(1024)S(1)} %exponential_multiply_fusion), channel_id=1, replica_groups=mesh['user'=4,'item'=8] {'item'}, use_global_device_ids=true, to_apply=%region_7.8 | all-reduce | flops 4096 | bytes 32768 | tf_op jit(solution)/shard_map/psum | solution.py:85
  85.0 29.1 %while.31 = (s32[]{:T(128)}, f32[1024,256]{1,0:T(8,128)}, f32[4,512,256]{2,1,0:T(8,128)}, s32[4]{0:T(128)S(1)}, s32[2048]{0:T(1024)S(1)}, /*index=5*/bf16[2048,2...) while((s32[]{:T(128)}, f32[1024,256]{1,0:T(8,128)}, ...), condition=%wide.region_12.13_spmd.clone, body=%wide.region_11.12_spmd.clone.sunk | while | flops 809501696 | bytes 9457917 | solution.py:102
  86.4 1.9 fusion.55
  88.3 2.5 convolution_add_fusion.2
  95.3 2.8 convolution_add_fusion.2
  100.8 1.9 fusion.55
  102.7 2.8 convolution_add_fusion.2
  108.1 1.9 fusion.55
  110.1 2.8 convolution_add_fusion.2
  117.3 28.4 %reduce-scatter.5.cloned.1.call-done = f32[256,256]{1,0:T(8,128)} async-done(((f32[1024,256]{1,0:T(8,128)}), f32[256,256]{1,0:T(8,128)}) %reduce-scatter.5.cloned.1.call-update) | async-done | bytes 262160 | tf_op jit(solution)/shard_map/reduce_scatter | solution.py:109
  147.2 2.3 pad_maximum_fusion.1
  149.5 5.3 %all-to-all-start.2 = ((bf16[32,16,8,512]{3,2,1,0:T(8,128)(2,1)}), bf16[32,16,8,512]{3,2,1,0:T(8,128)(2,1)}, u32[]{:S(2)}, u32[]{:S(2)}) async-start(bf16[32,16,8,512]{3,2,1,0:T(8,128)(2,1)} %pad_maximum_fusion.1), calls=%async_computation.4 | async-start | bytes 8388608 | tf_op jit(solution)/shard_map/all_to_all | solution.py:42
  157.1 21.8 %reduce-scatter.3.cloned.1.call-done = f32[256,256]{1,0:T(8,128)} async-done(((f32[2048,256]{1,0:T(8,128)}), f32[256,256]{1,0:T(8,128)}) %reduce-scatter.3.cloned.1.call-update) | async-done | bytes 262160 | tf_op jit(solution)/shard_map/reduce_scatter | solution.py:108
  180.4 2.3 pad_maximum_fusion
  182.8 18.5 %all-to-all-done.2 = bf16[32,16,8,512]{3,2,1,0:T(8,128)(2,1)} async-done(((bf16[32,16,8,512]{3,2,1,0:T(8,128)(2,1)}), bf16[32,16,8,512]{3,2,1,0:T(8,128)(2,1)}, u32[]{:S(2)}, u32[]{:S(2)}) %all-to-all-start.2) | async-done | bytes 4194336 | tf_op jit(solution)/shard_map/all_to_all | solution.py:42
  201.3 5.2 %all-to-all-start = ((bf16[32,16,8,512]{3,2,1,0:T(8,128)(2,1)}), bf16[32,16,8,512]{3,2,1,0:T(8,128)(2,1)}, u32[]{:S(2)}, u32[]{:S(2)}) async-start(bf16[32,16,8,512]{3,2,1,0:T(8,128)(2,1)} %pad_maximum_fusion), calls=%async_computation.1 | async-start | bytes 8388608 | tf_op jit(solution)/shard_map/all_to_all | solution.py:42
  206.5 5.6 %copy.25 = bf16[4,8,16,8,512]{4,2,0,1,3:T(8,128)(2,1)} copy(bf16[4,8,16,8,512]{4,3,2,1,0:T(8,128)(2,1)} %bitcast.17) | data formatting | bytes 8388608 | tf_op jit(solution)/shard_map/all_to_all | solution.py:42
  212.1 40.1 %all-to-all-done = bf16[32,16,8,512]{3,2,1,0:T(8,128)(2,1)} async-done(((bf16[32,16,8,512]{3,2,1,0:T(8,128)(2,1)}), bf16[32,16,8,512]{3,2,1,0:T(8,128)(2,1)}, u32[]{:S(2)}, u32[]{:S(2)}) %all-to-all-start) | async-done | bytes 4194336 | tf_op jit(solution)/shard_map/all_to_all | solution.py:42
  252.2 7.2 %all-to-all-start.3 = ((bf16[8,64,8,512]{3,1,0,2:T(8,128)(2,1)}), bf16[8,64,8,512]{3,1,0,2:T(8,128)(2,1)}, u32[]{:S(2)}, u32[]{:S(2)}) async-start(bf16[8,64,8,512]{3,1,0,2:T(8,128)(2,1)} %bitcast.106), calls=%async_computation.5 | async-start | bytes 8388608 | tf_op jit(solution)/shard_map/all_to_all | solution.py:41
  259.4 5.6 %copy.21 = bf16[4,8,16,8,512]{4,2,0,1,3:T(8,128)(2,1)} copy(bf16[4,8,16,8,512]{4,3,2,1,0:T(8,128)(2,1)} %bitcast.7) | data formatting | bytes 8388608 | tf_op jit(solution)/shard_map/all_to_all | solution.py:42
  264.9 84.9 %all-to-all-done.3 = bf16[8,64,8,512]{3,1,0,2:T(8,128)(2,1)} async-done(((bf16[8,64,8,512]{3,1,0,2:T(8,128)(2,1)}), bf16[8,64,8,512]{3,1,0,2:T(8,128)(2,1)}, u32[]{:S(2)}, u32[]{:S(2)}) %all-to-all-start.3) | async-done | bytes 4194336 | tf_op jit(solution)/shard_map/all_to_all | solution.py:41
  349.8 8.1 %all-to-all-start.1 = ((bf16[8,64,8,512]{3,1,0,2:T(8,128)(2,1)}), bf16[8,64,8,512]{3,1,0,2:T(8,128)(2,1)}, u32[]{:S(2)}, u32[]{:S(2)}) async-start(bf16[8,64,8,512]{3,1,0,2:T(8,128)(2,1)} %bitcast.105), calls=%async_computation.2 | async-start | bytes 8388608 | tf_op jit(solution)/shard_map/all_to_all | solution.py:41
  358.5 2.7 copy.26
  361.2 2.1 fusion.14
  363.4 85.0 %all-to-all-done.1 = bf16[8,64,8,512]{3,1,0,2:T(8,128)(2,1)} async-done(((bf16[8,64,8,512]{3,1,0,2:T(8,128)(2,1)}), bf16[8,64,8,512]{3,1,0,2:T(8,128)(2,1)}, u32[]{:S(2)}, u32[]{:S(2)}) %all-to-all-start.1) | async-done | bytes 4194336 | tf_op jit(solution)/shard_map/all_to_all | solution.py:41
  448.4 2.7 copy.22
  451.0 2.1 fusion.17
  (112 shorter events, 33.0 us)
Async XLA Ops:
  7.2 108.7 %copy-start = (bf16[256,2048]{1,0:T(8,128)(2,1)S(1)}, bf16[256,2048]{1,0:T(8,128)(2,1)}, u32[]{:S(2)}) copy-start(bf16[256,2048]{1,0:T(8,128)(2,1)} %param.14) | copy-start | bytes 3145732
  7.2 26.4 %all-gather.3.cloned.1.call-start = ((), (), s32[]{:S(2)}) async-start(), calls=%async_computation.6 | async-start | bytes 1179648 | tf_op jit(solution)/shard_map/all_gather | solution.py:60
  7.9 137.7 %reduce-scatter.5.cloned.1.call-start = ((), (), s32[]{:S(2)}) async-start(), calls=%async_computation.8 | async-start | bytes 1310720 | tf_op jit(solution)/shard_map/reduce_scatter | solution.py:109
  88.3 2.5 copy-start.2
  95.3 2.8 copy-start.2
  102.7 2.8 copy-start.2
  110.1 2.8 copy-start.2
  114.1 0.8 copy-start.4
  114.1 64.8 %reduce-scatter.3.cloned.1.call-start = ((), (), s32[]{:S(2)}) async-start(), calls=%async_computation.7 | async-start | bytes 2359296 | tf_op jit(solution)/shard_map/reduce_scatter | solution.py:108
  149.5 5.3 %copy-start.5 = (s32[256,1]{0,1:T(1,128)S(1)}, s32[256,1]{0,1:T(1,128)}, u32[]{:S(2)}) copy-start(s32[256,1]{0,1:T(1,128)} %param.15) | copy-start | bytes 3076
  149.5 6.2 %copy-start.3 = (bf16[256,2048]{1,0:T(8,128)(2,1)S(1)}, bf16[256,2048]{1,0:T(8,128)(2,1)}, u32[]{:S(2)}) copy-start(bf16[256,2048]{1,0:T(8,128)(2,1)} %param.13) | copy-start | bytes 3145732
  149.5 51.8 %all-to-all-start.2 = ((bf16[32,16,8,512]{3,2,1,0:T(8,128)(2,1)}), bf16[32,16,8,512]{3,2,1,0:T(8,128)(2,1)}, u32[]{:S(2)}, u32[]{:S(2)}) async-start(bf16[32,16,8,512]{3,2,1,0:T(8,128)(2,1)} %pad_maximum_fusion.1), calls=%async_computation.4 | async-start | bytes 8388608 | tf_op jit(solution)/shard_map/all_to_all | solution.py:42
  201.3 50.9 %all-to-all-start = ((bf16[32,16,8,512]{3,2,1,0:T(8,128)(2,1)}), bf16[32,16,8,512]{3,2,1,0:T(8,128)(2,1)}, u32[]{:S(2)}, u32[]{:S(2)}) async-start(bf16[32,16,8,512]{3,2,1,0:T(8,128)(2,1)} %pad_maximum_fusion), calls=%async_computation.1 | async-start | bytes 8388608 | tf_op jit(solution)/shard_map/all_to_all | solution.py:42
  252.2 97.6 %all-to-all-start.3 = ((bf16[8,64,8,512]{3,1,0,2:T(8,128)(2,1)}), bf16[8,64,8,512]{3,1,0,2:T(8,128)(2,1)}, u32[]{:S(2)}, u32[]{:S(2)}) async-start(bf16[8,64,8,512]{3,1,0,2:T(8,128)(2,1)} %bitcast.106), calls=%async_computation.5 | async-start | bytes 8388608 | tf_op jit(solution)/shard_map/all_to_all | solution.py:41
  349.8 98.5 %all-to-all-start.1 = ((bf16[8,64,8,512]{3,1,0,2:T(8,128)(2,1)}), bf16[8,64,8,512]{3,1,0,2:T(8,128)(2,1)}, u32[]{:S(2)}, u32[]{:S(2)}) async-start(bf16[8,64,8,512]{3,1,0,2:T(8,128)(2,1)} %bitcast.105), calls=%async_computation.2 | async-start | bytes 8388608 | tf_op jit(solution)/shard_map/all_to_all | solution.py:41
  451.0 2.1 copy-start.1
Sparse Core Ops, SparseCore 0:
  9.6 23.8 all-gather.2
  114.3 31.3 reduce-scatter.4
  148.6 30.2 reduce-scatter.2
where the time goes:
time: 465 us; the launch traced here: 460 us
  waiting for transfers between devices  285 us (61%)
  blocking collectives  55.7 us (12%)
  matrix products  38.2 us (8%)
  starting transfers between devices  25.8 us (6%)
  local copies, waits for them, and re-layouts  25.2 us (5%)
  between operations  14 us (3%)
  other arithmetic  10 us (2%)
  loops' own time  5.44 us (1%)
    all_to_all x2, waiting for transfers between devices, expert_grads(): lax.all_to_all(lax.all_to_all(packed, 'user', split_axis=0, concat_axis=1...  170 us
    all_to_all x2, waiting for transfers between devices, expert_grads(): lax.all_to_all(packed, 'user', split_axis=0, concat_axis=1, tiled=True)  58.7 us
    reduce_scatter x1, waiting for transfers between devices, shards(): lax.psum_scatter(item_total, 'user', scatter_dimension=0, tiled=True)  28.4 us
    psum x1, blocking collectives, shards(): total, picked = lax.psum((total * jnp.exp(top - peak), picked), 'item')  25.6 us
    reduce_scatter x1, waiting for transfers between devices, shards(): lax.psum_scatter(user_full, 'item', scatter_dimension=0, tiled=True)  21.8 us
    all_to_all x2, starting transfers between devices, expert_grads(): lax.all_to_all(lax.all_to_all(packed, 'user', split_axis=0, concat_axis=1...  15.2 us
    dot_general x8, matrix products, score_block(): lax.dot_general(queries, keys, (((1,), (1,)), ((), ())), preferred_elemen...  14.3 us
    all_to_all x2, local copies, waits for them, and re-layouts, expert_grads(): lax.all_to_all(packed, 'user', split_axis=0, concat_axis=1, tiled=True)  11.1 us
  transfers between devices with their start and end apart: 7, of which 7 were waited for; matrix products, arithmetic and copies ran while one was open for 6% of the time, Pallas kernels for 0%

commit v1 on v0

v1 whole, which is shorter than its diff:
```python
import functools
import math

import jax
import jax.numpy as jnp
from jax import lax
from jax.experimental import pallas as pl
from jax.experimental.pallas import tpu as pltpu
from jax.sharding import PartitionSpec as P

EMB = 256
EXPERTS = 32
CAP = 16
SCALE = 1.0 / math.sqrt(EMB)
EXTRA = 16
DIGIT = 128
MIB = 1 << 20

F32 = jnp.float32
BF16 = jnp.bfloat16
SCALARS = pl.BlockSpec(memory_space=pltpu.SMEM)


def mm(a, b, ca, cb):
    return lax.dot_general(a, b, (((ca,), (cb,)), ((), ())), preferred_element_type=F32)


def number(rows, index):
    rows = rows.astype(F32)
    high = rows[2 * index : 2 * index + 1]
    return (high * DIGIT + rows[2 * index + 1 : 2 * index + 2]).astype(jnp.int32)


def exchange(pieces, axis):
    size = lax.axis_size(axis)
    return [
        piece if k == 0 else lax.ppermute(piece, axis, [(j, j ^ k) for j in range(size)])
        for k, piece in enumerate(pieces)
    ]


def pack_kernel(emb_ref, positive_ref, user_ref, item_ref, out_ref, target_ref):
    rows = emb_ref.shape[0]
    down = lax.broadcasted_iota(jnp.int32, (rows, rows), 0)
    across = lax.broadcasted_iota(jnp.int32, (rows, rows), 1)

    def slots(expert):
        wide = jnp.broadcast_to(expert.astype(F32), (rows, rows))
        before = jnp.where((wide == wide.T) & (down < across), 1.0, 0.0)
        return expert * CAP + jnp.sum(before, axis=0, keepdims=True).astype(jnp.int32)

    user = slots(user_ref[...])
    item = slots(item_ref[...])
    target_ref[0:1, :] = user
    target_ref[1:2, :] = item
    line = lax.broadcasted_iota(jnp.int32, (EXTRA, rows), 0)
    block = jnp.zeros((EXTRA, rows), jnp.int32)
    for index, values in enumerate((positive_ref[...], user, item)):
        block = jnp.where(line == 2 * index, values // DIGIT, block)
        block = jnp.where(line == 2 * index + 1, values % DIGIT, block)
    out_ref[:rows, :] = emb_ref[...]
    out_ref[rows:, :] = block.astype(F32).astype(BF16)


def pack(emb, positive, user_expert, item_expert):
    rows, width = emb.shape
    return pl.pallas_call(
        pack_kernel,
        out_shape=[
            jax.ShapeDtypeStruct((rows + EXTRA, width), BF16),
            jax.ShapeDtypeStruct((2, rows), jnp.int32),
        ],
    )(emb, positive.reshape(1, rows), user_expert.reshape(1, rows), item_expert.reshape(1, rows))


def stats_kernel(first_ref, users_ref, *refs, rows, chunk):
    *items_refs, out_ref, s_ref = refs
    own = items_refs[0].shape[0]
    n_cols = own * len(items_refs)
    for half in range(users_ref.shape[0]):
        queries = users_ref[half, :rows, :] * jnp.asarray(SCALE, BF16)
        for k, items_ref in enumerate(items_refs):
            s_ref[half, k * own : (k + 1) * own, :] = mm(items_ref[...], queries, 1, 1)
        positive = number(users_ref[half, rows:, :], 0)
        tops = jnp.full((8, rows), -jnp.inf, F32)
        for c in range(0, n_cols, chunk):
            part = s_ref[half, c : c + chunk, :]
            tops = jnp.maximum(tops, jnp.max(part.reshape(chunk // 8, 8, rows), axis=0))
        top = jnp.max(tops, axis=0, keepdims=True)
        total = jnp.zeros((8, rows), F32)
        picked = jnp.zeros((8, rows), F32)
        for c in range(0, n_cols, chunk):
            part = s_ref[half, c : c + chunk, :]
            probs = jnp.exp(part - top)
            total = total + jnp.sum(probs.reshape(chunk // 8, 8, rows), axis=0)
            wanted = positive - (first_ref[c // own] + c % own)
            hit = lax.broadcasted_iota(jnp.int32, (chunk, rows), 0) == wanted
            chosen = jnp.where(hit, part, 0.0)
            picked = picked + jnp.sum(chosen.reshape(chunk // 8, 8, rows), axis=0)
        here = pl.ds(half * rows, rows)
        out_ref[0:1, here] = top
        out_ref[1:2, here] = jnp.sum(total, axis=0, keepdims=True)
        out_ref[2:3, here] = jnp.sum(picked, axis=0, keepdims=True)


def stats(first, users, items, rows):
    blocks, height, emb = users.shape
    own = items[0].shape[0]
    n_cols = own * len(items)
    pair = 2
    return pl.pallas_call(
        functools.partial(stats_kernel, rows=rows, chunk=64),
        grid=(blocks // pair,),
        in_specs=[SCALARS, pl.BlockSpec((pair, height, emb), lambda b: (b, 0, 0))]
        + [pl.BlockSpec((own, emb), lambda b: (0, 0))] * len(items),
        out_specs=pl.BlockSpec((3, pair * rows), lambda b: (0, b)),
        out_shape=jax.ShapeDtypeStruct((3, blocks * rows), F32),
        scratch_shapes=[pltpu.VMEM((pair, n_cols, rows), F32)],
        compiler_params=pltpu.CompilerParams(vmem_limit_bytes=40 * MIB),
        cost_estimate=pl.CostEstimate(
            flops=6 * 2 * blocks * rows * n_cols * emb,
            bytes_accessed=blocks * rows * emb * 2 + n_cols * emb * 2,
            transcendentals=blocks * rows * n_cols,
        ),
    )(first, users, *items)


def grad_kernel(first_ref, users_ref, stats_ref, *refs, rows, chunk, count):
    items_refs = refs[:count]
    loss_ref, user_ref = refs[count : count + 2]
    part_refs = refs[count + 2 : 2 * count + 2]
    s_ref, g_ref, flip_ref = refs[2 * count + 2 :]
    own = items_refs[0].shape[0]
    n_cols = own * count
    step = pl.program_id(0)

    @pl.when(step == 0)
    def _():
        for k in range(count):
            flip_ref[:, k * own : (k + 1) * own] = items_refs[k][...].T
            part_refs[k][...] = jnp.zeros_like(part_refs[k])

    for half in range(users_ref.shape[0]):
        here = pl.ds(half * rows, rows)
        queries = users_ref[half, :rows, :]
        scaled = queries * jnp.asarray(SCALE, BF16)
        for k in range(count):
            s_ref[half, k * own : (k + 1) * own, :] = mm(items_refs[k][...], scaled, 1, 1)
        positive = number(users_ref[half, rows:, :], 0)
        tops = stats_ref[:, 0, here]
        top = jnp.max(tops, axis=0, keepdims=True)
        total = jnp.sum(stats_ref[:, 1, here] * jnp.exp(tops - top), axis=0, keepdims=True)
        level = top + jnp.log(total)
        loss_ref[0:1, here] = level - jnp.sum(stats_ref[:, 2, here], axis=0, keepdims=True)
        for c in range(0, n_cols, chunk):
            probs = jnp.exp(s_ref[half, c : c + chunk, :] - level)
            wanted = positive - (first_ref[c // own] + c % own)
            hit = lax.broadcasted_iota(jnp.int32, (chunk, rows), 0) == wanted
            g_ref[half, c : c + chunk, :] = jnp.where(hit, probs - 1.0, probs).astype(BF16)
        for k in range(count):
            part_refs[k][...] += mm(g_ref[half, k * own : (k + 1) * own, :], queries, 1, 0)
        user_ref[here, :] = mm(flip_ref[...], g_ref[half], 1, 0).T * SCALE

    @pl.when(step == pl.num_programs(0) - 1)
    def _():
        for k in range(count):
            part_refs[k][...] = part_refs[k][...] * SCALE


def grads(first, users, items, gathered, rows):
    blocks, height, emb = users.shape
    count = len(items)
    own = items[0].shape[0]
    n_cols = own * count
    pair = 2
    groups = gathered.shape[0]
    results = pl.pallas_call(
        functools.partial(grad_kernel, rows=rows, chunk=64, count=count),
        grid=(blocks // pair,),
        in_specs=[
            SCALARS,
            pl.BlockSpec((pair, height, emb), lambda b: (b, 0, 0)),
            pl.BlockSpec((groups, 3, pair * rows), lambda b: (0, 0, b)),
        ]
        + [pl.BlockSpec((own, emb), lambda b: (0, 0))] * count,
        out_specs=[
            pl.BlockSpec((1, pair * rows), lambda b: (0, b)),
            pl.BlockSpec((pair * rows, emb), lambda b: (b, 0)),
        ]
        + [pl.BlockSpec((own, emb), lambda b: (0, 0))] * count,
        out_shape=[
            jax.ShapeDtypeStruct((1, blocks * rows), F32),
            jax.ShapeDtypeStruct((blocks * rows, emb), F32),
        ]
        + [jax.ShapeDtypeStruct((own, emb), F32)] * count,
        scratch_shapes=[
            pltpu.VMEM((pair, n_cols, rows), F32),
            pltpu.VMEM((pair, n_cols, rows), BF16),
            pltpu.VMEM((emb, n_cols), BF16),
        ],
        compiler_params=pltpu.CompilerParams(vmem_limit_bytes=48 * MIB),
        cost_estimate=pl.CostEstimate(
            flops=8 * 2 * blocks * rows * n_cols * emb,
            bytes_accessed=blocks * rows * emb * 6 + n_cols * emb * 6,
            transcendentals=blocks * rows * n_cols,
        ),
    )(first, users, gathered, *items)
    return results[0], results[1], results[2:]


def hidden_kernel(me_ref, users_ref, hidden_ref, *out_refs):
    rows = users_ref.shape[2]
    span = out_refs[0].shape[2]
    place = lax.broadcasted_iota(jnp.int32, (span, rows), 0)
    for tower in range(2):
        target = number(users_ref[0], 1 + tower)
        values = hidden_ref[0, tower * rows : (tower + 1) * rows, :]
        for k, out_ref in enumerate(out_refs):
            onehot = (place == target - (me_ref[0] ^ k) * span).astype(F32).astype(BF16)
            out_ref[tower, 0] = mm(onehot, values, 1, 0).astype(BF16)


def slot_hidden(me, users, hidden, groups):
    blocks, height, rows = users.shape
    width = hidden.shape[2]
    span = EXPERTS * CAP // groups
    return pl.pallas_call(
        hidden_kernel,
        grid=(blocks,),
        in_specs=[
            SCALARS,
            pl.BlockSpec((1, EXTRA, rows), lambda b: (b, rows // EXTRA, 0)),
            pl.BlockSpec((1, 2 * rows, width), lambda b: (b, 0, 0)),
        ],
        out_specs=[pl.BlockSpec((2, 1, span, width), lambda b: (0, b, 0, 0))] * groups,
        out_shape=[jax.ShapeDtypeStruct((2, blocks, span, width), BF16)] * groups,
        cost_estimate=pl.CostEstimate(
            flops=4 * blocks * EXPERTS * CAP * rows * width,
            bytes_accessed=2 * blocks * (rows + EXPERTS * CAP) * width * 2,
            transcendentals=0,
        ),
    )(me, users, hidden)


def route_kernel(me_ref, target_ref, *refs, tower, count):
    total = refs[0][...]
    for ref in refs[1:count]:
        total = total + ref[...]
    low = total.astype(BF16)
    span = refs[count].shape[0]
    place = lax.broadcasted_iota(jnp.int32, (span, low.shape[0]), 0)
    target = target_ref[tower : tower + 1, :]
    for k, out_ref in enumerate(refs[count:]):
        onehot = (place == target - (me_ref[0] ^ k) * span).astype(F32).astype(BF16)
        out_ref[...] = mm(onehot, low, 1, 0).astype(BF16)


def route(me, targets, pieces, tower, groups):
    rows, emb = pieces[0].shape
    span = EXPERTS * CAP // groups
    return pl.pallas_call(
        functools.partial(route_kernel, tower=tower, count=len(pieces)),
        in_specs=[SCALARS] + [pl.BlockSpec(memory_space=pltpu.VMEM)] * (1 + len(pieces)),
        out_shape=[jax.ShapeDtypeStruct((span, emb), BF16)] * groups,
        cost_estimate=pl.CostEstimate(
            flops=2 * EXPERTS * CAP * rows * emb,
            bytes_accessed=len(pieces) * rows * emb * 4 + EXPERTS * CAP * emb * 2,
            transcendentals=0,
        ),
    )(me, targets, *pieces)


def outer_kernel(*refs):
    *hidden_refs, grad_ref, out_ref = refs
    _, blocks, span, width = hidden_refs[0].shape
    emb = grad_ref.shape[-1]
    for e in range(span // CAP):
        here = slice(e * CAP, (e + 1) * CAP)
        left = [ref[0, :, here, :].reshape(blocks * CAP, width) for ref in hidden_refs]
        right = [
            grad_ref[:, k, here, :].reshape(blocks * CAP, emb) for k in range(len(hidden_refs))
        ]
        out_ref[e] = mm(jnp.concatenate(left), jnp.concatenate(right), 0, 0)


def outer(hidden, grad, tower):
    _, blocks, span, width = hidden[0].shape
    emb = grad.shape[-1]
    own = span // CAP
    return pl.pallas_call(
        outer_kernel,
        grid=(1,),
        in_specs=[pl.BlockSpec((1, blocks, span, width), lambda _: (tower, 0, 0, 0))] * len(hidden)
        + [pl.BlockSpec(grad.shape, lambda _: (0, 0, 0, 0))],
        out_specs=pl.BlockSpec((own, width, emb), lambda _: (0, 0, 0)),
        out_shape=jax.ShapeDtypeStruct((own, width, emb), F32),
        compiler_params=pltpu.CompilerParams(vmem_limit_bytes=40 * MIB),
        cost_estimate=pl.CostEstimate(
            flops=2 * own * width * emb * len(hidden) * blocks * CAP,
            bytes_accessed=len(hidden) * blocks * span * (width + emb) * 2 + own * width * emb * 4,
            transcendentals=0,
        ),
    )(*hidden, grad)


def shards(user_emb, item_emb, user_hidden, item_hidden, user_expert, item_expert, positive):
    rows, emb = user_emb.shape
    groups = lax.axis_size("user")
    parts = lax.axis_size("item")
    width = user_hidden.shape[1] // parts
    me = lax.axis_index("user").astype(jnp.int32)
    others = me ^ jnp.arange(groups, dtype=jnp.int32)
    first = (lax.axis_index("item").astype(jnp.int32) * groups + others) * rows
    me = me.reshape(1)

    packed, targets = pack(user_emb, positive, user_expert, item_expert)
    users = lax.all_gather(packed, "item", axis=0)
    items = exchange([item_emb] * groups, "user")

    def by_part(hidden):
        return hidden.reshape(rows, parts, width).transpose(1, 0, 2)

    cut = jnp.concatenate([by_part(user_hidden), by_part(item_hidden)], axis=1)
    cols = lax.all_to_all(cut, "item", split_axis=0, concat_axis=0, tiled=True)

    gathered = lax.all_gather(stats(first, users, items, rows), "item", axis=0)
    gathered, cols = lax.optimization_barrier((gathered, cols))
    hidden_rows = exchange(slot_hidden(me, users, cols, groups), "user")

    losses, user_part, item_parts = grads(first, users, items, gathered, rows)
    row_loss = lax.dynamic_slice_in_dim(losses[0], lax.axis_index("item") * rows, rows)
    item_pieces = exchange(item_parts, "user")
    user_grad = lax.psum_scatter(user_part, "item", scatter_dimension=0, tiled=True)

    def spread(pieces, tower):
        got = exchange(route(me, targets, pieces, tower, groups), "user")
        return lax.all_gather(jnp.stack(got), "item", axis=0)

    item_weight_grad = outer(hidden_rows, spread(item_pieces, 1), 1)
    user_weight_grad = outer(hidden_rows, spread([user_grad], 0), 0)
    return (row_loss, user_weight_grad, item_weight_grad)


def solution(mesh):
    placed = (
        P(("user", "item"), None),
        P(("item", "user"), None),
        P(("user", "item"), None),
        P(("item", "user"), None),
        P(("user", "item"), None),
        P(("item", "user"), None),
        P(("user", "item")),
    )
    return jax.shard_map(
        shards,
        mesh=mesh,
        in_specs=placed,
        out_specs=(P(("user", "item")), P("user", "item", None), P("user", "item", None)),
        check_vma=False,
    )
```

time: 465 us -> 209 us (0.45)
  the two profiles are of different devices: /device:TPU:11 before, /device:TPU:0 now
where the time goes in v1:
time: 209 us; the launch traced here: 208 us
  waiting for transfers between devices  98.8 us (47%)
  Pallas kernels  28.2 us (13%)
  starting transfers between devices  24.2 us (12%)
  blocking collectives  24 us (11%)
  local copies, waits for them, and re-layouts  14.4 us (7%)
  between operations  13.9 us (7%)
  other arithmetic  4.63 us (2%)
    ppermute x15, waiting for transfers between devices, exchange(): lax.ppermute(piece, axis, [(j, j ^ k) for j in range(size)])  66 us
    all_gather x1, blocking collectives, shards(): gathered = lax.all_gather(stats(first, users, items, rows), 'item', axis=0)  24 us
    all_gather x1, waiting for transfers between devices, shards(): users = lax.all_gather(packed, 'item', axis=0)  23.7 us
    ppermute x15, starting transfers between devices, exchange(): lax.ppermute(piece, axis, [(j, j ^ k) for j in range(size)])  17.6 us
    unnamed x32, local copies, waits for them, and re-layouts  12.7 us
    reduce_scatter x1, waiting for transfers between devices, shards(): lax.psum_scatter(user_part, 'item', scatter_dimension=0, tiled=True)  9.05 us
    pallas_call x1, Pallas kernels, slot_hidden(): pl.pallas_call(hidden_kernel, grid=(blocks,), in_specs=[SCALARS, pl.Block...  7.17 us
    pallas_call x1, Pallas kernels, grads(): pl.pallas_call(functools.partial(grad_kernel, rows=rows, chunk=64, count=...  7.02 us
  transfers between devices with their start and end apart: 20, of which 15 were waited for; matrix products, arithmetic and copies ran while one was open for 2% of the time, Pallas kernels for 9%

profile of v1, /device:TPU:0, one launch (start us, length us, event | category | flops | bytes accessed | tf_op | source)
XLA Modules:
  0.0 208.1 jit_solution(17495171393533468184)
XLA Ops:
  7.2 1.6 copy.16
  11.8 6.5 %all-to-all-start = ((bf16[8,512,256]{2,1,0:T(8,128)(2,1)}), bf16[8,512,256]{2,1,0:T(8,128)(2,1)}, u32[]{:S(2)}, u32[]{:S(2)}) async-start(bf16[8,512,256]{2,1,0:T(8,128)(2,1)} %pad_maximum_fusion), calls=%async_computation | async-start | bytes 4194304 | tf_op jit(solution)/shard_map/all_to_all | solution.py:324
  18.3 1.8 shard_map.94
  20.2 1.6 collective-permute-start
  21.7 1.5 collective-permute-start.1
  23.7 2.7 %collective-permute-done.refs_1_ = bf16[256,256]{1,0:T(8,128)(2,1)S(1)} collective-permute-done((bf16[256,256]{1,0:T(8,128)(2,1)S(1)}, bf16[256,256]{1,0:T(8,128)(2,1)S(1)}, u32[]{:S(2)}, u32[]{:S(2)}) %collective-permute-start) | collective-permute-done | bytes 131104 | tf_op jit(solution)/shard_map/ppermute | solution.py:37
  26.4 3.7 %collective-permute-done.1.refs_2_ = bf16[256,256]{1,0:T(8,128)(2,1)S(1)} collective-permute-done((bf16[256,256]{1,0:T(8,128)(2,1)S(1)}, bf16[256,256]{1,0:T(8,128)(2,1)S(1)}, u32[]{:S(2)}, u32[]{:S(2)}) %collective-permute-start.1) | collective-permute-done | bytes 131104 | tf_op jit(solution)/shard_map/ppermute | solution.py:37
  30.1 23.7 %all-gather.9.cloned.1.call-done = bf16[2176,256]{1,0:T(8,128)(2,1)} async-done(((bf16[272,256]{1,0:T(8,128)(2,1)}), bf16[2176,256]{1,0:T(8,128)(2,1)}) %all-gather.9.cloned.1.call-update) | async-done | bytes 1114128 | tf_op jit(solution)/shard_map/all_gather | solution.py:317
  55.1 4.1 %shard_map.95 = f32[3,2048]{1,0:T(4,128)S(1)} custom-call(s32[4]{0:T(128)S(1)} %add_multiply_fusion.first_ref, bf16[8,272,256]{2,1,0:T(8,128)(2,1)S(1)} %bitcast.25, bf16[256,256]{1,0:T(8,128)(2,1)S(1)} %copy-done.10, bf16[256,256]{1,0:T(8,128)(2,1)S(1)} %collective-permute-done.refs_1_, bf16[256,256]{1,0:T(8,128)(2,1)S(1)} %collective-permute-done.1.refs_2_, ...), custom_call_target="tpu_custom_call" | custom-call | flops 6442450944 | bytes 1572864 | tf_op jit(solution)/shard_map/pallas_call | solution.py:111
  59.2 24.0 %all-gather.4.stats_ref = f32[8,3,2048]{2,1,0:T(4,128)S(1)} all-gather(f32[1,3,2048]{2,1,0:T(4,128)S(1)} %bitcast.23), channel_id=3, replica_groups=mesh['user'=4,'item'=8] {'item'}, dimensions={0}, use_global_device_ids=true | all-gather | bytes 221184 | tf_op jit(solution)/shard_map/all_gather | solution.py:326
  83.2 7.0 %shard_map.96 = (f32[1,2048]{1,0:T(1,128)S(1)}, f32[2048,256]{1,0:T(8,128)}, f32[256,256]{1,0:T(8,128)S(1)}, f32[256,256]{1,0:T(8,128)S(1)}, f32[256,256]{1,0:T(8,128)S(1)}, /*index=5*/f32[256,256]{1,0:T(8,128)S(1)}) custom-call(s32[4]{0:T(128)S(1)} %add_multiply_fusion.first_ref, bf16[8,272,256]{2,1,0:T(8,128)(2,1)S(1)} %bitcast.26, ...), custom_call_target="tpu_custom_call" | custom-call | flops 8589934592 | bytes 4718592 | tf_op jit(solution)/shard_map/pallas_call | solution.py:177
  91.0 1.6 collective-permute-start.9
  92.6 1.5 collective-permute-start.10
  94.6 5.6 %collective-permute-done.9.refs_1_ = f32[256,256]{1,0:T(8,128)S(1)} collective-permute-done((f32[256,256]{1,0:T(8,128)S(1)}, f32[256,256]{1,0:T(8,128)S(1)}, u32[]{:S(2)}, u32[]{:S(2)}) %collective-permute-start.9) | collective-permute-done | bytes 262176 | tf_op jit(solution)/shard_map/ppermute | solution.py:37
  100.2 6.3 %collective-permute-done.10.refs_2_ = f32[256,256]{1,0:T(8,128)S(1)} collective-permute-done((f32[256,256]{1,0:T(8,128)S(1)}, f32[256,256]{1,0:T(8,128)S(1)}, u32[]{:S(2)}, u32[]{:S(2)}) %collective-permute-start.10) | collective-permute-done | bytes 262176 | tf_op jit(solution)/shard_map/ppermute | solution.py:37
  107.3 2.1 %shard_map.100 = (bf16[128,256]{1,0:T(8,128)(2,1)}, bf16[128,256]{1,0:T(8,128)(2,1)}, bf16[128,256]{1,0:T(8,128)(2,1)}, bf16[128,256]{1,0:T(8,128)(2,1)}) custom-call(s32[1]{0:T(128)} %bitcast.10.me_ref, s32[2,256]{1,0:T(2,128)} %get-tuple-element.33.target_ref, f32[256,256]{1,0:T(8,128)} %copy-done.7, f32[256,256]{1,0:T(8,128)} %copy-done.12, ...), custom_call_target="tpu_custom_call" | custom-call | flops 67108864 | bytes 1310720 | tf_op jit(solution)/shard_map/pallas_call | solution.py:261
  112.9 2.5 %collective-permute-done.14 = bf16[128,256]{1,0:T(8,128)(2,1)S(1)} collective-permute-done((bf16[128,256]{1,0:T(8,128)(2,1)}, bf16[128,256]{1,0:T(8,128)(2,1)S(1)}, u32[]{:S(2)}, u32[]{:S(2)}) %collective-permute-start.14) | collective-permute-done | bytes 65568 | tf_op jit(solution)/shard_map/ppermute | solution.py:37
  116.5 1.6 pad_maximum_fusion.2
  118.1 9.0 %reduce-scatter.2.cloned.1.call-done.refs_0_ = f32[256,256]{1,0:T(8,128)} async-done(((f32[2048,256]{1,0:T(8,128)}), f32[256,256]{1,0:T(8,128)}) %reduce-scatter.2.cloned.1.call-update) | async-done | bytes 262160 | tf_op jit(solution)/shard_map/reduce_scatter | solution.py:333
  127.2 1.8 shard_map.98
  129.0 2.4 %collective-permute-start.8 = (bf16[128,256]{1,0:T(8,128)(2,1)}, bf16[128,256]{1,0:T(8,128)(2,1)S(1)}, u32[]{:S(2)}, u32[]{:S(2)}) collective-permute-start(bf16[128,256]{1,0:T(8,128)(2,1)} %get-tuple-element.38), channel_id=1, source_target_pairs={{0,24},{8,16},{16,8},{24,0},{1,25},{9,17},{17,9},{25,1},{2,26},{10... | collective-permute-start | bytes 196616 | tf_op jit(solution)/shard_map/ppermute | solution.py:37
  132.5 1.9 collective-permute-done.8
  136.4 1.6 pad_maximum_fusion.1
  138.0 7.2 %shard_map.97 = (bf16[2,8,128,256]{3,2,1,0:T(8,128)(2,1)}, bf16[2,8,128,256]{3,2,1,0:T(8,128)(2,1)}, bf16[2,8,128,256]{3,2,1,0:T(8,128)(2,1)}, bf16[2,8,128,256]{3,2,1,0:T(8,128)(2,1)}) custom-call(s32[1]{0:T(128)} %bitcast.10.me_ref, bf16[8,272,256]{2,1,0:T(8,128)(2,1)} %bitcast.24, bf16[8,512,256]{2,1,0:T(8,128)(2,1)} %all-to-all-done.hidden_ref), custom_call_target="tpu_custom_call" | custom-call | flops 1073741824 | bytes 6291456 | tf_op jit(solution)/shard_map/pallas_call | solution.py:227
  145.8 1.5 collective-permute-start.4
  149.3 22.3 %collective-permute-done.3.refs_1_ = bf16[2,8,128,256]{3,2,1,0:T(8,128)(2,1)S(1)} collective-permute-done((bf16[2,8,128,256]{3,2,1,0:T(8,128)(2,1)}, bf16[2,8,128,256]{3,2,1,0:T(8,128)(2,1)S(1)}, u32[]{:S(2)}, u32[]{:S(2)}) %collective-permute-start.3) | collective-permute-done | bytes 1048608 | tf_op jit(solution)/shard_map/ppermute | solution.py:37
  171.5 16.4 %collective-permute-done.4.refs_2_ = bf16[2,8,128,256]{3,2,1,0:T(8,128)(2,1)S(1)} collective-permute-done((bf16[2,8,128,256]{3,2,1,0:T(8,128)(2,1)}, bf16[2,8,128,256]{3,2,1,0:T(8,128)(2,1)S(1)}, u32[]{:S(2)}, u32[]{:S(2)}) %collective-permute-start.4) | collective-permute-done | bytes 1048608 | tf_op jit(solution)/shard_map/ppermute | solution.py:37
  188.0 1.5 collective-permute-done.5.refs_3_
  193.0 1.6 copy-done.5
  194.6 2.1 %shard_map.101 = f32[8,256,256]{2,1,0:T(8,128)} custom-call(bf16[2,8,128,256]{3,2,1,0:T(8,128)(2,1)S(1)} %copy-done, bf16[2,8,128,256]{3,2,1,0:T(8,128)(2,1)S(1)} %collective-permute-done.3.refs_1_, bf16[2,8,128,256]{3,2,1,0:T(8,128)(2,1)S(1)} %collective-permute-done.4.refs_2_, bf16[2,8,128,256]{3,2,1,0:T(8,128)(2,1)S(1)} %copy-done.3, ...), custom_call_target="tpu_custom_call" | custom-call | flops 536870912 | bytes 6291456 | tf_op jit(solution)/shard_map/pallas_call | solution.py:290
  197.9 1.6 copy-done.6
  199.5 2.1 shard_map.99
  (60 shorter events, 21.9 us)
Async XLA Ops:
  7.2 2.1 %copy-start.11 = (bf16[256,2048]{1,0:T(8,128)(2,1)S(1)}, bf16[256,2048]{1,0:T(8,128)(2,1)}, u32[]{:S(2)}) copy-start(bf16[256,2048]{1,0:T(8,128)(2,1)} %param.9) | copy-start | bytes 3145732
  11.8 8.3 %copy-start.10 = (bf16[256,256]{1,0:T(8,128)(2,1)S(1)}, bf16[256,256]{1,0:T(8,128)(2,1)}, u32[]{:S(2)}) copy-start(bf16[256,256]{1,0:T(8,128)(2,1)} %refs_0_.3) | copy-start | bytes 393220
  11.8 71.4 %all-to-all-start = ((bf16[8,512,256]{2,1,0:T(8,128)(2,1)}), bf16[8,512,256]{2,1,0:T(8,128)(2,1)}, u32[]{:S(2)}, u32[]{:S(2)}) async-start(bf16[8,512,256]{2,1,0:T(8,128)(2,1)} %pad_maximum_fusion), calls=%async_computation | async-start | bytes 4194304 | tf_op jit(solution)/shard_map/all_to_all | solution.py:324
  18.3 35.5 %all-gather.9.cloned.1.call-start = ((), (), s32[]{:S(2)}) async-start(), calls=%async_computation.3 | async-start | bytes 1253376 | tf_op jit(solution)/shard_map/all_gather | solution.py:317
  20.1 107.1 %reduce-scatter.2.cloned.1.call-start = ((), (), s32[]{:S(2)}) async-start(), calls=%async_computation.2 | async-start | bytes 2359296 | tf_op jit(solution)/shard_map/reduce_scatter | solution.py:333
  20.2 6.3 %collective-permute-start = (bf16[256,256]{1,0:T(8,128)(2,1)S(1)}, bf16[256,256]{1,0:T(8,128)(2,1)S(1)}, u32[]{:S(2)}, u32[]{:S(2)}) collective-permute-start(bf16[256,256]{1,0:T(8,128)(2,1)S(1)} %copy-done.10), channel_id=1, source_target_pairs={{0,8},{8,0},{16,24},{24,16},{1,9},{9,1},{17,25},{25,17},{2,10},{10... | collective-permute-start | bytes 393224 | tf_op jit(solution)/shard_map/ppermute | solution.py:37
  21.7 8.4 %collective-permute-start.1 = (bf16[256,256]{1,0:T(8,128)(2,1)S(1)}, bf16[256,256]{1,0:T(8,128)(2,1)S(1)}, u32[]{:S(2)}, u32[]{:S(2)}) collective-permute-start(bf16[256,256]{1,0:T(8,128)(2,1)S(1)} %copy-done.10), channel_id=1, source_target_pairs={{0,16},{8,24},{16,0},{24,8},{1,17},{9,25},{17,1},{25,9},{2,18},{10... | collective-permute-start | bytes 393224 | tf_op jit(solution)/shard_map/ppermute | solution.py:37
  23.2 6.9 %collective-permute-start.2 = (bf16[256,256]{1,0:T(8,128)(2,1)S(1)}, bf16[256,256]{1,0:T(8,128)(2,1)S(1)}, u32[]{:S(2)}, u32[]{:S(2)}) collective-permute-start(bf16[256,256]{1,0:T(8,128)(2,1)S(1)} %copy-done.10), channel_id=1, source_target_pairs={{0,24},{8,16},{16,8},{24,0},{1,25},{9,17},{17,9},{25,1},{2,26},{10... | collective-permute-start | bytes 393224 | tf_op jit(solution)/shard_map/ppermute | solution.py:37
  53.8 1.2 copy-start.8
  55.1 28.2 %copy-start.9 = (bf16[2176,256]{1,0:T(8,128)(2,1)S(1)}, bf16[2176,256]{1,0:T(8,128)(2,1)}, u32[]{:S(2)}) copy-start(bf16[2176,256]{1,0:T(8,128)(2,1)} %all-gather.9.cloned.1.call-done) | copy-start | bytes 3342340
  91.0 99.5 %all-gather.13.cloned.1.call-start = ((), (), s32[]{:S(2)}) async-start(), calls=%async_computation.5 | async-start | bytes 2359296 | tf_op jit(solution)/shard_map/all_gather | solution.py:337
  91.0 9.2 %collective-permute-start.9 = (f32[256,256]{1,0:T(8,128)S(1)}, f32[256,256]{1,0:T(8,128)S(1)}, u32[]{:S(2)}, u32[]{:S(2)}) collective-permute-start(f32[256,256]{1,0:T(8,128)S(1)} %get-tuple-element.40), channel_id=1, source_target_pairs={{0,8},{8,0},{16,24},{24,16},{1,9},{9,1},{17,25},{25,17},{2,10},{10... | collective-permute-start | bytes 786440 | tf_op jit(solution)/shard_map/ppermute | solution.py:37
  92.6 13.9 %collective-permute-start.10 = (f32[256,256]{1,0:T(8,128)S(1)}, f32[256,256]{1,0:T(8,128)S(1)}, u32[]{:S(2)}, u32[]{:S(2)}) collective-permute-start(f32[256,256]{1,0:T(8,128)S(1)} %get-tuple-element.41), channel_id=1, source_target_pairs={{0,16},{8,24},{16,0},{24,8},{1,17},{9,25},{17,1},{25,9},{2,18},{10... | collective-permute-start | bytes 786440 | tf_op jit(solution)/shard_map/ppermute | solution.py:37
  94.1 12.4 %collective-permute-start.11 = (f32[256,256]{1,0:T(8,128)S(1)}, f32[256,256]{1,0:T(8,128)S(1)}, u32[]{:S(2)}, u32[]{:S(2)}) collective-permute-start(f32[256,256]{1,0:T(8,128)S(1)} %get-tuple-element.42), channel_id=1, source_target_pairs={{0,24},{8,16},{16,8},{24,0},{1,25},{9,17},{17,9},{25,1},{2,26},{10... | collective-permute-start | bytes 786440 | tf_op jit(solution)/shard_map/ppermute | solution.py:37
  100.2 6.3 %copy-start.12 = (f32[256,256]{1,0:T(8,128)}, f32[256,256]{1,0:T(8,128)S(1)}, u32[]{:S(2)}) copy-start(f32[256,256]{1,0:T(8,128)S(1)} %collective-permute-done.9.refs_1_) | copy-start | bytes 786436
  109.4 6.0 %collective-permute-start.14 = (bf16[128,256]{1,0:T(8,128)(2,1)}, bf16[128,256]{1,0:T(8,128)(2,1)S(1)}, u32[]{:S(2)}, u32[]{:S(2)}) collective-permute-start(bf16[128,256]{1,0:T(8,128)(2,1)} %get-tuple-element.46), channel_id=1, source_target_pairs={{0,24},{8,16},{16,8},{24,0},{1,25},{9,17},{17,9},{25,1},{2,26},{10... | collective-permute-start | bytes 196616 | tf_op jit(solution)/shard_map/ppermute | solution.py:37
  110.9 4.9 %collective-permute-start.13 = (bf16[128,256]{1,0:T(8,128)(2,1)}, bf16[128,256]{1,0:T(8,128)(2,1)S(1)}, u32[]{:S(2)}, u32[]{:S(2)}) collective-permute-start(bf16[128,256]{1,0:T(8,128)(2,1)} %get-tuple-element.45), channel_id=1, source_target_pairs={{0,16},{8,24},{16,0},{24,8},{1,17},{9,25},{17,1},{25,9},{2,18},{10... | collective-permute-start | bytes 196616 | tf_op jit(solution)/shard_map/ppermute | solution.py:37
  112.0 4.5 %collective-permute-start.12 = (bf16[128,256]{1,0:T(8,128)(2,1)}, bf16[128,256]{1,0:T(8,128)(2,1)S(1)}, u32[]{:S(2)}, u32[]{:S(2)}) collective-permute-start(bf16[128,256]{1,0:T(8,128)(2,1)} %get-tuple-element.44), channel_id=1, source_target_pairs={{0,8},{8,0},{16,24},{24,16},{1,9},{9,1},{17,25},{25,17},{2,10},{10... | collective-permute-start | bytes 196616 | tf_op jit(solution)/shard_map/ppermute | solution.py:37
  118.1 78.6 %all-gather.11.cloned.1.call-start = ((), (), s32[]{:S(2)}) async-start(), calls=%async_computation.4 | async-start | bytes 2359296 | tf_op jit(solution)/shard_map/all_gather | solution.py:337
  129.0 5.4 %collective-permute-start.8 = (bf16[128,256]{1,0:T(8,128)(2,1)}, bf16[128,256]{1,0:T(8,128)(2,1)S(1)}, u32[]{:S(2)}, u32[]{:S(2)}) collective-permute-start(bf16[128,256]{1,0:T(8,128)(2,1)} %get-tuple-element.38), channel_id=1, source_target_pairs={{0,24},{8,16},{16,8},{24,0},{1,25},{9,17},{17,9},{25,1},{2,26},{10... | collective-permute-start | bytes 196616 | tf_op jit(solution)/shard_map/ppermute | solution.py:37
  131.4 4.5 %collective-permute-start.7 = (bf16[128,256]{1,0:T(8,128)(2,1)}, bf16[128,256]{1,0:T(8,128)(2,1)S(1)}, u32[]{:S(2)}, u32[]{:S(2)}) collective-permute-start(bf16[128,256]{1,0:T(8,128)(2,1)} %get-tuple-element.37), channel_id=1, source_target_pairs={{0,16},{8,24},{16,0},{24,8},{1,17},{9,25},{17,1},{25,9},{2,18},{10... | collective-permute-start | bytes 196616 | tf_op jit(solution)/shard_map/ppermute | solution.py:37
  131.9 4.5 %collective-permute-start.6 = (bf16[128,256]{1,0:T(8,128)(2,1)}, bf16[128,256]{1,0:T(8,128)(2,1)S(1)}, u32[]{:S(2)}, u32[]{:S(2)}) collective-permute-start(bf16[128,256]{1,0:T(8,128)(2,1)} %get-tuple-element.36), channel_id=1, source_target_pairs={{0,8},{8,0},{16,24},{24,16},{1,9},{9,1},{17,25},{25,17},{2,10},{10... | collective-permute-start | bytes 196616 | tf_op jit(solution)/shard_map/ppermute | solution.py:37
  145.2 26.3 %collective-permute-start.3 = (bf16[2,8,128,256]{3,2,1,0:T(8,128)(2,1)}, bf16[2,8,128,256]{3,2,1,0:T(8,128)(2,1)S(1)}, u32[]{:S(2)}, u32[]{:S(2)}) collective-permute-start(bf16[2,8,128,256]{3,2,1,0:T(8,128)(2,1)} %get-tuple-element.30), channel_id=1, source_target_pairs={{0,8},{8,0},{16,24},{24,16},{1,9},{9,1},{17,25},{25,17},{2,10},{10... | collective-permute-start | bytes 3145736 | tf_op jit(solution)/shard_map/ppermute | solution.py:37
  145.8 42.1 %collective-permute-start.4 = (bf16[2,8,128,256]{3,2,1,0:T(8,128)(2,1)}, bf16[2,8,128,256]{3,2,1,0:T(8,128)(2,1)S(1)}, u32[]{:S(2)}, u32[]{:S(2)}) collective-permute-start(bf16[2,8,128,256]{3,2,1,0:T(8,128)(2,1)} %get-tuple-element.31), channel_id=1, source_target_pairs={{0,16},{8,24},{16,0},{24,8},{1,17},{9,25},{17,1},{25,9},{2,18},{10... | collective-permute-start | bytes 3145736 | tf_op jit(solution)/shard_map/ppermute | solution.py:37
  147.4 42.1 %collective-permute-start.5 = (bf16[2,8,128,256]{3,2,1,0:T(8,128)(2,1)}, bf16[2,8,128,256]{3,2,1,0:T(8,128)(2,1)S(1)}, u32[]{:S(2)}, u32[]{:S(2)}) collective-permute-start(bf16[2,8,128,256]{3,2,1,0:T(8,128)(2,1)} %get-tuple-element.32), channel_id=1, source_target_pairs={{0,24},{8,16},{16,8},{24,0},{1,25},{9,17},{17,9},{25,1},{2,26},{10... | collective-permute-start | bytes 3145736 | tf_op jit(solution)/shard_map/ppermute | solution.py:37
  189.5 1.0 copy-start.2
  190.5 1.2 copy-start
  191.7 1.2 copy-start.3
  193.0 1.6 copy-start.5
  194.6 2.1 %copy-start.1 = (bf16[2,8,128,256]{3,2,1,0:T(8,128)(2,1)S(1)}, bf16[2,8,128,256]{3,2,1,0:T(8,128)(2,1)}, u32[]{:S(2)}) copy-start(bf16[2,8,128,256]{3,2,1,0:T(8,128)(2,1)} %get-tuple-element.29.refs_0_) | copy-start | bytes 3145732
  196.6 1.2 copy-start.4
  197.9 1.6 copy-start.6
  (3 other events, 2.3 us)
Sparse Core Ops, SparseCore 0:
  21.3 32.4 all-gather.8
  91.1 36.0 reduce-scatter.1
  128.8 27.8 all-gather.12
  158.2 28.5 all-gather.10

commit v2 on v0

v2 whole, which is shorter than its diff:
```python
import functools
import math

import jax
import jax.numpy as jnp
from jax import lax
from jax.experimental import pallas as pl
from jax.experimental.pallas import tpu as pltpu
from jax.sharding import PartitionSpec as P

EMB = 256
EXPERTS = 32
CAP = 16
SCALE = 1.0 / math.sqrt(EMB)
EXTRA = 16
DIGIT = 128
CORES = 2
MIB = 1 << 20

F32 = jnp.float32
BF16 = jnp.bfloat16
SCALARS = pl.BlockSpec(memory_space=pltpu.SMEM)
WHOLE = pl.BlockSpec(memory_space=pltpu.VMEM)


def mm(a, b, ca, cb):
    return lax.dot_general(a, b, (((ca,), (cb,)), ((), ())), preferred_element_type=F32)


def number(rows, index):
    rows = rows.astype(F32)
    high = rows[2 * index : 2 * index + 1]
    return (high * DIGIT + rows[2 * index + 1 : 2 * index + 2]).astype(jnp.int32)


def swap(piece, axis, bits):
    size = lax.axis_size(axis)
    return lax.ppermute(piece, axis, [(j, j ^ bits) for j in range(size)])


def exchange(pieces, axis, unit=1):
    return [piece if k == 0 else swap(piece, axis, k * unit) for k, piece in enumerate(pieces)]


def tie(*values):
    return lax.optimization_barrier(values)


def pack_kernel(emb_ref, positive_ref, user_ref, item_ref, out_ref):
    rows = emb_ref.shape[0]
    down = lax.broadcasted_iota(jnp.int32, (rows, rows), 0)
    across = lax.broadcasted_iota(jnp.int32, (rows, rows), 1)

    def slots(expert):
        wide = jnp.broadcast_to(expert.astype(F32), (rows, rows))
        before = jnp.where((wide == wide.T) & (down < across), 1.0, 0.0)
        return expert * CAP + jnp.sum(before, axis=0, keepdims=True).astype(jnp.int32)

    user = slots(user_ref[...])
    item = slots(item_ref[...])
    line = lax.broadcasted_iota(jnp.int32, (EXTRA, rows), 0)
    block = jnp.zeros((EXTRA, rows), jnp.int32)
    for index, values in enumerate((positive_ref[...], user, item)):
        block = jnp.where(line == 2 * index, values // DIGIT, block)
        block = jnp.where(line == 2 * index + 1, values % DIGIT, block)
    out_ref[:rows, :] = emb_ref[...]
    out_ref[rows:, :] = block.astype(F32).astype(BF16)


def pack(emb, positive, user_expert, item_expert):
    rows, width = emb.shape
    return pl.pallas_call(
        pack_kernel,
        out_shape=jax.ShapeDtypeStruct((rows + EXTRA, width), BF16),
    )(emb, positive.reshape(1, rows), user_expert.reshape(1, rows), item_expert.reshape(1, rows))


def stats_kernel(first_ref, *refs, blocks, count, chunk):
    users_refs, items_refs = refs[:blocks], refs[blocks : blocks + count]
    out_ref, all_ref, col_ref, s_ref = refs[blocks + count :]
    own, emb = items_refs[0].shape
    rows = users_refs[0].shape[0] - EXTRA
    n_cols = own * count
    for k, ref in enumerate(users_refs):
        all_ref[k] = ref[...]
    for k, ref in enumerate(items_refs):
        col_ref[k * own : (k + 1) * own, :] = ref[...]

    def pair(step, carry):
        for half in range(2):
            block = step * 2 + half
            queries = all_ref[block, :rows, :] * jnp.asarray(SCALE, BF16)
            s_ref[half] = mm(col_ref[...], queries, 1, 1)
            positive = number(all_ref[block, rows:, :], 0)
            tops = jnp.full((8, rows), -jnp.inf, F32)
            for c in range(0, n_cols, chunk):
                part = s_ref[half, c : c + chunk, :]
                tops = jnp.maximum(tops, jnp.max(part.reshape(chunk // 8, 8, rows), axis=0))
            top = jnp.max(tops, axis=0, keepdims=True)
            total = jnp.zeros((8, rows), F32)
            picked = jnp.zeros((8, rows), F32)
            for c in range(0, n_cols, chunk):
                part = s_ref[half, c : c + chunk, :]
                probs = jnp.exp(part - top)
                total = total + jnp.sum(probs.reshape(chunk // 8, 8, rows), axis=0)
                wanted = positive - (first_ref[c // own] + c % own)
                hit = lax.broadcasted_iota(jnp.int32, (chunk, rows), 0) == wanted
                chosen = jnp.where(hit, part, 0.0)
                picked = picked + jnp.sum(chosen.reshape(chunk // 8, 8, rows), axis=0)
            out_ref[block, 0:1, :] = top
            out_ref[block, 1:2, :] = jnp.sum(total, axis=0, keepdims=True)
            out_ref[block, 2:3, :] = jnp.sum(picked, axis=0, keepdims=True)
        return carry

    lax.fori_loop(0, blocks // 2, pair, 0)


def stats(first, users, items):
    height, emb = users[0].shape
    rows = height - EXTRA
    own = items[0].shape[0]
    blocks, count = len(users), len(items)
    return pl.pallas_call(
        functools.partial(stats_kernel, blocks=blocks, count=count, chunk=64),
        in_specs=[SCALARS] + [WHOLE] * (blocks + count),
        out_specs=WHOLE,
        out_shape=jax.ShapeDtypeStruct((blocks, 3, rows), F32),
        scratch_shapes=[
            pltpu.VMEM((blocks, height, emb), BF16),
            pltpu.VMEM((own * count, emb), BF16),
            pltpu.VMEM((2, own * count, rows), F32),
        ],
        compiler_params=pltpu.CompilerParams(vmem_limit_bytes=40 * MIB),
        cost_estimate=pl.CostEstimate(
            flops=6 * 2 * blocks * rows * own * count * emb,
            bytes_accessed=(blocks * rows + own * count) * emb * 2,
            transcendentals=blocks * rows * own * count,
        ),
    )(first, *users, *items)


def grad_kernel(first_ref, *refs, blocks, count, chunk):
    users_refs, items_refs = refs[:blocks], refs[blocks : blocks + count]
    refs = refs[blocks + count :]
    stats_refs, refs = refs[:blocks], refs[blocks:]
    loss_ref, near_ref, far_ref = refs[:3]
    user_refs, refs = refs[3 : 3 + blocks], refs[3 + blocks :]
    all_ref, col_ref, flip_ref, s_ref, g_ref, user_ref = refs
    own, emb = items_refs[0].shape
    rows = users_refs[0].shape[0] - EXTRA
    n_cols = own * count
    for k, ref in enumerate(users_refs):
        all_ref[k] = ref[...]
    for k, ref in enumerate(items_refs):
        col_ref[k * own : (k + 1) * own, :] = ref[...]
        flip_ref[:, k * own : (k + 1) * own] = ref[...].T

    def pair(step, carry):
        for half in range(2):
            block = step * 2 + half
            queries = all_ref[block, :rows, :] * jnp.asarray(SCALE, BF16)
            s_ref[half] = mm(col_ref[...], queries, 1, 1)
            positive = number(all_ref[block, rows:, :], 0)
            found = [ref[block ^ k] for k, ref in enumerate(stats_refs)]
            top = functools.reduce(jnp.maximum, [f[0:1] for f in found])
            total = sum(f[1:2] * jnp.exp(f[0:1] - top) for f in found)
            level = top + jnp.log(total)
            loss_ref[pl.ds(block, 1), :] = level - sum(f[2:3] for f in found)
            for c in range(0, n_cols, chunk):
                probs = jnp.exp(s_ref[half, c : c + chunk, :] - level)
                wanted = positive - (first_ref[c // own] + c % own)
                hit = lax.broadcasted_iota(jnp.int32, (chunk, rows), 0) == wanted
                g_ref[block, c : c + chunk, :] = jnp.where(hit, probs - 1.0, probs).astype(BF16)
            user_ref[block] = mm(flip_ref[...], g_ref[block], 1, 0).T * SCALE
        return carry

    lax.fori_loop(0, blocks // 2, pair, 0)
    for k, ref in enumerate(user_refs):
        ref[...] = user_ref[k]
    for k in range(count):
        left = jnp.concatenate([g_ref[b, k * own : (k + 1) * own, :] for b in range(blocks)], axis=1)
        right = jnp.concatenate([all_ref[b, :rows, :] for b in range(blocks)], axis=0)
        out_ref = near_ref if k < count // CORES else far_ref
        out_ref[k % (count // CORES)] = mm(left, right, 1, 0) * SCALE


def grads(first, users, items, gathered):
    height, emb = users[0].shape
    rows = height - EXTRA
    own = items[0].shape[0]
    blocks, count = len(users), len(items)
    results = pl.pallas_call(
        functools.partial(grad_kernel, blocks=blocks, count=count, chunk=64),
        in_specs=[SCALARS] + [WHOLE] * (2 * blocks + count),
        out_specs=[WHOLE] * (3 + blocks),
        out_shape=[jax.ShapeDtypeStruct((blocks, rows), F32)]
        + [jax.ShapeDtypeStruct((count // CORES, own, emb), F32)] * CORES
        + [jax.ShapeDtypeStruct((rows, emb), F32)] * blocks,
        scratch_shapes=[
            pltpu.VMEM((blocks, height, emb), BF16),
            pltpu.VMEM((own * count, emb), BF16),
            pltpu.VMEM((emb, own * count), BF16),
            pltpu.VMEM((2, own * count, rows), F32),
            pltpu.VMEM((blocks, own * count, rows), BF16),
            pltpu.VMEM((blocks, rows, emb), F32),
        ],
        compiler_params=pltpu.CompilerParams(vmem_limit_bytes=56 * MIB),
        cost_estimate=pl.CostEstimate(
            flops=8 * 2 * blocks * rows * own * count * emb,
            bytes_accessed=(blocks * rows + own * count) * emb * 6,
            transcendentals=blocks * rows * own * count,
        ),
    )(first, *users, *items, *gathered)
    return results[0][0], results[1], results[2], results[3:]


def add_kernel(a_ref, b_ref, *out_refs):
    for k, out_ref in enumerate(out_refs):
        out_ref[...] = a_ref[k] + b_ref[k]


def add(a, b):
    return pl.pallas_call(
        add_kernel,
        in_specs=[WHOLE] * 2,
        out_specs=[WHOLE] * a.shape[0],
        out_shape=[jax.ShapeDtypeStruct(a.shape[1:], F32)] * a.shape[0],
        cost_estimate=pl.CostEstimate(flops=a.size, bytes_accessed=12 * a.size, transcendentals=0),
    )(a, b)


def cut_kernel(in_ref, out_ref):
    width = out_ref.shape[2]
    for k in range(out_ref.shape[0]):
        out_ref[k] = in_ref[:, k * width : (k + 1) * width]


def cut(hidden, parts):
    rows, total = hidden.shape
    return pl.pallas_call(
        cut_kernel,
        in_specs=[WHOLE],
        out_specs=WHOLE,
        out_shape=jax.ShapeDtypeStruct((parts, rows, total // parts), hidden.dtype),
        cost_estimate=pl.CostEstimate(flops=0, bytes_accessed=4 * hidden.size, transcendentals=0),
    )(hidden)


def onehot_of(target, start, span):
    place = lax.broadcasted_iota(jnp.int32, (span, target.shape[1]), 0)
    return (place == target - start).astype(F32).astype(BF16)


def hidden_kernel(me_ref, near_ref, far_ref, hidden_ref, *out_refs, tower):
    span = out_refs[0].shape[1]
    apart = me_ref[1] ^ pl.program_id(0)
    line = apart // CORES
    extra = jnp.where(apart % CORES == 0, near_ref[line].astype(F32), far_ref[line].astype(F32))
    target = number(extra, 1 + tower)
    for k, out_ref in enumerate(out_refs):
        onehot = onehot_of(target, (me_ref[0] ^ k) * span, span)
        out_ref[0] = mm(onehot, hidden_ref[0], 1, 0).astype(BF16)


def slot_hidden(me, near, far, hidden, groups, tower):
    blocks, rows, width = hidden.shape
    span = EXPERTS * CAP // groups
    return pl.pallas_call(
        functools.partial(hidden_kernel, tower=tower),
        grid=(blocks,),
        in_specs=[
            SCALARS,
            pl.BlockSpec(near.shape, lambda b: (0, 0, 0)),
            pl.BlockSpec(far.shape, lambda b: (0, 0, 0)),
            pl.BlockSpec((1, rows, width), lambda b: (b, 0, 0)),
        ],
        out_specs=[pl.BlockSpec((1, span, width), lambda b: (b, 0, 0))] * groups,
        out_shape=[jax.ShapeDtypeStruct((blocks, span, width), BF16)] * groups,
        cost_estimate=pl.CostEstimate(
            flops=2 * blocks * EXPERTS * CAP * rows * width,
            bytes_accessed=blocks * (rows + EXPERTS * CAP) * width * 2,
            transcendentals=0,
        ),
    )(me, near, far, hidden)


def total_kernel(*refs):
    total = refs[0][...]
    for ref in refs[1:-1]:
        total = total + ref[...]
    refs[-1][...] = total.astype(BF16)


def total(pieces):
    shape = pieces[0].shape
    size = shape[0] * shape[1]
    return pl.pallas_call(
        total_kernel,
        in_specs=[WHOLE] * len(pieces),
        out_specs=WHOLE,
        out_shape=jax.ShapeDtypeStruct(shape, BF16),
        cost_estimate=pl.CostEstimate(
            flops=len(pieces) * size, bytes_accessed=4 * len(pieces) * size, transcendentals=0
        ),
    )(*pieces)


def select_kernel(me_ref, extra_ref, *refs, tower, lines):
    out_refs = refs[lines:]
    span = out_refs[0].shape[1]
    for j, grad_ref in enumerate(refs[:lines]):
        target = number(extra_ref[j], 1 + tower)
        for k, out_ref in enumerate(out_refs):
            onehot = onehot_of(target, (me_ref[0] ^ k) * span, span)
            out_ref[j] = mm(onehot, grad_ref[...], 1, 0).astype(BF16)


def select(me, extra, grads, groups, tower):
    lines = len(grads)
    rows, emb = grads[0].shape
    span = EXPERTS * CAP // groups
    return pl.pallas_call(
        functools.partial(select_kernel, tower=tower, lines=lines),
        in_specs=[SCALARS] + [WHOLE] * (1 + lines),
        out_specs=[WHOLE] * groups,
        out_shape=[jax.ShapeDtypeStruct((lines, span, emb), BF16)] * groups,
        cost_estimate=pl.CostEstimate(
            flops=2 * lines * EXPERTS * CAP * rows * emb,
            bytes_accessed=lines * (rows + EXPERTS * CAP) * emb * 2,
            transcendentals=0,
        ),
    )(me, extra, *grads)


def outer_kernel(order_ref, *refs, groups):
    hidden_refs, grad_refs, out_ref = refs[:groups], refs[groups:-1], refs[-1]
    lines = grad_refs[0].shape[0]
    for e in range(out_ref.shape[0]):
        here = slice(e * CAP, (e + 1) * CAP)
        left, right = [], []
        for index, grad_ref in enumerate(grad_refs):
            for j in range(lines):
                block = order_ref[index // groups * lines + j]
                left.append(hidden_refs[index % groups][block, here, :])
                right.append(grad_ref[j, here, :])
        out_ref[e] = mm(jnp.concatenate(left), jnp.concatenate(right), 0, 0)


def outer(order, hidden, grad):
    blocks, span, width = hidden[0].shape
    groups, emb = len(hidden), grad[0].shape[-1]
    own = span // CAP
    return pl.pallas_call(
        functools.partial(outer_kernel, groups=groups),
        in_specs=[SCALARS] + [WHOLE] * (groups + len(grad)),
        out_specs=WHOLE,
        out_shape=jax.ShapeDtypeStruct((own, width, emb), F32),
        compiler_params=pltpu.CompilerParams(vmem_limit_bytes=40 * MIB),
        cost_estimate=pl.CostEstimate(
            flops=2 * width * emb * groups * blocks * span,
            bytes_accessed=groups * blocks * span * (width + emb) * 2 + own * width * emb * 4,
            transcendentals=0,
        ),
    )(order, *hidden, *grad)


def shards(user_emb, item_emb, user_hidden, item_hidden, user_expert, item_expert, positive):
    rows, emb = user_emb.shape
    groups = lax.axis_size("user")
    parts = lax.axis_size("item")
    lines = parts // CORES
    me = lax.axis_index("user").astype(jnp.int32)
    part = lax.axis_index("item").astype(jnp.int32)
    others = me ^ jnp.arange(groups, dtype=jnp.int32)
    both = part ^ jnp.arange(CORES, dtype=jnp.int32)
    first = ((both[:, None] * groups + others[None, :]) * rows).reshape(-1)
    order = (both[:, None] ^ (CORES * jnp.arange(lines, dtype=jnp.int32))[None, :]).reshape(-1)
    me = jnp.stack([me, part])

    def by_part(hidden):
        return lax.all_to_all(cut(hidden, parts), "item", split_axis=0, concat_axis=0, tiled=True)

    def slots_of(cols, tower):
        return slot_hidden(me, extra_near, extra_far, cols, groups, tower)

    packed = pack(user_emb, positive, user_expert, item_expert)
    users = exchange([packed] * lines, "item", CORES)
    near = exchange([item_emb] * groups, "user")
    item_hidden, user_hidden, _ = tie(item_hidden, user_hidden, packed)
    item_cols = by_part(item_hidden)

    items = near + [swap(piece, "item", 1) for piece in near]
    extra_near = jnp.stack([block[rows:] for block in users])
    extra_far = swap(extra_near, "item", 1)
    gathered = exchange([stats(first, users, items)] * lines, "item", CORES)
    *gathered, item_cols, user_hidden = tie(*gathered, item_cols, user_hidden)
    user_cols = by_part(user_hidden)

    row_loss, item_near, item_far, user_parts = grads(first, users, items, gathered)
    user_pieces = exchange(user_parts, "item", CORES)
    item_cols, item_far = tie(item_cols, item_far)
    item_slots = slots_of(item_cols, 1)
    item_pieces = exchange(add(item_near, swap(item_far, "item", 1)), "user")
    *item_slots, item_pieces[0] = tie(*item_slots, item_pieces[0])
    item_rows = exchange(item_slots, "user")

    *user_pieces, user_cols = tie(*user_pieces, user_cols)
    user_lines = exchange([total(user_pieces)] * lines, "item", CORES)
    item_lines = exchange([total(item_pieces)] * lines, "item", CORES)
    user_rows = exchange(slots_of(user_cols, 0), "user")

    def spread(grad_lines, tower):
        got = exchange(select(me, extra_near, grad_lines, groups, tower), "user")
        return got + [swap(piece, "item", 1) for piece in got]

    *user_lines, item_rows[1] = tie(*user_lines, item_rows[1])
    user_grad = spread(user_lines, 0)
    item_grad = spread(item_lines, 1)
    item_weight_grad = outer(order, item_rows, item_grad)
    user_weight_grad = outer(order, user_rows, user_grad)
    return (row_loss, user_weight_grad, item_weight_grad)


def solution(mesh):
    placed = (
        P(("user", "item"), None),
        P(("item", "user"), None),
        P(("user", "item"), None),
        P(("item", "user"), None),
        P(("user", "item"), None),
        P(("item", "user"), None),
        P(("user", "item")),
    )
    return jax.shard_map(
        shards,
        mesh=mesh,
        in_specs=placed,
        out_specs=(P(("user", "item")), P("user", "item", None), P("user", "item", None)),
        check_vma=False,
    )
```

time: 465 us -> 213 us (0.46)
  waiting for transfers between devices: 285 us -> 92.6 us
  blocking collectives: 55.7 us -> 0 us
  Pallas kernels: 0 us -> 48.9 us
  matrix products: 38.2 us -> 0 us
  starting transfers between devices: 25.8 us -> 57 us
  local copies, waits for them, and re-layouts: 25.2 us -> 10.5 us
  between operations: 14 us -> 1.03 us
  other arithmetic: 10 us -> 0.8 us
  loops' own time: 5.44 us -> 0 us
    all_to_all x4 -> x2, waiting for transfers between devices: 229 us -> 0.01 us  [by_part(): lax.all_to_all(cut(hidden, parts), 'item', split_axis=0, concat_axis=0, t...]
    ppermute x0 -> x47, waiting for transfers between devices: none -> 92.6 us  [swap(): return lax.ppermute(piece, axis, [(j, j ^ bits) for j in range(size)])]
    reduce_scatter x2 -> x0, waiting for transfers between devices: 50.2 us -> none  [the longest x1 28.4 us: shards(): lax.psum_scatter(item_total, 'user', scatter_dimension=0, tiled=True)]
    pallas_call x0 -> x14, Pallas kernels: none -> 48.9 us  [the longest x2 12.3 us: slot_hidden(): pl.pallas_call(functools.partial(hidden_kernel, tower=tower), grid=(block...]
    ppermute x0 -> x47, starting transfers between devices: none -> 45.6 us  [swap(): return lax.ppermute(piece, axis, [(j, j ^ bits) for j in range(size)])]
    dot_general x22 -> x0, matrix products: 38.2 us -> none  [the longest x8 14.3 us: score_block(): lax.dot_general(queries, keys, (((1,), (1,)), ((), ())), preferred_elemen...]
    psum x1 -> x0, blocking collectives: 25.6 us -> none  [shards(): total, picked = lax.psum((total * jnp.exp(top - peak), picked), 'item')]
    all_gather x2 -> x0, blocking collectives: 20.3 us -> none  [the longest x1 10.5 us: shards(): items = lax.all_gather(item_emb, 'user', axis=0, tiled=True)]
  transfers between devices with their start and end apart: 7 -> 49, of which waited for: 7 -> 19; matrix products, arithmetic and copies ran while one was open for 6% -> 2% of each run, Pallas kernels for 0% -> 16%
where the time goes in v2:
time: 213 us; the launch traced here: 211 us
  waiting for transfers between devices  92.6 us (43%)
  starting transfers between devices  57 us (27%)
  Pallas kernels  48.9 us (23%)
  local copies, waits for them, and re-layouts  10.5 us (5%)
    ppermute x47, waiting for transfers between devices, swap(): return lax.ppermute(piece, axis, [(j, j ^ bits) for j in range(size)])  92.6 us
    ppermute x47, starting transfers between devices, swap(): return lax.ppermute(piece, axis, [(j, j ^ bits) for j in range(size)])  45.6 us
    pallas_call x2, Pallas kernels, slot_hidden(): pl.pallas_call(functools.partial(hidden_kernel, tower=tower), grid=(block...  12.3 us
    all_to_all x2, starting transfers between devices, by_part(): lax.all_to_all(cut(hidden, parts), 'item', split_axis=0, concat_axis=0, t...  11.4 us
    pallas_call x1, Pallas kernels, grads(): pl.pallas_call(functools.partial(grad_kernel, blocks=blocks, count=count,...  8.21 us
    pallas_call x2, Pallas kernels, outer(): pl.pallas_call(functools.partial(outer_kernel, groups=groups), in_specs=[...  7.06 us
    unnamed x90, local copies, waits for them, and re-layouts  6.26 us
    pallas_call x2, Pallas kernels, select(): pl.pallas_call(functools.partial(select_kernel, tower=tower, lines=lines)...  5.03 us
  transfers between devices with their start and end apart: 49, of which 19 were waited for; matrix products, arithmetic and copies ran while one was open for 2% of the time, Pallas kernels for 16%

profile of v2, /device:TPU:11, one launch (start us, length us, event | category | flops | bytes accessed | tf_op | source)
XLA Modules:
  0.0 210.7 jit_solution(8936269540437231651)
XLA Ops:
  0.6 1.7 shard_map.94.refs_0_
  2.4 2.3 %shard_map.96 = bf16[8,256,256]{2,1,0:T(8,128)(2,1)} custom-call(bf16[256,2048]{1,0:T(8,128)(2,1)} %in_ref), custom_call_target="tpu_custom_call" | custom-call | bytes 2097152 | tf_op jit(solution)/shard_map/pallas_call | solution.py:240
  4.7 5.6 %all-to-all-start = ((bf16[8,256,256]{2,1,0:T(8,128)(2,1)}), bf16[8,256,256]{2,1,0:T(8,128)(2,1)S(1)}, u32[]{:S(2)}, u32[]{:S(2)}) async-start(bf16[8,256,256]{2,1,0:T(8,128)(2,1)} %shard_map.96), calls=%async_computation | async-start | bytes 2097152 | tf_op jit(solution)/shard_map/all_to_all | solution.py:381
  15.1 2.0 collective-permute-start.1
  18.9 2.1 %collective-permute-start.7 = (bf16[256,256]{1,0:T(8,128)(2,1)S(1)}, bf16[256,256]{1,0:T(8,128)(2,1)S(1)}, u32[]{:S(2)}, u32[]{:S(2)}) collective-permute-start(bf16[256,256]{1,0:T(8,128)(2,1)S(1)} %collective-permute-done.3.refs_5_), channel_id=1, source_target_pairs={{0,1},{1,0},{2,3},{3,2},{4,5},{5,4},{6,7},{7,6},{8,9},{9,8},{10,11... | collective-permute-start | bytes 393224 | tf_op jit(solution)/shard_map/ppermute | solution.py:38
  21.1 10.4 %collective-permute-done.refs_1_ = bf16[272,256]{1,0:T(8,128)(2,1)S(1)} collective-permute-done((bf16[272,256]{1,0:T(8,128)(2,1)S(1)}, bf16[272,256]{1,0:T(8,128)(2,1)S(1)}, u32[]{:S(2)}, u32[]{:S(2)}) %collective-permute-start) | collective-permute-done | bytes 139296 | tf_op jit(solution)/shard_map/ppermute | solution.py:38
  32.5 9.7 %collective-permute-done.1.refs_2_ = bf16[272,256]{1,0:T(8,128)(2,1)S(1)} collective-permute-done((bf16[272,256]{1,0:T(8,128)(2,1)S(1)}, bf16[272,256]{1,0:T(8,128)(2,1)S(1)}, u32[]{:S(2)}, u32[]{:S(2)}) %collective-permute-start.1) | collective-permute-done | bytes 139296 | tf_op jit(solution)/shard_map/ppermute | solution.py:38
  42.2 4.7 %collective-permute-done.2.refs_3_ = bf16[272,256]{1,0:T(8,128)(2,1)S(1)} collective-permute-done((bf16[272,256]{1,0:T(8,128)(2,1)S(1)}, bf16[272,256]{1,0:T(8,128)(2,1)S(1)}, u32[]{:S(2)}, u32[]{:S(2)}) %collective-permute-start.2) | collective-permute-done | bytes 139296 | tf_op jit(solution)/shard_map/ppermute | solution.py:38
  46.9 3.6 %shard_map.95.refs_12_ = f32[4,3,256]{2,1,0:T(4,128)S(1)} custom-call(s32[8]{0:T(128)S(1)} %mul.24.first_ref, bf16[272,256]{1,0:T(8,128)(2,1)S(1)} %copy-done.10, bf16[272,256]{1,0:T(8,128)(2,1)S(1)} %collective-permute-done.refs_1_, bf16[272,256]{1,0:T(8,128)(2,1)S(1)} %collective-permute-done.1.refs_2_, ...), custom_call_target="tpu_custom_call" | custom-call | flops 6442450944 | bytes 1572864 | tf_op jit(solution)/shard_map/pallas_call | solution.py:123
  55.6 8.2 %shard_map.97 = (f32[4,256]{1,0:T(4,128)}, f32[4,256,256]{2,1,0:T(8,128)}, f32[4,256,256]{2,1,0:T(8,128)}, f32[256,256]{1,0:T(8,128)}, f32[256,256]{1,0:T(8,128)...) custom-call(s32[8]{0:T(128)} %copy-done.23, bf16[272,256]{1,0:T(8,128)(2,1)} %shard_map.94.refs_0_, ...), custom_call_target="tpu_custom_call" | custom-call | flops 8589934592 | bytes 4718592 | tf_op jit(solution)/shard_map/pallas_call | solution.py:192
  63.8 2.2 %collective-permute-start.23 = (f32[4,256,256]{2,1,0:T(8,128)}, f32[4,256,256]{2,1,0:T(8,128)S(1)}, u32[]{:S(2)}, u32[]{:S(2)}) collective-permute-start(f32[4,256,256]{2,1,0:T(8,128)} %get-tuple-element.84), channel_id=1, source_target_pairs={{0,1},{1,0},{2,3},{3,2},{4,5},{5,4},{6,7},{7,6},{8,9},{9,8},{10,11... | collective-permute-start | bytes 3145736 | tf_op jit(solution)/shard_map/ppermute | solution.py:38
  66.1 2.3 %shard_map.98 = bf16[8,256,256]{2,1,0:T(8,128)(2,1)} custom-call(bf16[256,2048]{1,0:T(8,128)(2,1)} %in_ref.1), custom_call_target="tpu_custom_call" | custom-call | bytes 2097152 | tf_op jit(solution)/shard_map/pallas_call | solution.py:240
  68.3 5.8 %all-to-all-start.1 = ((bf16[8,256,256]{2,1,0:T(8,128)(2,1)}), bf16[8,256,256]{2,1,0:T(8,128)(2,1)}, u32[]{:S(2)}, u32[]{:S(2)}) async-start(bf16[8,256,256]{2,1,0:T(8,128)(2,1)} %shard_map.98), calls=%async_computation.1 | async-start | bytes 2097152 | tf_op jit(solution)/shard_map/all_to_all | solution.py:381
  77.9 2.5 %shard_map.102 = (f32[256,256]{1,0:T(8,128)}, f32[256,256]{1,0:T(8,128)}, f32[256,256]{1,0:T(8,128)}, f32[256,256]{1,0:T(8,128)}) custom-call(f32[4,256,256]{2,1,0:T(8,128)} %get-tuple-element.83.a_ref, f32[4,256,256]{2,1,0:T(8,128)} %copy-done.25), custom_call_target="tpu_custom_call" | custom-call | flops 262144 | bytes 3145728 | tf_op jit(solution)/shard_map/pallas_call | solution.py:223
  85.9 6.1 %shard_map.101 = (bf16[8,128,256]{2,1,0:T(8,128)(2,1)}, bf16[8,128,256]{2,1,0:T(8,128)(2,1)}, bf16[8,128,256]{2,1,0:T(8,128)(2,1)}, bf16[8,128,256]{2,1,0:T(8,128)(2,1)}) custom-call(s32[2]{0:T(128)} %pad_add_fusion.me_ref, bf16[4,16,256]{2,1,0:T(8,128)(2,1)} %copy-done.32, bf16[4,16,256]{2,1,0:T(8,128)(2,1)} %copy-done.41, bf16[8,256,256]{2,1,0:T(8,128)(2,1)} %copy-done.24), custom_call_target="tpu_custom_call" | custom-call | flops 536870912 | bytes 3145728 | tf_op jit(solution)/shard_map/pallas_call | solution.py:268
  92.0 2.7 %collective-permute-done.36.refs_3_ = f32[256,256]{1,0:T(8,128)S(1)} collective-permute-done((f32[256,256]{1,0:T(8,128)}, f32[256,256]{1,0:T(8,128)S(1)}, u32[]{:S(2)}, u32[]{:S(2)}) %collective-permute-start.36) | collective-permute-done | bytes 262176 | tf_op jit(solution)/shard_map/ppermute | solution.py:38
  95.5 1.9 shard_map.105.refs_0_
  100.1 1.9 collective-permute-start.32
  105.3 6.4 %collective-permute-done.39.refs_3_ = bf16[256,256]{1,0:T(8,128)(2,1)S(1)} collective-permute-done((bf16[256,256]{1,0:T(8,128)(2,1)}, bf16[256,256]{1,0:T(8,128)(2,1)S(1)}, u32[]{:S(2)}, u32[]{:S(2)}) %collective-permute-start.39) | collective-permute-done | bytes 131104 | tf_op jit(solution)/shard_map/ppermute | solution.py:38
  112.8 2.5 %shard_map.106 = (bf16[4,128,256]{2,1,0:T(8,128)(2,1)}, bf16[4,128,256]{2,1,0:T(8,128)(2,1)}, bf16[4,128,256]{2,1,0:T(8,128)(2,1)}, bf16[4,128,256]{2,1,0:T(8,128)(2,1)}) custom-call(s32[2]{0:T(128)} %pad_add_fusion.me_ref, bf16[4,16,256]{2,1,0:T(8,128)(2,1)} %copy-done.32, bf16[256,256]{1,0:T(8,128)(2,1)} %shard_map.105.refs_0_, ...), custom_call_target="tpu_custom_call" | custom-call | flops 268435456 | bytes 1572864 | tf_op jit(solution)/shard_map/pallas_call | solution.py:322
  115.4 11.7 %collective-permute-done.15.refs_2_ = f32[256,256]{1,0:T(8,128)S(1)} collective-permute-done((f32[256,256]{1,0:T(8,128)S(1)}, f32[256,256]{1,0:T(8,128)S(1)}, u32[]{:S(2)}, u32[]{:S(2)}) %collective-permute-start.15) | collective-permute-done | bytes 262176 | tf_op jit(solution)/shard_map/ppermute | solution.py:38
  128.4 6.2 %collective-permute-done.16.refs_3_ = f32[256,256]{1,0:T(8,128)S(1)} collective-permute-done((f32[256,256]{1,0:T(8,128)}, f32[256,256]{1,0:T(8,128)S(1)}, u32[]{:S(2)}, u32[]{:S(2)}) %collective-permute-start.16) | collective-permute-done | bytes 262176 | tf_op jit(solution)/shard_map/ppermute | solution.py:38
  135.3 1.9 shard_map.100.refs_0_
  143.1 6.7 %collective-permute-start.43 = (bf16[4,128,256]{2,1,0:T(8,128)(2,1)}, bf16[4,128,256]{2,1,0:T(8,128)(2,1)}, u32[]{:S(2)}, u32[]{:S(2)}) collective-permute-start(bf16[4,128,256]{2,1,0:T(8,128)(2,1)} %get-tuple-element.103.refs_4_), channel_id=1, source_target_pairs={{0,1},{1,0},{2,3},{3,2},{4,5},{5,4},{6,7},{7,6},{8,9},{9,8},{10,11... | collective-permute-start | bytes 786440 | tf_op jit(solution)/shard_map/ppermute | solution.py:38
  149.8 2.3 %collective-permute-done.22.refs_3_ = bf16[256,256]{1,0:T(8,128)(2,1)S(1)} collective-permute-done((bf16[256,256]{1,0:T(8,128)(2,1)}, bf16[256,256]{1,0:T(8,128)(2,1)S(1)}, u32[]{:S(2)}, u32[]{:S(2)}) %collective-permute-start.22) | collective-permute-done | bytes 131104 | tf_op jit(solution)/shard_map/ppermute | solution.py:38
  152.9 6.1 %shard_map.99 = (bf16[8,128,256]{2,1,0:T(8,128)(2,1)}, bf16[8,128,256]{2,1,0:T(8,128)(2,1)}, bf16[8,128,256]{2,1,0:T(8,128)(2,1)}, bf16[8,128,256]{2,1,0:T(8,128)(2,1)}) custom-call(s32[2]{0:T(128)} %pad_add_fusion.me_ref, bf16[4,16,256]{2,1,0:T(8,128)(2,1)} %copy-done.32, bf16[4,16,256]{2,1,0:T(8,128)(2,1)} %copy-done.41, ...), custom_call_target="tpu_custom_call" | custom-call | flops 536870912 | bytes 3145728 | tf_op jit(solution)/shard_map/pallas_call | solution.py:268
  159.8 2.5 %shard_map.103 = (bf16[4,128,256]{2,1,0:T(8,128)(2,1)}, bf16[4,128,256]{2,1,0:T(8,128)(2,1)}, bf16[4,128,256]{2,1,0:T(8,128)(2,1)}, bf16[4,128,256]{2,1,0:T(8,128)(2,1)}) custom-call(s32[2]{0:T(128)} %pad_add_fusion.me_ref, bf16[4,16,256]{2,1,0:T(8,128)(2,1)} %copy-done.32, bf16[256,256]{1,0:T(8,128)(2,1)} %shard_map.100.refs_0_, ...), custom_call_target="tpu_custom_call" | custom-call | flops 268435456 | bytes 1572864 | tf_op jit(solution)/shard_map/pallas_call | solution.py:322
  165.9 13.2 %collective-permute-done.25.refs_5_ = bf16[4,128,256]{2,1,0:T(8,128)(2,1)} collective-permute-done((bf16[4,128,256]{2,1,0:T(8,128)(2,1)}, bf16[4,128,256]{2,1,0:T(8,128)(2,1)}, u32[]{:S(2)}, u32[]{:S(2)}) %collective-permute-start.25) | collective-permute-done | bytes 262176 | tf_op jit(solution)/shard_map/ppermute | solution.py:38
  180.5 3.9 %collective-permute-done.27.refs_7_ = bf16[4,128,256]{2,1,0:T(8,128)(2,1)} collective-permute-done((bf16[4,128,256]{2,1,0:T(8,128)(2,1)}, bf16[4,128,256]{2,1,0:T(8,128)(2,1)}, u32[]{:S(2)}, u32[]{:S(2)}) %collective-permute-start.27) | collective-permute-done | bytes 262176 | tf_op jit(solution)/shard_map/ppermute | solution.py:38
  190.3 3.5 %shard_map.107 = f32[8,256,256]{2,1,0:T(8,128)} custom-call(s32[8]{0:T(128)S(1)} %xor.47.order_ref, bf16[8,128,256]{2,1,0:T(8,128)(2,1)S(1)} %copy-done, bf16[8,128,256]{2,1,0:T(8,128)(2,1)S(1)} %collective-permute-done.24.refs_1_, bf16[8,128,256]{2,1,0:T(8,128)(2,1)S(1)} %collective-permute-done.32.refs_2_, ...), custom_call_target="tpu_custom_call" | custom-call | flops 536870912 | bytes 6291456 | tf_op jit(solution)/shard_map/pallas_call | solution.py:353
  193.7 13.3 %collective-permute-done.18.refs_2_ = bf16[8,128,256]{2,1,0:T(8,128)(2,1)S(1)} collective-permute-done((bf16[8,128,256]{2,1,0:T(8,128)(2,1)}, bf16[8,128,256]{2,1,0:T(8,128)(2,1)S(1)}, u32[]{:S(2)}, u32[]{:S(2)}) %collective-permute-start.18) | collective-permute-done | bytes 524320 | tf_op jit(solution)/shard_map/ppermute | solution.py:38
  207.1 3.6 %shard_map.104 = f32[8,256,256]{2,1,0:T(8,128)} custom-call(s32[8]{0:T(128)S(1)} %xor.47.order_ref, bf16[8,128,256]{2,1,0:T(8,128)(2,1)S(1)} %copy-done.1, bf16[8,128,256]{2,1,0:T(8,128)(2,1)S(1)} %collective-permute-done.17.refs_1_, bf16[8,128,256]{2,1,0:T(8,128)(2,1)S(1)} %collective-permute-done.18.refs_2_, ...), custom_call_target="tpu_custom_call" | custom-call | flops 536870912 | bytes 6291456 | tf_op jit(solution)/shard_map/pallas_call | solution.py:353
  (184 shorter events, 49.9 us)
Async XLA Ops:
  4.7 50.3 %all-to-all-start = ((bf16[8,256,256]{2,1,0:T(8,128)(2,1)}), bf16[8,256,256]{2,1,0:T(8,128)(2,1)S(1)}, u32[]{:S(2)}, u32[]{:S(2)}) async-start(bf16[8,256,256]{2,1,0:T(8,128)(2,1)} %shard_map.96), calls=%async_computation | async-start | bytes 2097152 | tf_op jit(solution)/shard_map/all_to_all | solution.py:381
  10.3 21.2 %collective-permute-start = (bf16[272,256]{1,0:T(8,128)(2,1)S(1)}, bf16[272,256]{1,0:T(8,128)(2,1)S(1)}, u32[]{:S(2)}, u32[]{:S(2)}) collective-permute-start(bf16[272,256]{1,0:T(8,128)(2,1)S(1)} %copy-done.10), channel_id=1, source_target_pairs={{0,2},{1,3},{2,0},{3,1},{4,6},{5,7},{6,4},{7,5},{8,10},{9,11},{10,... | collective-permute-start | bytes 417800 | tf_op jit(solution)/shard_map/ppermute | solution.py:38
  15.1 27.1 %collective-permute-start.1 = (bf16[272,256]{1,0:T(8,128)(2,1)S(1)}, bf16[272,256]{1,0:T(8,128)(2,1)S(1)}, u32[]{:S(2)}, u32[]{:S(2)}) collective-permute-start(bf16[272,256]{1,0:T(8,128)(2,1)S(1)} %copy-done.10), channel_id=1, source_target_pairs={{0,4},{1,5},{2,6},{3,7},{4,0},{5,1},{6,2},{7,3},{8,12},{9,13},{10,... | collective-permute-start | bytes 417800 | tf_op jit(solution)/shard_map/ppermute | solution.py:38
  17.1 29.8 %collective-permute-start.2 = (bf16[272,256]{1,0:T(8,128)(2,1)S(1)}, bf16[272,256]{1,0:T(8,128)(2,1)S(1)}, u32[]{:S(2)}, u32[]{:S(2)}) collective-permute-start(bf16[272,256]{1,0:T(8,128)(2,1)S(1)} %copy-done.10), channel_id=1, source_target_pairs={{0,6},{1,7},{2,4},{3,5},{4,2},{5,3},{6,0},{7,1},{8,14},{9,15},{10,... | collective-permute-start | bytes 417800 | tf_op jit(solution)/shard_map/ppermute | solution.py:38
  18.9 28.0 %collective-permute-start.7 = (bf16[256,256]{1,0:T(8,128)(2,1)S(1)}, bf16[256,256]{1,0:T(8,128)(2,1)S(1)}, u32[]{:S(2)}, u32[]{:S(2)}) collective-permute-start(bf16[256,256]{1,0:T(8,128)(2,1)S(1)} %collective-permute-done.3.refs_5_), channel_id=1, source_target_pairs={{0,1},{1,0},{2,3},{3,2},{4,5},{5,4},{6,7},{7,6},{8,9},{9,8},{10,11... | collective-permute-start | bytes 393224 | tf_op jit(solution)/shard_map/ppermute | solution.py:38
  21.0 25.9 %collective-permute-start.8 = (bf16[256,256]{1,0:T(8,128)(2,1)S(1)}, bf16[256,256]{1,0:T(8,128)(2,1)S(1)}, u32[]{:S(2)}, u32[]{:S(2)}) collective-permute-start(bf16[256,256]{1,0:T(8,128)(2,1)S(1)} %collective-permute-done.4.refs_6_), channel_id=1, source_target_pairs={{0,1},{1,0},{2,3},{3,2},{4,5},{5,4},{6,7},{7,6},{8,9},{9,8},{10,11... | collective-permute-start | bytes 393224 | tf_op jit(solution)/shard_map/ppermute | solution.py:38
  31.6 15.4 %collective-permute-start.9 = (bf16[256,256]{1,0:T(8,128)(2,1)S(1)}, bf16[256,256]{1,0:T(8,128)(2,1)S(1)}, u32[]{:S(2)}, u32[]{:S(2)}) collective-permute-start(bf16[256,256]{1,0:T(8,128)(2,1)S(1)} %collective-permute-done.5.refs_7_), channel_id=1, source_target_pairs={{0,1},{1,0},{2,3},{3,2},{4,5},{5,4},{6,7},{7,6},{8,9},{9,8},{10,11... | collective-permute-start | bytes 393224 | tf_op jit(solution)/shard_map/ppermute | solution.py:38
  63.8 13.1 %collective-permute-start.23 = (f32[4,256,256]{2,1,0:T(8,128)}, f32[4,256,256]{2,1,0:T(8,128)S(1)}, u32[]{:S(2)}, u32[]{:S(2)}) collective-permute-start(f32[4,256,256]{2,1,0:T(8,128)} %get-tuple-element.84), channel_id=1, source_target_pairs={{0,1},{1,0},{2,3},{3,2},{4,5},{5,4},{6,7},{7,6},{8,9},{9,8},{10,11... | collective-permute-start | bytes 3145736 | tf_op jit(solution)/shard_map/ppermute | solution.py:38
  68.3 66.3 %all-to-all-start.1 = ((bf16[8,256,256]{2,1,0:T(8,128)(2,1)}), bf16[8,256,256]{2,1,0:T(8,128)(2,1)}, u32[]{:S(2)}, u32[]{:S(2)}) async-start(bf16[8,256,256]{2,1,0:T(8,128)(2,1)} %shard_map.98), calls=%async_computation.1 | async-start | bytes 2097152 | tf_op jit(solution)/shard_map/all_to_all | solution.py:381
  81.9 12.8 %collective-permute-start.36 = (f32[256,256]{1,0:T(8,128)}, f32[256,256]{1,0:T(8,128)S(1)}, u32[]{:S(2)}, u32[]{:S(2)}) collective-permute-start(f32[256,256]{1,0:T(8,128)} %get-tuple-element.102), channel_id=1, source_target_pairs={{0,24},{8,16},{16,8},{24,0},{1,25},{9,17},{17,9},{25,1},{2,26},{10... | collective-permute-start | bytes 786440 | tf_op jit(solution)/shard_map/ppermute | solution.py:38
  99.8 37.4 %collective-permute-start.24 = (bf16[8,128,256]{2,1,0:T(8,128)(2,1)}, bf16[8,128,256]{2,1,0:T(8,128)(2,1)S(1)}, u32[]{:S(2)}, u32[]{:S(2)}) collective-permute-start(bf16[8,128,256]{2,1,0:T(8,128)(2,1)} %get-tuple-element.86), channel_id=1, source_target_pairs={{0,8},{8,0},{16,24},{24,16},{1,9},{9,1},{17,25},{25,17},{2,10},{10... | collective-permute-start | bytes 1572872 | tf_op jit(solution)/shard_map/ppermute | solution.py:38
  100.1 38.6 %collective-permute-start.32 = (bf16[8,128,256]{2,1,0:T(8,128)(2,1)}, bf16[8,128,256]{2,1,0:T(8,128)(2,1)S(1)}, u32[]{:S(2)}, u32[]{:S(2)}) collective-permute-start(bf16[8,128,256]{2,1,0:T(8,128)(2,1)} %get-tuple-element.97), channel_id=1, source_target_pairs={{0,16},{8,24},{16,0},{24,8},{1,17},{9,25},{17,1},{25,9},{2,18},{10... | collective-permute-start | bytes 1572872 | tf_op jit(solution)/shard_map/ppermute | solution.py:38
  102.3 13.0 %collective-permute-start.14 = (f32[256,256]{1,0:T(8,128)S(1)}, f32[256,256]{1,0:T(8,128)S(1)}, u32[]{:S(2)}, u32[]{:S(2)}) collective-permute-start(f32[256,256]{1,0:T(8,128)S(1)} %copy-done.34), channel_id=1, source_target_pairs={{0,2},{1,3},{2,0},{3,1},{4,6},{5,7},{6,4},{7,5},{8,10},{9,11},{10,... | collective-permute-start | bytes 786440 | tf_op jit(solution)/shard_map/ppermute | solution.py:38
  104.8 22.3 %collective-permute-start.15 = (f32[256,256]{1,0:T(8,128)S(1)}, f32[256,256]{1,0:T(8,128)S(1)}, u32[]{:S(2)}, u32[]{:S(2)}) collective-permute-start(f32[256,256]{1,0:T(8,128)S(1)} %copy-done.33), channel_id=1, source_target_pairs={{0,4},{1,5},{2,6},{3,7},{4,0},{5,1},{6,2},{7,3},{8,12},{9,13},{10,... | collective-permute-start | bytes 786440 | tf_op jit(solution)/shard_map/ppermute | solution.py:38
  111.7 22.9 %collective-permute-start.16 = (f32[256,256]{1,0:T(8,128)}, f32[256,256]{1,0:T(8,128)S(1)}, u32[]{:S(2)}, u32[]{:S(2)}) collective-permute-start(f32[256,256]{1,0:T(8,128)} %get-tuple-element.65), channel_id=1, source_target_pairs={{0,6},{1,7},{2,4},{3,5},{4,2},{5,3},{6,0},{7,1},{8,14},{9,15},{10,... | collective-permute-start | bytes 786440 | tf_op jit(solution)/shard_map/ppermute | solution.py:38
  115.3 24.5 %collective-permute-start.40 = (bf16[4,128,256]{2,1,0:T(8,128)(2,1)}, bf16[4,128,256]{2,1,0:T(8,128)(2,1)S(1)}, u32[]{:S(2)}, u32[]{:S(2)}) collective-permute-start(bf16[4,128,256]{2,1,0:T(8,128)(2,1)} %get-tuple-element.104), channel_id=1, source_target_pairs={{0,8},{8,0},{16,24},{24,16},{1,9},{9,1},{17,25},{25,17},{2,10},{10... | collective-permute-start | bytes 786440 | tf_op jit(solution)/shard_map/ppermute | solution.py:38
  127.1 32.6 %collective-permute-start.33 = (bf16[8,128,256]{2,1,0:T(8,128)(2,1)}, bf16[8,128,256]{2,1,0:T(8,128)(2,1)S(1)}, u32[]{:S(2)}, u32[]{:S(2)}) collective-permute-start(bf16[8,128,256]{2,1,0:T(8,128)(2,1)} %get-tuple-element.98), channel_id=1, source_target_pairs={{0,24},{8,16},{16,8},{24,0},{1,25},{9,17},{17,9},{25,1},{2,26},{10... | collective-permute-start | bytes 1572872 | tf_op jit(solution)/shard_map/ppermute | solution.py:38
  138.7 13.4 %collective-permute-start.22 = (bf16[256,256]{1,0:T(8,128)(2,1)}, bf16[256,256]{1,0:T(8,128)(2,1)S(1)}, u32[]{:S(2)}, u32[]{:S(2)}) collective-permute-start(bf16[256,256]{1,0:T(8,128)(2,1)} %shard_map.100.refs_0_), channel_id=1, source_target_pairs={{0,6},{1,7},{2,4},{3,5},{4,2},{5,3},{6,0},{7,1},{8,14},{9,15},{10,... | collective-permute-start | bytes 393224 | tf_op jit(solution)/shard_map/ppermute | solution.py:38
  139.9 19.2 %collective-permute-start.41 = (bf16[4,128,256]{2,1,0:T(8,128)(2,1)}, bf16[4,128,256]{2,1,0:T(8,128)(2,1)S(1)}, u32[]{:S(2)}, u32[]{:S(2)}) collective-permute-start(bf16[4,128,256]{2,1,0:T(8,128)(2,1)} %get-tuple-element.105), channel_id=1, source_target_pairs={{0,16},{8,24},{16,0},{24,8},{1,17},{9,25},{17,1},{25,9},{2,18},{10... | collective-permute-start | bytes 786440 | tf_op jit(solution)/shard_map/ppermute | solution.py:38
  141.5 17.7 %collective-permute-start.42 = (bf16[4,128,256]{2,1,0:T(8,128)(2,1)}, bf16[4,128,256]{2,1,0:T(8,128)(2,1)}, u32[]{:S(2)}, u32[]{:S(2)}) collective-permute-start(bf16[4,128,256]{2,1,0:T(8,128)(2,1)} %get-tuple-element.106), channel_id=1, source_target_pairs={{0,24},{8,16},{16,8},{24,0},{1,25},{9,17},{17,9},{25,1},{2,26},{10... | collective-permute-start | bytes 786440 | tf_op jit(solution)/shard_map/ppermute | solution.py:38
  143.1 19.2 %collective-permute-start.43 = (bf16[4,128,256]{2,1,0:T(8,128)(2,1)}, bf16[4,128,256]{2,1,0:T(8,128)(2,1)}, u32[]{:S(2)}, u32[]{:S(2)}) collective-permute-start(bf16[4,128,256]{2,1,0:T(8,128)(2,1)} %get-tuple-element.103.refs_4_), channel_id=1, source_target_pairs={{0,1},{1,0},{2,3},{3,2},{4,5},{5,4},{6,7},{7,6},{8,9},{9,8},{10,11... | collective-permute-start | bytes 786440 | tf_op jit(solution)/shard_map/ppermute | solution.py:38
  152.0 11.7 %collective-permute-start.44 = (bf16[4,128,256]{2,1,0:T(8,128)(2,1)S(1)}, bf16[4,128,256]{2,1,0:T(8,128)(2,1)}, u32[]{:S(2)}, u32[]{:S(2)}) collective-permute-start(bf16[4,128,256]{2,1,0:T(8,128)(2,1)S(1)} %collective-permute-done.40.refs_5_), channel_id=1, source_target_pairs={{0,1},{1,0},{2,3},{3,2},{4,5},{5,4},{6,7},{7,6},{8,9},{9,8},{10,11... | collective-permute-start | bytes 786440 | tf_op jit(solution)/shard_map/ppermute | solution.py:38
  159.7 26.8 %collective-permute-start.17 = (bf16[8,128,256]{2,1,0:T(8,128)(2,1)}, bf16[8,128,256]{2,1,0:T(8,128)(2,1)S(1)}, u32[]{:S(2)}, u32[]{:S(2)}) collective-permute-start(bf16[8,128,256]{2,1,0:T(8,128)(2,1)} %get-tuple-element.69), channel_id=1, source_target_pairs={{0,8},{8,0},{16,24},{24,16},{1,9},{9,1},{17,25},{25,17},{2,10},{10... | collective-permute-start | bytes 1572872 | tf_op jit(solution)/shard_map/ppermute | solution.py:38
  162.3 16.9 %collective-permute-start.25 = (bf16[4,128,256]{2,1,0:T(8,128)(2,1)}, bf16[4,128,256]{2,1,0:T(8,128)(2,1)}, u32[]{:S(2)}, u32[]{:S(2)}) collective-permute-start(bf16[4,128,256]{2,1,0:T(8,128)(2,1)} %get-tuple-element.92), channel_id=1, source_target_pairs={{0,8},{8,0},{16,24},{24,16},{1,9},{9,1},{17,25},{25,17},{2,10},{10... | collective-permute-start | bytes 786440 | tf_op jit(solution)/shard_map/ppermute | solution.py:38
  163.8 15.4 %collective-permute-start.26 = (bf16[4,128,256]{2,1,0:T(8,128)(2,1)}, bf16[4,128,256]{2,1,0:T(8,128)(2,1)}, u32[]{:S(2)}, u32[]{:S(2)}) collective-permute-start(bf16[4,128,256]{2,1,0:T(8,128)(2,1)} %get-tuple-element.93), channel_id=1, source_target_pairs={{0,16},{8,24},{16,0},{24,8},{1,17},{9,25},{17,1},{25,9},{2,18},{10... | collective-permute-start | bytes 786440 | tf_op jit(solution)/shard_map/ppermute | solution.py:38
  163.8 20.6 %collective-permute-start.27 = (bf16[4,128,256]{2,1,0:T(8,128)(2,1)}, bf16[4,128,256]{2,1,0:T(8,128)(2,1)}, u32[]{:S(2)}, u32[]{:S(2)}) collective-permute-start(bf16[4,128,256]{2,1,0:T(8,128)(2,1)} %get-tuple-element.94), channel_id=1, source_target_pairs={{0,24},{8,16},{16,8},{24,0},{1,25},{9,17},{17,9},{25,1},{2,26},{10... | collective-permute-start | bytes 786440 | tf_op jit(solution)/shard_map/ppermute | solution.py:38
  165.0 20.7 %collective-permute-start.28 = (bf16[4,128,256]{2,1,0:T(8,128)(2,1)}, bf16[4,128,256]{2,1,0:T(8,128)(2,1)S(1)}, u32[]{:S(2)}, u32[]{:S(2)}) collective-permute-start(bf16[4,128,256]{2,1,0:T(8,128)(2,1)} %get-tuple-element.91.refs_4_), channel_id=1, source_target_pairs={{0,1},{1,0},{2,3},{3,2},{4,5},{5,4},{6,7},{7,6},{8,9},{9,8},{10,11... | collective-permute-start | bytes 786440 | tf_op jit(solution)/shard_map/ppermute | solution.py:38
  179.2 27.9 %collective-permute-start.18 = (bf16[8,128,256]{2,1,0:T(8,128)(2,1)}, bf16[8,128,256]{2,1,0:T(8,128)(2,1)S(1)}, u32[]{:S(2)}, u32[]{:S(2)}) collective-permute-start(bf16[8,128,256]{2,1,0:T(8,128)(2,1)} %get-tuple-element.70), channel_id=1, source_target_pairs={{0,16},{8,24},{16,0},{24,8},{1,17},{9,25},{17,1},{25,9},{2,18},{10... | collective-permute-start | bytes 1572872 | tf_op jit(solution)/shard_map/ppermute | solution.py:38
  179.2 27.9 %collective-permute-start.19 = (bf16[8,128,256]{2,1,0:T(8,128)(2,1)}, bf16[8,128,256]{2,1,0:T(8,128)(2,1)}, u32[]{:S(2)}, u32[]{:S(2)}) collective-permute-start(bf16[8,128,256]{2,1,0:T(8,128)(2,1)} %get-tuple-element.71), channel_id=1, source_target_pairs={{0,24},{8,16},{16,8},{24,0},{1,25},{9,17},{17,9},{25,1},{2,26},{10... | collective-permute-start | bytes 1572872 | tf_op jit(solution)/shard_map/ppermute | solution.py:38
  184.4 22.7 %collective-permute-start.29 = (bf16[4,128,256]{2,1,0:T(8,128)(2,1)}, bf16[4,128,256]{2,1,0:T(8,128)(2,1)}, u32[]{:S(2)}, u32[]{:S(2)}) collective-permute-start(bf16[4,128,256]{2,1,0:T(8,128)(2,1)} %collective-permute-done.25.refs_5_), channel_id=1, source_target_pairs={{0,1},{1,0},{2,3},{3,2},{4,5},{5,4},{6,7},{7,6},{8,9},{9,8},{10,11... | collective-permute-start | bytes 786440 | tf_op jit(solution)/shard_map/ppermute | solution.py:38
  186.4 20.6 %collective-permute-start.30 = (bf16[4,128,256]{2,1,0:T(8,128)(2,1)}, bf16[4,128,256]{2,1,0:T(8,128)(2,1)}, u32[]{:S(2)}, u32[]{:S(2)}) collective-permute-start(bf16[4,128,256]{2,1,0:T(8,128)(2,1)} %collective-permute-done.26.refs_6_), channel_id=1, source_target_pairs={{0,1},{1,0},{2,3},{3,2},{4,5},{5,4},{6,7},{7,6},{8,9},{9,8},{10,11... | collective-permute-start | bytes 786440 | tf_op jit(solution)/shard_map/ppermute | solution.py:38
  186.4 20.6 %collective-permute-start.31 = (bf16[4,128,256]{2,1,0:T(8,128)(2,1)}, bf16[4,128,256]{2,1,0:T(8,128)(2,1)}, u32[]{:S(2)}, u32[]{:S(2)}) collective-permute-start(bf16[4,128,256]{2,1,0:T(8,128)(2,1)} %collective-permute-done.27.refs_7_), channel_id=1, source_target_pairs={{0,1},{1,0},{2,3},{3,2},{4,5},{5,4},{6,7},{7,6},{8,9},{9,8},{10,11... | collective-permute-start | bytes 786440 | tf_op jit(solution)/shard_map/ppermute | solution.py:38
  (62 other events, 728.4 us)

commit v3 on v2

--- a/solution.py
+++ b/solution.py
@@ -21,6 +21,7 @@
 BF16 = jnp.bfloat16
 SCALARS = pl.BlockSpec(memory_space=pltpu.SMEM)
 WHOLE = pl.BlockSpec(memory_space=pltpu.VMEM)
+SMALL = pl.CostEstimate(flops=1024, bytes_accessed=1024, transcendentals=0)
 
 
 def mm(a, b, ca, cb):
@@ -72,17 +73,19 @@
     return pl.pallas_call(
         pack_kernel,
         out_shape=jax.ShapeDtypeStruct((rows + EXTRA, width), BF16),
+        cost_estimate=SMALL,
     )(emb, positive.reshape(1, rows), user_expert.reshape(1, rows), item_expert.reshape(1, rows))
 
 
 def stats_kernel(first_ref, *refs, blocks, count, chunk):
     users_refs, items_refs = refs[:blocks], refs[blocks : blocks + count]
-    out_ref, all_ref, col_ref, s_ref = refs[blocks + count :]
+    out_ref, extra_ref, all_ref, col_ref, s_ref = refs[blocks + count :]
     own, emb = items_refs[0].shape
     rows = users_refs[0].shape[0] - EXTRA
     n_cols = own * count
     for k, ref in enumerate(users_refs):
         all_ref[k] = ref[...]
+        extra_ref[k] = ref[rows:, :]
     for k, ref in enumerate(items_refs):
         col_ref[k * own : (k + 1) * own, :] = ref[...]
 
@@ -123,19 +126,18 @@
     return pl.pallas_call(
         functools.partial(stats_kernel, blocks=blocks, count=count, chunk=64),
         in_specs=[SCALARS] + [WHOLE] * (blocks + count),
-        out_specs=WHOLE,
-        out_shape=jax.ShapeDtypeStruct((blocks, 3, rows), F32),
+        out_specs=[WHOLE] * 2,
+        out_shape=[
+            jax.ShapeDtypeStruct((blocks, 3, rows), F32),
+            jax.ShapeDtypeStruct((blocks, EXTRA, emb), BF16),
+        ],
         scratch_shapes=[
             pltpu.VMEM((blocks, height, emb), BF16),
             pltpu.VMEM((own * count, emb), BF16),
             pltpu.VMEM((2, own * count, rows), F32),
         ],
         compiler_params=pltpu.CompilerParams(vmem_limit_bytes=40 * MIB),
-        cost_estimate=pl.CostEstimate(
-            flops=6 * 2 * blocks * rows * own * count * emb,
-            bytes_accessed=(blocks * rows + own * count) * emb * 2,
-            transcendentals=blocks * rows * own * count,
-        ),
+        cost_estimate=SMALL,
     )(first, *users, *items)
 
 
@@ -205,11 +207,7 @@
             pltpu.VMEM((blocks, rows, emb), F32),
         ],
         compiler_params=pltpu.CompilerParams(vmem_limit_bytes=56 * MIB),
-        cost_estimate=pl.CostEstimate(
-            flops=8 * 2 * blocks * rows * own * count * emb,
-            bytes_accessed=(blocks * rows + own * count) * emb * 6,
-            transcendentals=blocks * rows * own * count,
-        ),
+        cost_estimate=SMALL,
     )(first, *users, *items, *gathered)
     return results[0][0], results[1], results[2], results[3:]
 
@@ -225,7 +223,7 @@
         in_specs=[WHOLE] * 2,
         out_specs=[WHOLE] * a.shape[0],
         out_shape=[jax.ShapeDtypeStruct(a.shape[1:], F32)] * a.shape[0],
-        cost_estimate=pl.CostEstimate(flops=a.size, bytes_accessed=12 * a.size, transcendentals=0),
+        cost_estimate=SMALL,
     )(a, b)
 
 
@@ -242,45 +240,45 @@
         in_specs=[WHOLE],
         out_specs=WHOLE,
         out_shape=jax.ShapeDtypeStruct((parts, rows, total // parts), hidden.dtype),
-        cost_estimate=pl.CostEstimate(flops=0, bytes_accessed=4 * hidden.size, transcendentals=0),
+        cost_estimate=SMALL,
     )(hidden)
 
 
-def onehot_of(target, start, span):
-    place = lax.broadcasted_iota(jnp.int32, (span, target.shape[1]), 0)
-    return (place == target - start).astype(F32).astype(BF16)
+def onehot_of(target, me, groups):
+    span = EXPERTS * CAP // groups
+    place = lax.broadcasted_iota(jnp.int32, (EXPERTS * CAP, target.shape[1]), 0)
+    place = (((place // span) ^ me) * span) + place % span
+    return (place == target).astype(F32).astype(BF16)
 
 
 def hidden_kernel(me_ref, near_ref, far_ref, hidden_ref, *out_refs, tower):
-    span = out_refs[0].shape[1]
-    apart = me_ref[1] ^ pl.program_id(0)
-    line = apart // CORES
-    extra = jnp.where(apart % CORES == 0, near_ref[line].astype(F32), far_ref[line].astype(F32))
-    target = number(extra, 1 + tower)
-    for k, out_ref in enumerate(out_refs):
-        onehot = onehot_of(target, (me_ref[0] ^ k) * span, span)
-        out_ref[0] = mm(onehot, hidden_ref[0], 1, 0).astype(BF16)
+    pair, span = out_refs[0].shape[:2]
+    for half in range(pair):
+        apart = me_ref[1] ^ (pl.program_id(0) * pair + half)
+        line = apart // CORES
+        extra = jnp.where(apart % CORES == 0, near_ref[line].astype(F32), far_ref[line].astype(F32))
+        onehot = onehot_of(number(extra, 1 + tower), me_ref[0], len(out_refs))
+        moved = mm(onehot, hidden_ref[half], 1, 0).astype(BF16)
+        for k, out_ref in enumerate(out_refs):
+            out_ref[half] = moved[k * span : (k + 1) * span, :]
 
 
 def slot_hidden(me, near, far, hidden, groups, tower):
     blocks, rows, width = hidden.shape
     span = EXPERTS * CAP // groups
+    pair = 2
     return pl.pallas_call(
         functools.partial(hidden_kernel, tower=tower),
-        grid=(blocks,),
+        grid=(blocks // pair,),
         in_specs=[
             SCALARS,
             pl.BlockSpec(near.shape, lambda b: (0, 0, 0)),
             pl.BlockSpec(far.shape, lambda b: (0, 0, 0)),
-            pl.BlockSpec((1, rows, width), lambda b: (b, 0, 0)),
+            pl.BlockSpec((pair, rows, width), lambda b: (b, 0, 0)),
         ],
-        out_specs=[pl.BlockSpec((1, span, width), lambda b: (b, 0, 0))] * groups,
+        out_specs=[pl.BlockSpec((pair, span, width), lambda b: (b, 0, 0))] * groups,
         out_shape=[jax.ShapeDtypeStruct((blocks, span, width), BF16)] * groups,
-        cost_estimate=pl.CostEstimate(
-            flops=2 * blocks * EXPERTS * CAP * rows * width,
-            bytes_accessed=blocks * (rows + EXPERTS * CAP) * width * 2,
-            transcendentals=0,
-        ),
+        cost_estimate=SMALL,
     )(me, near, far, hidden)
 
 
@@ -299,9 +297,7 @@
         in_specs=[WHOLE] * len(pieces),
         out_specs=WHOLE,
         out_shape=jax.ShapeDtypeStruct(shape, BF16),
-        cost_estimate=pl.CostEstimate(
-            flops=len(pieces) * size, bytes_accessed=4 * len(pieces) * size, transcendentals=0
-        ),
+        cost_estimate=SMALL,
     )(*pieces)
 
 
@@ -309,10 +305,10 @@
     out_refs = refs[lines:]
     span = out_refs[0].shape[1]
     for j, grad_ref in enumerate(refs[:lines]):
-        target = number(extra_ref[j], 1 + tower)
+        onehot = onehot_of(number(extra_ref[j], 1 + tower), me_ref[0], len(out_refs))
+        moved = mm(onehot, grad_ref[...], 1, 0).astype(BF16)
         for k, out_ref in enumerate(out_refs):
-            onehot = onehot_of(target, (me_ref[0] ^ k) * span, span)
-            out_ref[j] = mm(onehot, grad_ref[...], 1, 0).astype(BF16)
+            out_ref[j] = moved[k * span : (k + 1) * span, :]
 
 
 def select(me, extra, grads, groups, tower):
@@ -324,11 +320,7 @@
         in_specs=[SCALARS] + [WHOLE] * (1 + lines),
         out_specs=[WHOLE] * groups,
         out_shape=[jax.ShapeDtypeStruct((lines, span, emb), BF16)] * groups,
-        cost_estimate=pl.CostEstimate(
-            flops=2 * lines * EXPERTS * CAP * rows * emb,
-            bytes_accessed=lines * (rows + EXPERTS * CAP) * emb * 2,
-            transcendentals=0,
-        ),
+        cost_estimate=SMALL,
     )(me, extra, *grads)
 
 
@@ -356,11 +348,7 @@
         out_specs=WHOLE,
         out_shape=jax.ShapeDtypeStruct((own, width, emb), F32),
         compiler_params=pltpu.CompilerParams(vmem_limit_bytes=40 * MIB),
-        cost_estimate=pl.CostEstimate(
-            flops=2 * width * emb * groups * blocks * span,
-            bytes_accessed=groups * blocks * span * (width + emb) * 2 + own * width * emb * 4,
-            transcendentals=0,
-        ),
+        cost_estimate=SMALL,
     )(order, *hidden, *grad)
 
 
@@ -386,25 +374,21 @@
     packed = pack(user_emb, positive, user_expert, item_expert)
     users = exchange([packed] * lines, "item", CORES)
     near = exchange([item_emb] * groups, "user")
-    item_hidden, user_hidden, _ = tie(item_hidden, user_hidden, packed)
+    item_hidden, user_hidden, *near = tie(item_hidden, user_hidden, *near)
     item_cols = by_part(item_hidden)
 
     items = near + [swap(piece, "item", 1) for piece in near]
-    extra_near = jnp.stack([block[rows:] for block in users])
+    found, extra_near = stats(first, users, items)
+    gathered = exchange([found] * lines, "item", CORES)
     extra_far = swap(extra_near, "item", 1)
-    gathered = exchange([stats(first, users, items)] * lines, "item", CORES)
-    *gathered, item_cols, user_hidden = tie(*gathered, item_cols, user_hidden)
-    user_cols = by_part(user_hidden)
 
     row_loss, item_near, item_far, user_parts = grads(first, users, items, gathered)
     user_pieces = exchange(user_parts, "item", CORES)
-    item_cols, item_far = tie(item_cols, item_far)
-    item_slots = slots_of(item_cols, 1)
+    item_cols, user_hidden, item_far = tie(item_cols, user_hidden, item_far)
+    user_cols = by_part(user_hidden)
     item_pieces = exchange(add(item_near, swap(item_far, "item", 1)), "user")
-    *item_slots, item_pieces[0] = tie(*item_slots, item_pieces[0])
-    item_rows = exchange(item_slots, "user")
-
-    *user_pieces, user_cols = tie(*user_pieces, user_cols)
+    item_rows = exchange(slots_of(item_cols, 1), "user")
+
     user_lines = exchange([total(user_pieces)] * lines, "item", CORES)
     item_lines = exchange([total(item_pieces)] * lines, "item", CORES)
     user_rows = exchange(slots_of(user_cols, 0), "user")
@@ -413,7 +397,6 @@
         got = exchange(select(me, extra_near, grad_lines, groups, tower), "user")
         return got + [swap(piece, "item", 1) for piece in got]
 
-    *user_lines, item_rows[1] = tie(*user_lines, item_rows[1])
     user_grad = spread(user_lines, 0)
     item_grad = spread(item_lines, 1)
     item_weight_grad = outer(order, item_rows, item_grad)

time: 213 us -> 247 us (1.16)
  waiting for transfers between devices: 92.6 us -> 127 us
  starting transfers between devices: 57 us -> 62.9 us
  Pallas kernels: 48.9 us -> 43.9 us
  local copies, waits for them, and re-layouts: 10.5 us -> 7.95 us
    ppermute x47, waiting for transfers between devices: 92.6 us -> 127 us  [swap(): return lax.ppermute(piece, axis, [(j, j ^ bits) for j in range(size)])]
    ppermute x47, starting transfers between devices: 45.6 us -> 50.2 us  [swap(): return lax.ppermute(piece, axis, [(j, j ^ bits) for j in range(size)])]
    pallas_call x2, Pallas kernels: 12.3 us -> 7.82 us  [slot_hidden(): pl.pallas_call(functools.partial(hidden_kernel, tower=tower), grid=(block...]
    another operation x4 -> x0, local copies, waits for them, and re-layouts: 2.79 us -> none  [shards(): extra_near = jnp.stack([block[rows:] for block in users])]
    unnamed x90 -> x92, local copies, waits for them, and re-layouts: 6.26 us -> 6.55 us
  transfers between devices with their start and end apart: 49 -> 49, of which waited for: 19 -> 20; matrix products, arithmetic and copies ran while one was open for 2% -> 1% of each run, Pallas kernels for 16% -> 16%
where the time goes in v3:
time: 247 us; the launch traced here: 244 us
  waiting for transfers between devices  127 us (51%)
  starting transfers between devices  62.9 us (25%)
  Pallas kernels  43.9 us (18%)
  local copies, waits for them, and re-layouts  7.95 us (3%)
    ppermute x47, waiting for transfers between devices, swap(): return lax.ppermute(piece, axis, [(j, j ^ bits) for j in range(size)])  127 us
    ppermute x47, starting transfers between devices, swap(): return lax.ppermute(piece, axis, [(j, j ^ bits) for j in range(size)])  50.2 us
    all_to_all x2, starting transfers between devices, by_part(): lax.all_to_all(cut(hidden, parts), 'item', split_axis=0, concat_axis=0, t...  12.7 us
    pallas_call x1, Pallas kernels, grads(): pl.pallas_call(functools.partial(grad_kernel, blocks=blocks, count=count,...  7.84 us
    pallas_call x2, Pallas kernels, slot_hidden(): pl.pallas_call(functools.partial(hidden_kernel, tower=tower), grid=(block...  7.82 us
    pallas_call x2, Pallas kernels, outer(): pl.pallas_call(functools.partial(outer_kernel, groups=groups), in_specs=[...  7.07 us
    unnamed x92, local copies, waits for them, and re-layouts  6.55 us
  transfers between devices with their start and end apart: 49, of which 20 were waited for; matrix products, arithmetic and copies ran while one was open for 1% of the time, Pallas kernels for 16%

profile of v3, /device:TPU:11, one launch (start us, length us, event | category | flops | bytes accessed | tf_op | source)
XLA Modules:
  0.0 243.5 jit_solution(14436266510201145897)
XLA Ops:
  5.3 3.8 %collective-permute-done.5.refs_7_ = bf16[256,256]{1,0:T(8,128)(2,1)S(1)} collective-permute-done((bf16[256,256]{1,0:T(8,128)(2,1)}, bf16[256,256]{1,0:T(8,128)(2,1)S(1)}, u32[]{:S(2)}, u32[]{:S(2)}) %collective-permute-start.5) | collective-permute-done | bytes 131104 | tf_op jit(solution)/shard_map/ppermute | solution.py:39
  9.1 2.3 shard_map.97
  11.4 6.5 %all-to-all-start = ((bf16[8,256,256]{2,1,0:T(8,128)(2,1)}), bf16[8,256,256]{2,1,0:T(8,128)(2,1)S(1)}, u32[]{:S(2)}, u32[]{:S(2)}) async-start(bf16[8,256,256]{2,1,0:T(8,128)(2,1)} %shard_map.97), calls=%async_computation | async-start | bytes 2097152 | tf_op jit(solution)/shard_map/all_to_all | solution.py:369
  19.7 2.3 collective-permute-start.1
  23.6 15.5 %collective-permute-done.refs_1_ = bf16[272,256]{1,0:T(8,128)(2,1)S(1)} collective-permute-done((bf16[272,256]{1,0:T(8,128)(2,1)}, bf16[272,256]{1,0:T(8,128)(2,1)S(1)}, u32[]{:S(2)}, u32[]{:S(2)}) %collective-permute-start) | collective-permute-done | bytes 139296 | tf_op jit(solution)/shard_map/ppermute | solution.py:39
  39.9 10.0 %collective-permute-done.1.refs_2_ = bf16[272,256]{1,0:T(8,128)(2,1)S(1)} collective-permute-done((bf16[272,256]{1,0:T(8,128)(2,1)}, bf16[272,256]{1,0:T(8,128)(2,1)S(1)}, u32[]{:S(2)}, u32[]{:S(2)}) %collective-permute-start.1) | collective-permute-done | bytes 139296 | tf_op jit(solution)/shard_map/ppermute | solution.py:39
  50.5 3.9 %collective-permute-done.2.refs_3_ = bf16[272,256]{1,0:T(8,128)(2,1)S(1)} collective-permute-done((bf16[272,256]{1,0:T(8,128)(2,1)}, bf16[272,256]{1,0:T(8,128)(2,1)S(1)}, u32[]{:S(2)}, u32[]{:S(2)}) %collective-permute-start.2) | collective-permute-done | bytes 139296 | tf_op jit(solution)/shard_map/ppermute | solution.py:39
  55.6 3.6 %shard_map.95 = (f32[4,3,256]{2,1,0:T(4,128)S(1)}, bf16[4,16,256]{2,1,0:T(8,128)(2,1)S(1)}) custom-call(s32[8]{0:T(128)S(1)} %mul.24.first_ref, bf16[272,256]{1,0:T(8,128)(2,1)S(1)} %copy-done, bf16[272,256]{1,0:T(8,128)(2,1)S(1)} %collective-permute-done.refs_1_, bf16[272,256]{1,0:T(8,128)(2,1)S(1)} %collective-permute-done.1.refs_2_, ...), custom_call_target="tpu_custom_call" | custom-call | flops 1024 | bytes 1024 | tf_op jit(solution)/shard_map/pallas_call | solution.py:126
  64.4 7.8 %shard_map.96 = (f32[4,256]{1,0:T(4,128)}, f32[4,256,256]{2,1,0:T(8,128)}, f32[4,256,256]{2,1,0:T(8,128)}, f32[256,256]{1,0:T(8,128)}, f32[256,256]{1,0:T(8,128)...) custom-call(s32[8]{0:T(128)} %copy-done.24, bf16[272,256]{1,0:T(8,128)(2,1)} %shard_map.94.refs_0_, bf16[272,256]{1,0:T(8,128)(2,1)} %copy-done.1, ...), custom_call_target="tpu_custom_call" | custom-call | flops 1024 | bytes 1024 | tf_op jit(solution)/shard_map/pallas_call | solution.py:194
  76.6 6.2 %all-to-all-start.1 = ((bf16[8,256,256]{2,1,0:T(8,128)(2,1)}), bf16[8,256,256]{2,1,0:T(8,128)(2,1)}, u32[]{:S(2)}, u32[]{:S(2)}) async-start(bf16[8,256,256]{2,1,0:T(8,128)(2,1)} %shard_map.98), calls=%async_computation.1 | async-start | bytes 2097152 | tf_op jit(solution)/shard_map/all_to_all | solution.py:369
  82.9 2.3 collective-permute-start.18
  85.5 21.1 %collective-permute-done.17.refs_1_ = f32[256,256]{1,0:T(8,128)S(1)} collective-permute-done((f32[256,256]{1,0:T(8,128)}, f32[256,256]{1,0:T(8,128)S(1)}, u32[]{:S(2)}, u32[]{:S(2)}) %collective-permute-start.17) | collective-permute-done | bytes 262176 | tf_op jit(solution)/shard_map/ppermute | solution.py:39
  106.6 16.1 %collective-permute-done.18.refs_2_ = f32[256,256]{1,0:T(8,128)S(1)} collective-permute-done((f32[256,256]{1,0:T(8,128)S(1)}, f32[256,256]{1,0:T(8,128)S(1)}, u32[]{:S(2)}, u32[]{:S(2)}) %collective-permute-start.18) | collective-permute-done | bytes 262176 | tf_op jit(solution)/shard_map/ppermute | solution.py:39
  122.7 7.3 %collective-permute-done.19.refs_3_ = f32[256,256]{1,0:T(8,128)S(1)} collective-permute-done((f32[256,256]{1,0:T(8,128)S(1)}, f32[256,256]{1,0:T(8,128)S(1)}, u32[]{:S(2)}, u32[]{:S(2)}) %collective-permute-start.19) | collective-permute-done | bytes 262176 | tf_op jit(solution)/shard_map/ppermute | solution.py:39
  133.5 2.5 %shard_map.104 = (f32[256,256]{1,0:T(8,128)}, f32[256,256]{1,0:T(8,128)}, f32[256,256]{1,0:T(8,128)}, f32[256,256]{1,0:T(8,128)}) custom-call(f32[4,256,256]{2,1,0:T(8,128)} %get-tuple-element.69.a_ref, f32[4,256,256]{2,1,0:T(8,128)} %copy-done.26), custom_call_target="tpu_custom_call" | custom-call | flops 1024 | bytes 1024 | tf_op jit(solution)/shard_map/pallas_call | solution.py:221
  143.2 3.7 %collective-permute-done.21.refs_2_ = bf16[256,256]{1,0:T(8,128)(2,1)S(1)} collective-permute-done((bf16[256,256]{1,0:T(8,128)(2,1)S(1)}, bf16[256,256]{1,0:T(8,128)(2,1)S(1)}, u32[]{:S(2)}, u32[]{:S(2)}) %collective-permute-start.21) | collective-permute-done | bytes 131104 | tf_op jit(solution)/shard_map/ppermute | solution.py:39
  148.1 3.3 %collective-permute-done.22.refs_3_ = bf16[256,256]{1,0:T(8,128)(2,1)S(1)} collective-permute-done((bf16[256,256]{1,0:T(8,128)(2,1)S(1)}, bf16[256,256]{1,0:T(8,128)(2,1)S(1)}, u32[]{:S(2)}, u32[]{:S(2)}) %collective-permute-start.22) | collective-permute-done | bytes 131104 | tf_op jit(solution)/shard_map/ppermute | solution.py:39
  152.1 2.5 %shard_map.101 = (bf16[4,128,256]{2,1,0:T(8,128)(2,1)}, bf16[4,128,256]{2,1,0:T(8,128)(2,1)}, bf16[4,128,256]{2,1,0:T(8,128)(2,1)}, bf16[4,128,256]{2,1,0:T(8,128)(2,1)}) custom-call(s32[2]{0:T(128)} %pad_add_fusion.me_ref, bf16[4,16,256]{2,1,0:T(8,128)(2,1)} %copy-done.14, bf16[256,256]{1,0:T(8,128)(2,1)} %shard_map.100.refs_0_, ...), custom_call_target="tpu_custom_call" | custom-call | flops 1024 | bytes 1024 | tf_op jit(solution)/shard_map/pallas_call | solution.py:318
  157.2 3.9 %shard_map.103 = (bf16[8,128,256]{2,1,0:T(8,128)(2,1)}, bf16[8,128,256]{2,1,0:T(8,128)(2,1)}, bf16[8,128,256]{2,1,0:T(8,128)(2,1)}, bf16[8,128,256]{2,1,0:T(8,128)(2,1)}) custom-call(s32[2]{0:T(128)} %pad_add_fusion.me_ref, bf16[4,16,256]{2,1,0:T(8,128)(2,1)} %copy-done.14, bf16[4,16,256]{2,1,0:T(8,128)(2,1)} %copy-done.40, bf16[8,256,256]{2,1,0:T(8,128)(2,1)} %copy-done.25), custom_call_target="tpu_custom_call" | custom-call | flops 1024 | bytes 1024 | tf_op jit(solution)/shard_map/pallas_call | solution.py:270
  165.3 2.3 collective-permute-start.26
  170.7 7.2 %collective-permute-done.38.refs_2_ = bf16[256,256]{1,0:T(8,128)(2,1)S(1)} collective-permute-done((bf16[256,256]{1,0:T(8,128)(2,1)}, bf16[256,256]{1,0:T(8,128)(2,1)S(1)}, u32[]{:S(2)}, u32[]{:S(2)}) %collective-permute-start.38) | collective-permute-done | bytes 131104 | tf_op jit(solution)/shard_map/ppermute | solution.py:39
  177.9 2.4 collective-permute-start.27
  180.3 2.4 collective-permute-done.39.refs_3_
  183.8 2.4 shard_map.106
  189.3 3.3 %collective-permute-start.43 = (bf16[4,128,256]{2,1,0:T(8,128)(2,1)}, bf16[4,128,256]{2,1,0:T(8,128)(2,1)}, u32[]{:S(2)}, u32[]{:S(2)}) collective-permute-start(bf16[4,128,256]{2,1,0:T(8,128)(2,1)} %get-tuple-element.75.refs_4_), channel_id=1, source_target_pairs={{0,1},{1,0},{2,3},{3,2},{4,5},{5,4},{6,7},{7,6},{8,9},{9,8},{10,11... | collective-permute-start | bytes 786440 | tf_op jit(solution)/shard_map/ppermute | solution.py:39
  192.6 9.6 %collective-permute-done.40.refs_5_ = bf16[4,128,256]{2,1,0:T(8,128)(2,1)} collective-permute-done((bf16[4,128,256]{2,1,0:T(8,128)(2,1)}, bf16[4,128,256]{2,1,0:T(8,128)(2,1)}, u32[]{:S(2)}, u32[]{:S(2)}) %collective-permute-start.40) | collective-permute-done | bytes 262176 | tf_op jit(solution)/shard_map/ppermute | solution.py:39
  202.2 4.0 %collective-permute-start.44 = (bf16[4,128,256]{2,1,0:T(8,128)(2,1)}, bf16[4,128,256]{2,1,0:T(8,128)(2,1)}, u32[]{:S(2)}, u32[]{:S(2)}) collective-permute-start(bf16[4,128,256]{2,1,0:T(8,128)(2,1)} %collective-permute-done.40.refs_5_), channel_id=1, source_target_pairs={{0,1},{1,0},{2,3},{3,2},{4,5},{5,4},{6,7},{7,6},{8,9},{9,8},{10,11... | collective-permute-start | bytes 786440 | tf_op jit(solution)/shard_map/ppermute | solution.py:39
  210.2 3.9 %shard_map.99 = (bf16[8,128,256]{2,1,0:T(8,128)(2,1)}, bf16[8,128,256]{2,1,0:T(8,128)(2,1)}, bf16[8,128,256]{2,1,0:T(8,128)(2,1)}, bf16[8,128,256]{2,1,0:T(8,128)(2,1)}) custom-call(s32[2]{0:T(128)} %pad_add_fusion.me_ref, bf16[4,16,256]{2,1,0:T(8,128)(2,1)} %copy-done.14, bf16[4,16,256]{2,1,0:T(8,128)(2,1)} %copy-done.40, ...), custom_call_target="tpu_custom_call" | custom-call | flops 1024 | bytes 1024 | tf_op jit(solution)/shard_map/pallas_call | solution.py:270
  220.2 3.6 %shard_map.107 = f32[8,256,256]{2,1,0:T(8,128)} custom-call(s32[8]{0:T(128)S(1)} %xor.47.order_ref, bf16[8,128,256]{2,1,0:T(8,128)(2,1)S(1)} %copy-done.4, bf16[8,128,256]{2,1,0:T(8,128)(2,1)S(1)} %collective-permute-done.30.refs_1_, bf16[8,128,256]{2,1,0:T(8,128)(2,1)S(1)} %collective-permute-done.31.refs_2_, ...), custom_call_target="tpu_custom_call" | custom-call | flops 1024 | bytes 1024 | tf_op jit(solution)/shard_map/pallas_call | solution.py:345
  223.8 4.2 %collective-permute-done.14.refs_1_ = bf16[8,128,256]{2,1,0:T(8,128)(2,1)S(1)} collective-permute-done((bf16[8,128,256]{2,1,0:T(8,128)(2,1)}, bf16[8,128,256]{2,1,0:T(8,128)(2,1)S(1)}, u32[]{:S(2)}, u32[]{:S(2)}) %collective-permute-start.14) | collective-permute-done | bytes 524320 | tf_op jit(solution)/shard_map/ppermute | solution.py:39
  228.1 12.0 %collective-permute-done.16.refs_3_ = bf16[8,128,256]{2,1,0:T(8,128)(2,1)} collective-permute-done((bf16[8,128,256]{2,1,0:T(8,128)(2,1)}, bf16[8,128,256]{2,1,0:T(8,128)(2,1)}, u32[]{:S(2)}, u32[]{:S(2)}) %collective-permute-start.16) | collective-permute-done | bytes 524320 | tf_op jit(solution)/shard_map/ppermute | solution.py:39
  240.1 3.4 %shard_map.102 = f32[8,256,256]{2,1,0:T(8,128)} custom-call(s32[8]{0:T(128)S(1)} %xor.47.order_ref, bf16[8,128,256]{2,1,0:T(8,128)(2,1)S(1)} %copy-done.5, bf16[8,128,256]{2,1,0:T(8,128)(2,1)S(1)} %collective-permute-done.14.refs_1_, bf16[8,128,256]{2,1,0:T(8,128)(2,1)S(1)} %collective-permute-done.15.refs_2_, ...), custom_call_target="tpu_custom_call" | custom-call | flops 1024 | bytes 1024 | tf_op jit(solution)/shard_map/pallas_call | solution.py:345
  (181 shorter events, 57.1 us)
Async XLA Ops:
  11.4 60.9 %all-to-all-start = ((bf16[8,256,256]{2,1,0:T(8,128)(2,1)}), bf16[8,256,256]{2,1,0:T(8,128)(2,1)S(1)}, u32[]{:S(2)}, u32[]{:S(2)}) async-start(bf16[8,256,256]{2,1,0:T(8,128)(2,1)} %shard_map.97), calls=%async_computation | async-start | bytes 2097152 | tf_op jit(solution)/shard_map/all_to_all | solution.py:369
  19.6 19.5 %collective-permute-start = (bf16[272,256]{1,0:T(8,128)(2,1)}, bf16[272,256]{1,0:T(8,128)(2,1)S(1)}, u32[]{:S(2)}, u32[]{:S(2)}) collective-permute-start(bf16[272,256]{1,0:T(8,128)(2,1)} %shard_map.94.refs_0_), channel_id=1, source_target_pairs={{0,2},{1,3},{2,0},{3,1},{4,6},{5,7},{6,4},{7,5},{8,10},{9,11},{10,... | collective-permute-start | bytes 417800 | tf_op jit(solution)/shard_map/ppermute | solution.py:39
  19.7 30.2 %collective-permute-start.1 = (bf16[272,256]{1,0:T(8,128)(2,1)}, bf16[272,256]{1,0:T(8,128)(2,1)S(1)}, u32[]{:S(2)}, u32[]{:S(2)}) collective-permute-start(bf16[272,256]{1,0:T(8,128)(2,1)} %shard_map.94.refs_0_), channel_id=1, source_target_pairs={{0,4},{1,5},{2,6},{3,7},{4,0},{5,1},{6,2},{7,3},{8,12},{9,13},{10,... | collective-permute-start | bytes 417800 | tf_op jit(solution)/shard_map/ppermute | solution.py:39
  22.0 32.5 %collective-permute-start.2 = (bf16[272,256]{1,0:T(8,128)(2,1)}, bf16[272,256]{1,0:T(8,128)(2,1)S(1)}, u32[]{:S(2)}, u32[]{:S(2)}) collective-permute-start(bf16[272,256]{1,0:T(8,128)(2,1)} %shard_map.94.refs_0_), channel_id=1, source_target_pairs={{0,6},{1,7},{2,4},{3,5},{4,2},{5,3},{6,0},{7,1},{8,14},{9,15},{10,... | collective-permute-start | bytes 417800 | tf_op jit(solution)/shard_map/ppermute | solution.py:39
  22.3 32.2 %collective-permute-start.6 = (bf16[256,256]{1,0:T(8,128)(2,1)S(1)}, bf16[256,256]{1,0:T(8,128)(2,1)S(1)}, u32[]{:S(2)}, u32[]{:S(2)}) collective-permute-start(bf16[256,256]{1,0:T(8,128)(2,1)S(1)} %copy-done.6), channel_id=1, source_target_pairs={{0,1},{1,0},{2,3},{3,2},{4,5},{5,4},{6,7},{7,6},{8,9},{9,8},{10,11... | collective-permute-start | bytes 393224 | tf_op jit(solution)/shard_map/ppermute | solution.py:39
  23.5 30.9 %collective-permute-start.7 = (bf16[256,256]{1,0:T(8,128)(2,1)S(1)}, bf16[256,256]{1,0:T(8,128)(2,1)S(1)}, u32[]{:S(2)}, u32[]{:S(2)}) collective-permute-start(bf16[256,256]{1,0:T(8,128)(2,1)S(1)} %collective-permute-done.3.refs_5_), channel_id=1, source_target_pairs={{0,1},{1,0},{2,3},{3,2},{4,5},{5,4},{6,7},{7,6},{8,9},{9,8},{10,11... | collective-permute-start | bytes 393224 | tf_op jit(solution)/shard_map/ppermute | solution.py:39
  39.1 15.4 %collective-permute-start.8 = (bf16[256,256]{1,0:T(8,128)(2,1)S(1)}, bf16[256,256]{1,0:T(8,128)(2,1)S(1)}, u32[]{:S(2)}, u32[]{:S(2)}) collective-permute-start(bf16[256,256]{1,0:T(8,128)(2,1)S(1)} %collective-permute-done.4.refs_6_), channel_id=1, source_target_pairs={{0,1},{1,0},{2,3},{3,2},{4,5},{5,4},{6,7},{7,6},{8,9},{9,8},{10,11... | collective-permute-start | bytes 393224 | tf_op jit(solution)/shard_map/ppermute | solution.py:39
  72.3 60.3 %collective-permute-start.33 = (f32[4,256,256]{2,1,0:T(8,128)}, f32[4,256,256]{2,1,0:T(8,128)S(1)}, u32[]{:S(2)}, u32[]{:S(2)}) collective-permute-start(f32[4,256,256]{2,1,0:T(8,128)} %get-tuple-element.70), channel_id=1, source_target_pairs={{0,1},{1,0},{2,3},{3,2},{4,5},{5,4},{6,7},{7,6},{8,9},{9,8},{10,11... | collective-permute-start | bytes 3145736 | tf_op jit(solution)/shard_map/ppermute | solution.py:39
  76.6 133.6 %all-to-all-start.1 = ((bf16[8,256,256]{2,1,0:T(8,128)(2,1)}), bf16[8,256,256]{2,1,0:T(8,128)(2,1)}, u32[]{:S(2)}, u32[]{:S(2)}) async-start(bf16[8,256,256]{2,1,0:T(8,128)(2,1)} %shard_map.98), calls=%async_computation.1 | async-start | bytes 2097152 | tf_op jit(solution)/shard_map/all_to_all | solution.py:369
  82.8 23.7 %collective-permute-start.17 = (f32[256,256]{1,0:T(8,128)}, f32[256,256]{1,0:T(8,128)S(1)}, u32[]{:S(2)}, u32[]{:S(2)}) collective-permute-start(f32[256,256]{1,0:T(8,128)} %get-tuple-element.57), channel_id=1, source_target_pairs={{0,2},{1,3},{2,0},{3,1},{4,6},{5,7},{6,4},{7,5},{8,10},{9,11},{10,... | collective-permute-start | bytes 786440 | tf_op jit(solution)/shard_map/ppermute | solution.py:39
  82.9 39.8 %collective-permute-start.18 = (f32[256,256]{1,0:T(8,128)S(1)}, f32[256,256]{1,0:T(8,128)S(1)}, u32[]{:S(2)}, u32[]{:S(2)}) collective-permute-start(f32[256,256]{1,0:T(8,128)S(1)} %copy-done.45), channel_id=1, source_target_pairs={{0,4},{1,5},{2,6},{3,7},{4,0},{5,1},{6,2},{7,3},{8,12},{9,13},{10,... | collective-permute-start | bytes 786440 | tf_op jit(solution)/shard_map/ppermute | solution.py:39
  85.2 44.7 %collective-permute-start.19 = (f32[256,256]{1,0:T(8,128)S(1)}, f32[256,256]{1,0:T(8,128)S(1)}, u32[]{:S(2)}, u32[]{:S(2)}) collective-permute-start(f32[256,256]{1,0:T(8,128)S(1)} %copy-done.44), channel_id=1, source_target_pairs={{0,6},{1,7},{2,4},{3,5},{4,2},{5,3},{6,0},{7,1},{8,14},{9,15},{10,... | collective-permute-start | bytes 786440 | tf_op jit(solution)/shard_map/ppermute | solution.py:39
  136.1 19.9 %collective-permute-start.34 = (f32[256,256]{1,0:T(8,128)}, f32[256,256]{1,0:T(8,128)S(1)}, u32[]{:S(2)}, u32[]{:S(2)}) collective-permute-start(f32[256,256]{1,0:T(8,128)} %get-tuple-element.72), channel_id=1, source_target_pairs={{0,8},{8,0},{16,24},{24,16},{1,9},{9,1},{17,25},{25,17},{2,10},{10... | collective-permute-start | bytes 786440 | tf_op jit(solution)/shard_map/ppermute | solution.py:39
  138.4 13.0 %collective-permute-start.22 = (bf16[256,256]{1,0:T(8,128)(2,1)S(1)}, bf16[256,256]{1,0:T(8,128)(2,1)S(1)}, u32[]{:S(2)}, u32[]{:S(2)}) collective-permute-start(bf16[256,256]{1,0:T(8,128)(2,1)S(1)} %copy-done.27), channel_id=1, source_target_pairs={{0,6},{1,7},{2,4},{3,5},{4,2},{5,3},{6,0},{7,1},{8,14},{9,15},{10,... | collective-permute-start | bytes 393224 | tf_op jit(solution)/shard_map/ppermute | solution.py:39
  139.3 16.1 %collective-permute-start.13 = (bf16[4,16,256]{2,1,0:T(8,128)(2,1)S(1)}, bf16[4,16,256]{2,1,0:T(8,128)(2,1)S(1)}, u32[]{:S(2)}, u32[]{:S(2)}) collective-permute-start(bf16[4,16,256]{2,1,0:T(8,128)(2,1)S(1)} %get-tuple-element.47.near_ref.extra_ref), channel_id=1, source_target_pairs={{0,1},{1,0},{2,3},{3,2},{4,5},{5,4},{6,7},{7,6},{8,9},{9,8},{10,11... | collective-permute-start | bytes 98312 | tf_op jit(solution)/shard_map/ppermute | solution.py:39
  141.3 19.8 %collective-permute-start.35 = (f32[256,256]{1,0:T(8,128)}, f32[256,256]{1,0:T(8,128)S(1)}, u32[]{:S(2)}, u32[]{:S(2)}) collective-permute-start(f32[256,256]{1,0:T(8,128)} %get-tuple-element.73), channel_id=1, source_target_pairs={{0,16},{8,24},{16,0},{24,8},{1,17},{9,25},{17,1},{25,9},{2,18},{10... | collective-permute-start | bytes 786440 | tf_op jit(solution)/shard_map/ppermute | solution.py:39
  146.9 15.1 %collective-permute-start.36 = (f32[256,256]{1,0:T(8,128)}, f32[256,256]{1,0:T(8,128)S(1)}, u32[]{:S(2)}, u32[]{:S(2)}) collective-permute-start(f32[256,256]{1,0:T(8,128)} %get-tuple-element.74), channel_id=1, source_target_pairs={{0,24},{8,16},{16,8},{24,0},{1,25},{9,17},{17,9},{25,1},{2,26},{10... | collective-permute-start | bytes 786440 | tf_op jit(solution)/shard_map/ppermute | solution.py:39
  156.0 12.8 %collective-permute-start.25 = (bf16[4,128,256]{2,1,0:T(8,128)(2,1)}, bf16[4,128,256]{2,1,0:T(8,128)(2,1)}, u32[]{:S(2)}, u32[]{:S(2)}) collective-permute-start(bf16[4,128,256]{2,1,0:T(8,128)(2,1)} %get-tuple-element.63), channel_id=1, source_target_pairs={{0,24},{8,16},{16,8},{24,0},{1,25},{9,17},{17,9},{25,1},{2,26},{10... | collective-permute-start | bytes 786440 | tf_op jit(solution)/shard_map/ppermute | solution.py:39
  161.1 27.4 %collective-permute-start.30 = (bf16[8,128,256]{2,1,0:T(8,128)(2,1)}, bf16[8,128,256]{2,1,0:T(8,128)(2,1)S(1)}, u32[]{:S(2)}, u32[]{:S(2)}) collective-permute-start(bf16[8,128,256]{2,1,0:T(8,128)(2,1)} %get-tuple-element.66), channel_id=1, source_target_pairs={{0,8},{8,0},{16,24},{24,16},{1,9},{9,1},{17,25},{25,17},{2,10},{10... | collective-permute-start | bytes 1572872 | tf_op jit(solution)/shard_map/ppermute | solution.py:39
  164.7 24.7 %collective-permute-start.31 = (bf16[8,128,256]{2,1,0:T(8,128)(2,1)}, bf16[8,128,256]{2,1,0:T(8,128)(2,1)S(1)}, u32[]{:S(2)}, u32[]{:S(2)}) collective-permute-start(bf16[8,128,256]{2,1,0:T(8,128)(2,1)} %get-tuple-element.67), channel_id=1, source_target_pairs={{0,16},{8,24},{16,0},{24,8},{1,17},{9,25},{17,1},{25,9},{2,18},{10... | collective-permute-start | bytes 1572872 | tf_op jit(solution)/shard_map/ppermute | solution.py:39
  165.3 20.8 %collective-permute-start.26 = (bf16[4,128,256]{2,1,0:T(8,128)(2,1)S(1)}, bf16[4,128,256]{2,1,0:T(8,128)(2,1)S(1)}, u32[]{:S(2)}, u32[]{:S(2)}) collective-permute-start(bf16[4,128,256]{2,1,0:T(8,128)(2,1)S(1)} %copy-done.15), channel_id=1, source_target_pairs={{0,1},{1,0},{2,3},{3,2},{4,5},{5,4},{6,7},{7,6},{8,9},{9,8},{10,11... | collective-permute-start | bytes 786440 | tf_op jit(solution)/shard_map/ppermute | solution.py:39
  169.8 13.0 %collective-permute-start.39 = (bf16[256,256]{1,0:T(8,128)(2,1)}, bf16[256,256]{1,0:T(8,128)(2,1)S(1)}, u32[]{:S(2)}, u32[]{:S(2)}) collective-permute-start(bf16[256,256]{1,0:T(8,128)(2,1)} %shard_map.105.refs_0_), channel_id=1, source_target_pairs={{0,6},{1,7},{2,4},{3,5},{4,2},{5,3},{6,0},{7,1},{8,14},{9,15},{10,... | collective-permute-start | bytes 393224 | tf_op jit(solution)/shard_map/ppermute | solution.py:39
  183.4 30.7 %collective-permute-start.32 = (bf16[8,128,256]{2,1,0:T(8,128)(2,1)}, bf16[8,128,256]{2,1,0:T(8,128)(2,1)S(1)}, u32[]{:S(2)}, u32[]{:S(2)}) collective-permute-start(bf16[8,128,256]{2,1,0:T(8,128)(2,1)} %get-tuple-element.68), channel_id=1, source_target_pairs={{0,24},{8,16},{16,8},{24,0},{1,25},{9,17},{17,9},{25,1},{2,26},{10... | collective-permute-start | bytes 1572872 | tf_op jit(solution)/shard_map/ppermute | solution.py:39
  186.2 16.0 %collective-permute-start.40 = (bf16[4,128,256]{2,1,0:T(8,128)(2,1)}, bf16[4,128,256]{2,1,0:T(8,128)(2,1)}, u32[]{:S(2)}, u32[]{:S(2)}) collective-permute-start(bf16[4,128,256]{2,1,0:T(8,128)(2,1)} %get-tuple-element.76), channel_id=1, source_target_pairs={{0,8},{8,0},{16,24},{24,16},{1,9},{9,1},{17,25},{25,17},{2,10},{10... | collective-permute-start | bytes 786440 | tf_op jit(solution)/shard_map/ppermute | solution.py:39
  188.0 18.2 %collective-permute-start.41 = (bf16[4,128,256]{2,1,0:T(8,128)(2,1)}, bf16[4,128,256]{2,1,0:T(8,128)(2,1)}, u32[]{:S(2)}, u32[]{:S(2)}) collective-permute-start(bf16[4,128,256]{2,1,0:T(8,128)(2,1)} %get-tuple-element.77), channel_id=1, source_target_pairs={{0,16},{8,24},{16,0},{24,8},{1,17},{9,25},{17,1},{25,9},{2,18},{10... | collective-permute-start | bytes 786440 | tf_op jit(solution)/shard_map/ppermute | solution.py:39
  188.6 19.8 %collective-permute-start.42 = (bf16[4,128,256]{2,1,0:T(8,128)(2,1)}, bf16[4,128,256]{2,1,0:T(8,128)(2,1)}, u32[]{:S(2)}, u32[]{:S(2)}) collective-permute-start(bf16[4,128,256]{2,1,0:T(8,128)(2,1)} %get-tuple-element.78), channel_id=1, source_target_pairs={{0,24},{8,16},{16,8},{24,0},{1,25},{9,17},{17,9},{25,1},{2,26},{10... | collective-permute-start | bytes 786440 | tf_op jit(solution)/shard_map/ppermute | solution.py:39
  189.3 25.3 %collective-permute-start.43 = (bf16[4,128,256]{2,1,0:T(8,128)(2,1)}, bf16[4,128,256]{2,1,0:T(8,128)(2,1)}, u32[]{:S(2)}, u32[]{:S(2)}) collective-permute-start(bf16[4,128,256]{2,1,0:T(8,128)(2,1)} %get-tuple-element.75.refs_4_), channel_id=1, source_target_pairs={{0,1},{1,0},{2,3},{3,2},{4,5},{5,4},{6,7},{7,6},{8,9},{9,8},{10,11... | collective-permute-start | bytes 786440 | tf_op jit(solution)/shard_map/ppermute | solution.py:39
  202.2 13.1 %collective-permute-start.44 = (bf16[4,128,256]{2,1,0:T(8,128)(2,1)}, bf16[4,128,256]{2,1,0:T(8,128)(2,1)}, u32[]{:S(2)}, u32[]{:S(2)}) collective-permute-start(bf16[4,128,256]{2,1,0:T(8,128)(2,1)} %collective-permute-done.40.refs_5_), channel_id=1, source_target_pairs={{0,1},{1,0},{2,3},{3,2},{4,5},{5,4},{6,7},{7,6},{8,9},{9,8},{10,11... | collective-permute-start | bytes 786440 | tf_op jit(solution)/shard_map/ppermute | solution.py:39
  206.2 10.7 %collective-permute-start.45 = (bf16[4,128,256]{2,1,0:T(8,128)(2,1)}, bf16[4,128,256]{2,1,0:T(8,128)(2,1)}, u32[]{:S(2)}, u32[]{:S(2)}) collective-permute-start(bf16[4,128,256]{2,1,0:T(8,128)(2,1)} %collective-permute-done.41.refs_6_), channel_id=1, source_target_pairs={{0,1},{1,0},{2,3},{3,2},{4,5},{5,4},{6,7},{7,6},{8,9},{9,8},{10,11... | collective-permute-start | bytes 786440 | tf_op jit(solution)/shard_map/ppermute | solution.py:39
  214.2 13.8 %collective-permute-start.14 = (bf16[8,128,256]{2,1,0:T(8,128)(2,1)}, bf16[8,128,256]{2,1,0:T(8,128)(2,1)S(1)}, u32[]{:S(2)}, u32[]{:S(2)}) collective-permute-start(bf16[8,128,256]{2,1,0:T(8,128)(2,1)} %get-tuple-element.53), channel_id=1, source_target_pairs={{0,8},{8,0},{16,24},{24,16},{1,9},{9,1},{17,25},{25,17},{2,10},{10... | collective-permute-start | bytes 1572872 | tf_op jit(solution)/shard_map/ppermute | solution.py:39
  214.6 13.4 %collective-permute-start.15 = (bf16[8,128,256]{2,1,0:T(8,128)(2,1)}, bf16[8,128,256]{2,1,0:T(8,128)(2,1)S(1)}, u32[]{:S(2)}, u32[]{:S(2)}) collective-permute-start(bf16[8,128,256]{2,1,0:T(8,128)(2,1)} %get-tuple-element.54), channel_id=1, source_target_pairs={{0,16},{8,24},{16,0},{24,8},{1,17},{9,25},{17,1},{25,9},{2,18},{10... | collective-permute-start | bytes 1572872 | tf_op jit(solution)/shard_map/ppermute | solution.py:39
  215.3 24.7 %collective-permute-start.16 = (bf16[8,128,256]{2,1,0:T(8,128)(2,1)}, bf16[8,128,256]{2,1,0:T(8,128)(2,1)}, u32[]{:S(2)}, u32[]{:S(2)}) collective-permute-start(bf16[8,128,256]{2,1,0:T(8,128)(2,1)} %get-tuple-element.55), channel_id=1, source_target_pairs={{0,24},{8,16},{16,8},{24,0},{1,25},{9,17},{17,9},{25,1},{2,26},{10... | collective-permute-start | bytes 1572872 | tf_op jit(solution)/shard_map/ppermute | solution.py:39
  (63 other events, 828.0 us)

commit v4 on v3

--- a/solution.py
+++ b/solution.py
@@ -77,15 +77,24 @@
     )(emb, positive.reshape(1, rows), user_expert.reshape(1, rows), item_expert.reshape(1, rows))
 
 
+def gather_rows(refs, to_ref):
+    height = to_ref.shape[1]
+    for k, ref in enumerate(refs):
+        to_ref[k] = ref[:height, :]
+
+
+def hits(first_ref, positive, c, own, shape):
+    wanted = positive - (first_ref[c // own] + c % own)
+    return lax.broadcasted_iota(jnp.int32, shape, 0) == wanted
+
+
 def stats_kernel(first_ref, *refs, blocks, count, chunk):
     users_refs, items_refs = refs[:blocks], refs[blocks : blocks + count]
-    out_ref, extra_ref, all_ref, col_ref, s_ref = refs[blocks + count :]
+    out_ref, all_ref, col_ref, s_ref = refs[blocks + count :]
     own, emb = items_refs[0].shape
     rows = users_refs[0].shape[0] - EXTRA
     n_cols = own * count
-    for k, ref in enumerate(users_refs):
-        all_ref[k] = ref[...]
-        extra_ref[k] = ref[rows:, :]
+    gather_rows(users_refs, all_ref)
     for k, ref in enumerate(items_refs):
         col_ref[k * own : (k + 1) * own, :] = ref[...]
 
@@ -106,9 +115,7 @@
                 part = s_ref[half, c : c + chunk, :]
                 probs = jnp.exp(part - top)
                 total = total + jnp.sum(probs.reshape(chunk // 8, 8, rows), axis=0)
-                wanted = positive - (first_ref[c // own] + c % own)
-                hit = lax.broadcasted_iota(jnp.int32, (chunk, rows), 0) == wanted
-                chosen = jnp.where(hit, part, 0.0)
+                chosen = jnp.where(hits(first_ref, positive, c, own, part.shape), part, 0.0)
                 picked = picked + jnp.sum(chosen.reshape(chunk // 8, 8, rows), axis=0)
             out_ref[block, 0:1, :] = top
             out_ref[block, 1:2, :] = jnp.sum(total, axis=0, keepdims=True)
@@ -126,11 +133,8 @@
     return pl.pallas_call(
         functools.partial(stats_kernel, blocks=blocks, count=count, chunk=64),
         in_specs=[SCALARS] + [WHOLE] * (blocks + count),
-        out_specs=[WHOLE] * 2,
-        out_shape=[
-            jax.ShapeDtypeStruct((blocks, 3, rows), F32),
-            jax.ShapeDtypeStruct((blocks, EXTRA, emb), BF16),
-        ],
+        out_specs=WHOLE,
+        out_shape=jax.ShapeDtypeStruct((blocks, 3, rows), F32),
         scratch_shapes=[
             pltpu.VMEM((blocks, height, emb), BF16),
             pltpu.VMEM((own * count, emb), BF16),
@@ -141,18 +145,39 @@
     )(first, *users, *items)
 
 
-def grad_kernel(first_ref, *refs, blocks, count, chunk):
+def merge(refs, block):
+    found = [ref[block ^ k] for k, ref in enumerate(refs)]
+    top = functools.reduce(jnp.maximum, [f[0:1] for f in found])
+    total = sum(f[1:2] * jnp.exp(f[0:1] - top) for f in found)
+    return top + jnp.log(total), sum(f[2:3] for f in found)
+
+
+def level_kernel(*refs):
+    level, picked = merge(refs[:-2], 0)
+    refs[-2][...] = level
+    refs[-1][...] = level - picked
+
+
+def levels(found):
+    rows = found[0].shape[2]
+    return pl.pallas_call(
+        level_kernel,
+        in_specs=[WHOLE] * len(found),
+        out_specs=[WHOLE] * 2,
+        out_shape=[jax.ShapeDtypeStruct((1, rows), F32)] * 2,
+        cost_estimate=SMALL,
+    )(*found)
+
+
+def user_kernel(first_ref, *refs, blocks, count, chunk):
     users_refs, items_refs = refs[:blocks], refs[blocks : blocks + count]
     refs = refs[blocks + count :]
-    stats_refs, refs = refs[:blocks], refs[blocks:]
-    loss_ref, near_ref, far_ref = refs[:3]
-    user_refs, refs = refs[3 : 3 + blocks], refs[3 + blocks :]
-    all_ref, col_ref, flip_ref, s_ref, g_ref, user_ref = refs
+    stats_refs, out_refs, refs = refs[:blocks], refs[blocks : 2 * blocks], refs[2 * blocks :]
+    all_ref, col_ref, flip_ref, s_ref, g_ref, sum_ref = refs
     own, emb = items_refs[0].shape
     rows = users_refs[0].shape[0] - EXTRA
     n_cols = own * count
-    for k, ref in enumerate(users_refs):
-        all_ref[k] = ref[...]
+    gather_rows(users_refs, all_ref)
     for k, ref in enumerate(items_refs):
         col_ref[k * own : (k + 1) * own, :] = ref[...]
         flip_ref[:, k * own : (k + 1) * own] = ref[...].T
@@ -163,68 +188,98 @@
             queries = all_ref[block, :rows, :] * jnp.asarray(SCALE, BF16)
             s_ref[half] = mm(col_ref[...], queries, 1, 1)
             positive = number(all_ref[block, rows:, :], 0)
-            found = [ref[block ^ k] for k, ref in enumerate(stats_refs)]
-            top = functools.reduce(jnp.maximum, [f[0:1] for f in found])
-            total = sum(f[1:2] * jnp.exp(f[0:1] - top) for f in found)
-            level = top + jnp.log(total)
-            loss_ref[pl.ds(block, 1), :] = level - sum(f[2:3] for f in found)
+            level, _ = merge(stats_refs, block)
             for c in range(0, n_cols, chunk):
                 probs = jnp.exp(s_ref[half, c : c + chunk, :] - level)
-                wanted = positive - (first_ref[c // own] + c % own)
-                hit = lax.broadcasted_iota(jnp.int32, (chunk, rows), 0) == wanted
-                g_ref[block, c : c + chunk, :] = jnp.where(hit, probs - 1.0, probs).astype(BF16)
-            user_ref[block] = mm(flip_ref[...], g_ref[block], 1, 0).T * SCALE
+                hit = hits(first_ref, positive, c, own, probs.shape)
+                g_ref[half, c : c + chunk, :] = jnp.where(hit, probs - 1.0, probs).astype(BF16)
+            sum_ref[block] = mm(flip_ref[...], g_ref[half], 1, 0).T * SCALE
         return carry
 
     lax.fori_loop(0, blocks // 2, pair, 0)
-    for k, ref in enumerate(user_refs):
-        ref[...] = user_ref[k]
-    for k in range(count):
-        left = jnp.concatenate([g_ref[b, k * own : (k + 1) * own, :] for b in range(blocks)], axis=1)
-        right = jnp.concatenate([all_ref[b, :rows, :] for b in range(blocks)], axis=0)
-        out_ref = near_ref if k < count // CORES else far_ref
-        out_ref[k % (count // CORES)] = mm(left, right, 1, 0) * SCALE
-
-
-def grads(first, users, items, gathered):
+    for k, ref in enumerate(out_refs):
+        ref[...] = sum_ref[k]
+
+
+def user_grads(first, users, items, found):
+    height, emb = users[0].shape
+    rows = height - EXTRA
+    own = items[0].shape[0]
+    blocks, count = len(users), len(items)
+    return pl.pallas_call(
+        functools.partial(user_kernel, blocks=blocks, count=count, chunk=64),
+        in_specs=[SCALARS] + [WHOLE] * (2 * blocks + count),
+        out_specs=[WHOLE] * blocks,
+        out_shape=[jax.ShapeDtypeStruct((rows, emb), F32)] * blocks,
+        scratch_shapes=[
+            pltpu.VMEM((blocks, height, emb), BF16),
+            pltpu.VMEM((own * count, emb), BF16),
+            pltpu.VMEM((emb, own * count), BF16),
+            pltpu.VMEM((2, own * count, rows), F32),
+            pltpu.VMEM((2, own * count, rows), BF16),
+            pltpu.VMEM((blocks, rows, emb), F32),
+        ],
+        compiler_params=pltpu.CompilerParams(vmem_limit_bytes=48 * MIB),
+        cost_estimate=SMALL,
+    )(first, *users, *items, *found)
+
+
+def item_kernel(first_ref, *refs, blocks, count, chunk):
+    users_refs, items_refs = refs[:blocks], refs[blocks : blocks + count]
+    near_ref, far_ref, refs = refs[blocks + count], refs[blocks + count + 1], refs[blocks + count + 2 :]
+    out_refs, refs = refs[:count], refs[count:]
+    extra_ref, all_ref, row_ref, col_ref, level_ref, s_ref, g_ref = refs
+    own, emb = items_refs[0].shape
+    rows = users_refs[0].shape[0] - EXTRA
+    n_cols = own * count
+    gather_rows(users_refs, all_ref)
+    level_ref[: blocks // 2] = near_ref[...]
+    level_ref[blocks // 2 :] = far_ref[...]
+    for k, ref in enumerate(users_refs):
+        extra_ref[k] = ref[rows:, :]
+        row_ref[k * rows : (k + 1) * rows, :] = ref[:rows, :]
+    for k, ref in enumerate(items_refs):
+        col_ref[k * own : (k + 1) * own, :] = ref[...]
+
+    for block in range(blocks):
+        half = block % 2
+        queries = all_ref[block, :rows, :] * jnp.asarray(SCALE, BF16)
+        s_ref[half] = mm(col_ref[...], queries, 1, 1)
+        positive = number(all_ref[block, rows:, :], 0)
+        level = level_ref[block]
+        for c in range(0, n_cols, chunk):
+            probs = jnp.exp(s_ref[half, c : c + chunk, :] - level)
+            hit = hits(first_ref, positive, c, own, probs.shape)
+            low = jnp.where(hit, probs - 1.0, probs).astype(BF16)
+            g_ref[c : c + chunk, block * rows : (block + 1) * rows] = low
+
+    for k, ref in enumerate(out_refs):
+        ref[...] = mm(g_ref[k * own : (k + 1) * own, :], row_ref[...], 1, 0) * SCALE
+
+
+def item_grads(first, users, items, near, far):
     height, emb = users[0].shape
     rows = height - EXTRA
     own = items[0].shape[0]
     blocks, count = len(users), len(items)
     results = pl.pallas_call(
-        functools.partial(grad_kernel, blocks=blocks, count=count, chunk=64),
-        in_specs=[SCALARS] + [WHOLE] * (2 * blocks + count),
-        out_specs=[WHOLE] * (3 + blocks),
-        out_shape=[jax.ShapeDtypeStruct((blocks, rows), F32)]
-        + [jax.ShapeDtypeStruct((count // CORES, own, emb), F32)] * CORES
-        + [jax.ShapeDtypeStruct((rows, emb), F32)] * blocks,
+        functools.partial(item_kernel, blocks=blocks, count=count, chunk=64),
+        in_specs=[SCALARS] + [WHOLE] * (blocks + count + 2),
+        out_specs=[WHOLE] * (count + 1),
+        out_shape=[jax.ShapeDtypeStruct((own, emb), F32)] * count
+        + [jax.ShapeDtypeStruct((blocks, EXTRA, emb), BF16)],
         scratch_shapes=[
             pltpu.VMEM((blocks, height, emb), BF16),
+            pltpu.VMEM((blocks * rows, emb), BF16),
             pltpu.VMEM((own * count, emb), BF16),
-            pltpu.VMEM((emb, own * count), BF16),
+            pltpu.VMEM((blocks, 1, rows), F32),
             pltpu.VMEM((2, own * count, rows), F32),
-            pltpu.VMEM((blocks, own * count, rows), BF16),
-            pltpu.VMEM((blocks, rows, emb), F32),
+            pltpu.VMEM((own * count, blocks * rows), BF16),
         ],
-        compiler_params=pltpu.CompilerParams(vmem_limit_bytes=56 * MIB),
-        cost_estimate=SMALL,
-    )(first, *users, *items, *gathered)
-    return results[0][0], results[1], results[2], results[3:]
-
-
-def add_kernel(a_ref, b_ref, *out_refs):
-    for k, out_ref in enumerate(out_refs):
-        out_ref[...] = a_ref[k] + b_ref[k]
-
-
-def add(a, b):
-    return pl.pallas_call(
-        add_kernel,
-        in_specs=[WHOLE] * 2,
-        out_specs=[WHOLE] * a.shape[0],
-        out_shape=[jax.ShapeDtypeStruct(a.shape[1:], F32)] * a.shape[0],
-        cost_estimate=SMALL,
-    )(a, b)
+        compiler_params=pltpu.CompilerParams(vmem_limit_bytes=48 * MIB),
+        cost_estimate=SMALL,
+    )(first, *users, *items, near, far)
+    return results[:count], results[count]
 
 
 def cut_kernel(in_ref, out_ref):
@@ -251,19 +306,18 @@
     return (place == target).astype(F32).astype(BF16)
 
 
-def hidden_kernel(me_ref, near_ref, far_ref, hidden_ref, *out_refs, tower):
+def hidden_kernel(me_ref, extra_ref, hidden_ref, *out_refs, tower):
     pair, span = out_refs[0].shape[:2]
     for half in range(pair):
         apart = me_ref[1] ^ (pl.program_id(0) * pair + half)
-        line = apart // CORES
-        extra = jnp.where(apart % CORES == 0, near_ref[line].astype(F32), far_ref[line].astype(F32))
-        onehot = onehot_of(number(extra, 1 + tower), me_ref[0], len(out_refs))
+        place = apart % CORES * (extra_ref.shape[0] // CORES) + apart // CORES
+        onehot = onehot_of(number(extra_ref[place], 1 + tower), me_ref[0], len(out_refs))
         moved = mm(onehot, hidden_ref[half], 1, 0).astype(BF16)
         for k, out_ref in enumerate(out_refs):
             out_ref[half] = moved[k * span : (k + 1) * span, :]
 
 
-def slot_hidden(me, near, far, hidden, groups, tower):
+def slot_hidden(me, extra, hidden, groups, tower):
     blocks, rows, width = hidden.shape
     span = EXPERTS * CAP // groups
     pair = 2
@@ -272,14 +326,13 @@
         grid=(blocks // pair,),
         in_specs=[
             SCALARS,
-            pl.BlockSpec(near.shape, lambda b: (0, 0, 0)),
-            pl.BlockSpec(far.shape, lambda b: (0, 0, 0)),
+            pl.BlockSpec(extra.shape, lambda b: (0, 0, 0)),
             pl.BlockSpec((pair, rows, width), lambda b: (b, 0, 0)),
         ],
         out_specs=[pl.BlockSpec((pair, span, width), lambda b: (b, 0, 0))] * groups,
         out_shape=[jax.ShapeDtypeStruct((blocks, span, width), BF16)] * groups,
         cost_estimate=SMALL,
-    )(me, near, far, hidden)
+    )(me, extra, hidden)
 
 
 def total_kernel(*refs):
@@ -361,46 +414,54 @@
     part = lax.axis_index("item").astype(jnp.int32)
     others = me ^ jnp.arange(groups, dtype=jnp.int32)
     both = part ^ jnp.arange(CORES, dtype=jnp.int32)
-    first = ((both[:, None] * groups + others[None, :]) * rows).reshape(-1)
     order = (both[:, None] ^ (CORES * jnp.arange(lines, dtype=jnp.int32))[None, :]).reshape(-1)
+    first_cross = (order * groups + me) * rows
+    first_plane = (part * groups + others) * rows
     me = jnp.stack([me, part])
 
     def by_part(hidden):
         return lax.all_to_all(cut(hidden, parts), "item", split_axis=0, concat_axis=0, tiled=True)
 
-    def slots_of(cols, tower):
-        return slot_hidden(me, extra_near, extra_far, cols, groups, tower)
-
+    item_line = exchange([item_emb] * lines, "item", CORES)
     packed = pack(user_emb, positive, user_expert, item_expert)
-    users = exchange([packed] * lines, "item", CORES)
-    near = exchange([item_emb] * groups, "user")
-    item_hidden, user_hidden, *near = tie(item_hidden, user_hidden, *near)
+    user_plane = exchange([packed] * groups, "user")
+    item_hidden, again, item_emb, *item_line = tie(item_hidden, packed, item_emb, *item_line)
+    item_cross = item_line + [swap(piece, "item", 1) for piece in item_line]
+    user_line = exchange([again] * lines, "item", CORES)
     item_cols = by_part(item_hidden)
-
-    items = near + [swap(piece, "item", 1) for piece in near]
-    found, extra_near = stats(first, users, items)
-    gathered = exchange([found] * lines, "item", CORES)
-    extra_far = swap(extra_near, "item", 1)
-
-    row_loss, item_near, item_far, user_parts = grads(first, users, items, gathered)
-    user_pieces = exchange(user_parts, "item", CORES)
-    item_cols, user_hidden, item_far = tie(item_cols, user_hidden, item_far)
+    item_plane = exchange([item_emb] * groups, "user")
+    user_cross = user_line + [swap(piece, "item", 1) for piece in user_line]
+
+    found = exchange([stats(first_cross, user_plane, item_cross)] * groups, "user")
+    level, loss = levels(found)
+    level_near = jnp.stack(exchange([level] * lines, "item", CORES))
+    level_far = swap(level_near, "item", 1)
+    user_pieces = exchange(user_grads(first_cross, user_plane, item_cross, found), "user")
+    item_parts, extra = item_grads(first_plane, user_cross, item_plane, level_near, level_far)
+    item_cols, user_hidden, extra = tie(item_cols, user_hidden, extra)
     user_cols = by_part(user_hidden)
-    item_pieces = exchange(add(item_near, swap(item_far, "item", 1)), "user")
-    item_rows = exchange(slots_of(item_cols, 1), "user")
+    item_pieces = exchange(item_parts, "user")
+    user_pieces[0], *item_slots = tie(
+        user_pieces[0], *slot_hidden(me, extra, item_cols, groups, 1)
+    )
+    item_rows = exchange(item_slots, "user")
 
     user_lines = exchange([total(user_pieces)] * lines, "item", CORES)
     item_lines = exchange([total(item_pieces)] * lines, "item", CORES)
-    user_rows = exchange(slots_of(user_cols, 0), "user")
+    item_lines[0], *user_slots = tie(
+        item_lines[0], *slot_hidden(me, extra, user_cols, groups, 0)
+    )
+    user_rows = exchange(user_slots, "user")
 
     def spread(grad_lines, tower):
-        got = exchange(select(me, extra_near, grad_lines, groups, tower), "user")
+        got = exchange(select(me, extra[:lines], grad_lines, groups, tower), "user")
         return got + [swap(piece, "item", 1) for piece in got]
 
     user_grad = spread(user_lines, 0)
     item_grad = spread(item_lines, 1)
     item_weight_grad = outer(order, item_rows, item_grad)
     user_weight_grad = outer(order, user_rows, user_grad)
+    row_loss = loss[0]
     return (row_loss, user_weight_grad, item_weight_grad)
 
 

time: 247 us -> 221 us (0.89)
  waiting for transfers between devices: 127 us -> 98.9 us
  starting transfers between devices: 62.9 us -> 69.3 us
  Pallas kernels: 43.9 us -> 41.2 us
    ppermute x47 -> x59, waiting for transfers between devices: 127 us -> 98.9 us  [swap(): return lax.ppermute(piece, axis, [(j, j ^ bits) for j in range(size)])]
    ppermute x47 -> x59, starting transfers between devices: 50.2 us -> 56.9 us  [swap(): return lax.ppermute(piece, axis, [(j, j ^ bits) for j in range(size)])]
    unnamed x92 -> x60, local copies, waits for them, and re-layouts: 6.55 us -> 5.64 us
    pallas_call x2 -> x3, Pallas kernels: 10.4 us -> 9.5 us  [the longest x1 4.51 us: user_grads(): pl.pallas_call(functools.partial(user_kernel, blocks=blocks, count=count,...]
  transfers between devices with their start and end apart: 49 -> 61, of which waited for: 20 -> 22; matrix products, arithmetic and copies ran while one was open for 1% -> 1% of each run, Pallas kernels for 16% -> 16%
where the time goes in v4:
time: 221 us; the launch traced here: 218 us
  waiting for transfers between devices  98.9 us (45%)
  starting transfers between devices  69.3 us (31%)
  Pallas kernels  41.2 us (19%)
  local copies, waits for them, and re-layouts  6.33 us (3%)
    ppermute x59, waiting for transfers between devices, swap(): return lax.ppermute(piece, axis, [(j, j ^ bits) for j in range(size)])  98.9 us
    ppermute x59, starting transfers between devices, swap(): return lax.ppermute(piece, axis, [(j, j ^ bits) for j in range(size)])  56.9 us
    all_to_all x2, starting transfers between devices, by_part(): lax.all_to_all(cut(hidden, parts), 'item', split_axis=0, concat_axis=0, t...  12.3 us
    pallas_call x2, Pallas kernels, slot_hidden(): pl.pallas_call(functools.partial(hidden_kernel, tower=tower), grid=(block...  7.85 us
    unnamed x60, local copies, waits for them, and re-layouts  5.64 us
    pallas_call x2, Pallas kernels, outer(): pl.pallas_call(functools.partial(outer_kernel, groups=groups), in_specs=[...  5.26 us
    pallas_call x2, Pallas kernels, select(): pl.pallas_call(functools.partial(select_kernel, tower=tower, lines=lines)...  4.88 us
    pallas_call x2, Pallas kernels, cut(): pl.pallas_call(cut_kernel, in_specs=[WHOLE], out_specs=WHOLE, out_shape=j...  4.59 us
  transfers between devices with their start and end apart: 61, of which 22 were waited for; matrix products, arithmetic and copies ran while one was open for 1% of the time, Pallas kernels for 16%

profile of v4, /device:TPU:11, one launch (start us, length us, event | category | flops | bytes accessed | tf_op | source)
XLA Modules:
  0.0 218.0 jit_solution(7195729275670617518)
XLA Ops:
  0.9 2.3 %collective-permute-start.4 = (bf16[256,256]{1,0:T(8,128)(2,1)}, bf16[256,256]{1,0:T(8,128)(2,1)S(1)}, u32[]{:S(2)}, u32[]{:S(2)}) collective-permute-start(bf16[256,256]{1,0:T(8,128)(2,1)} %refs_4_.1), channel_id=1, source_target_pairs={{0,4},{1,5},{2,6},{3,7},{4,0},{5,1},{6,2},{7,3},{8,12},{9,13},{10,... | collective-permute-start | bytes 393224 | tf_op jit(solution)/shard_map/ppermute | solution.py:39
  5.3 3.8 %collective-permute-done.4.refs_6_ = bf16[256,256]{1,0:T(8,128)(2,1)S(1)} collective-permute-done((bf16[256,256]{1,0:T(8,128)(2,1)}, bf16[256,256]{1,0:T(8,128)(2,1)S(1)}, u32[]{:S(2)}, u32[]{:S(2)}) %collective-permute-start.4) | collective-permute-done | bytes 131104 | tf_op jit(solution)/shard_map/ppermute | solution.py:39
  9.1 5.3 %collective-permute-done.5.refs_7_ = bf16[256,256]{1,0:T(8,128)(2,1)S(1)} collective-permute-done((bf16[256,256]{1,0:T(8,128)(2,1)}, bf16[256,256]{1,0:T(8,128)(2,1)S(1)}, u32[]{:S(2)}, u32[]{:S(2)}) %collective-permute-start.5) | collective-permute-done | bytes 131104 | tf_op jit(solution)/shard_map/ppermute | solution.py:39
  16.7 6.0 %all-to-all-start = ((bf16[8,256,256]{2,1,0:T(8,128)(2,1)}), bf16[8,256,256]{2,1,0:T(8,128)(2,1)}, u32[]{:S(2)}, u32[]{:S(2)}) async-start(bf16[8,256,256]{2,1,0:T(8,128)(2,1)} %shard_map.99), calls=%async_computation | async-start | bytes 2097152 | tf_op jit(solution)/shard_map/all_to_all | solution.py:423
  37.3 3.6 %shard_map.95.refs_0_.refs_12_ = f32[4,3,256]{2,1,0:T(4,128)S(1)} custom-call(s32[8]{0:T(128)S(1)} %add_multiply_fusion.1.first_ref, bf16[272,256]{1,0:T(8,128)(2,1)S(1)} %copy-done, bf16[272,256]{1,0:T(8,128)(2,1)S(1)} %collective-permute-done.refs_1_, bf16[272,256]{1,0:T(8,128)(2,1)S(1)} %collective-permute-done.1.refs_2_, ...), custom_call_target="tpu_custom_call" | custom-call | flops 1024 | bytes 1024 | tf_op jit(solution)/shard_map/pallas_call | solution.py:133
  41.3 2.7 %collective-permute-done.10.refs_1_.refs_13_ = f32[4,3,256]{2,1,0:T(4,128)S(1)} collective-permute-done((f32[4,3,256]{2,1,0:T(4,128)S(1)}, f32[4,3,256]{2,1,0:T(4,128)S(1)}, u32[]{:S(2)}, u32[]{:S(2)}) %collective-permute-start.10) | collective-permute-done | bytes 12320 | tf_op jit(solution)/shard_map/ppermute | solution.py:39
  44.2 2.7 %collective-permute-done.11.refs_2_.refs_14_ = f32[4,3,256]{2,1,0:T(4,128)S(1)} collective-permute-done((f32[4,3,256]{2,1,0:T(4,128)S(1)}, f32[4,3,256]{2,1,0:T(4,128)S(1)}, u32[]{:S(2)}, u32[]{:S(2)}) %collective-permute-start.11) | collective-permute-done | bytes 12320 | tf_op jit(solution)/shard_map/ppermute | solution.py:39
  46.9 3.5 %collective-permute-done.12.refs_3_.refs_15_ = f32[4,3,256]{2,1,0:T(4,128)S(1)} collective-permute-done((f32[4,3,256]{2,1,0:T(4,128)S(1)}, f32[4,3,256]{2,1,0:T(4,128)S(1)}, u32[]{:S(2)}, u32[]{:S(2)}) %collective-permute-start.12) | collective-permute-done | bytes 12320 | tf_op jit(solution)/shard_map/ppermute | solution.py:39
  53.5 2.4 %collective-permute-start.24 = (f32[1,256]{1,0:T(1,128)}, f32[1,256]{1,0:T(1,128)S(1)}, u32[]{:S(2)}, u32[]{:S(2)}) collective-permute-start(f32[1,256]{1,0:T(1,128)} %get-tuple-element.57), channel_id=1, source_target_pairs={{0,4},{1,5},{2,6},{3,7},{4,0},{5,1},{6,2},{7,3},{8,12},{9,13},{10,... | collective-permute-start | bytes 3080 | tf_op jit(solution)/shard_map/ppermute | solution.py:39
  59.3 2.6 %collective-permute-start.16 = (bf16[272,256]{1,0:T(8,128)(2,1)S(1)}, bf16[272,256]{1,0:T(8,128)(2,1)S(1)}, u32[]{:S(2)}, u32[]{:S(2)}) collective-permute-start(bf16[272,256]{1,0:T(8,128)(2,1)S(1)} %copy-done), channel_id=1, source_target_pairs={{0,1},{1,0},{2,3},{3,2},{4,5},{5,4},{6,7},{7,6},{8,9},{9,8},{10,11... | collective-permute-start | bytes 417800 | tf_op jit(solution)/shard_map/ppermute | solution.py:39
  66.4 3.6 %shard_map.97 = (f32[256,256]{1,0:T(8,128)S(1)}, f32[256,256]{1,0:T(8,128)S(1)}, f32[256,256]{1,0:T(8,128)S(1)}, f32[256,256]{1,0:T(8,128)S(1)}, bf16[8,16,256]{2,1,0:T(8,128)(2,1)S(1)}) custom-call(s32[4]{0:T(128)S(1)} %add_multiply_fusion.first_ref, bf16[272,256]{1,0:T(8,128)(2,1)S(1)} %copy-done, bf16[272,256]{1,0:T(8,128)(2,1)S(1)} %collective-permute-done.13.refs_1_, ...), custom_call_target="tpu_custom_call" | custom-call | flops 1024 | bytes 1024 | tf_op jit(solution)/shard_map/pallas_call | solution.py:265
  71.4 2.3 %shard_map.100 = bf16[8,256,256]{2,1,0:T(8,128)(2,1)} custom-call(bf16[256,2048]{1,0:T(8,128)(2,1)} %in_ref.1), custom_call_target="tpu_custom_call" | custom-call | flops 1024 | bytes 1024 | tf_op jit(solution)/shard_map/pallas_call | solution.py:293
  73.7 6.3 %all-to-all-start.1 = ((bf16[8,256,256]{2,1,0:T(8,128)(2,1)}), bf16[8,256,256]{2,1,0:T(8,128)(2,1)}, u32[]{:S(2)}, u32[]{:S(2)}) async-start(bf16[8,256,256]{2,1,0:T(8,128)(2,1)} %shard_map.100), calls=%async_computation.1 | async-start | bytes 2097152 | tf_op jit(solution)/shard_map/all_to_all | solution.py:423
  80.0 4.5 %shard_map.102 = (f32[256,256]{1,0:T(8,128)S(1)}, f32[256,256]{1,0:T(8,128)S(1)}, f32[256,256]{1,0:T(8,128)S(1)}, f32[256,256]{1,0:T(8,128)S(1)}) custom-call(s32[8]{0:T(128)S(1)} %add_multiply_fusion.1.first_ref, bf16[272,256]{1,0:T(8,128)(2,1)S(1)} %copy-done, bf16[272,256]{1,0:T(8,128)(2,1)S(1)} %collective-permute-done.refs_1_, ...), custom_call_target="tpu_custom_call" | custom-call | flops 1024 | bytes 1024 | tf_op jit(solution)/shard_map/pallas_call | solution.py:209
  88.6 3.9 %shard_map.103 = (bf16[8,128,256]{2,1,0:T(8,128)(2,1)}, bf16[8,128,256]{2,1,0:T(8,128)(2,1)}, bf16[8,128,256]{2,1,0:T(8,128)(2,1)}, bf16[8,128,256]{2,1,0:T(8,128)(2,1)}) custom-call(s32[2]{0:T(128)} %pad_add_fusion.me_ref, bf16[8,16,256]{2,1,0:T(8,128)(2,1)} %copy-done.4, bf16[8,256,256]{2,1,0:T(8,128)(2,1)} %all-to-all-done.hidden_ref), custom_call_target="tpu_custom_call" | custom-call | flops 1024 | bytes 1024 | tf_op jit(solution)/shard_map/pallas_call | solution.py:324
  93.1 5.7 %collective-permute-done.35.refs_3_ = f32[256,256]{1,0:T(8,128)S(1)} collective-permute-done((f32[256,256]{1,0:T(8,128)S(1)}, f32[256,256]{1,0:T(8,128)S(1)}, u32[]{:S(2)}, u32[]{:S(2)}) %collective-permute-start.35) | collective-permute-done | bytes 262176 | tf_op jit(solution)/shard_map/ppermute | solution.py:39
  107.3 4.2 %collective-permute-done.37.refs_2_ = bf16[256,256]{1,0:T(8,128)(2,1)S(1)} collective-permute-done((bf16[256,256]{1,0:T(8,128)(2,1)}, bf16[256,256]{1,0:T(8,128)(2,1)S(1)}, u32[]{:S(2)}, u32[]{:S(2)}) %collective-permute-start.37) | collective-permute-done | bytes 131104 | tf_op jit(solution)/shard_map/ppermute | solution.py:39
  111.6 5.8 %collective-permute-done.38.refs_3_ = bf16[256,256]{1,0:T(8,128)(2,1)S(1)} collective-permute-done((bf16[256,256]{1,0:T(8,128)(2,1)}, bf16[256,256]{1,0:T(8,128)(2,1)S(1)}, u32[]{:S(2)}, u32[]{:S(2)}) %collective-permute-start.38) | collective-permute-done | bytes 131104 | tf_op jit(solution)/shard_map/ppermute | solution.py:39
  118.0 2.4 %shard_map.105 = (bf16[4,128,256]{2,1,0:T(8,128)(2,1)}, bf16[4,128,256]{2,1,0:T(8,128)(2,1)}, bf16[4,128,256]{2,1,0:T(8,128)(2,1)}, bf16[4,128,256]{2,1,0:T(8,128)(2,1)}) custom-call(s32[2]{0:T(128)} %pad_add_fusion.me_ref, bf16[4,16,256]{2,1,0:T(8,128)(2,1)} %slice.4.extra_ref, bf16[256,256]{1,0:T(8,128)(2,1)} %shard_map.104.refs_0_, ...), custom_call_target="tpu_custom_call" | custom-call | flops 1024 | bytes 1024 | tf_op jit(solution)/shard_map/pallas_call | solution.py:371
  125.0 2.7 %collective-permute-start.50 = (bf16[256,256]{1,0:T(8,128)(2,1)}, bf16[256,256]{1,0:T(8,128)(2,1)S(1)}, u32[]{:S(2)}, u32[]{:S(2)}) collective-permute-start(bf16[256,256]{1,0:T(8,128)(2,1)} %shard_map.98.refs_0_), channel_id=1, source_target_pairs={{0,4},{1,5},{2,6},{3,7},{4,0},{5,1},{6,2},{7,3},{8,12},{9,13},{10,... | collective-permute-start | bytes 393224 | tf_op jit(solution)/shard_map/ppermute | solution.py:39
  129.3 6.6 %collective-permute-done.50.refs_2_ = bf16[256,256]{1,0:T(8,128)(2,1)S(1)} collective-permute-done((bf16[256,256]{1,0:T(8,128)(2,1)}, bf16[256,256]{1,0:T(8,128)(2,1)S(1)}, u32[]{:S(2)}, u32[]{:S(2)}) %collective-permute-start.50) | collective-permute-done | bytes 131104 | tf_op jit(solution)/shard_map/ppermute | solution.py:39
  136.1 2.7 %collective-permute-done.51.refs_3_ = bf16[256,256]{1,0:T(8,128)(2,1)S(1)} collective-permute-done((bf16[256,256]{1,0:T(8,128)(2,1)}, bf16[256,256]{1,0:T(8,128)(2,1)S(1)}, u32[]{:S(2)}, u32[]{:S(2)}) %collective-permute-start.51) | collective-permute-done | bytes 131104 | tf_op jit(solution)/shard_map/ppermute | solution.py:39
  139.5 2.3 %collective-permute-start.42 = (bf16[4,128,256]{2,1,0:T(8,128)(2,1)}, bf16[4,128,256]{2,1,0:T(8,128)(2,1)S(1)}, u32[]{:S(2)}, u32[]{:S(2)}) collective-permute-start(bf16[4,128,256]{2,1,0:T(8,128)(2,1)} %get-tuple-element.84.refs_4_), channel_id=1, source_target_pairs={{0,1},{1,0},{2,3},{3,2},{4,5},{5,4},{6,7},{7,6},{8,9},{9,8},{10,11... | collective-permute-start | bytes 786440 | tf_op jit(solution)/shard_map/ppermute | solution.py:39
  141.8 8.3 %collective-permute-done.40.refs_6_ = bf16[4,128,256]{2,1,0:T(8,128)(2,1)S(1)} collective-permute-done((bf16[4,128,256]{2,1,0:T(8,128)(2,1)}, bf16[4,128,256]{2,1,0:T(8,128)(2,1)S(1)}, u32[]{:S(2)}, u32[]{:S(2)}) %collective-permute-start.40) | collective-permute-done | bytes 262176 | tf_op jit(solution)/shard_map/ppermute | solution.py:39
  150.1 4.9 %collective-permute-start.43 = (bf16[4,128,256]{2,1,0:T(8,128)(2,1)S(1)}, bf16[4,128,256]{2,1,0:T(8,128)(2,1)S(1)}, u32[]{:S(2)}, u32[]{:S(2)}) collective-permute-start(bf16[4,128,256]{2,1,0:T(8,128)(2,1)S(1)} %collective-permute-done.39.refs_5_), channel_id=1, source_target_pairs={{0,1},{1,0},{2,3},{3,2},{4,5},{5,4},{6,7},{7,6},{8,9},{9,8},{10,11... | collective-permute-start | bytes 786440 | tf_op jit(solution)/shard_map/ppermute | solution.py:39
  155.6 3.9 %shard_map.101 = (bf16[8,128,256]{2,1,0:T(8,128)(2,1)}, bf16[8,128,256]{2,1,0:T(8,128)(2,1)}, bf16[8,128,256]{2,1,0:T(8,128)(2,1)}, bf16[8,128,256]{2,1,0:T(8,128)(2,1)}) custom-call(s32[2]{0:T(128)} %pad_add_fusion.me_ref, bf16[8,16,256]{2,1,0:T(8,128)(2,1)} %copy-done.4, bf16[8,256,256]{2,1,0:T(8,128)(2,1)} %all-to-all-done.1.hidden_ref), custom_call_target="tpu_custom_call" | custom-call | flops 1024 | bytes 1024 | tf_op jit(solution)/shard_map/pallas_call | solution.py:324
  159.5 2.4 %shard_map.107 = (bf16[4,128,256]{2,1,0:T(8,128)(2,1)}, bf16[4,128,256]{2,1,0:T(8,128)(2,1)}, bf16[4,128,256]{2,1,0:T(8,128)(2,1)}, bf16[4,128,256]{2,1,0:T(8,128)(2,1)}) custom-call(s32[2]{0:T(128)} %pad_add_fusion.me_ref, bf16[4,16,256]{2,1,0:T(8,128)(2,1)} %slice.4.extra_ref, bf16[256,256]{1,0:T(8,128)(2,1)} %shard_map.98.refs_0_, ...), custom_call_target="tpu_custom_call" | custom-call | flops 1024 | bytes 1024 | tf_op jit(solution)/shard_map/pallas_call | solution.py:371
  165.1 16.1 %collective-permute-done.52.refs_5_ = bf16[4,128,256]{2,1,0:T(8,128)(2,1)S(1)} collective-permute-done((bf16[4,128,256]{2,1,0:T(8,128)(2,1)}, bf16[4,128,256]{2,1,0:T(8,128)(2,1)S(1)}, u32[]{:S(2)}, u32[]{:S(2)}) %collective-permute-start.52) | collective-permute-done | bytes 262176 | tf_op jit(solution)/shard_map/ppermute | solution.py:39
  183.6 14.3 %collective-permute-done.54.refs_7_ = bf16[4,128,256]{2,1,0:T(8,128)(2,1)S(1)} collective-permute-done((bf16[4,128,256]{2,1,0:T(8,128)(2,1)}, bf16[4,128,256]{2,1,0:T(8,128)(2,1)S(1)}, u32[]{:S(2)}, u32[]{:S(2)}) %collective-permute-start.54) | collective-permute-done | bytes 262176 | tf_op jit(solution)/shard_map/ppermute | solution.py:39
  199.3 10.8 %collective-permute-done.31.refs_2_ = bf16[8,128,256]{2,1,0:T(8,128)(2,1)S(1)} collective-permute-done((bf16[8,128,256]{2,1,0:T(8,128)(2,1)}, bf16[8,128,256]{2,1,0:T(8,128)(2,1)S(1)}, u32[]{:S(2)}, u32[]{:S(2)}) %collective-permute-start.31) | collective-permute-done | bytes 524320 | tf_op jit(solution)/shard_map/ppermute | solution.py:39
  212.7 2.6 %shard_map.106 = f32[8,256,256]{2,1,0:T(8,128)} custom-call(s32[8]{0:T(128)S(1)} %xor.38.order_ref, bf16[8,128,256]{2,1,0:T(8,128)(2,1)S(1)} %copy-done.3, bf16[8,128,256]{2,1,0:T(8,128)(2,1)S(1)} %collective-permute-done.30.refs_1_, bf16[8,128,256]{2,1,0:T(8,128)(2,1)S(1)} %collective-permute-done.31.refs_2_, ...), custom_call_target="tpu_custom_call" | custom-call | flops 1024 | bytes 1024 | tf_op jit(solution)/shard_map/pallas_call | solution.py:398
  215.4 2.6 %shard_map.108 = f32[8,256,256]{2,1,0:T(8,128)} custom-call(s32[8]{0:T(128)S(1)} %xor.38.order_ref, bf16[8,128,256]{2,1,0:T(8,128)(2,1)S(1)} %copy-done.2, bf16[8,128,256]{2,1,0:T(8,128)(2,1)S(1)} %collective-permute-done.46.refs_1_, bf16[8,128,256]{2,1,0:T(8,128)(2,1)S(1)} %collective-permute-done.47.refs_2_, ...), custom_call_target="tpu_custom_call" | custom-call | flops 1024 | bytes 1024 | tf_op jit(solution)/shard_map/pallas_call | solution.py:398
  (174 shorter events, 62.9 us)
Async XLA Ops:
  3.2 11.2 %collective-permute-start.5 = (bf16[256,256]{1,0:T(8,128)(2,1)}, bf16[256,256]{1,0:T(8,128)(2,1)S(1)}, u32[]{:S(2)}, u32[]{:S(2)}) collective-permute-start(bf16[256,256]{1,0:T(8,128)(2,1)} %refs_4_.1), channel_id=1, source_target_pairs={{0,6},{1,7},{2,4},{3,5},{4,2},{5,3},{6,0},{7,1},{8,14},{9,15},{10,... | collective-permute-start | bytes 393224 | tf_op jit(solution)/shard_map/ppermute | solution.py:39
  16.7 54.7 %all-to-all-start = ((bf16[8,256,256]{2,1,0:T(8,128)(2,1)}), bf16[8,256,256]{2,1,0:T(8,128)(2,1)}, u32[]{:S(2)}, u32[]{:S(2)}) async-start(bf16[8,256,256]{2,1,0:T(8,128)(2,1)} %shard_map.99), calls=%async_computation | async-start | bytes 2097152 | tf_op jit(solution)/shard_map/all_to_all | solution.py:423
  31.5 22.0 %collective-permute-start.13 = (bf16[272,256]{1,0:T(8,128)(2,1)S(1)}, bf16[272,256]{1,0:T(8,128)(2,1)S(1)}, u32[]{:S(2)}, u32[]{:S(2)}) collective-permute-start(bf16[272,256]{1,0:T(8,128)(2,1)S(1)} %copy-done), channel_id=1, source_target_pairs={{0,2},{1,3},{2,0},{3,1},{4,6},{5,7},{6,4},{7,5},{8,10},{9,11},{10,... | collective-permute-start | bytes 417800 | tf_op jit(solution)/shard_map/ppermute | solution.py:39
  32.0 24.0 %collective-permute-start.14 = (bf16[272,256]{1,0:T(8,128)(2,1)S(1)}, bf16[272,256]{1,0:T(8,128)(2,1)S(1)}, u32[]{:S(2)}, u32[]{:S(2)}) collective-permute-start(bf16[272,256]{1,0:T(8,128)(2,1)S(1)} %copy-done), channel_id=1, source_target_pairs={{0,4},{1,5},{2,6},{3,7},{4,0},{5,1},{6,2},{7,3},{8,12},{9,13},{10,... | collective-permute-start | bytes 417800 | tf_op jit(solution)/shard_map/ppermute | solution.py:39
  33.8 25.5 %collective-permute-start.15 = (bf16[272,256]{1,0:T(8,128)(2,1)S(1)}, bf16[272,256]{1,0:T(8,128)(2,1)S(1)}, u32[]{:S(2)}, u32[]{:S(2)}) collective-permute-start(bf16[272,256]{1,0:T(8,128)(2,1)S(1)} %copy-done), channel_id=1, source_target_pairs={{0,6},{1,7},{2,4},{3,5},{4,2},{5,3},{6,0},{7,1},{8,14},{9,15},{10,... | collective-permute-start | bytes 417800 | tf_op jit(solution)/shard_map/ppermute | solution.py:39
  36.1 16.3 %collective-permute-start.21 = (bf16[256,256]{1,0:T(8,128)(2,1)S(1)}, bf16[256,256]{1,0:T(8,128)(2,1)S(1)}, u32[]{:S(2)}, u32[]{:S(2)}) collective-permute-start(bf16[256,256]{1,0:T(8,128)(2,1)S(1)} %copy-done.1), channel_id=1, source_target_pairs={{0,16},{8,24},{16,0},{24,8},{1,17},{9,25},{17,1},{25,9},{2,18},{10... | collective-permute-start | bytes 393224 | tf_op jit(solution)/shard_map/ppermute | solution.py:39
  50.4 14.8 %collective-permute-start.22 = (bf16[256,256]{1,0:T(8,128)(2,1)S(1)}, bf16[256,256]{1,0:T(8,128)(2,1)S(1)}, u32[]{:S(2)}, u32[]{:S(2)}) collective-permute-start(bf16[256,256]{1,0:T(8,128)(2,1)S(1)} %copy-done.1), channel_id=1, source_target_pairs={{0,24},{8,16},{16,8},{24,0},{1,25},{9,17},{17,9},{25,1},{2,26},{10... | collective-permute-start | bytes 393224 | tf_op jit(solution)/shard_map/ppermute | solution.py:39
  73.7 81.9 %all-to-all-start.1 = ((bf16[8,256,256]{2,1,0:T(8,128)(2,1)}), bf16[8,256,256]{2,1,0:T(8,128)(2,1)}, u32[]{:S(2)}, u32[]{:S(2)}) async-start(bf16[8,256,256]{2,1,0:T(8,128)(2,1)} %shard_map.100), calls=%async_computation.1 | async-start | bytes 2097152 | tf_op jit(solution)/shard_map/all_to_all | solution.py:423
  87.0 11.8 %collective-permute-start.35 = (f32[256,256]{1,0:T(8,128)S(1)}, f32[256,256]{1,0:T(8,128)S(1)}, u32[]{:S(2)}, u32[]{:S(2)}) collective-permute-start(f32[256,256]{1,0:T(8,128)S(1)} %get-tuple-element.83), channel_id=1, source_target_pairs={{0,24},{8,16},{16,8},{24,0},{1,25},{9,17},{17,9},{25,1},{2,26},{10... | collective-permute-start | bytes 786440 | tf_op jit(solution)/shard_map/ppermute | solution.py:39
  101.4 20.7 %collective-permute-start.27 = (f32[256,256]{1,0:T(8,128)S(1)}, f32[256,256]{1,0:T(8,128)S(1)}, u32[]{:S(2)}, u32[]{:S(2)}) collective-permute-start(f32[256,256]{1,0:T(8,128)S(1)} %get-tuple-element.59), channel_id=1, source_target_pairs={{0,8},{8,0},{16,24},{24,16},{1,9},{9,1},{17,25},{25,17},{2,10},{10... | collective-permute-start | bytes 786440 | tf_op jit(solution)/shard_map/ppermute | solution.py:39
  102.6 19.6 %collective-permute-start.28 = (f32[256,256]{1,0:T(8,128)S(1)}, f32[256,256]{1,0:T(8,128)S(1)}, u32[]{:S(2)}, u32[]{:S(2)}) collective-permute-start(f32[256,256]{1,0:T(8,128)S(1)} %get-tuple-element.60), channel_id=1, source_target_pairs={{0,16},{8,24},{16,0},{24,8},{1,17},{9,25},{17,1},{25,9},{2,18},{10... | collective-permute-start | bytes 786440 | tf_op jit(solution)/shard_map/ppermute | solution.py:39
  102.9 19.3 %collective-permute-start.29 = (f32[256,256]{1,0:T(8,128)S(1)}, f32[256,256]{1,0:T(8,128)S(1)}, u32[]{:S(2)}, u32[]{:S(2)}) collective-permute-start(f32[256,256]{1,0:T(8,128)S(1)} %get-tuple-element.61), channel_id=1, source_target_pairs={{0,24},{8,16},{16,8},{24,0},{1,25},{9,17},{17,9},{25,1},{2,26},{10... | collective-permute-start | bytes 786440 | tf_op jit(solution)/shard_map/ppermute | solution.py:39
  106.4 10.9 %collective-permute-start.38 = (bf16[256,256]{1,0:T(8,128)(2,1)}, bf16[256,256]{1,0:T(8,128)(2,1)S(1)}, u32[]{:S(2)}, u32[]{:S(2)}) collective-permute-start(bf16[256,256]{1,0:T(8,128)(2,1)} %shard_map.104.refs_0_), channel_id=1, source_target_pairs={{0,6},{1,7},{2,4},{3,5},{4,2},{5,3},{6,0},{7,1},{8,14},{9,15},{10,... | collective-permute-start | bytes 393224 | tf_op jit(solution)/shard_map/ppermute | solution.py:39
  120.4 19.1 %collective-permute-start.39 = (bf16[4,128,256]{2,1,0:T(8,128)(2,1)}, bf16[4,128,256]{2,1,0:T(8,128)(2,1)S(1)}, u32[]{:S(2)}, u32[]{:S(2)}) collective-permute-start(bf16[4,128,256]{2,1,0:T(8,128)(2,1)} %get-tuple-element.85), channel_id=1, source_target_pairs={{0,8},{8,0},{16,24},{24,16},{1,9},{9,1},{17,25},{25,17},{2,10},{10... | collective-permute-start | bytes 786440 | tf_op jit(solution)/shard_map/ppermute | solution.py:39
  125.0 10.9 %collective-permute-start.50 = (bf16[256,256]{1,0:T(8,128)(2,1)}, bf16[256,256]{1,0:T(8,128)(2,1)S(1)}, u32[]{:S(2)}, u32[]{:S(2)}) collective-permute-start(bf16[256,256]{1,0:T(8,128)(2,1)} %shard_map.98.refs_0_), channel_id=1, source_target_pairs={{0,4},{1,5},{2,6},{3,7},{4,0},{5,1},{6,2},{7,3},{8,12},{9,13},{10,... | collective-permute-start | bytes 393224 | tf_op jit(solution)/shard_map/ppermute | solution.py:39
  127.6 11.2 %collective-permute-start.51 = (bf16[256,256]{1,0:T(8,128)(2,1)}, bf16[256,256]{1,0:T(8,128)(2,1)S(1)}, u32[]{:S(2)}, u32[]{:S(2)}) collective-permute-start(bf16[256,256]{1,0:T(8,128)(2,1)} %shard_map.98.refs_0_), channel_id=1, source_target_pairs={{0,6},{1,7},{2,4},{3,5},{4,2},{5,3},{6,0},{7,1},{8,14},{9,15},{10,... | collective-permute-start | bytes 393224 | tf_op jit(solution)/shard_map/ppermute | solution.py:39
  127.6 34.3 %collective-permute-start.46 = (bf16[8,128,256]{2,1,0:T(8,128)(2,1)}, bf16[8,128,256]{2,1,0:T(8,128)(2,1)S(1)}, u32[]{:S(2)}, u32[]{:S(2)}) collective-permute-start(bf16[8,128,256]{2,1,0:T(8,128)(2,1)} %get-tuple-element.89), channel_id=1, source_target_pairs={{0,8},{8,0},{16,24},{24,16},{1,9},{9,1},{17,25},{25,17},{2,10},{10... | collective-permute-start | bytes 1572872 | tf_op jit(solution)/shard_map/ppermute | solution.py:39
  129.2 32.7 %collective-permute-start.47 = (bf16[8,128,256]{2,1,0:T(8,128)(2,1)}, bf16[8,128,256]{2,1,0:T(8,128)(2,1)S(1)}, u32[]{:S(2)}, u32[]{:S(2)}) collective-permute-start(bf16[8,128,256]{2,1,0:T(8,128)(2,1)} %get-tuple-element.90), channel_id=1, source_target_pairs={{0,16},{8,24},{16,0},{24,8},{1,17},{9,25},{17,1},{25,9},{2,18},{10... | collective-permute-start | bytes 1572872 | tf_op jit(solution)/shard_map/ppermute | solution.py:39
  135.9 14.2 %collective-permute-start.40 = (bf16[4,128,256]{2,1,0:T(8,128)(2,1)}, bf16[4,128,256]{2,1,0:T(8,128)(2,1)S(1)}, u32[]{:S(2)}, u32[]{:S(2)}) collective-permute-start(bf16[4,128,256]{2,1,0:T(8,128)(2,1)} %get-tuple-element.86), channel_id=1, source_target_pairs={{0,16},{8,24},{16,0},{24,8},{1,17},{9,25},{17,1},{25,9},{2,18},{10... | collective-permute-start | bytes 786440 | tf_op jit(solution)/shard_map/ppermute | solution.py:39
  138.8 16.2 %collective-permute-start.41 = (bf16[4,128,256]{2,1,0:T(8,128)(2,1)}, bf16[4,128,256]{2,1,0:T(8,128)(2,1)S(1)}, u32[]{:S(2)}, u32[]{:S(2)}) collective-permute-start(bf16[4,128,256]{2,1,0:T(8,128)(2,1)} %get-tuple-element.87), channel_id=1, source_target_pairs={{0,24},{8,16},{16,8},{24,0},{1,25},{9,17},{17,9},{25,1},{2,26},{10... | collective-permute-start | bytes 786440 | tf_op jit(solution)/shard_map/ppermute | solution.py:39
  139.5 15.5 %collective-permute-start.42 = (bf16[4,128,256]{2,1,0:T(8,128)(2,1)}, bf16[4,128,256]{2,1,0:T(8,128)(2,1)S(1)}, u32[]{:S(2)}, u32[]{:S(2)}) collective-permute-start(bf16[4,128,256]{2,1,0:T(8,128)(2,1)} %get-tuple-element.84.refs_4_), channel_id=1, source_target_pairs={{0,1},{1,0},{2,3},{3,2},{4,5},{5,4},{6,7},{7,6},{8,9},{9,8},{10,11... | collective-permute-start | bytes 786440 | tf_op jit(solution)/shard_map/ppermute | solution.py:39
  150.1 13.3 %collective-permute-start.43 = (bf16[4,128,256]{2,1,0:T(8,128)(2,1)S(1)}, bf16[4,128,256]{2,1,0:T(8,128)(2,1)S(1)}, u32[]{:S(2)}, u32[]{:S(2)}) collective-permute-start(bf16[4,128,256]{2,1,0:T(8,128)(2,1)S(1)} %collective-permute-done.39.refs_5_), channel_id=1, source_target_pairs={{0,1},{1,0},{2,3},{3,2},{4,5},{5,4},{6,7},{7,6},{8,9},{9,8},{10,11... | collective-permute-start | bytes 786440 | tf_op jit(solution)/shard_map/ppermute | solution.py:39
  155.0 9.8 %collective-permute-start.45 = (bf16[4,128,256]{2,1,0:T(8,128)(2,1)S(1)}, bf16[4,128,256]{2,1,0:T(8,128)(2,1)S(1)}, u32[]{:S(2)}, u32[]{:S(2)}) collective-permute-start(bf16[4,128,256]{2,1,0:T(8,128)(2,1)S(1)} %collective-permute-done.41.refs_7_), channel_id=1, source_target_pairs={{0,1},{1,0},{2,3},{3,2},{4,5},{5,4},{6,7},{7,6},{8,9},{9,8},{10,11... | collective-permute-start | bytes 786440 | tf_op jit(solution)/shard_map/ppermute | solution.py:39
  161.9 37.3 %collective-permute-start.30 = (bf16[8,128,256]{2,1,0:T(8,128)(2,1)}, bf16[8,128,256]{2,1,0:T(8,128)(2,1)S(1)}, u32[]{:S(2)}, u32[]{:S(2)}) collective-permute-start(bf16[8,128,256]{2,1,0:T(8,128)(2,1)} %get-tuple-element.71), channel_id=1, source_target_pairs={{0,8},{8,0},{16,24},{24,16},{1,9},{9,1},{17,25},{25,17},{2,10},{10... | collective-permute-start | bytes 1572872 | tf_op jit(solution)/shard_map/ppermute | solution.py:39
  162.0 19.3 %collective-permute-start.52 = (bf16[4,128,256]{2,1,0:T(8,128)(2,1)}, bf16[4,128,256]{2,1,0:T(8,128)(2,1)S(1)}, u32[]{:S(2)}, u32[]{:S(2)}) collective-permute-start(bf16[4,128,256]{2,1,0:T(8,128)(2,1)} %get-tuple-element.94), channel_id=1, source_target_pairs={{0,8},{8,0},{16,24},{24,16},{1,9},{9,1},{17,25},{25,17},{2,10},{10... | collective-permute-start | bytes 786440 | tf_op jit(solution)/shard_map/ppermute | solution.py:39
  163.4 18.1 %collective-permute-start.53 = (bf16[4,128,256]{2,1,0:T(8,128)(2,1)}, bf16[4,128,256]{2,1,0:T(8,128)(2,1)S(1)}, u32[]{:S(2)}, u32[]{:S(2)}) collective-permute-start(bf16[4,128,256]{2,1,0:T(8,128)(2,1)} %get-tuple-element.95), channel_id=1, source_target_pairs={{0,16},{8,24},{16,0},{24,8},{1,17},{9,25},{17,1},{25,9},{2,18},{10... | collective-permute-start | bytes 786440 | tf_op jit(solution)/shard_map/ppermute | solution.py:39
  163.4 46.7 %collective-permute-start.31 = (bf16[8,128,256]{2,1,0:T(8,128)(2,1)}, bf16[8,128,256]{2,1,0:T(8,128)(2,1)S(1)}, u32[]{:S(2)}, u32[]{:S(2)}) collective-permute-start(bf16[8,128,256]{2,1,0:T(8,128)(2,1)} %get-tuple-element.72), channel_id=1, source_target_pairs={{0,16},{8,24},{16,0},{24,8},{1,17},{9,25},{17,1},{25,9},{2,18},{10... | collective-permute-start | bytes 1572872 | tf_op jit(solution)/shard_map/ppermute | solution.py:39
  164.9 46.8 %collective-permute-start.32 = (bf16[8,128,256]{2,1,0:T(8,128)(2,1)}, bf16[8,128,256]{2,1,0:T(8,128)(2,1)S(1)}, u32[]{:S(2)}, u32[]{:S(2)}) collective-permute-start(bf16[8,128,256]{2,1,0:T(8,128)(2,1)} %get-tuple-element.73), channel_id=1, source_target_pairs={{0,24},{8,16},{16,8},{24,0},{1,25},{9,17},{17,9},{25,1},{2,26},{10... | collective-permute-start | bytes 1572872 | tf_op jit(solution)/shard_map/ppermute | solution.py:39
  181.2 16.6 %collective-permute-start.54 = (bf16[4,128,256]{2,1,0:T(8,128)(2,1)}, bf16[4,128,256]{2,1,0:T(8,128)(2,1)S(1)}, u32[]{:S(2)}, u32[]{:S(2)}) collective-permute-start(bf16[4,128,256]{2,1,0:T(8,128)(2,1)} %get-tuple-element.96), channel_id=1, source_target_pairs={{0,24},{8,16},{16,8},{24,0},{1,25},{9,17},{17,9},{25,1},{2,26},{10... | collective-permute-start | bytes 786440 | tf_op jit(solution)/shard_map/ppermute | solution.py:39
  181.5 33.9 %collective-permute-start.48 = (bf16[8,128,256]{2,1,0:T(8,128)(2,1)}, bf16[8,128,256]{2,1,0:T(8,128)(2,1)S(1)}, u32[]{:S(2)}, u32[]{:S(2)}) collective-permute-start(bf16[8,128,256]{2,1,0:T(8,128)(2,1)} %get-tuple-element.91), channel_id=1, source_target_pairs={{0,24},{8,16},{16,8},{24,0},{1,25},{9,17},{17,9},{25,1},{2,26},{10... | collective-permute-start | bytes 1572872 | tf_op jit(solution)/shard_map/ppermute | solution.py:39
  197.8 17.5 %collective-permute-start.55 = (bf16[4,128,256]{2,1,0:T(8,128)(2,1)}, bf16[4,128,256]{2,1,0:T(8,128)(2,1)S(1)}, u32[]{:S(2)}, u32[]{:S(2)}) collective-permute-start(bf16[4,128,256]{2,1,0:T(8,128)(2,1)} %get-tuple-element.93.refs_4_), channel_id=1, source_target_pairs={{0,1},{1,0},{2,3},{3,2},{4,5},{5,4},{6,7},{7,6},{8,9},{9,8},{10,11... | collective-permute-start | bytes 786440 | tf_op jit(solution)/shard_map/ppermute | solution.py:39
  199.2 16.1 %collective-permute-start.56 = (bf16[4,128,256]{2,1,0:T(8,128)(2,1)S(1)}, bf16[4,128,256]{2,1,0:T(8,128)(2,1)S(1)}, u32[]{:S(2)}, u32[]{:S(2)}) collective-permute-start(bf16[4,128,256]{2,1,0:T(8,128)(2,1)S(1)} %collective-permute-done.52.refs_5_), channel_id=1, source_target_pairs={{0,1},{1,0},{2,3},{3,2},{4,5},{5,4},{6,7},{7,6},{8,9},{9,8},{10,11... | collective-permute-start | bytes 786440 | tf_op jit(solution)/shard_map/ppermute | solution.py:39
  (59 other events, 509.4 us)

commit v5 on v4

--- a/solution.py
+++ b/solution.py
@@ -47,7 +47,7 @@
     return lax.optimization_barrier(values)
 
 
-def pack_kernel(emb_ref, positive_ref, user_ref, item_ref, out_ref):
+def pack_kernel(emb_ref, other_ref, positive_ref, user_ref, item_ref, line_ref, plane_ref):
     rows = emb_ref.shape[0]
     down = lax.broadcasted_iota(jnp.int32, (rows, rows), 0)
     across = lax.broadcasted_iota(jnp.int32, (rows, rows), 1)
@@ -57,24 +57,35 @@
         before = jnp.where((wide == wide.T) & (down < across), 1.0, 0.0)
         return expert * CAP + jnp.sum(before, axis=0, keepdims=True).astype(jnp.int32)
 
-    user = slots(user_ref[...])
-    item = slots(item_ref[...])
     line = lax.broadcasted_iota(jnp.int32, (EXTRA, rows), 0)
     block = jnp.zeros((EXTRA, rows), jnp.int32)
-    for index, values in enumerate((positive_ref[...], user, item)):
+    numbers = (positive_ref[...], slots(user_ref[...]), slots(item_ref[...]))
+    for index, values in enumerate(numbers):
         block = jnp.where(line == 2 * index, values // DIGIT, block)
         block = jnp.where(line == 2 * index + 1, values % DIGIT, block)
-    out_ref[:rows, :] = emb_ref[...]
-    out_ref[rows:, :] = block.astype(F32).astype(BF16)
-
-
-def pack(emb, positive, user_expert, item_expert):
+    extra = block.astype(F32).astype(BF16)
+    for ref in (line_ref, plane_ref):
+        ref[:rows, :] = emb_ref[...]
+        ref[rows : rows + EXTRA, :] = extra
+    plane_ref[rows + EXTRA :, :] = other_ref[...]
+
+
+def pack(emb, other, positive, user_expert, item_expert):
     rows, width = emb.shape
     return pl.pallas_call(
         pack_kernel,
-        out_shape=jax.ShapeDtypeStruct((rows + EXTRA, width), BF16),
-        cost_estimate=SMALL,
-    )(emb, positive.reshape(1, rows), user_expert.reshape(1, rows), item_expert.reshape(1, rows))
+        out_shape=[
+            jax.ShapeDtypeStruct((rows + EXTRA, width), BF16),
+            jax.ShapeDtypeStruct((2 * rows + EXTRA, width), BF16),
+        ],
+        cost_estimate=SMALL,
+    )(
+        emb,
+        other,
+        positive.reshape(1, rows),
+        user_expert.reshape(1, rows),
+        item_expert.reshape(1, rows),
+    )
 
 
 def gather_rows(refs, to_ref):
@@ -92,7 +103,7 @@
     users_refs, items_refs = refs[:blocks], refs[blocks : blocks + count]
     out_ref, all_ref, col_ref, s_ref = refs[blocks + count :]
     own, emb = items_refs[0].shape
-    rows = users_refs[0].shape[0] - EXTRA
+    rows = all_ref.shape[1] - EXTRA
     n_cols = own * count
     gather_rows(users_refs, all_ref)
     for k, ref in enumerate(items_refs):
@@ -126,9 +137,9 @@
 
 
 def stats(first, users, items):
-    height, emb = users[0].shape
-    rows = height - EXTRA
-    own = items[0].shape[0]
+    own, emb = items[0].shape
+    rows = (users[0].shape[0] - EXTRA) // 2
+    height = rows + EXTRA
     blocks, count = len(users), len(items)
     return pl.pallas_call(
         functools.partial(stats_kernel, blocks=blocks, count=count, chunk=64),
@@ -175,7 +186,7 @@
     stats_refs, out_refs, refs = refs[:blocks], refs[blocks : 2 * blocks], refs[2 * blocks :]
     all_ref, col_ref, flip_ref, s_ref, g_ref, sum_ref = refs
     own, emb = items_refs[0].shape
-    rows = users_refs[0].shape[0] - EXTRA
+    rows = all_ref.shape[1] - EXTRA
     n_cols = own * count
     gather_rows(users_refs, all_ref)
     for k, ref in enumerate(items_refs):
@@ -202,9 +213,9 @@
 
 
 def user_grads(first, users, items, found):
-    height, emb = users[0].shape
-    rows = height - EXTRA
-    own = items[0].shape[0]
+    own, emb = items[0].shape
+    rows = (users[0].shape[0] - EXTRA) // 2
+    height = rows + EXTRA
     blocks, count = len(users), len(items)
     return pl.pallas_call(
         functools.partial(user_kernel, blocks=blocks, count=count, chunk=64),
@@ -225,28 +236,26 @@
 
 
 def item_kernel(first_ref, *refs, blocks, count, chunk):
-    users_refs, items_refs = refs[:blocks], refs[blocks : blocks + count]
-    near_ref, far_ref, refs = refs[blocks + count], refs[blocks + count + 1], refs[blocks + count + 2 :]
-    out_refs, refs = refs[:count], refs[count:]
-    extra_ref, all_ref, row_ref, col_ref, level_ref, s_ref, g_ref = refs
-    own, emb = items_refs[0].shape
+    users_refs, plane_refs = refs[:blocks], refs[blocks : blocks + count]
+    refs = refs[blocks + count :]
+    level_refs, out_refs, refs = refs[:blocks], refs[blocks : blocks + count], refs[blocks + count :]
+    extra_ref, row_ref, col_ref, s_ref, g_ref = refs
+    own, emb = out_refs[0].shape
     rows = users_refs[0].shape[0] - EXTRA
     n_cols = own * count
-    gather_rows(users_refs, all_ref)
-    level_ref[: blocks // 2] = near_ref[...]
-    level_ref[blocks // 2 :] = far_ref[...]
+    for k in range(blocks // CORES):
+        extra_ref[k] = users_refs[k][rows:, :]
     for k, ref in enumerate(users_refs):
-        extra_ref[k] = ref[rows:, :]
         row_ref[k * rows : (k + 1) * rows, :] = ref[:rows, :]
-    for k, ref in enumerate(items_refs):
-        col_ref[k * own : (k + 1) * own, :] = ref[...]
+    for k, ref in enumerate(plane_refs):
+        col_ref[k * own : (k + 1) * own, :] = ref[rows + EXTRA :, :]
 
     for block in range(blocks):
         half = block % 2
-        queries = all_ref[block, :rows, :] * jnp.asarray(SCALE, BF16)
+        queries = users_refs[block][:rows, :] * jnp.asarray(SCALE, BF16)
         s_ref[half] = mm(col_ref[...], queries, 1, 1)
-        positive = number(all_ref[block, rows:, :], 0)
-        level = level_ref[block]
+        positive = number(users_refs[block][rows:, :], 0)
+        level = level_refs[block][...]
         for c in range(0, n_cols, chunk):
             probs = jnp.exp(s_ref[half, c : c + chunk, :] - level)
             hit = hits(first_ref, positive, c, own, probs.shape)
@@ -257,46 +266,50 @@
         ref[...] = mm(g_ref[k * own : (k + 1) * own, :], row_ref[...], 1, 0) * SCALE
 
 
-def item_grads(first, users, items, near, far):
+def item_grads(first, users, planes, level):
     height, emb = users[0].shape
     rows = height - EXTRA
-    own = items[0].shape[0]
-    blocks, count = len(users), len(items)
+    own = planes[0].shape[0] - height
+    blocks, count = len(users), len(planes)
     results = pl.pallas_call(
         functools.partial(item_kernel, blocks=blocks, count=count, chunk=64),
-        in_specs=[SCALARS] + [WHOLE] * (blocks + count + 2),
+        in_specs=[SCALARS] + [WHOLE] * (2 * blocks + count),
         out_specs=[WHOLE] * (count + 1),
         out_shape=[jax.ShapeDtypeStruct((own, emb), F32)] * count
-        + [jax.ShapeDtypeStruct((blocks, EXTRA, emb), BF16)],
+        + [jax.ShapeDtypeStruct((blocks // CORES, EXTRA, emb), BF16)],
         scratch_shapes=[
-            pltpu.VMEM((blocks, height, emb), BF16),
             pltpu.VMEM((blocks * rows, emb), BF16),
             pltpu.VMEM((own * count, emb), BF16),
-            pltpu.VMEM((blocks, 1, rows), F32),
             pltpu.VMEM((2, own * count, rows), F32),
             pltpu.VMEM((own * count, blocks * rows), BF16),
         ],
         compiler_params=pltpu.CompilerParams(vmem_limit_bytes=48 * MIB),
         cost_estimate=SMALL,
-    )(first, *users, *items, near, far)
+    )(first, *users, *planes, *level)
     return results[:count], results[count]
 
 
-def cut_kernel(in_ref, out_ref):
+def cut_kernel(in_ref, line_ref, out_ref):
+    rows = in_ref.shape[0]
     width = out_ref.shape[2]
     for k in range(out_ref.shape[0]):
-        out_ref[k] = in_ref[:, k * width : (k + 1) * width]
-
-
-def cut(hidden, parts):
+        out_ref[k, :rows, :] = in_ref[:, k * width : (k + 1) * width]
+        for cut_at in range(0, rows, width):
+            place = rows + cut_at // width * EXTRA
+            out_ref[k, place : place + EXTRA, :] = line_ref[rows:, cut_at : cut_at + width]
+
+
+def cut(hidden, line, parts):
     rows, total = hidden.shape
+    width = total // parts
+    height = rows + EXTRA * max(1, rows // width)
     return pl.pallas_call(
         cut_kernel,
-        in_specs=[WHOLE],
+        in_specs=[WHOLE] * 2,
         out_specs=WHOLE,
-        out_shape=jax.ShapeDtypeStruct((parts, rows, total // parts), hidden.dtype),
-        cost_estimate=SMALL,
-    )(hidden)
+        out_shape=jax.ShapeDtypeStruct((parts, height, width), hidden.dtype),
+        cost_estimate=SMALL,
+    )(hidden, line)
 
 
 def onehot_of(target, me, groups):
@@ -306,33 +319,32 @@
     return (place == target).astype(F32).astype(BF16)
 
 
-def hidden_kernel(me_ref, extra_ref, hidden_ref, *out_refs, tower):
-    pair, span = out_refs[0].shape[:2]
+def hidden_kernel(me_ref, hidden_ref, *out_refs, tower, rows):
+    pair, span, width = out_refs[0].shape
     for half in range(pair):
-        apart = me_ref[1] ^ (pl.program_id(0) * pair + half)
-        place = apart % CORES * (extra_ref.shape[0] // CORES) + apart // CORES
-        onehot = onehot_of(number(extra_ref[place], 1 + tower), me_ref[0], len(out_refs))
-        moved = mm(onehot, hidden_ref[half], 1, 0).astype(BF16)
+        extra = [
+            hidden_ref[half, place : place + EXTRA, :]
+            for place in range(rows, hidden_ref.shape[1], EXTRA)
+        ]
+        extra = extra[0] if len(extra) == 1 else jnp.concatenate(extra, axis=1)
+        onehot = onehot_of(number(extra, 1 + tower), me_ref[0], len(out_refs))
+        moved = mm(onehot, hidden_ref[half, :rows, :], 1, 0).astype(BF16)
         for k, out_ref in enumerate(out_refs):
             out_ref[half] = moved[k * span : (k + 1) * span, :]
 
 
-def slot_hidden(me, extra, hidden, groups, tower):
-    blocks, rows, width = hidden.shape
+def slot_hidden(me, hidden, rows, groups, tower):
+    blocks, height, width = hidden.shape
     span = EXPERTS * CAP // groups
     pair = 2
     return pl.pallas_call(
-        functools.partial(hidden_kernel, tower=tower),
+        functools.partial(hidden_kernel, tower=tower, rows=rows),
         grid=(blocks // pair,),
-        in_specs=[
-            SCALARS,
-            pl.BlockSpec(extra.shape, lambda b: (0, 0, 0)),
-            pl.BlockSpec((pair, rows, width), lambda b: (b, 0, 0)),
-        ],
+        in_specs=[SCALARS, pl.BlockSpec((pair, height, width), lambda b: (b, 0, 0))],
         out_specs=[pl.BlockSpec((pair, span, width), lambda b: (b, 0, 0))] * groups,
         out_shape=[jax.ShapeDtypeStruct((blocks, span, width), BF16)] * groups,
         cost_estimate=SMALL,
-    )(me, extra, hidden)
+    )(me, hidden)
 
 
 def total_kernel(*refs):
@@ -419,46 +431,57 @@
     first_plane = (part * groups + others) * rows
     me = jnp.stack([me, part])
 
-    def by_part(hidden):
-        return lax.all_to_all(cut(hidden, parts), "item", split_axis=0, concat_axis=0, tiled=True)
+    def by_part(blocks):
+        return lax.all_to_all(blocks, "item", split_axis=0, concat_axis=0, tiled=True)
+
+    def across(pieces):
+        return pieces + [swap(piece, "item", 1) for piece in pieces]
 
     item_line = exchange([item_emb] * lines, "item", CORES)
-    packed = pack(user_emb, positive, user_expert, item_expert)
-    user_plane = exchange([packed] * groups, "user")
-    item_hidden, again, item_emb, *item_line = tie(item_hidden, packed, item_emb, *item_line)
-    item_cross = item_line + [swap(piece, "item", 1) for piece in item_line]
+    line, plane = pack(user_emb, item_emb, positive, user_expert, item_expert)
+    plane = exchange([plane] * groups, "user")
+    item_blocks = cut(item_hidden, line, parts)
+    user_blocks = cut(user_hidden, line, parts)
+    again, *item_line = tie(line, *item_line)
+    item_cross = across(item_line)
     user_line = exchange([again] * lines, "item", CORES)
-    item_cols = by_part(item_hidden)
-    item_plane = exchange([item_emb] * groups, "user")
-    user_cross = user_line + [swap(piece, "item", 1) for piece in user_line]
-
-    found = exchange([stats(first_cross, user_plane, item_cross)] * groups, "user")
+
+    found = stats(first_cross, plane, item_cross)
+    item_blocks, found = tie(item_blocks, found)
+    found = exchange([found] * groups, "user")
+    item_cols = by_part(item_blocks)
     level, loss = levels(found)
-    level_near = jnp.stack(exchange([level] * lines, "item", CORES))
-    level_far = swap(level_near, "item", 1)
-    user_pieces = exchange(user_grads(first_cross, user_plane, item_cross, found), "user")
-    item_parts, extra = item_grads(first_plane, user_cross, item_plane, level_near, level_far)
-    item_cols, user_hidden, extra = tie(item_cols, user_hidden, extra)
-    user_cols = by_part(user_hidden)
+    level, *found = tie(level, *found)
+    level = across(exchange([level] * lines, "item", CORES))
+    user_parts = list(user_grads(first_cross, plane, item_cross, found))
+    user_pieces = exchange(user_parts, "user")
+    user_parts[0], *level = tie(user_parts[0], *level)
+    item_parts, extra = item_grads(first_plane, across(user_line), plane, level)
     item_pieces = exchange(item_parts, "user")
+    item_cols, user_blocks, extra = tie(item_cols, user_blocks, extra)
+    user_cols = by_part(user_blocks)
+
     user_pieces[0], *item_slots = tie(
-        user_pieces[0], *slot_hidden(me, extra, item_cols, groups, 1)
+        user_parts[0], *slot_hidden(me, item_cols, rows, groups, 1)
     )
-    item_rows = exchange(item_slots, "user")
-
+    early = groups // 2 + 1
+    item_rows = exchange(item_slots[:early], "user")
     user_lines = exchange([total(user_pieces)] * lines, "item", CORES)
     item_lines = exchange([total(item_pieces)] * lines, "item", CORES)
-    item_lines[0], *user_slots = tie(
-        item_lines[0], *slot_hidden(me, extra, user_cols, groups, 0)
-    )
-    user_rows = exchange(user_slots, "user")
-
-    def spread(grad_lines, tower):
-        got = exchange(select(me, extra[:lines], grad_lines, groups, tower), "user")
-        return got + [swap(piece, "item", 1) for piece in got]
-
-    user_grad = spread(user_lines, 0)
-    item_grad = spread(item_lines, 1)
+    *user_lines, item_slots[-1] = tie(*user_lines, item_slots[-1])
+    item_rows += [swap(item_slots[k], "user", k) for k in range(early, groups)]
+
+    def spread(chosen):
+        return across(exchange(chosen, "user"))
+
+    user_chosen = select(me, extra, user_lines, groups, 0)
+    user_cols, *user_chosen = tie(user_cols, *user_chosen)
+    user_grad = spread(user_chosen)
+    user_slots = list(slot_hidden(me, user_cols, rows, groups, 0))
+    user_rows = exchange(user_slots[:early], "user")
+    item_grad = spread(select(me, extra, item_lines, groups, 1))
+    *user_grad, user_slots[-1] = tie(*user_grad, user_slots[-1])
+    user_rows += [swap(user_slots[k], "user", k) for k in range(early, groups)]
     item_weight_grad = outer(order, item_rows, item_grad)
     user_weight_grad = outer(order, user_rows, user_grad)
     row_loss = loss[0]

time: 221 us -> 258 us (1.17)
  waiting for transfers between devices: 98.9 us -> 123 us
  starting transfers between devices: 69.3 us -> 78.8 us
  local copies, waits for them, and re-layouts: 6.33 us -> 10.1 us
    ppermute x59, waiting for transfers between devices: 98.9 us -> 123 us  [swap(): return lax.ppermute(piece, axis, [(j, j ^ bits) for j in range(size)])]
    ppermute x59, starting transfers between devices: 56.9 us -> 67.5 us  [swap(): return lax.ppermute(piece, axis, [(j, j ^ bits) for j in range(size)])]
    unnamed x60 -> x82, local copies, waits for them, and re-layouts: 5.64 us -> 9.99 us
  transfers between devices with their start and end apart: 61 -> 61, of which waited for: 22 -> 25; matrix products, arithmetic and copies ran while one was open for 1% -> 0% of each run, Pallas kernels for 16% -> 14%
where the time goes in v5:
time: 258 us; the launch traced here: 256 us
  waiting for transfers between devices  123 us (48%)
  starting transfers between devices  78.8 us (31%)
  Pallas kernels  42.2 us (16%)
  local copies, waits for them, and re-layouts  10.1 us (4%)
    ppermute x59, waiting for transfers between devices, swap(): return lax.ppermute(piece, axis, [(j, j ^ bits) for j in range(size)])  123 us
    ppermute x59, starting transfers between devices, swap(): return lax.ppermute(piece, axis, [(j, j ^ bits) for j in range(size)])  67.5 us
    all_to_all x2, starting transfers between devices, by_part(): lax.all_to_all(blocks, 'item', split_axis=0, concat_axis=0, tiled=True)  11.3 us
    unnamed x82, local copies, waits for them, and re-layouts  9.99 us
    pallas_call x2, Pallas kernels, slot_hidden(): pl.pallas_call(functools.partial(hidden_kernel, tower=tower, rows=rows),...  7.86 us
    pallas_call x2, Pallas kernels, outer(): pl.pallas_call(functools.partial(outer_kernel, groups=groups), in_specs=[...  6.02 us
  transfers between devices with their start and end apart: 61, of which 25 were waited for; matrix products, arithmetic and copies ran while one was open for 0% of the time, Pallas kernels for 14%

profile of v5, /device:TPU:11, one launch (start us, length us, event | category | flops | bytes accessed | tf_op | source)
XLA Modules:
  0.0 256.1 jit_solution(2281364056741581178)
XLA Ops:
  9.1 5.6 %collective-permute-done.5.refs_7_ = bf16[256,256]{1,0:T(8,128)(2,1)S(1)} collective-permute-done((bf16[256,256]{1,0:T(8,128)(2,1)}, bf16[256,256]{1,0:T(8,128)(2,1)S(1)}, u32[]{:S(2)}, u32[]{:S(2)}) %collective-permute-start.5) | collective-permute-done | bytes 131104 | tf_op jit(solution)/shard_map/ppermute | solution.py:39
  20.9 3.6 %shard_map.96.refs_0_.refs_12_ = f32[4,3,256]{2,1,0:T(4,128)S(1)} custom-call(s32[8]{0:T(128)S(1)} %add_multiply_fusion.1.first_ref, bf16[528,256]{1,0:T(8,128)(2,1)S(1)} %copy-done, bf16[528,256]{1,0:T(8,128)(2,1)S(1)} %collective-permute-done.refs_1_.refs_9_, bf16[528,256]{1,0:T(8,128)(2,1)S(1)} %collective-permute-done.1.refs_2_.refs_10_, ...), custom_call_target="tpu_custom_call" | custom-call | flops 1024 | bytes 1024 | tf_op jit(solution)/shard_map/pallas_call | solution.py:144
  24.5 6.2 %all-to-all-start = ((bf16[8,272,256]{2,1,0:T(8,128)(2,1)}), bf16[8,272,256]{2,1,0:T(8,128)(2,1)}, u32[]{:S(2)}, u32[]{:S(2)}) async-start(bf16[8,272,256]{2,1,0:T(8,128)(2,1)} %shard_map.95), calls=%async_computation | async-start | bytes 2228224 | tf_op jit(solution)/shard_map/all_to_all | solution.py:435
  35.2 18.0 %collective-permute-done.13.refs_1_ = bf16[272,256]{1,0:T(8,128)(2,1)S(1)} collective-permute-done((bf16[272,256]{1,0:T(8,128)(2,1)S(1)}, bf16[272,256]{1,0:T(8,128)(2,1)S(1)}, u32[]{:S(2)}, u32[]{:S(2)}) %collective-permute-start.13) | collective-permute-done | bytes 139296 | tf_op jit(solution)/shard_map/ppermute | solution.py:39
  53.8 10.3 %collective-permute-done.14.refs_2_ = bf16[272,256]{1,0:T(8,128)(2,1)S(1)} collective-permute-done((bf16[272,256]{1,0:T(8,128)(2,1)S(1)}, bf16[272,256]{1,0:T(8,128)(2,1)S(1)}, u32[]{:S(2)}, u32[]{:S(2)}) %collective-permute-start.14) | collective-permute-done | bytes 139296 | tf_op jit(solution)/shard_map/ppermute | solution.py:39
  64.5 4.2 %collective-permute-done.15.refs_3_ = bf16[272,256]{1,0:T(8,128)(2,1)S(1)} collective-permute-done((bf16[272,256]{1,0:T(8,128)(2,1)S(1)}, bf16[272,256]{1,0:T(8,128)(2,1)S(1)}, u32[]{:S(2)}, u32[]{:S(2)}) %collective-permute-start.15) | collective-permute-done | bytes 139296 | tf_op jit(solution)/shard_map/ppermute | solution.py:39
  75.2 2.5 collective-permute-done.20.refs_13_
  77.7 3.4 %collective-permute-done.21.refs_14_ = f32[1,256]{1,0:T(1,128)S(1)} collective-permute-done((f32[1,256]{1,0:T(1,128)}, f32[1,256]{1,0:T(1,128)S(1)}, u32[]{:S(2)}, u32[]{:S(2)}) %collective-permute-start.21) | collective-permute-done | bytes 1056 | tf_op jit(solution)/shard_map/ppermute | solution.py:39
  81.1 2.4 collective-permute-done.22.refs_15_
  83.5 5.5 %collective-permute-start.23 = (f32[1,256]{1,0:T(1,128)}, f32[1,256]{1,0:T(1,128)S(1)}, u32[]{:S(2)}, u32[]{:S(2)}) collective-permute-start(f32[1,256]{1,0:T(1,128)} %get-tuple-element.97.refs_12_), channel_id=1, source_target_pairs={{0,1},{1,0},{2,3},{3,2},{4,5},{5,4},{6,7},{7,6},{8,9},{9,8},{10,11... | collective-permute-start | bytes 3080 | tf_op jit(solution)/shard_map/ppermute | solution.py:39
  95.1 4.5 %shard_map.99 = (f32[256,256]{1,0:T(8,128)S(1)}, f32[256,256]{1,0:T(8,128)S(1)}, f32[256,256]{1,0:T(8,128)S(1)}, f32[256,256]{1,0:T(8,128)S(1)}) custom-call(s32[8]{0:T(128)S(1)} %add_multiply_fusion.1.first_ref, bf16[528,256]{1,0:T(8,128)(2,1)S(1)} %copy-done, bf16[528,256]{1,0:T(8,128)(2,1)S(1)} %collective-permute-done.refs_1_.refs_9_, ...), custom_call_target="tpu_custom_call" | custom-call | flops 1024 | bytes 1024 | tf_op jit(solution)/shard_map/pallas_call | solution.py:220
  102.5 3.5 %shard_map.100 = (f32[256,256]{1,0:T(8,128)S(1)}, f32[256,256]{1,0:T(8,128)S(1)}, f32[256,256]{1,0:T(8,128)S(1)}, f32[256,256]{1,0:T(8,128)S(1)}, bf16[4,16,256]{2,1,0:T(8,128)(2,1)S(1)}) custom-call(s32[4]{0:T(128)S(1)} %add_multiply_fusion.first_ref, bf16[272,256]{1,0:T(8,128)(2,1)S(1)} %copy-done.2, bf16[272,256]{1,0:T(8,128)(2,1)S(1)} %collective-permute-done.13.refs_1_, ...), custom_call_target="tpu_custom_call" | custom-call | flops 1024 | bytes 1024 | tf_op jit(solution)/shard_map/pallas_call | solution.py:274
  107.3 5.1 %all-to-all-start.1 = ((bf16[8,272,256]{2,1,0:T(8,128)(2,1)}), bf16[8,272,256]{2,1,0:T(8,128)(2,1)S(1)}, u32[]{:S(2)}, u32[]{:S(2)}) async-start(bf16[8,272,256]{2,1,0:T(8,128)(2,1)} %shard_map.98), calls=%async_computation.1 | async-start | bytes 2228224 | tf_op jit(solution)/shard_map/all_to_all | solution.py:435
  115.1 4.9 %collective-permute-done.46.refs_1_ = f32[256,256]{1,0:T(8,128)S(1)} collective-permute-done((f32[256,256]{1,0:T(8,128)S(1)}, f32[256,256]{1,0:T(8,128)S(1)}, u32[]{:S(2)}, u32[]{:S(2)}) %collective-permute-start.46) | collective-permute-done | bytes 262176 | tf_op jit(solution)/shard_map/ppermute | solution.py:39
  120.2 5.7 %collective-permute-done.48.refs_3_ = f32[256,256]{1,0:T(8,128)S(1)} collective-permute-done((f32[256,256]{1,0:T(8,128)S(1)}, f32[256,256]{1,0:T(8,128)S(1)}, u32[]{:S(2)}, u32[]{:S(2)}) %collective-permute-start.48) | collective-permute-done | bytes 262176 | tf_op jit(solution)/shard_map/ppermute | solution.py:39
  133.6 3.0 %collective-permute-start.51 = (bf16[256,256]{1,0:T(8,128)(2,1)}, bf16[256,256]{1,0:T(8,128)(2,1)S(1)}, u32[]{:S(2)}, u32[]{:S(2)}) collective-permute-start(bf16[256,256]{1,0:T(8,128)(2,1)} %shard_map.106.refs_0_), channel_id=1, source_target_pairs={{0,6},{1,7},{2,4},{3,5},{4,2},{5,3},{6,0},{7,1},{8,14},{9,15},{10,... | collective-permute-start | bytes 393224 | tf_op jit(solution)/shard_map/ppermute | solution.py:39
  137.2 8.1 %collective-permute-done.50.refs_2_ = bf16[256,256]{1,0:T(8,128)(2,1)S(1)} collective-permute-done((bf16[256,256]{1,0:T(8,128)(2,1)}, bf16[256,256]{1,0:T(8,128)(2,1)S(1)}, u32[]{:S(2)}, u32[]{:S(2)}) %collective-permute-start.50) | collective-permute-done | bytes 131104 | tf_op jit(solution)/shard_map/ppermute | solution.py:39
  145.3 4.4 %collective-permute-done.51.refs_3_ = bf16[256,256]{1,0:T(8,128)(2,1)S(1)} collective-permute-done((bf16[256,256]{1,0:T(8,128)(2,1)}, bf16[256,256]{1,0:T(8,128)(2,1)S(1)}, u32[]{:S(2)}, u32[]{:S(2)}) %collective-permute-start.51) | collective-permute-done | bytes 131104 | tf_op jit(solution)/shard_map/ppermute | solution.py:39
  150.3 2.5 shard_map.107
  153.3 3.9 %shard_map.101 = (bf16[8,128,256]{2,1,0:T(8,128)(2,1)}, bf16[8,128,256]{2,1,0:T(8,128)(2,1)}, bf16[8,128,256]{2,1,0:T(8,128)(2,1)}, bf16[8,128,256]{2,1,0:T(8,128)(2,1)}) custom-call(s32[2]{0:T(128)} %pad_add_fusion.me_ref, bf16[8,272,256]{2,1,0:T(8,128)(2,1)} %all-to-all-done.hidden_ref), custom_call_target="tpu_custom_call" | custom-call | flops 1024 | bytes 1024 | tf_op jit(solution)/shard_map/pallas_call | solution.py:340
  164.7 3.6 %collective-permute-done.31.refs_2_ = bf16[256,256]{1,0:T(8,128)(2,1)S(1)} collective-permute-done((bf16[256,256]{1,0:T(8,128)(2,1)}, bf16[256,256]{1,0:T(8,128)(2,1)S(1)}, u32[]{:S(2)}, u32[]{:S(2)}) %collective-permute-start.31) | collective-permute-done | bytes 131104 | tf_op jit(solution)/shard_map/ppermute | solution.py:39
  168.3 6.4 %collective-permute-done.32.refs_3_ = bf16[256,256]{1,0:T(8,128)(2,1)S(1)} collective-permute-done((bf16[256,256]{1,0:T(8,128)(2,1)}, bf16[256,256]{1,0:T(8,128)(2,1)S(1)}, u32[]{:S(2)}, u32[]{:S(2)}) %collective-permute-start.32) | collective-permute-done | bytes 131104 | tf_op jit(solution)/shard_map/ppermute | solution.py:39
  175.3 2.4 shard_map.103
  182.6 2.9 %collective-permute-start.38 = (bf16[4,128,256]{2,1,0:T(8,128)(2,1)}, bf16[4,128,256]{2,1,0:T(8,128)(2,1)S(1)}, u32[]{:S(2)}, u32[]{:S(2)}) collective-permute-start(bf16[4,128,256]{2,1,0:T(8,128)(2,1)} %get-tuple-element.137.refs_4_), channel_id=1, source_target_pairs={{0,1},{1,0},{2,3},{3,2},{4,5},{5,4},{6,7},{7,6},{8,9},{9,8},{10,11... | collective-permute-start | bytes 786440 | tf_op jit(solution)/shard_map/ppermute | solution.py:39
  185.5 4.5 %collective-permute-start.39 = (bf16[4,128,256]{2,1,0:T(8,128)(2,1)S(1)}, bf16[4,128,256]{2,1,0:T(8,128)(2,1)S(1)}, u32[]{:S(2)}, u32[]{:S(2)}) collective-permute-start(bf16[4,128,256]{2,1,0:T(8,128)(2,1)S(1)} %collective-permute-done.35.refs_5_), channel_id=1, source_target_pairs={{0,1},{1,0},{2,3},{3,2},{4,5},{5,4},{6,7},{7,6},{8,9},{9,8},{10,11... | collective-permute-start | bytes 786440 | tf_op jit(solution)/shard_map/ppermute | solution.py:39
  189.9 8.4 %collective-permute-start.40 = (bf16[4,128,256]{2,1,0:T(8,128)(2,1)S(1)}, bf16[4,128,256]{2,1,0:T(8,128)(2,1)S(1)}, u32[]{:S(2)}, u32[]{:S(2)}) collective-permute-start(bf16[4,128,256]{2,1,0:T(8,128)(2,1)S(1)} %collective-permute-done.36.refs_6_), channel_id=1, source_target_pairs={{0,1},{1,0},{2,3},{3,2},{4,5},{5,4},{6,7},{7,6},{8,9},{9,8},{10,11... | collective-permute-start | bytes 786440 | tf_op jit(solution)/shard_map/ppermute | solution.py:39
  202.5 3.9 %shard_map.104 = (bf16[8,128,256]{2,1,0:T(8,128)(2,1)}, bf16[8,128,256]{2,1,0:T(8,128)(2,1)}, bf16[8,128,256]{2,1,0:T(8,128)(2,1)}, bf16[8,128,256]{2,1,0:T(8,128)(2,1)}) custom-call(s32[2]{0:T(128)} %pad_add_fusion.me_ref, bf16[8,272,256]{2,1,0:T(8,128)(2,1)} %copy-done.28), custom_call_target="tpu_custom_call" | custom-call | flops 1024 | bytes 1024 | tf_op jit(solution)/shard_map/pallas_call | solution.py:340
  211.6 3.0 %collective-permute-start.42 = (bf16[8,128,256]{2,1,0:T(8,128)(2,1)}, bf16[8,128,256]{2,1,0:T(8,128)(2,1)S(1)}, u32[]{:S(2)}, u32[]{:S(2)}) collective-permute-start(bf16[8,128,256]{2,1,0:T(8,128)(2,1)} %get-tuple-element.136), channel_id=1, source_target_pairs={{0,24},{8,16},{16,8},{24,0},{1,25},{9,17},{17,9},{25,1},{2,26},{10... | collective-permute-start | bytes 1572872 | tf_op jit(solution)/shard_map/ppermute | solution.py:39
  214.7 16.3 %collective-permute-done.44.refs_2_ = bf16[8,128,256]{2,1,0:T(8,128)(2,1)S(1)} collective-permute-done((bf16[8,128,256]{2,1,0:T(8,128)(2,1)}, bf16[8,128,256]{2,1,0:T(8,128)(2,1)S(1)}, u32[]{:S(2)}, u32[]{:S(2)}) %collective-permute-start.44) | collective-permute-done | bytes 524320 | tf_op jit(solution)/shard_map/ppermute | solution.py:39
  231.0 3.4 %shard_map.108 = f32[8,256,256]{2,1,0:T(8,128)} custom-call(s32[8]{0:T(128)S(1)} %xor.38.order_ref, bf16[8,128,256]{2,1,0:T(8,128)(2,1)S(1)} %copy-done.4, bf16[8,128,256]{2,1,0:T(8,128)(2,1)S(1)} %collective-permute-done.43.refs_1_, bf16[8,128,256]{2,1,0:T(8,128)(2,1)S(1)} %collective-permute-done.44.refs_2_, ...), custom_call_target="tpu_custom_call" | custom-call | flops 1024 | bytes 1024 | tf_op jit(solution)/shard_map/pallas_call | solution.py:410
  234.4 19.1 %collective-permute-done.34.refs_2_ = bf16[8,128,256]{2,1,0:T(8,128)(2,1)S(1)} collective-permute-done((bf16[8,128,256]{2,1,0:T(8,128)(2,1)}, bf16[8,128,256]{2,1,0:T(8,128)(2,1)S(1)}, u32[]{:S(2)}, u32[]{:S(2)}) %collective-permute-start.34) | collective-permute-done | bytes 524320 | tf_op jit(solution)/shard_map/ppermute | solution.py:39
  253.5 2.7 %shard_map.105 = f32[8,256,256]{2,1,0:T(8,128)} custom-call(s32[8]{0:T(128)S(1)} %xor.38.order_ref, bf16[8,128,256]{2,1,0:T(8,128)(2,1)S(1)} %copy-done.5, bf16[8,128,256]{2,1,0:T(8,128)(2,1)S(1)} %collective-permute-done.33.refs_1_, bf16[8,128,256]{2,1,0:T(8,128)(2,1)S(1)} %collective-permute-done.34.refs_2_, ...), custom_call_target="tpu_custom_call" | custom-call | flops 1024 | bytes 1024 | tf_op jit(solution)/shard_map/pallas_call | solution.py:410
  (194 shorter events, 71.6 us)
Async XLA Ops:
  5.2 15.6 %collective-permute-start = (bf16[528,256]{1,0:T(8,128)(2,1)}, bf16[528,256]{1,0:T(8,128)(2,1)S(1)}, u32[]{:S(2)}, u32[]{:S(2)}) collective-permute-start(bf16[528,256]{1,0:T(8,128)(2,1)} %get-tuple-element.81.refs_0_.refs_8_), channel_id=1, source_target_pairs={{0,8},{8,0},{16,24},{24,16},{1,9},{9,1},{17,25},{25,17},{2,10},{10... | collective-permute-start | bytes 811016 | tf_op jit(solution)/shard_map/ppermute | solution.py:39
  5.5 15.4 %collective-permute-start.1 = (bf16[528,256]{1,0:T(8,128)(2,1)}, bf16[528,256]{1,0:T(8,128)(2,1)S(1)}, u32[]{:S(2)}, u32[]{:S(2)}) collective-permute-start(bf16[528,256]{1,0:T(8,128)(2,1)} %get-tuple-element.81.refs_0_.refs_8_), channel_id=1, source_target_pairs={{0,16},{8,24},{16,0},{24,8},{1,17},{9,25},{17,1},{25,9},{2,18},{10... | collective-permute-start | bytes 811016 | tf_op jit(solution)/shard_map/ppermute | solution.py:39
  6.8 14.1 %collective-permute-start.2 = (bf16[528,256]{1,0:T(8,128)(2,1)}, bf16[528,256]{1,0:T(8,128)(2,1)S(1)}, u32[]{:S(2)}, u32[]{:S(2)}) collective-permute-start(bf16[528,256]{1,0:T(8,128)(2,1)} %get-tuple-element.81.refs_0_.refs_8_), channel_id=1, source_target_pairs={{0,24},{8,16},{16,8},{24,0},{1,25},{9,17},{17,9},{25,1},{2,26},{10... | collective-permute-start | bytes 811016 | tf_op jit(solution)/shard_map/ppermute | solution.py:39
  24.5 82.8 %all-to-all-start = ((bf16[8,272,256]{2,1,0:T(8,128)(2,1)}), bf16[8,272,256]{2,1,0:T(8,128)(2,1)}, u32[]{:S(2)}, u32[]{:S(2)}) async-start(bf16[8,272,256]{2,1,0:T(8,128)(2,1)} %shard_map.95), calls=%async_computation | async-start | bytes 2228224 | tf_op jit(solution)/shard_map/all_to_all | solution.py:435
  30.7 22.4 %collective-permute-start.13 = (bf16[272,256]{1,0:T(8,128)(2,1)S(1)}, bf16[272,256]{1,0:T(8,128)(2,1)S(1)}, u32[]{:S(2)}, u32[]{:S(2)}) collective-permute-start(bf16[272,256]{1,0:T(8,128)(2,1)S(1)} %copy-done.1), channel_id=1, source_target_pairs={{0,2},{1,3},{2,0},{3,1},{4,6},{5,7},{6,4},{7,5},{8,10},{9,11},{10,... | collective-permute-start | bytes 417800 | tf_op jit(solution)/shard_map/ppermute | solution.py:39
  30.8 33.2 %collective-permute-start.14 = (bf16[272,256]{1,0:T(8,128)(2,1)S(1)}, bf16[272,256]{1,0:T(8,128)(2,1)S(1)}, u32[]{:S(2)}, u32[]{:S(2)}) collective-permute-start(bf16[272,256]{1,0:T(8,128)(2,1)S(1)} %copy-done.1), channel_id=1, source_target_pairs={{0,4},{1,5},{2,6},{3,7},{4,0},{5,1},{6,2},{7,3},{8,12},{9,13},{10,... | collective-permute-start | bytes 417800 | tf_op jit(solution)/shard_map/ppermute | solution.py:39
  33.1 35.6 %collective-permute-start.15 = (bf16[272,256]{1,0:T(8,128)(2,1)S(1)}, bf16[272,256]{1,0:T(8,128)(2,1)S(1)}, u32[]{:S(2)}, u32[]{:S(2)}) collective-permute-start(bf16[272,256]{1,0:T(8,128)(2,1)S(1)} %copy-done.1), channel_id=1, source_target_pairs={{0,6},{1,7},{2,4},{3,5},{4,2},{5,3},{6,0},{7,1},{8,14},{9,15},{10,... | collective-permute-start | bytes 417800 | tf_op jit(solution)/shard_map/ppermute | solution.py:39
  33.4 36.2 %collective-permute-start.10 = (f32[4,3,256]{2,1,0:T(4,128)S(1)}, f32[4,3,256]{2,1,0:T(4,128)S(1)}, u32[]{:S(2)}, u32[]{:S(2)}) collective-permute-start(f32[4,3,256]{2,1,0:T(4,128)S(1)} %shard_map.96.refs_0_.refs_12_), channel_id=1, source_target_pairs={{0,8},{8,0},{16,24},{24,16},{1,9},{9,1},{17,25},{25,17},{2,10},{10... | collective-permute-start | bytes 36872 | tf_op jit(solution)/shard_map/ppermute | solution.py:39
  33.9 35.8 %collective-permute-start.11 = (f32[4,3,256]{2,1,0:T(4,128)S(1)}, f32[4,3,256]{2,1,0:T(4,128)S(1)}, u32[]{:S(2)}, u32[]{:S(2)}) collective-permute-start(f32[4,3,256]{2,1,0:T(4,128)S(1)} %shard_map.96.refs_0_.refs_12_), channel_id=1, source_target_pairs={{0,16},{8,24},{16,0},{24,8},{1,17},{9,25},{17,1},{25,9},{2,18},{10... | collective-permute-start | bytes 36872 | tf_op jit(solution)/shard_map/ppermute | solution.py:39
  53.1 49.3 %collective-permute-start.16 = (bf16[272,256]{1,0:T(8,128)(2,1)S(1)}, bf16[272,256]{1,0:T(8,128)(2,1)S(1)}, u32[]{:S(2)}, u32[]{:S(2)}) collective-permute-start(bf16[272,256]{1,0:T(8,128)(2,1)S(1)} %copy-done.1), channel_id=1, source_target_pairs={{0,1},{1,0},{2,3},{3,2},{4,5},{5,4},{6,7},{7,6},{8,9},{9,8},{10,11... | collective-permute-start | bytes 417800 | tf_op jit(solution)/shard_map/ppermute | solution.py:39
  64.0 38.4 %collective-permute-start.17 = (bf16[272,256]{1,0:T(8,128)(2,1)S(1)}, bf16[272,256]{1,0:T(8,128)(2,1)S(1)}, u32[]{:S(2)}, u32[]{:S(2)}) collective-permute-start(bf16[272,256]{1,0:T(8,128)(2,1)S(1)} %collective-permute-done.13.refs_1_), channel_id=1, source_target_pairs={{0,1},{1,0},{2,3},{3,2},{4,5},{5,4},{6,7},{7,6},{8,9},{9,8},{10,11... | collective-permute-start | bytes 417800 | tf_op jit(solution)/shard_map/ppermute | solution.py:39
  68.7 33.7 %collective-permute-start.18 = (bf16[272,256]{1,0:T(8,128)(2,1)S(1)}, bf16[272,256]{1,0:T(8,128)(2,1)S(1)}, u32[]{:S(2)}, u32[]{:S(2)}) collective-permute-start(bf16[272,256]{1,0:T(8,128)(2,1)S(1)} %collective-permute-done.14.refs_2_), channel_id=1, source_target_pairs={{0,1},{1,0},{2,3},{3,2},{4,5},{5,4},{6,7},{7,6},{8,9},{9,8},{10,11... | collective-permute-start | bytes 417800 | tf_op jit(solution)/shard_map/ppermute | solution.py:39
  69.6 32.8 %collective-permute-start.19 = (bf16[272,256]{1,0:T(8,128)(2,1)S(1)}, bf16[272,256]{1,0:T(8,128)(2,1)S(1)}, u32[]{:S(2)}, u32[]{:S(2)}) collective-permute-start(bf16[272,256]{1,0:T(8,128)(2,1)S(1)} %collective-permute-done.15.refs_3_), channel_id=1, source_target_pairs={{0,1},{1,0},{2,3},{3,2},{4,5},{5,4},{6,7},{7,6},{8,9},{9,8},{10,11... | collective-permute-start | bytes 417800 | tf_op jit(solution)/shard_map/ppermute | solution.py:39
  107.3 70.5 %all-to-all-start.1 = ((bf16[8,272,256]{2,1,0:T(8,128)(2,1)}), bf16[8,272,256]{2,1,0:T(8,128)(2,1)S(1)}, u32[]{:S(2)}, u32[]{:S(2)}) async-start(bf16[8,272,256]{2,1,0:T(8,128)(2,1)} %shard_map.98), calls=%async_computation.1 | async-start | bytes 2228224 | tf_op jit(solution)/shard_map/all_to_all | solution.py:435
  128.8 28.5 %collective-permute-start.27 = (f32[256,256]{1,0:T(8,128)S(1)}, f32[256,256]{1,0:T(8,128)S(1)}, u32[]{:S(2)}, u32[]{:S(2)}) collective-permute-start(f32[256,256]{1,0:T(8,128)S(1)} %copy-done.27), channel_id=1, source_target_pairs={{0,8},{8,0},{16,24},{24,16},{1,9},{9,1},{17,25},{25,17},{2,10},{10... | collective-permute-start | bytes 786440 | tf_op jit(solution)/shard_map/ppermute | solution.py:39
  130.0 27.3 %collective-permute-start.28 = (f32[256,256]{1,0:T(8,128)S(1)}, f32[256,256]{1,0:T(8,128)S(1)}, u32[]{:S(2)}, u32[]{:S(2)}) collective-permute-start(f32[256,256]{1,0:T(8,128)S(1)} %copy-done.25), channel_id=1, source_target_pairs={{0,16},{8,24},{16,0},{24,8},{1,17},{9,25},{17,1},{25,9},{2,18},{10... | collective-permute-start | bytes 786440 | tf_op jit(solution)/shard_map/ppermute | solution.py:39
  130.2 27.1 %collective-permute-start.29 = (f32[256,256]{1,0:T(8,128)S(1)}, f32[256,256]{1,0:T(8,128)S(1)}, u32[]{:S(2)}, u32[]{:S(2)}) collective-permute-start(f32[256,256]{1,0:T(8,128)S(1)} %copy-done.23), channel_id=1, source_target_pairs={{0,24},{8,16},{16,8},{24,0},{1,25},{9,17},{17,9},{25,1},{2,26},{10... | collective-permute-start | bytes 786440 | tf_op jit(solution)/shard_map/ppermute | solution.py:39
  131.4 13.9 %collective-permute-start.50 = (bf16[256,256]{1,0:T(8,128)(2,1)}, bf16[256,256]{1,0:T(8,128)(2,1)S(1)}, u32[]{:S(2)}, u32[]{:S(2)}) collective-permute-start(bf16[256,256]{1,0:T(8,128)(2,1)} %shard_map.106.refs_0_), channel_id=1, source_target_pairs={{0,4},{1,5},{2,6},{3,7},{4,0},{5,1},{6,2},{7,3},{8,12},{9,13},{10,... | collective-permute-start | bytes 393224 | tf_op jit(solution)/shard_map/ppermute | solution.py:39
  133.6 16.1 %collective-permute-start.51 = (bf16[256,256]{1,0:T(8,128)(2,1)}, bf16[256,256]{1,0:T(8,128)(2,1)S(1)}, u32[]{:S(2)}, u32[]{:S(2)}) collective-permute-start(bf16[256,256]{1,0:T(8,128)(2,1)} %shard_map.106.refs_0_), channel_id=1, source_target_pairs={{0,6},{1,7},{2,4},{3,5},{4,2},{5,3},{6,0},{7,1},{8,14},{9,15},{10,... | collective-permute-start | bytes 393224 | tf_op jit(solution)/shard_map/ppermute | solution.py:39
  152.8 28.6 %collective-permute-start.52 = (bf16[4,128,256]{2,1,0:T(8,128)(2,1)}, bf16[4,128,256]{2,1,0:T(8,128)(2,1)S(1)}, u32[]{:S(2)}, u32[]{:S(2)}) collective-permute-start(bf16[4,128,256]{2,1,0:T(8,128)(2,1)} %get-tuple-element.154), channel_id=1, source_target_pairs={{0,8},{8,0},{16,24},{24,16},{1,9},{9,1},{17,25},{25,17},{2,10},{10... | collective-permute-start | bytes 786440 | tf_op jit(solution)/shard_map/ppermute | solution.py:39
  162.4 12.3 %collective-permute-start.32 = (bf16[256,256]{1,0:T(8,128)(2,1)}, bf16[256,256]{1,0:T(8,128)(2,1)S(1)}, u32[]{:S(2)}, u32[]{:S(2)}) collective-permute-start(bf16[256,256]{1,0:T(8,128)(2,1)} %shard_map.102.refs_0_), channel_id=1, source_target_pairs={{0,6},{1,7},{2,4},{3,5},{4,2},{5,3},{6,0},{7,1},{8,14},{9,15},{10,... | collective-permute-start | bytes 393224 | tf_op jit(solution)/shard_map/ppermute | solution.py:39
  163.3 19.3 %collective-permute-start.53 = (bf16[4,128,256]{2,1,0:T(8,128)(2,1)}, bf16[4,128,256]{2,1,0:T(8,128)(2,1)S(1)}, u32[]{:S(2)}, u32[]{:S(2)}) collective-permute-start(bf16[4,128,256]{2,1,0:T(8,128)(2,1)} %get-tuple-element.155), channel_id=1, source_target_pairs={{0,16},{8,24},{16,0},{24,8},{1,17},{9,25},{17,1},{25,9},{2,18},{10... | collective-permute-start | bytes 786440 | tf_op jit(solution)/shard_map/ppermute | solution.py:39
  180.2 18.1 %collective-permute-start.37 = (bf16[4,128,256]{2,1,0:T(8,128)(2,1)}, bf16[4,128,256]{2,1,0:T(8,128)(2,1)S(1)}, u32[]{:S(2)}, u32[]{:S(2)}) collective-permute-start(bf16[4,128,256]{2,1,0:T(8,128)(2,1)} %get-tuple-element.134), channel_id=1, source_target_pairs={{0,24},{8,16},{16,8},{24,0},{1,25},{9,17},{17,9},{25,1},{2,26},{10... | collective-permute-start | bytes 786440 | tf_op jit(solution)/shard_map/ppermute | solution.py:39
  181.4 17.0 %collective-permute-start.54 = (bf16[4,128,256]{2,1,0:T(8,128)(2,1)}, bf16[4,128,256]{2,1,0:T(8,128)(2,1)}, u32[]{:S(2)}, u32[]{:S(2)}) collective-permute-start(bf16[4,128,256]{2,1,0:T(8,128)(2,1)} %get-tuple-element.156), channel_id=1, source_target_pairs={{0,24},{8,16},{16,8},{24,0},{1,25},{9,17},{17,9},{25,1},{2,26},{10... | collective-permute-start | bytes 786440 | tf_op jit(solution)/shard_map/ppermute | solution.py:39
  182.6 17.8 %collective-permute-start.38 = (bf16[4,128,256]{2,1,0:T(8,128)(2,1)}, bf16[4,128,256]{2,1,0:T(8,128)(2,1)S(1)}, u32[]{:S(2)}, u32[]{:S(2)}) collective-permute-start(bf16[4,128,256]{2,1,0:T(8,128)(2,1)} %get-tuple-element.137.refs_4_), channel_id=1, source_target_pairs={{0,1},{1,0},{2,3},{3,2},{4,5},{5,4},{6,7},{7,6},{8,9},{9,8},{10,11... | collective-permute-start | bytes 786440 | tf_op jit(solution)/shard_map/ppermute | solution.py:39
  185.5 15.7 %collective-permute-start.39 = (bf16[4,128,256]{2,1,0:T(8,128)(2,1)S(1)}, bf16[4,128,256]{2,1,0:T(8,128)(2,1)S(1)}, u32[]{:S(2)}, u32[]{:S(2)}) collective-permute-start(bf16[4,128,256]{2,1,0:T(8,128)(2,1)S(1)} %collective-permute-done.35.refs_5_), channel_id=1, source_target_pairs={{0,1},{1,0},{2,3},{3,2},{4,5},{5,4},{6,7},{7,6},{8,9},{9,8},{10,11... | collective-permute-start | bytes 786440 | tf_op jit(solution)/shard_map/ppermute | solution.py:39
  198.4 13.3 %collective-permute-start.43 = (bf16[8,128,256]{2,1,0:T(8,128)(2,1)}, bf16[8,128,256]{2,1,0:T(8,128)(2,1)S(1)}, u32[]{:S(2)}, u32[]{:S(2)}) collective-permute-start(bf16[8,128,256]{2,1,0:T(8,128)(2,1)} %get-tuple-element.146), channel_id=1, source_target_pairs={{0,8},{8,0},{16,24},{24,16},{1,9},{9,1},{17,25},{25,17},{2,10},{10... | collective-permute-start | bytes 1572872 | tf_op jit(solution)/shard_map/ppermute | solution.py:39
  206.4 24.6 %collective-permute-start.44 = (bf16[8,128,256]{2,1,0:T(8,128)(2,1)}, bf16[8,128,256]{2,1,0:T(8,128)(2,1)S(1)}, u32[]{:S(2)}, u32[]{:S(2)}) collective-permute-start(bf16[8,128,256]{2,1,0:T(8,128)(2,1)} %get-tuple-element.147), channel_id=1, source_target_pairs={{0,16},{8,24},{16,0},{24,8},{1,17},{9,25},{17,1},{25,9},{2,18},{10... | collective-permute-start | bytes 1572872 | tf_op jit(solution)/shard_map/ppermute | solution.py:39
  207.7 23.3 %collective-permute-start.45 = (bf16[8,128,256]{2,1,0:T(8,128)(2,1)}, bf16[8,128,256]{2,1,0:T(8,128)(2,1)S(1)}, u32[]{:S(2)}, u32[]{:S(2)}) collective-permute-start(bf16[8,128,256]{2,1,0:T(8,128)(2,1)} %get-tuple-element.148), channel_id=1, source_target_pairs={{0,24},{8,16},{16,8},{24,0},{1,25},{9,17},{17,9},{25,1},{2,26},{10... | collective-permute-start | bytes 1572872 | tf_op jit(solution)/shard_map/ppermute | solution.py:39
  208.2 26.2 %collective-permute-start.33 = (bf16[8,128,256]{2,1,0:T(8,128)(2,1)}, bf16[8,128,256]{2,1,0:T(8,128)(2,1)S(1)}, u32[]{:S(2)}, u32[]{:S(2)}) collective-permute-start(bf16[8,128,256]{2,1,0:T(8,128)(2,1)} %get-tuple-element.129), channel_id=1, source_target_pairs={{0,8},{8,0},{16,24},{24,16},{1,9},{9,1},{17,25},{25,17},{2,10},{10... | collective-permute-start | bytes 1572872 | tf_op jit(solution)/shard_map/ppermute | solution.py:39
  209.1 44.3 %collective-permute-start.34 = (bf16[8,128,256]{2,1,0:T(8,128)(2,1)}, bf16[8,128,256]{2,1,0:T(8,128)(2,1)S(1)}, u32[]{:S(2)}, u32[]{:S(2)}) collective-permute-start(bf16[8,128,256]{2,1,0:T(8,128)(2,1)} %get-tuple-element.130), channel_id=1, source_target_pairs={{0,16},{8,24},{16,0},{24,8},{1,17},{9,25},{17,1},{25,9},{2,18},{10... | collective-permute-start | bytes 1572872 | tf_op jit(solution)/shard_map/ppermute | solution.py:39
  211.6 41.8 %collective-permute-start.42 = (bf16[8,128,256]{2,1,0:T(8,128)(2,1)}, bf16[8,128,256]{2,1,0:T(8,128)(2,1)S(1)}, u32[]{:S(2)}, u32[]{:S(2)}) collective-permute-start(bf16[8,128,256]{2,1,0:T(8,128)(2,1)} %get-tuple-element.136), channel_id=1, source_target_pairs={{0,24},{8,16},{16,8},{24,0},{1,25},{9,17},{17,9},{25,1},{2,26},{10... | collective-permute-start | bytes 1572872 | tf_op jit(solution)/shard_map/ppermute | solution.py:39
  (70 other events, 618.1 us)

commit v6 on v5

--- a/solution.py
+++ b/solution.py
@@ -43,11 +43,12 @@
     return [piece if k == 0 else swap(piece, axis, k * unit) for k, piece in enumerate(pieces)]
 
 
-def tie(*values):
-    return lax.optimization_barrier(values)
-
-
-def pack_kernel(emb_ref, other_ref, positive_ref, user_ref, item_ref, line_ref, plane_ref):
+def tie(*lists):
+    flat = iter(lax.optimization_barrier([value for values in lists for value in values]))
+    return [[next(flat) for _ in values] for values in lists]
+
+
+def pack_kernel(emb_ref, other_ref, positive_ref, user_ref, item_ref, out_ref):
     rows = emb_ref.shape[0]
     down = lax.broadcasted_iota(jnp.int32, (rows, rows), 0)
     across = lax.broadcasted_iota(jnp.int32, (rows, rows), 1)
@@ -63,21 +64,16 @@
     for index, values in enumerate(numbers):
         block = jnp.where(line == 2 * index, values // DIGIT, block)
         block = jnp.where(line == 2 * index + 1, values % DIGIT, block)
-    extra = block.astype(F32).astype(BF16)
-    for ref in (line_ref, plane_ref):
-        ref[:rows, :] = emb_ref[...]
-        ref[rows : rows + EXTRA, :] = extra
-    plane_ref[rows + EXTRA :, :] = other_ref[...]
+    out_ref[:rows, :] = emb_ref[...]
+    out_ref[rows : rows + EXTRA, :] = block.astype(F32).astype(BF16)
+    out_ref[rows + EXTRA :, :] = other_ref[...]
 
 
 def pack(emb, other, positive, user_expert, item_expert):
     rows, width = emb.shape
     return pl.pallas_call(
         pack_kernel,
-        out_shape=[
-            jax.ShapeDtypeStruct((rows + EXTRA, width), BF16),
-            jax.ShapeDtypeStruct((2 * rows + EXTRA, width), BF16),
-        ],
+        out_shape=jax.ShapeDtypeStruct((2 * rows + EXTRA, width), BF16),
         cost_estimate=SMALL,
     )(
         emb,
@@ -102,12 +98,12 @@
 def stats_kernel(first_ref, *refs, blocks, count, chunk):
     users_refs, items_refs = refs[:blocks], refs[blocks : blocks + count]
     out_ref, all_ref, col_ref, s_ref = refs[blocks + count :]
-    own, emb = items_refs[0].shape
-    rows = all_ref.shape[1] - EXTRA
+    rows, emb = all_ref.shape[1] - EXTRA, all_ref.shape[2]
+    own = col_ref.shape[0] // count
     n_cols = own * count
     gather_rows(users_refs, all_ref)
     for k, ref in enumerate(items_refs):
-        col_ref[k * own : (k + 1) * own, :] = ref[...]
+        col_ref[k * own : (k + 1) * own, :] = ref[rows + EXTRA :, :]
 
     def pair(step, carry):
         for half in range(2):
@@ -137,8 +133,8 @@
 
 
 def stats(first, users, items):
-    own, emb = items[0].shape
-    rows = (users[0].shape[0] - EXTRA) // 2
+    emb = users[0].shape[1]
+    rows = own = (users[0].shape[0] - EXTRA) // 2
     height = rows + EXTRA
     blocks, count = len(users), len(items)
     return pl.pallas_call(
@@ -185,13 +181,13 @@
     refs = refs[blocks + count :]
     stats_refs, out_refs, refs = refs[:blocks], refs[blocks : 2 * blocks], refs[2 * blocks :]
     all_ref, col_ref, flip_ref, s_ref, g_ref, sum_ref = refs
-    own, emb = items_refs[0].shape
-    rows = all_ref.shape[1] - EXTRA
+    rows, emb = all_ref.shape[1] - EXTRA, all_ref.shape[2]
+    own = col_ref.shape[0] // count
     n_cols = own * count
     gather_rows(users_refs, all_ref)
     for k, ref in enumerate(items_refs):
-        col_ref[k * own : (k + 1) * own, :] = ref[...]
-        flip_ref[:, k * own : (k + 1) * own] = ref[...].T
+        col_ref[k * own : (k + 1) * own, :] = ref[rows + EXTRA :, :]
+        flip_ref[:, k * own : (k + 1) * own] = ref[rows + EXTRA :, :].T
 
     def pair(step, carry):
         for half in range(2):
@@ -213,8 +209,8 @@
 
 
 def user_grads(first, users, items, found):
-    own, emb = items[0].shape
-    rows = (users[0].shape[0] - EXTRA) // 2
+    emb = users[0].shape[1]
+    rows = own = (users[0].shape[0] - EXTRA) // 2
     height = rows + EXTRA
     blocks, count = len(users), len(items)
     return pl.pallas_call(
@@ -241,10 +237,10 @@
     level_refs, out_refs, refs = refs[:blocks], refs[blocks : blocks + count], refs[blocks + count :]
     extra_ref, row_ref, col_ref, s_ref, g_ref = refs
     own, emb = out_refs[0].shape
-    rows = users_refs[0].shape[0] - EXTRA
+    rows = row_ref.shape[0] // blocks
     n_cols = own * count
     for k in range(blocks // CORES):
-        extra_ref[k] = users_refs[k][rows:, :]
+        extra_ref[k] = users_refs[k][rows : rows + EXTRA, :]
     for k, ref in enumerate(users_refs):
         row_ref[k * rows : (k + 1) * rows, :] = ref[:rows, :]
     for k, ref in enumerate(plane_refs):
@@ -254,7 +250,7 @@
         half = block % 2
         queries = users_refs[block][:rows, :] * jnp.asarray(SCALE, BF16)
         s_ref[half] = mm(col_ref[...], queries, 1, 1)
-        positive = number(users_refs[block][rows:, :], 0)
+        positive = number(users_refs[block][rows : rows + EXTRA, :], 0)
         level = level_refs[block][...]
         for c in range(0, n_cols, chunk):
             probs = jnp.exp(s_ref[half, c : c + chunk, :] - level)
@@ -267,9 +263,8 @@
 
 
 def item_grads(first, users, planes, level):
-    height, emb = users[0].shape
-    rows = height - EXTRA
-    own = planes[0].shape[0] - height
+    emb = users[0].shape[1]
+    rows = own = (users[0].shape[0] - EXTRA) // 2
     blocks, count = len(users), len(planes)
     results = pl.pallas_call(
         functools.partial(item_kernel, blocks=blocks, count=count, chunk=64),
@@ -296,7 +291,7 @@
         out_ref[k, :rows, :] = in_ref[:, k * width : (k + 1) * width]
         for cut_at in range(0, rows, width):
             place = rows + cut_at // width * EXTRA
-            out_ref[k, place : place + EXTRA, :] = line_ref[rows:, cut_at : cut_at + width]
+            out_ref[k, place : place + EXTRA, :] = line_ref[rows : rows + EXTRA, cut_at : cut_at + width]
 
 
 def cut(hidden, line, parts):
@@ -348,50 +343,54 @@
 
 
 def total_kernel(*refs):
-    total = refs[0][...]
-    for ref in refs[1:-1]:
-        total = total + ref[...]
-    refs[-1][...] = total.astype(BF16)
-
-
-def total(pieces):
-    shape = pieces[0].shape
-    size = shape[0] * shape[1]
+    *in_refs, out_ref = refs
+    count = len(in_refs) // 2
+    rows = in_refs[0].shape[0]
+    for tower in range(2):
+        pieces = [ref[...] for ref in in_refs[tower * count : (tower + 1) * count]]
+        out_ref[tower * rows : (tower + 1) * rows, :] = sum(pieces[1:], pieces[0]).astype(BF16)
+
+
+def total(user_pieces, item_pieces):
+    rows, emb = user_pieces[0].shape
     return pl.pallas_call(
         total_kernel,
-        in_specs=[WHOLE] * len(pieces),
+        in_specs=[WHOLE] * (2 * len(user_pieces)),
         out_specs=WHOLE,
-        out_shape=jax.ShapeDtypeStruct(shape, BF16),
-        cost_estimate=SMALL,
-    )(*pieces)
-
-
-def select_kernel(me_ref, extra_ref, *refs, tower, lines):
+        out_shape=jax.ShapeDtypeStruct((2 * rows, emb), BF16),
+        cost_estimate=SMALL,
+    )(*user_pieces, *item_pieces)
+
+
+def select_kernel(me_ref, extra_ref, *refs, lines):
     out_refs = refs[lines:]
-    span = out_refs[0].shape[1]
+    span = out_refs[0].shape[2]
+    rows = refs[0].shape[0] // 2
     for j, grad_ref in enumerate(refs[:lines]):
-        onehot = onehot_of(number(extra_ref[j], 1 + tower), me_ref[0], len(out_refs))
-        moved = mm(onehot, grad_ref[...], 1, 0).astype(BF16)
-        for k, out_ref in enumerate(out_refs):
-            out_ref[j] = moved[k * span : (k + 1) * span, :]
-
-
-def select(me, extra, grads, groups, tower):
+        for tower in range(2):
+            onehot = onehot_of(number(extra_ref[j], 1 + tower), me_ref[0], len(out_refs))
+            values = grad_ref[tower * rows : (tower + 1) * rows, :]
+            moved = mm(onehot, values, 1, 0).astype(BF16)
+            for k, out_ref in enumerate(out_refs):
+                out_ref[tower, j] = moved[k * span : (k + 1) * span, :]
+
+
+def select(me, extra, grads, groups):
     lines = len(grads)
-    rows, emb = grads[0].shape
+    emb = grads[0].shape[1]
     span = EXPERTS * CAP // groups
     return pl.pallas_call(
-        functools.partial(select_kernel, tower=tower, lines=lines),
+        functools.partial(select_kernel, lines=lines),
         in_specs=[SCALARS] + [WHOLE] * (1 + lines),
         out_specs=[WHOLE] * groups,
-        out_shape=[jax.ShapeDtypeStruct((lines, span, emb), BF16)] * groups,
+        out_shape=[jax.ShapeDtypeStruct((2, lines, span, emb), BF16)] * groups,
         cost_estimate=SMALL,
     )(me, extra, *grads)
 
 
 def outer_kernel(order_ref, *refs, groups):
     hidden_refs, grad_refs, out_ref = refs[:groups], refs[groups:-1], refs[-1]
-    lines = grad_refs[0].shape[0]
+    lines = grad_refs[0].shape[1]
     for e in range(out_ref.shape[0]):
         here = slice(e * CAP, (e + 1) * CAP)
         left, right = [], []
@@ -399,18 +398,22 @@
             for j in range(lines):
                 block = order_ref[index // groups * lines + j]
                 left.append(hidden_refs[index % groups][block, here, :])
-                right.append(grad_ref[j, here, :])
+                right.append(grad_ref[0, j, here, :])
         out_ref[e] = mm(jnp.concatenate(left), jnp.concatenate(right), 0, 0)
 
 
-def outer(order, hidden, grad):
+def outer(order, hidden, grad, tower):
     blocks, span, width = hidden[0].shape
-    groups, emb = len(hidden), grad[0].shape[-1]
-    own = span // CAP
+    _, lines, _, emb = grad[0].shape
+    groups, own = len(hidden), span // CAP
+    one = pl.BlockSpec((1, lines, span, emb), lambda _: (tower, 0, 0, 0))
     return pl.pallas_call(
         functools.partial(outer_kernel, groups=groups),
-        in_specs=[SCALARS] + [WHOLE] * (groups + len(grad)),
-        out_specs=WHOLE,
+        grid=(1,),
+        in_specs=[SCALARS]
+        + [pl.BlockSpec((blocks, span, width), lambda _: (0, 0, 0))] * groups
+        + [one] * len(grad),
+        out_specs=pl.BlockSpec((own, width, emb), lambda _: (0, 0, 0)),
         out_shape=jax.ShapeDtypeStruct((own, width, emb), F32),
         compiler_params=pltpu.CompilerParams(vmem_limit_bytes=40 * MIB),
         cost_estimate=SMALL,
@@ -437,53 +440,55 @@
     def across(pieces):
         return pieces + [swap(piece, "item", 1) for piece in pieces]
 
-    item_line = exchange([item_emb] * lines, "item", CORES)
-    line, plane = pack(user_emb, item_emb, positive, user_expert, item_expert)
-    plane = exchange([plane] * groups, "user")
-    item_blocks = cut(item_hidden, line, parts)
-    user_blocks = cut(user_hidden, line, parts)
-    again, *item_line = tie(line, *item_line)
-    item_cross = across(item_line)
-    user_line = exchange([again] * lines, "item", CORES)
-
-    found = stats(first_cross, plane, item_cross)
-    item_blocks, found = tie(item_blocks, found)
-    found = exchange([found] * groups, "user")
+    early = groups // 2 + 1
+
+    def late(pieces):
+        return [swap(piece, "user", early + k) for k, piece in enumerate(pieces)]
+
+    packed = pack(user_emb, item_emb, positive, user_expert, item_expert)
+    line = exchange([packed] * lines, "item", CORES)
+    plane = exchange([packed] * early, "user")
+    item_blocks = cut(item_hidden, packed, parts)
+    user_blocks = cut(user_hidden, packed, parts)
+    (item_blocks, again), plane = tie([item_blocks, packed], plane)
+    plane += late([again] * (groups - early))
     item_cols = by_part(item_blocks)
+    (line,) = tie(line)
+    plane, cross = tie(plane, across(line))
+
+    found = exchange([stats(first_cross, plane, cross)] * groups, "user")
     level, loss = levels(found)
-    level, *found = tie(level, *found)
-    level = across(exchange([level] * lines, "item", CORES))
-    user_parts = list(user_grads(first_cross, plane, item_cross, found))
+    (level,), found = tie([level], found)
+    level = exchange([level] * lines, "item", CORES)
+    user_parts = user_grads(first_cross, plane, cross, found)
+    user_parts, level = tie(user_parts, level)
+    (level,) = tie(across(level))
     user_pieces = exchange(user_parts, "user")
-    user_parts[0], *level = tie(user_parts[0], *level)
-    item_parts, extra = item_grads(first_plane, across(user_line), plane, level)
-    item_pieces = exchange(item_parts, "user")
-    item_cols, user_blocks, extra = tie(item_cols, user_blocks, extra)
+    item_parts, extra = item_grads(first_plane, cross, plane, level)
+    item_pieces = exchange(item_parts[:early], "user")
+    (item_cols, user_blocks, extra), = tie([item_cols, user_blocks, extra])
     user_cols = by_part(user_blocks)
-
-    user_pieces[0], *item_slots = tie(
-        user_parts[0], *slot_hidden(me, item_cols, rows, groups, 1)
-    )
-    early = groups // 2 + 1
+    item_slots = slot_hidden(me, item_cols, rows, groups, 1)
+    user_pieces, item_parts, item_slots = tie(user_pieces, item_parts[early:], item_slots)
+    item_pieces, item_slots = tie(item_pieces + late(item_parts), item_slots)
+
+    both = exchange([total(user_pieces, item_pieces)] * lines, "item", CORES)
     item_rows = exchange(item_slots[:early], "user")
-    user_lines = exchange([total(user_pieces)] * lines, "item", CORES)
-    item_lines = exchange([total(item_pieces)] * lines, "item", CORES)
-    *user_lines, item_slots[-1] = tie(*user_lines, item_slots[-1])
-    item_rows += [swap(item_slots[k], "user", k) for k in range(early, groups)]
-
-    def spread(chosen):
-        return across(exchange(chosen, "user"))
-
-    user_chosen = select(me, extra, user_lines, groups, 0)
-    user_cols, *user_chosen = tie(user_cols, *user_chosen)
-    user_grad = spread(user_chosen)
-    user_slots = list(slot_hidden(me, user_cols, rows, groups, 0))
-    user_rows = exchange(user_slots[:early], "user")
-    item_grad = spread(select(me, extra, item_lines, groups, 1))
-    *user_grad, user_slots[-1] = tie(*user_grad, user_slots[-1])
-    user_rows += [swap(user_slots[k], "user", k) for k in range(early, groups)]
-    item_weight_grad = outer(order, item_rows, item_grad)
-    user_weight_grad = outer(order, user_rows, user_grad)
+    (user_cols,), item_slots, item_rows = tie([user_cols], item_slots[early:], item_rows)
+    item_rows += late(item_slots)
+    user_slots = slot_hidden(me, user_cols, rows, groups, 0)
+    user_rows = exchange(user_slots[:2], "user")
+    both, user_slots, item_rows = tie(both, user_slots, item_rows)
+
+    chosen = exchange(select(me, extra, both, groups), "user")
+    user_rows += [swap(user_slots[k], "user", k) for k in range(2, early)]
+    open_rows, user_slots = tie(user_rows[1:2], user_slots[early:])
+    user_rows[1:2] = open_rows
+    user_rows += late(user_slots)
+    (chosen,) = tie(chosen)
+    grad = across(chosen)
+    item_weight_grad = outer(order, item_rows, grad, 1)
+    user_weight_grad = outer(order, user_rows, grad, 0)
     row_loss = loss[0]
     return (row_loss, user_weight_grad, item_weight_grad)
 

time: 258 us -> 249 us (0.965); the launches traced: 256 us -> 244 us
  starting transfers between devices: 78.8 us -> 73.6 us
  Pallas kernels: 42.2 us -> 38.1 us
  waiting for transfers between devices: 123 us -> 120 us
    ppermute x59 -> x42, starting transfers between devices: 67.5 us -> 61 us  [swap(): return lax.ppermute(piece, axis, [(j, j ^ bits) for j in range(size)])]
    pallas_call x7 -> x5, Pallas kernels: 16.6 us -> 12.5 us  [the longest x2 5.25 us: outer(): pl.pallas_call(functools.partial(outer_kernel, groups=groups), grid=(1,),...]
    ppermute x59 -> x42, waiting for transfers between devices: 123 us -> 120 us  [swap(): return lax.ppermute(piece, axis, [(j, j ^ bits) for j in range(size)])]
    unnamed x82 -> x72, local copies, waits for them, and re-layouts: 9.99 us -> 11 us
  transfers between devices with their start and end apart: 61 -> 44, of which waited for: 25 -> 25; matrix products, arithmetic and copies ran while one was open for 0% -> 0% of each run, Pallas kernels for 14% -> 13%
where the time goes in v6:
time: 249 us; the launch traced here: 244 us
  waiting for transfers between devices  120 us (48%)
  starting transfers between devices  73.6 us (30%)
  Pallas kernels  38.1 us (15%)
  local copies, waits for them, and re-layouts  11 us (4%)
    ppermute x42, waiting for transfers between devices, swap(): return lax.ppermute(piece, axis, [(j, j ^ bits) for j in range(size)])  120 us
    ppermute x42, starting transfers between devices, swap(): return lax.ppermute(piece, axis, [(j, j ^ bits) for j in range(size)])  61 us
    all_to_all x2, starting transfers between devices, by_part(): lax.all_to_all(blocks, 'item', split_axis=0, concat_axis=0, tiled=True)  12.5 us
    unnamed x72, local copies, waits for them, and re-layouts  11 us
    pallas_call x2, Pallas kernels, slot_hidden(): pl.pallas_call(functools.partial(hidden_kernel, tower=tower, rows=rows),...  7.84 us
    pallas_call x2, Pallas kernels, outer(): pl.pallas_call(functools.partial(outer_kernel, groups=groups), grid=(1,),...  5.25 us
  transfers between devices with their start and end apart: 44, of which 25 were waited for; matrix products, arithmetic and copies ran while one was open for 0% of the time, Pallas kernels for 13%

profile of v6, /device:TPU:11, one launch (start us, length us, event | category | flops | bytes accessed | tf_op | source)
XLA Modules:
  0.0 243.9 jit_solution(7446708926061793237)
XLA Ops:
  4.0 2.3 shard_map.95
  6.3 3.7 %collective-permute-done.1.refs_2_.refs_10_ = bf16[528,256]{1,0:T(8,128)(2,1)S(1)} collective-permute-done((bf16[528,256]{1,0:T(8,128)(2,1)}, bf16[528,256]{1,0:T(8,128)(2,1)S(1)}, u32[]{:S(2)}, u32[]{:S(2)}) %collective-permute-start.1) | collective-permute-done | bytes 270368 | tf_op jit(solution)/shard_map/ppermute | solution.py:39
  11.0 6.8 %all-to-all-start = ((bf16[8,272,256]{2,1,0:T(8,128)(2,1)}), bf16[8,272,256]{2,1,0:T(8,128)(2,1)}, u32[]{:S(2)}, u32[]{:S(2)}) async-start(bf16[8,272,256]{2,1,0:T(8,128)(2,1)} %shard_map.95), calls=%async_computation | async-start | bytes 2228224 | tf_op jit(solution)/shard_map/all_to_all | solution.py:438
  21.1 40.1 %collective-permute-done.5.refs_7_.refs_3_ = bf16[528,256]{1,0:T(8,128)(2,1)S(1)} collective-permute-done((bf16[528,256]{1,0:T(8,128)(2,1)S(1)}, bf16[528,256]{1,0:T(8,128)(2,1)S(1)}, u32[]{:S(2)}, u32[]{:S(2)}) %collective-permute-start.5) | collective-permute-done | bytes 270368 | tf_op jit(solution)/shard_map/ppermute | solution.py:39
  61.2 4.1 %collective-permute-done.4.refs_6_.refs_2_ = bf16[528,256]{1,0:T(8,128)(2,1)S(1)} collective-permute-done((bf16[528,256]{1,0:T(8,128)(2,1)S(1)}, bf16[528,256]{1,0:T(8,128)(2,1)S(1)}, u32[]{:S(2)}, u32[]{:S(2)}) %collective-permute-start.4) | collective-permute-done | bytes 270368 | tf_op jit(solution)/shard_map/ppermute | solution.py:39
  68.1 6.7 %collective-permute-done.2.refs_3_.refs_11_ = bf16[528,256]{1,0:T(8,128)(2,1)S(1)} collective-permute-done((bf16[528,256]{1,0:T(8,128)(2,1)S(1)}, bf16[528,256]{1,0:T(8,128)(2,1)S(1)}, u32[]{:S(2)}, u32[]{:S(2)}) %collective-permute-start.2) | collective-permute-done | bytes 270368 | tf_op jit(solution)/shard_map/ppermute | solution.py:39
  74.9 3.6 %shard_map.96.refs_0_.refs_12_ = f32[4,3,256]{2,1,0:T(4,128)S(1)} custom-call(s32[8]{0:T(128)S(1)} %add_multiply_fusion.1.first_ref, bf16[528,256]{1,0:T(8,128)(2,1)S(1)} %copy-done, bf16[528,256]{1,0:T(8,128)(2,1)S(1)} %collective-permute-done.refs_1_.refs_9_, bf16[528,256]{1,0:T(8,128)(2,1)S(1)} %collective-permute-done.1.refs_2_.refs_10_, ...), custom_call_target="tpu_custom_call" | custom-call | flops 1024 | bytes 1024 | tf_op jit(solution)/shard_map/pallas_call | solution.py:140
  85.8 4.0 %collective-permute-start.14 = (f32[1,256]{1,0:T(1,128)}, f32[1,256]{1,0:T(1,128)S(1)}, u32[]{:S(2)}, u32[]{:S(2)}) collective-permute-start(f32[1,256]{1,0:T(1,128)} %get-tuple-element.145.refs_12_), channel_id=1, source_target_pairs={{0,4},{1,5},{2,6},{3,7},{4,0},{5,1},{6,2},{7,3},{8,12},{9,13},{10,... | collective-permute-start | bytes 3080 | tf_op jit(solution)/shard_map/ppermute | solution.py:39
  92.7 4.5 %shard_map.99 = (f32[256,256]{1,0:T(8,128)S(1)}, f32[256,256]{1,0:T(8,128)S(1)}, f32[256,256]{1,0:T(8,128)S(1)}, f32[256,256]{1,0:T(8,128)S(1)}) custom-call(s32[8]{0:T(128)S(1)} %add_multiply_fusion.1.first_ref, bf16[528,256]{1,0:T(8,128)(2,1)S(1)} %copy-done, bf16[528,256]{1,0:T(8,128)(2,1)S(1)} %collective-permute-done.refs_1_.refs_9_, ...), custom_call_target="tpu_custom_call" | custom-call | flops 1024 | bytes 1024 | tf_op jit(solution)/shard_map/pallas_call | solution.py:216
  99.4 3.6 %collective-permute-start.16 = (f32[1,256]{1,0:T(1,128)S(1)}, f32[1,256]{1,0:T(1,128)S(1)}, u32[]{:S(2)}, u32[]{:S(2)}) collective-permute-start(f32[1,256]{1,0:T(1,128)S(1)} %copy-done.17), channel_id=1, source_target_pairs={{0,1},{1,0},{2,3},{3,2},{4,5},{5,4},{6,7},{7,6},{8,9},{9,8},{10,11... | collective-permute-start | bytes 3080 | tf_op jit(solution)/shard_map/ppermute | solution.py:39
  103.6 2.4 shard_map.98
  106.0 3.5 %shard_map.100 = (f32[256,256]{1,0:T(8,128)S(1)}, f32[256,256]{1,0:T(8,128)S(1)}, f32[256,256]{1,0:T(8,128)S(1)}, f32[256,256]{1,0:T(8,128)S(1)}, bf16[4,16,256]{2,1,0:T(8,128)(2,1)S(1)}) custom-call(s32[4]{0:T(128)S(1)} %add_multiply_fusion.first_ref, bf16[528,256]{1,0:T(8,128)(2,1)S(1)} %copy-done.1, ...), custom_call_target="tpu_custom_call" | custom-call | flops 1024 | bytes 1024 | tf_op jit(solution)/shard_map/pallas_call | solution.py:269
  113.0 5.7 %all-to-all-start.1 = ((bf16[8,272,256]{2,1,0:T(8,128)(2,1)}), bf16[8,272,256]{2,1,0:T(8,128)(2,1)S(1)}, u32[]{:S(2)}, u32[]{:S(2)}) async-start(bf16[8,272,256]{2,1,0:T(8,128)(2,1)} %shard_map.98), calls=%async_computation.1 | async-start | bytes 2228224 | tf_op jit(solution)/shard_map/all_to_all | solution.py:438
  123.6 3.9 %shard_map.101 = (bf16[8,128,256]{2,1,0:T(8,128)(2,1)}, bf16[8,128,256]{2,1,0:T(8,128)(2,1)}, bf16[8,128,256]{2,1,0:T(8,128)(2,1)}, bf16[8,128,256]{2,1,0:T(8,128)(2,1)}) custom-call(s32[2]{0:T(128)} %pad_add_fusion.me_ref, bf16[8,272,256]{2,1,0:T(8,128)(2,1)} %all-to-all-done.hidden_ref), custom_call_target="tpu_custom_call" | custom-call | flops 1024 | bytes 1024 | tf_op jit(solution)/shard_map/pallas_call | solution.py:335
  128.0 4.0 %collective-permute-done.24.refs_3_ = f32[256,256]{1,0:T(8,128)S(1)} collective-permute-done((f32[256,256]{1,0:T(8,128)S(1)}, f32[256,256]{1,0:T(8,128)S(1)}, u32[]{:S(2)}, u32[]{:S(2)}) %collective-permute-start.24) | collective-permute-done | bytes 262176 | tf_op jit(solution)/shard_map/ppermute | solution.py:39
  132.0 2.1 collective-permute-start.25
  134.1 3.6 %collective-permute-done.20.refs_5_ = f32[256,256]{1,0:T(8,128)} collective-permute-done((f32[256,256]{1,0:T(8,128)S(1)}, f32[256,256]{1,0:T(8,128)}, u32[]{:S(2)}, u32[]{:S(2)}) %collective-permute-start.20) | collective-permute-done | bytes 262176 | tf_op jit(solution)/shard_map/ppermute | solution.py:39
  139.3 3.5 %collective-permute-done.25.refs_7_ = f32[256,256]{1,0:T(8,128)S(1)} collective-permute-done((f32[256,256]{1,0:T(8,128)S(1)}, f32[256,256]{1,0:T(8,128)S(1)}, u32[]{:S(2)}, u32[]{:S(2)}) %collective-permute-start.25) | collective-permute-done | bytes 262176 | tf_op jit(solution)/shard_map/ppermute | solution.py:39
  145.6 9.0 %collective-permute-done.26.refs_1_ = bf16[8,128,256]{2,1,0:T(8,128)(2,1)S(1)} collective-permute-done((bf16[8,128,256]{2,1,0:T(8,128)(2,1)}, bf16[8,128,256]{2,1,0:T(8,128)(2,1)S(1)}, u32[]{:S(2)}, u32[]{:S(2)}) %collective-permute-start.26) | collective-permute-done | bytes 524320 | tf_op jit(solution)/shard_map/ppermute | solution.py:39
  157.9 2.3 shard_map.103.refs_0_
  163.5 3.9 %shard_map.102 = (bf16[8,128,256]{2,1,0:T(8,128)(2,1)}, bf16[8,128,256]{2,1,0:T(8,128)(2,1)}, bf16[8,128,256]{2,1,0:T(8,128)(2,1)}, bf16[8,128,256]{2,1,0:T(8,128)(2,1)}) custom-call(s32[2]{0:T(128)} %pad_add_fusion.me_ref, bf16[8,272,256]{2,1,0:T(8,128)(2,1)} %copy-done.28), custom_call_target="tpu_custom_call" | custom-call | flops 1024 | bytes 1024 | tf_op jit(solution)/shard_map/pallas_call | solution.py:335
  168.6 10.4 %collective-permute-done.31.refs_3_ = bf16[512,256]{1,0:T(8,128)(2,1)S(1)} collective-permute-done((bf16[512,256]{1,0:T(8,128)(2,1)}, bf16[512,256]{1,0:T(8,128)(2,1)S(1)}, u32[]{:S(2)}, u32[]{:S(2)}) %collective-permute-start.31) | collective-permute-done | bytes 262176 | tf_op jit(solution)/shard_map/ppermute | solution.py:39
  178.9 3.7 %collective-permute-done.30.refs_2_ = bf16[512,256]{1,0:T(8,128)(2,1)S(1)} collective-permute-done((bf16[512,256]{1,0:T(8,128)(2,1)}, bf16[512,256]{1,0:T(8,128)(2,1)S(1)}, u32[]{:S(2)}, u32[]{:S(2)}) %collective-permute-start.30) | collective-permute-done | bytes 262176 | tf_op jit(solution)/shard_map/ppermute | solution.py:39
  183.5 3.1 %shard_map.104 = (bf16[2,4,128,256]{3,2,1,0:T(8,128)(2,1)}, bf16[2,4,128,256]{3,2,1,0:T(8,128)(2,1)}, bf16[2,4,128,256]{3,2,1,0:T(8,128)(2,1)}, bf16[2,4,128,256]{3,2,1,0:T(8,128)(2,1)}) custom-call(s32[2]{0:T(128)} %pad_add_fusion.me_ref, bf16[4,16,256]{2,1,0:T(8,128)(2,1)} %copy-done.16, bf16[512,256]{1,0:T(8,128)(2,1)} %shard_map.103.refs_0_, ...), custom_call_target="tpu_custom_call" | custom-call | flops 1024 | bytes 1024 | tf_op jit(solution)/shard_map/pallas_call | solution.py:382
  189.6 2.0 collective-permute-start.34
  191.6 6.2 %collective-permute-done.35.refs_5_ = bf16[2,4,128,256]{3,2,1,0:T(8,128)(2,1)S(1)} collective-permute-done((bf16[2,4,128,256]{3,2,1,0:T(8,128)(2,1)}, bf16[2,4,128,256]{3,2,1,0:T(8,128)(2,1)S(1)}, u32[]{:S(2)}, u32[]{:S(2)}) %collective-permute-start.35) | collective-permute-done | bytes 524320 | tf_op jit(solution)/shard_map/ppermute | solution.py:39
  199.6 9.6 %collective-permute-done.37.refs_7_ = bf16[2,4,128,256]{3,2,1,0:T(8,128)(2,1)S(1)} collective-permute-done((bf16[2,4,128,256]{3,2,1,0:T(8,128)(2,1)}, bf16[2,4,128,256]{3,2,1,0:T(8,128)(2,1)S(1)}, u32[]{:S(2)}, u32[]{:S(2)}) %collective-permute-start.37) | collective-permute-done | bytes 524320 | tf_op jit(solution)/shard_map/ppermute | solution.py:39
  209.2 18.8 %collective-permute-start.38 = (bf16[2,4,128,256]{3,2,1,0:T(8,128)(2,1)}, bf16[2,4,128,256]{3,2,1,0:T(8,128)(2,1)S(1)}, u32[]{:S(2)}, u32[]{:S(2)}) collective-permute-start(bf16[2,4,128,256]{3,2,1,0:T(8,128)(2,1)} %get-tuple-element.207.refs_4_), channel_id=1, source_target_pairs={{0,1},{1,0},{2,3},{3,2},{4,5},{5,4},{6,7},{7,6},{8,9},{9,8},{10,11... | collective-permute-start | bytes 1572872 | tf_op jit(solution)/shard_map/ppermute | solution.py:39
  228.5 4.0 %collective-permute-done.33.refs_2_ = bf16[8,128,256]{2,1,0:T(8,128)(2,1)S(1)} collective-permute-done((bf16[8,128,256]{2,1,0:T(8,128)(2,1)}, bf16[8,128,256]{2,1,0:T(8,128)(2,1)S(1)}, u32[]{:S(2)}, u32[]{:S(2)}) %collective-permute-start.33) | collective-permute-done | bytes 524320 | tf_op jit(solution)/shard_map/ppermute | solution.py:39
  232.5 3.6 %collective-permute-start.41 = (bf16[2,4,128,256]{3,2,1,0:T(8,128)(2,1)S(1)}, bf16[2,4,128,256]{3,2,1,0:T(8,128)(2,1)S(1)}, u32[]{:S(2)}, u32[]{:S(2)}) collective-permute-start(bf16[2,4,128,256]{3,2,1,0:T(8,128)(2,1)S(1)} %collective-permute-done.37.refs_7_), channel_id=1, source_target_pairs={{0,1},{1,0},{2,3},{3,2},{4,5},{5,4},{6,7},{7,6},{8,9},{9,8},{10,11... | collective-permute-start | bytes 1572872 | tf_op jit(solution)/shard_map/ppermute | solution.py:39
  238.6 2.6 %shard_map.105 = f32[8,256,256]{2,1,0:T(8,128)} custom-call(s32[8]{0:T(128)S(1)} %xor.38.order_ref, bf16[8,128,256]{2,1,0:T(8,128)(2,1)S(1)} %copy-done.5, bf16[8,128,256]{2,1,0:T(8,128)(2,1)S(1)} %collective-permute-done.28.refs_1_, bf16[8,128,256]{2,1,0:T(8,128)(2,1)S(1)} %collective-permute-done.33.refs_2_, ...), custom_call_target="tpu_custom_call" | custom-call | flops 1024 | bytes 1024 | tf_op jit(solution)/shard_map/pallas_call | solution.py:410
  241.3 2.6 %shard_map.106 = f32[8,256,256]{2,1,0:T(8,128)} custom-call(s32[8]{0:T(128)S(1)} %xor.38.order_ref, bf16[8,128,256]{2,1,0:T(8,128)(2,1)S(1)} %copy-done.4, bf16[8,128,256]{2,1,0:T(8,128)(2,1)S(1)} %collective-permute-done.26.refs_1_, bf16[8,128,256]{2,1,0:T(8,128)(2,1)S(1)} %collective-permute-done.27.refs_2_, ...), custom_call_target="tpu_custom_call" | custom-call | flops 1024 | bytes 1024 | tf_op jit(solution)/shard_map/pallas_call | solution.py:410
  (148 shorter events, 52.8 us)
Async XLA Ops:
  2.5 7.6 %collective-permute-start.1 = (bf16[528,256]{1,0:T(8,128)(2,1)}, bf16[528,256]{1,0:T(8,128)(2,1)S(1)}, u32[]{:S(2)}, u32[]{:S(2)}) collective-permute-start(bf16[528,256]{1,0:T(8,128)(2,1)} %shard_map.94.line_ref.refs_0_.refs_4_.refs_8_), channel_id=1, source_target_pairs={{0,16},{8,24},{16,0},{24,8},{1,17},{9,25},{17,1},{25,9},{2,18},{10... | collective-permute-start | bytes 811016 | tf_op jit(solution)/shard_map/ppermute | solution.py:39
  3.7 7.2 %collective-permute-start = (bf16[528,256]{1,0:T(8,128)(2,1)}, bf16[528,256]{1,0:T(8,128)(2,1)S(1)}, u32[]{:S(2)}, u32[]{:S(2)}) collective-permute-start(bf16[528,256]{1,0:T(8,128)(2,1)} %shard_map.94.line_ref.refs_0_.refs_4_.refs_8_), channel_id=1, source_target_pairs={{0,8},{8,0},{16,24},{24,16},{1,9},{9,1},{17,25},{25,17},{2,10},{10... | collective-permute-start | bytes 811016 | tf_op jit(solution)/shard_map/ppermute | solution.py:39
  11.0 102.0 %all-to-all-start = ((bf16[8,272,256]{2,1,0:T(8,128)(2,1)}), bf16[8,272,256]{2,1,0:T(8,128)(2,1)}, u32[]{:S(2)}, u32[]{:S(2)}) async-start(bf16[8,272,256]{2,1,0:T(8,128)(2,1)} %shard_map.95), calls=%async_computation | async-start | bytes 2228224 | tf_op jit(solution)/shard_map/all_to_all | solution.py:438
  17.8 43.4 %collective-permute-start.5 = (bf16[528,256]{1,0:T(8,128)(2,1)S(1)}, bf16[528,256]{1,0:T(8,128)(2,1)S(1)}, u32[]{:S(2)}, u32[]{:S(2)}) collective-permute-start(bf16[528,256]{1,0:T(8,128)(2,1)S(1)} %copy-done), channel_id=1, source_target_pairs={{0,6},{1,7},{2,4},{3,5},{4,2},{5,3},{6,0},{7,1},{8,14},{9,15},{10,... | collective-permute-start | bytes 811016 | tf_op jit(solution)/shard_map/ppermute | solution.py:39
  19.0 46.4 %collective-permute-start.4 = (bf16[528,256]{1,0:T(8,128)(2,1)S(1)}, bf16[528,256]{1,0:T(8,128)(2,1)S(1)}, u32[]{:S(2)}, u32[]{:S(2)}) collective-permute-start(bf16[528,256]{1,0:T(8,128)(2,1)S(1)} %copy-done), channel_id=1, source_target_pairs={{0,4},{1,5},{2,6},{3,7},{4,0},{5,1},{6,2},{7,3},{8,12},{9,13},{10,... | collective-permute-start | bytes 811016 | tf_op jit(solution)/shard_map/ppermute | solution.py:39
  20.0 45.4 %collective-permute-start.3 = (bf16[528,256]{1,0:T(8,128)(2,1)S(1)}, bf16[528,256]{1,0:T(8,128)(2,1)S(1)}, u32[]{:S(2)}, u32[]{:S(2)}) collective-permute-start(bf16[528,256]{1,0:T(8,128)(2,1)S(1)} %copy-done), channel_id=1, source_target_pairs={{0,2},{1,3},{2,0},{3,1},{4,6},{5,7},{6,4},{7,5},{8,10},{9,11},{10,... | collective-permute-start | bytes 811016 | tf_op jit(solution)/shard_map/ppermute | solution.py:39
  66.4 8.5 %collective-permute-start.2 = (bf16[528,256]{1,0:T(8,128)(2,1)S(1)}, bf16[528,256]{1,0:T(8,128)(2,1)S(1)}, u32[]{:S(2)}, u32[]{:S(2)}) collective-permute-start(bf16[528,256]{1,0:T(8,128)(2,1)S(1)} %copy-done), channel_id=1, source_target_pairs={{0,24},{8,16},{16,8},{24,0},{1,25},{9,17},{17,9},{25,1},{2,26},{10... | collective-permute-start | bytes 811016 | tf_op jit(solution)/shard_map/ppermute | solution.py:39
  84.6 14.8 %collective-permute-start.15 = (f32[1,256]{1,0:T(1,128)}, f32[1,256]{1,0:T(1,128)S(1)}, u32[]{:S(2)}, u32[]{:S(2)}) collective-permute-start(f32[1,256]{1,0:T(1,128)} %get-tuple-element.145.refs_12_), channel_id=1, source_target_pairs={{0,6},{1,7},{2,4},{3,5},{4,2},{5,3},{6,0},{7,1},{8,14},{9,15},{10,... | collective-permute-start | bytes 3080 | tf_op jit(solution)/shard_map/ppermute | solution.py:39
  85.8 13.5 %collective-permute-start.14 = (f32[1,256]{1,0:T(1,128)}, f32[1,256]{1,0:T(1,128)S(1)}, u32[]{:S(2)}, u32[]{:S(2)}) collective-permute-start(f32[1,256]{1,0:T(1,128)} %get-tuple-element.145.refs_12_), channel_id=1, source_target_pairs={{0,4},{1,5},{2,6},{3,7},{4,0},{5,1},{6,2},{7,3},{8,12},{9,13},{10,... | collective-permute-start | bytes 3080 | tf_op jit(solution)/shard_map/ppermute | solution.py:39
  89.8 9.5 %collective-permute-start.13 = (f32[1,256]{1,0:T(1,128)}, f32[1,256]{1,0:T(1,128)S(1)}, u32[]{:S(2)}, u32[]{:S(2)}) collective-permute-start(f32[1,256]{1,0:T(1,128)} %get-tuple-element.145.refs_12_), channel_id=1, source_target_pairs={{0,2},{1,3},{2,0},{3,1},{4,6},{5,7},{6,4},{7,5},{8,10},{9,11},{10,... | collective-permute-start | bytes 3080 | tf_op jit(solution)/shard_map/ppermute | solution.py:39
  113.0 43.4 %all-to-all-start.1 = ((bf16[8,272,256]{2,1,0:T(8,128)(2,1)}), bf16[8,272,256]{2,1,0:T(8,128)(2,1)S(1)}, u32[]{:S(2)}, u32[]{:S(2)}) async-start(bf16[8,272,256]{2,1,0:T(8,128)(2,1)} %shard_map.98), calls=%async_computation.1 | async-start | bytes 2228224 | tf_op jit(solution)/shard_map/all_to_all | solution.py:438
  118.7 8.8 %collective-permute-start.22 = (f32[256,256]{1,0:T(8,128)S(1)}, f32[256,256]{1,0:T(8,128)S(1)}, u32[]{:S(2)}, u32[]{:S(2)}) collective-permute-start(f32[256,256]{1,0:T(8,128)S(1)} %copy-done.21), channel_id=1, source_target_pairs={{0,8},{8,0},{16,24},{24,16},{1,9},{9,1},{17,25},{25,17},{2,10},{10... | collective-permute-start | bytes 786440 | tf_op jit(solution)/shard_map/ppermute | solution.py:39
  120.0 8.0 %collective-permute-start.23 = (f32[256,256]{1,0:T(8,128)S(1)}, f32[256,256]{1,0:T(8,128)S(1)}, u32[]{:S(2)}, u32[]{:S(2)}) collective-permute-start(f32[256,256]{1,0:T(8,128)S(1)} %copy-done.19), channel_id=1, source_target_pairs={{0,16},{8,24},{16,0},{24,8},{1,17},{9,25},{17,1},{25,9},{2,18},{10... | collective-permute-start | bytes 786440 | tf_op jit(solution)/shard_map/ppermute | solution.py:39
  120.3 11.7 %collective-permute-start.24 = (f32[256,256]{1,0:T(8,128)S(1)}, f32[256,256]{1,0:T(8,128)S(1)}, u32[]{:S(2)}, u32[]{:S(2)}) collective-permute-start(f32[256,256]{1,0:T(8,128)S(1)} %get-tuple-element.161), channel_id=1, source_target_pairs={{0,24},{8,16},{16,8},{24,0},{1,25},{9,17},{17,9},{25,1},{2,26},{10... | collective-permute-start | bytes 786440 | tf_op jit(solution)/shard_map/ppermute | solution.py:39
  122.0 15.7 %collective-permute-start.20 = (f32[256,256]{1,0:T(8,128)S(1)}, f32[256,256]{1,0:T(8,128)}, u32[]{:S(2)}, u32[]{:S(2)}) collective-permute-start(f32[256,256]{1,0:T(8,128)S(1)} %copy-done.27), channel_id=1, source_target_pairs={{0,8},{8,0},{16,24},{24,16},{1,9},{9,1},{17,25},{25,17},{2,10},{10... | collective-permute-start | bytes 786440 | tf_op jit(solution)/shard_map/ppermute | solution.py:39
  123.3 16.1 %collective-permute-start.21 = (f32[256,256]{1,0:T(8,128)S(1)}, f32[256,256]{1,0:T(8,128)}, u32[]{:S(2)}, u32[]{:S(2)}) collective-permute-start(f32[256,256]{1,0:T(8,128)S(1)} %copy-done.25), channel_id=1, source_target_pairs={{0,16},{8,24},{16,0},{24,8},{1,17},{9,25},{17,1},{25,9},{2,18},{10... | collective-permute-start | bytes 786440 | tf_op jit(solution)/shard_map/ppermute | solution.py:39
  132.0 10.8 %collective-permute-start.25 = (f32[256,256]{1,0:T(8,128)S(1)}, f32[256,256]{1,0:T(8,128)S(1)}, u32[]{:S(2)}, u32[]{:S(2)}) collective-permute-start(f32[256,256]{1,0:T(8,128)S(1)} %copy-done.23), channel_id=1, source_target_pairs={{0,24},{8,16},{16,8},{24,0},{1,25},{9,17},{17,9},{25,1},{2,26},{10... | collective-permute-start | bytes 786440 | tf_op jit(solution)/shard_map/ppermute | solution.py:39
  142.8 11.7 %collective-permute-start.26 = (bf16[8,128,256]{2,1,0:T(8,128)(2,1)}, bf16[8,128,256]{2,1,0:T(8,128)(2,1)S(1)}, u32[]{:S(2)}, u32[]{:S(2)}) collective-permute-start(bf16[8,128,256]{2,1,0:T(8,128)(2,1)} %get-tuple-element.175), channel_id=1, source_target_pairs={{0,8},{8,0},{16,24},{24,16},{1,9},{9,1},{17,25},{25,17},{2,10},{10... | collective-permute-start | bytes 1572872 | tf_op jit(solution)/shard_map/ppermute | solution.py:39
  144.5 11.9 %collective-permute-start.27 = (bf16[8,128,256]{2,1,0:T(8,128)(2,1)}, bf16[8,128,256]{2,1,0:T(8,128)(2,1)S(1)}, u32[]{:S(2)}, u32[]{:S(2)}) collective-permute-start(bf16[8,128,256]{2,1,0:T(8,128)(2,1)} %get-tuple-element.176), channel_id=1, source_target_pairs={{0,16},{8,24},{16,0},{24,8},{1,17},{9,25},{17,1},{25,9},{2,18},{10... | collective-permute-start | bytes 1572872 | tf_op jit(solution)/shard_map/ppermute | solution.py:39
  156.4 26.2 %collective-permute-start.32 = (bf16[8,128,256]{2,1,0:T(8,128)(2,1)}, bf16[8,128,256]{2,1,0:T(8,128)(2,1)S(1)}, u32[]{:S(2)}, u32[]{:S(2)}) collective-permute-start(bf16[8,128,256]{2,1,0:T(8,128)(2,1)} %get-tuple-element.193), channel_id=1, source_target_pairs={{0,24},{8,16},{16,8},{24,0},{1,25},{9,17},{17,9},{25,1},{2,26},{10... | collective-permute-start | bytes 1572872 | tf_op jit(solution)/shard_map/ppermute | solution.py:39
  160.2 18.8 %collective-permute-start.31 = (bf16[512,256]{1,0:T(8,128)(2,1)}, bf16[512,256]{1,0:T(8,128)(2,1)S(1)}, u32[]{:S(2)}, u32[]{:S(2)}) collective-permute-start(bf16[512,256]{1,0:T(8,128)(2,1)} %shard_map.103.refs_0_), channel_id=1, source_target_pairs={{0,6},{1,7},{2,4},{3,5},{4,2},{5,3},{6,0},{7,1},{8,14},{9,15},{10,... | collective-permute-start | bytes 786440 | tf_op jit(solution)/shard_map/ppermute | solution.py:39
  161.4 21.3 %collective-permute-start.30 = (bf16[512,256]{1,0:T(8,128)(2,1)}, bf16[512,256]{1,0:T(8,128)(2,1)S(1)}, u32[]{:S(2)}, u32[]{:S(2)}) collective-permute-start(bf16[512,256]{1,0:T(8,128)(2,1)} %shard_map.103.refs_0_), channel_id=1, source_target_pairs={{0,4},{1,5},{2,6},{3,7},{4,0},{5,1},{6,2},{7,3},{8,12},{9,13},{10,... | collective-permute-start | bytes 786440 | tf_op jit(solution)/shard_map/ppermute | solution.py:39
  162.5 20.2 %collective-permute-start.29 = (bf16[512,256]{1,0:T(8,128)(2,1)}, bf16[512,256]{1,0:T(8,128)(2,1)S(1)}, u32[]{:S(2)}, u32[]{:S(2)}) collective-permute-start(bf16[512,256]{1,0:T(8,128)(2,1)} %shard_map.103.refs_0_), channel_id=1, source_target_pairs={{0,2},{1,3},{2,0},{3,1},{4,6},{5,7},{6,4},{7,5},{8,10},{9,11},{10,... | collective-permute-start | bytes 786440 | tf_op jit(solution)/shard_map/ppermute | solution.py:39
  167.4 22.2 %collective-permute-start.28 = (bf16[8,128,256]{2,1,0:T(8,128)(2,1)}, bf16[8,128,256]{2,1,0:T(8,128)(2,1)S(1)}, u32[]{:S(2)}, u32[]{:S(2)}) collective-permute-start(bf16[8,128,256]{2,1,0:T(8,128)(2,1)} %get-tuple-element.179), channel_id=1, source_target_pairs={{0,8},{8,0},{16,24},{24,16},{1,9},{9,1},{17,25},{25,17},{2,10},{10... | collective-permute-start | bytes 1572872 | tf_op jit(solution)/shard_map/ppermute | solution.py:39
  186.6 11.3 %collective-permute-start.35 = (bf16[2,4,128,256]{3,2,1,0:T(8,128)(2,1)}, bf16[2,4,128,256]{3,2,1,0:T(8,128)(2,1)S(1)}, u32[]{:S(2)}, u32[]{:S(2)}) collective-permute-start(bf16[2,4,128,256]{3,2,1,0:T(8,128)(2,1)} %get-tuple-element.204), channel_id=1, source_target_pairs={{0,8},{8,0},{16,24},{24,16},{1,9},{9,1},{17,25},{25,17},{2,10},{10... | collective-permute-start | bytes 1572872 | tf_op jit(solution)/shard_map/ppermute | solution.py:39
  187.8 11.8 %collective-permute-start.36 = (bf16[2,4,128,256]{3,2,1,0:T(8,128)(2,1)}, bf16[2,4,128,256]{3,2,1,0:T(8,128)(2,1)S(1)}, u32[]{:S(2)}, u32[]{:S(2)}) collective-permute-start(bf16[2,4,128,256]{3,2,1,0:T(8,128)(2,1)} %get-tuple-element.205), channel_id=1, source_target_pairs={{0,16},{8,24},{16,0},{24,8},{1,17},{9,25},{17,1},{25,9},{2,18},{10... | collective-permute-start | bytes 1572872 | tf_op jit(solution)/shard_map/ppermute | solution.py:39
  187.9 21.3 %collective-permute-start.37 = (bf16[2,4,128,256]{3,2,1,0:T(8,128)(2,1)}, bf16[2,4,128,256]{3,2,1,0:T(8,128)(2,1)S(1)}, u32[]{:S(2)}, u32[]{:S(2)}) collective-permute-start(bf16[2,4,128,256]{3,2,1,0:T(8,128)(2,1)} %get-tuple-element.206), channel_id=1, source_target_pairs={{0,24},{8,16},{16,8},{24,0},{1,25},{9,17},{17,9},{25,1},{2,26},{10... | collective-permute-start | bytes 1572872 | tf_op jit(solution)/shard_map/ppermute | solution.py:39
  189.3 43.2 %collective-permute-start.33 = (bf16[8,128,256]{2,1,0:T(8,128)(2,1)}, bf16[8,128,256]{2,1,0:T(8,128)(2,1)S(1)}, u32[]{:S(2)}, u32[]{:S(2)}) collective-permute-start(bf16[8,128,256]{2,1,0:T(8,128)(2,1)} %get-tuple-element.196), channel_id=1, source_target_pairs={{0,16},{8,24},{16,0},{24,8},{1,17},{9,25},{17,1},{25,9},{2,18},{10... | collective-permute-start | bytes 1572872 | tf_op jit(solution)/shard_map/ppermute | solution.py:39
  189.6 46.5 %collective-permute-start.34 = (bf16[8,128,256]{2,1,0:T(8,128)(2,1)}, bf16[8,128,256]{2,1,0:T(8,128)(2,1)S(1)}, u32[]{:S(2)}, u32[]{:S(2)}) collective-permute-start(bf16[8,128,256]{2,1,0:T(8,128)(2,1)} %get-tuple-element.197), channel_id=1, source_target_pairs={{0,24},{8,16},{16,8},{24,0},{1,25},{9,17},{17,9},{25,1},{2,26},{10... | collective-permute-start | bytes 1572872 | tf_op jit(solution)/shard_map/ppermute | solution.py:39
  209.2 26.9 %collective-permute-start.38 = (bf16[2,4,128,256]{3,2,1,0:T(8,128)(2,1)}, bf16[2,4,128,256]{3,2,1,0:T(8,128)(2,1)S(1)}, u32[]{:S(2)}, u32[]{:S(2)}) collective-permute-start(bf16[2,4,128,256]{3,2,1,0:T(8,128)(2,1)} %get-tuple-element.207.refs_4_), channel_id=1, source_target_pairs={{0,1},{1,0},{2,3},{3,2},{4,5},{5,4},{6,7},{7,6},{8,9},{9,8},{10,11... | collective-permute-start | bytes 1572872 | tf_op jit(solution)/shard_map/ppermute | solution.py:39
  228.0 8.1 %collective-permute-start.39 = (bf16[2,4,128,256]{3,2,1,0:T(8,128)(2,1)S(1)}, bf16[2,4,128,256]{3,2,1,0:T(8,128)(2,1)S(1)}, u32[]{:S(2)}, u32[]{:S(2)}) collective-permute-start(bf16[2,4,128,256]{3,2,1,0:T(8,128)(2,1)S(1)} %collective-permute-done.35.refs_5_), channel_id=1, source_target_pairs={{0,1},{1,0},{2,3},{3,2},{4,5},{5,4},{6,7},{7,6},{8,9},{9,8},{10,11... | collective-permute-start | bytes 1572872 | tf_op jit(solution)/shard_map/ppermute | solution.py:39
  228.0 8.1 %collective-permute-start.40 = (bf16[2,4,128,256]{3,2,1,0:T(8,128)(2,1)S(1)}, bf16[2,4,128,256]{3,2,1,0:T(8,128)(2,1)S(1)}, u32[]{:S(2)}, u32[]{:S(2)}) collective-permute-start(bf16[2,4,128,256]{3,2,1,0:T(8,128)(2,1)S(1)} %collective-permute-done.36.refs_6_), channel_id=1, source_target_pairs={{0,1},{1,0},{2,3},{3,2},{4,5},{5,4},{6,7},{7,6},{8,9},{9,8},{10,11... | collective-permute-start | bytes 1572872 | tf_op jit(solution)/shard_map/ppermute | solution.py:39
  (48 other events, 300.4 us)

commit v7 on v1

v7 whole, which is shorter than its diff:
```python
import functools
import math

import jax
import jax.numpy as jnp
from jax import lax
from jax.experimental import pallas as pl
from jax.experimental.pallas import tpu as pltpu
from jax.sharding import PartitionSpec as P

EMB = 256
EXPERTS = 32
CAP = 16
SCALE = 1.0 / math.sqrt(EMB)
EXTRA = 16
DIGIT = 128
MIB = 1 << 20

F32 = jnp.float32
BF16 = jnp.bfloat16
CORES = 2
SCALARS = pl.BlockSpec(memory_space=pltpu.SMEM)
WHOLE = pl.BlockSpec(memory_space=pltpu.VMEM)
ANYWHERE = pl.BlockSpec(memory_space=pl.ANY)
SMALL = pl.CostEstimate(flops=1024, bytes_accessed=1024, transcendentals=0)


def mm(a, b, ca, cb):
    return lax.dot_general(a, b, (((ca,), (cb,)), ((), ())), preferred_element_type=F32)


def number(rows, index):
    rows = rows.astype(F32)
    high = rows[2 * index : 2 * index + 1]
    return (high * DIGIT + rows[2 * index + 1 : 2 * index + 2]).astype(jnp.int32)


def swap(piece, axis, bits):
    size = lax.axis_size(axis)
    return lax.ppermute(piece, axis, [(j, j ^ bits) for j in range(size)])


def exchange(pieces, axis, unit=1):
    return [piece if k == 0 else swap(piece, axis, k * unit) for k, piece in enumerate(pieces)]


def pack_kernel(emb_ref, positive_ref, user_ref, item_ref, out_ref, target_ref):
    rows = emb_ref.shape[0]
    down = lax.broadcasted_iota(jnp.int32, (rows, rows), 0)
    across = lax.broadcasted_iota(jnp.int32, (rows, rows), 1)

    def slots(expert):
        wide = jnp.broadcast_to(expert.astype(F32), (rows, rows))
        before = jnp.where((wide == wide.T) & (down < across), 1.0, 0.0)
        return expert * CAP + jnp.sum(before, axis=0, keepdims=True).astype(jnp.int32)

    user = slots(user_ref[...])
    item = slots(item_ref[...])
    target_ref[0:1, :] = user
    target_ref[1:2, :] = item
    line = lax.broadcasted_iota(jnp.int32, (EXTRA, rows), 0)
    block = jnp.zeros((EXTRA, rows), jnp.int32)
    for index, values in enumerate((positive_ref[...], user, item)):
        block = jnp.where(line == 2 * index, values // DIGIT, block)
        block = jnp.where(line == 2 * index + 1, values % DIGIT, block)
    out_ref[:rows, :] = emb_ref[...]
    out_ref[rows:, :] = block.astype(F32).astype(BF16)


def pack(emb, positive, user_expert, item_expert):
    rows, width = emb.shape
    return pl.pallas_call(
        pack_kernel,
        out_shape=[
            jax.ShapeDtypeStruct((rows + EXTRA, width), BF16),
            jax.ShapeDtypeStruct((2, rows), jnp.int32),
        ],
        cost_estimate=SMALL,
    )(emb, positive.reshape(1, rows), user_expert.reshape(1, rows), item_expert.reshape(1, rows))


def stats_kernel(first_ref, users_ref, *refs, rows, chunk):
    *items_refs, _, out_ref, s_ref = refs
    own = items_refs[0].shape[0]
    n_cols = own * len(items_refs)
    for half in range(users_ref.shape[0]):
        queries = users_ref[half, :rows, :] * jnp.asarray(SCALE, BF16)
        for k, items_ref in enumerate(items_refs):
            s_ref[half, k * own : (k + 1) * own, :] = mm(items_ref[...], queries, 1, 1)
        positive = number(users_ref[half, rows:, :], 0)
        tops = jnp.full((8, rows), -jnp.inf, F32)
        for c in range(0, n_cols, chunk):
            part = s_ref[half, c : c + chunk, :]
            tops = jnp.maximum(tops, jnp.max(part.reshape(chunk // 8, 8, rows), axis=0))
        top = jnp.max(tops, axis=0, keepdims=True)
        total = jnp.zeros((8, rows), F32)
        picked = jnp.zeros((8, rows), F32)
        for c in range(0, n_cols, chunk):
            part = s_ref[half, c : c + chunk, :]
            probs = jnp.exp(part - top)
            total = total + jnp.sum(probs.reshape(chunk // 8, 8, rows), axis=0)
            wanted = positive - (first_ref[c // own] + c % own)
            hit = lax.broadcasted_iota(jnp.int32, (chunk, rows), 0) == wanted
            chosen = jnp.where(hit, part, 0.0)
            picked = picked + jnp.sum(chosen.reshape(chunk // 8, 8, rows), axis=0)
        here = pl.ds(half * rows, rows)
        out_ref[0:1, here] = top
        out_ref[1:2, here] = jnp.sum(total, axis=0, keepdims=True)
        out_ref[2:3, here] = jnp.sum(picked, axis=0, keepdims=True)


def stats(first, users, items, rows, after):
    blocks, height, emb = users.shape
    own = items[0].shape[0]
    n_cols = own * len(items)
    pair = 2
    return pl.pallas_call(
        functools.partial(stats_kernel, rows=rows, chunk=64),
        grid=(blocks // pair,),
        in_specs=[SCALARS, pl.BlockSpec((pair, height, emb), lambda b: (b, 0, 0))]
        + [pl.BlockSpec((own, emb), lambda b: (0, 0))] * len(items)
        + [ANYWHERE],
        out_specs=pl.BlockSpec((3, pair * rows), lambda b: (0, b)),
        out_shape=jax.ShapeDtypeStruct((3, blocks * rows), F32),
        scratch_shapes=[pltpu.VMEM((pair, n_cols, rows), F32)],
        compiler_params=pltpu.CompilerParams(vmem_limit_bytes=40 * MIB),
        cost_estimate=SMALL,
    )(first, users, *items, after)


def grad_kernel(first_ref, users_ref, *refs, rows, chunk, count, groups):
    stats_refs, refs = refs[:groups], refs[groups:]
    items_refs, refs = refs[:count], refs[count + 1 :]
    loss_ref, user_ref = refs[:2]
    part_refs = refs[2 : count + 2]
    s_ref, g_ref, flip_ref = refs[count + 2 :]
    own = items_refs[0].shape[0]
    n_cols = own * count
    step = pl.program_id(0)

    @pl.when(step == 0)
    def _():
        for k in range(count):
            flip_ref[:, k * own : (k + 1) * own] = items_refs[k][...].T
            part_refs[k][...] = jnp.zeros_like(part_refs[k])

    for half in range(users_ref.shape[0]):
        here = pl.ds(half * rows, rows)
        queries = users_ref[half, :rows, :]
        scaled = queries * jnp.asarray(SCALE, BF16)
        for k in range(count):
            s_ref[half, k * own : (k + 1) * own, :] = mm(items_refs[k][...], scaled, 1, 1)
        positive = number(users_ref[half, rows:, :], 0)
        top = functools.reduce(jnp.maximum, [ref[0:1, here] for ref in stats_refs])
        total = sum(ref[1:2, here] * jnp.exp(ref[0:1, here] - top) for ref in stats_refs)
        level = top + jnp.log(total)
        loss_ref[0:1, here] = level - sum(ref[2:3, here] for ref in stats_refs)
        for c in range(0, n_cols, chunk):
            probs = jnp.exp(s_ref[half, c : c + chunk, :] - level)
            wanted = positive - (first_ref[c // own] + c % own)
            hit = lax.broadcasted_iota(jnp.int32, (chunk, rows), 0) == wanted
            g_ref[half, c : c + chunk, :] = jnp.where(hit, probs - 1.0, probs).astype(BF16)
        for k in range(count):
            part_refs[k][...] += mm(g_ref[half, k * own : (k + 1) * own, :], queries, 1, 0)
        user_ref[here, :] = mm(flip_ref[...], g_ref[half], 1, 0).T * SCALE

    @pl.when(step == pl.num_programs(0) - 1)
    def _():
        for k in range(count):
            part_refs[k][...] = part_refs[k][...] * SCALE


def grads(first, users, items, gathered, rows, after):
    blocks, height, emb = users.shape
    count = len(items)
    own = items[0].shape[0]
    n_cols = own * count
    pair = 2
    groups = len(gathered)
    results = pl.pallas_call(
        functools.partial(grad_kernel, rows=rows, chunk=64, count=count, groups=groups),
        grid=(blocks // pair,),
        in_specs=[
            SCALARS,
            pl.BlockSpec((pair, height, emb), lambda b: (b, 0, 0)),
        ]
        + [pl.BlockSpec((3, pair * rows), lambda b: (0, b))] * groups
        + [pl.BlockSpec((own, emb), lambda b: (0, 0))] * count
        + [ANYWHERE],
        out_specs=[
            pl.BlockSpec((1, pair * rows), lambda b: (0, b)),
            pl.BlockSpec((pair * rows, emb), lambda b: (b, 0)),
        ]
        + [pl.BlockSpec((own, emb), lambda b: (0, 0))] * count,
        out_shape=[
            jax.ShapeDtypeStruct((1, blocks * rows), F32),
            jax.ShapeDtypeStruct((blocks * rows, emb), F32),
        ]
        + [jax.ShapeDtypeStruct((own, emb), F32)] * count,
        scratch_shapes=[
            pltpu.VMEM((pair, n_cols, rows), F32),
            pltpu.VMEM((pair, n_cols, rows), BF16),
            pltpu.VMEM((emb, n_cols), BF16),
        ],
        compiler_params=pltpu.CompilerParams(vmem_limit_bytes=48 * MIB),
        cost_estimate=SMALL,
    )(first, users, *gathered, *items, after)
    return results[0], results[1], results[2:]


def cut_kernel(user_ref, item_ref, _, out_ref):
    rows = user_ref.shape[0]
    width = out_ref.shape[2]
    for k in range(out_ref.shape[0]):
        out_ref[k, :rows, :] = user_ref[:, k * width : (k + 1) * width]
        out_ref[k, rows:, :] = item_ref[:, k * width : (k + 1) * width]


def cut(user_hidden, item_hidden, parts, after):
    rows, total = user_hidden.shape
    return pl.pallas_call(
        cut_kernel,
        in_specs=[WHOLE] * 2 + [ANYWHERE],
        out_specs=WHOLE,
        out_shape=jax.ShapeDtypeStruct((parts, 2 * rows, total // parts), BF16),
        compiler_params=pltpu.CompilerParams(vmem_limit_bytes=24 * MIB),
        cost_estimate=SMALL,
    )(user_hidden, item_hidden, after)


def onehot_of(target, me, groups):
    span = EXPERTS * CAP // groups
    place = lax.broadcasted_iota(jnp.int32, (EXPERTS * CAP, target.shape[1]), 0)
    place = (((place // span) ^ me) * span) + place % span
    return (place == target).astype(F32).astype(BF16)


def hidden_kernel(me_ref, users_ref, hidden_ref, _, *out_refs):
    rows = users_ref.shape[2]
    _, pair, span, _ = out_refs[0].shape
    for half in range(pair):
        for tower in range(2):
            onehot = onehot_of(number(users_ref[half], 1 + tower), me_ref[0], len(out_refs))
            values = hidden_ref[half, tower * rows : (tower + 1) * rows, :]
            moved = mm(onehot, values, 1, 0).astype(BF16)
            for k, out_ref in enumerate(out_refs):
                out_ref[tower, half] = moved[k * span : (k + 1) * span, :]


def slot_hidden(me, users, hidden, groups, after):
    blocks, height, rows = users.shape
    width = hidden.shape[2]
    span = EXPERTS * CAP // groups
    pair = 2
    return pl.pallas_call(
        hidden_kernel,
        grid=(blocks // pair,),
        in_specs=[
            SCALARS,
            pl.BlockSpec((pair, EXTRA, rows), lambda b: (b, rows // EXTRA, 0)),
            pl.BlockSpec((pair, 2 * rows, width), lambda b: (b, 0, 0)),
            ANYWHERE,
        ],
        out_specs=[pl.BlockSpec((2, pair, span, width), lambda b: (0, b, 0, 0))] * groups,
        out_shape=[jax.ShapeDtypeStruct((2, blocks, span, width), BF16)] * groups,
        cost_estimate=SMALL,
    )(me, users, hidden, after)


def route_kernel(me_ref, target_ref, *refs, tower, count):
    total = refs[0][...]
    for ref in refs[1:count]:
        total = total + ref[...]
    low = total.astype(BF16)
    out_refs = refs[count + 1 :]
    span = out_refs[0].shape[0]
    onehot = onehot_of(target_ref[tower : tower + 1, :], me_ref[0], len(out_refs))
    moved = mm(onehot, low, 1, 0).astype(BF16)
    for k, out_ref in enumerate(out_refs):
        out_ref[...] = moved[k * span : (k + 1) * span, :]


def route(me, targets, pieces, tower, groups, after):
    rows, emb = pieces[0].shape
    span = EXPERTS * CAP // groups
    return pl.pallas_call(
        functools.partial(route_kernel, tower=tower, count=len(pieces)),
        in_specs=[SCALARS] + [WHOLE] * (1 + len(pieces)) + [ANYWHERE],
        out_specs=[WHOLE] * groups,
        out_shape=[jax.ShapeDtypeStruct((span, emb), BF16)] * groups,
        cost_estimate=SMALL,
    )(me, targets, *pieces, after)


def outer_kernel(order_ref, *refs, groups):
    hidden_refs, grad_refs, out_ref = refs[:groups], refs[groups:-1], refs[-1]
    _, blocks, span, width = hidden_refs[0].shape
    for e in range(span // CAP):
        here = slice(e * CAP, (e + 1) * CAP)
        left, right = [], []
        for j in range(blocks):
            for k, hidden_ref in enumerate(hidden_refs):
                if len(grad_refs) == 1:
                    left.append(hidden_ref[0, j, here, :])
                    right.append(grad_refs[0][j, k, here, :])
                else:
                    left.append(hidden_ref[0, order_ref[j], here, :])
                    right.append(grad_refs[j][k, here, :])
        out_ref[e] = mm(jnp.concatenate(left), jnp.concatenate(right), 0, 0)


def outer(order, hidden, grads, tower):
    _, blocks, span, width = hidden[0].shape
    emb = grads[0].shape[-1]
    own = span // CAP
    return pl.pallas_call(
        functools.partial(outer_kernel, groups=len(hidden)),
        grid=(1,),
        in_specs=[SCALARS]
        + [pl.BlockSpec((1, blocks, span, width), lambda _: (tower, 0, 0, 0))] * len(hidden)
        + [pl.BlockSpec(g.shape, lambda _, d=g.ndim: (0,) * d) for g in grads],
        out_specs=pl.BlockSpec((own, width, emb), lambda _: (0, 0, 0)),
        out_shape=jax.ShapeDtypeStruct((own, width, emb), F32),
        compiler_params=pltpu.CompilerParams(vmem_limit_bytes=40 * MIB),
        cost_estimate=SMALL,
    )(order, *hidden, *grads)


def shards(user_emb, item_emb, user_hidden, item_hidden, user_expert, item_expert, positive):
    rows, emb = user_emb.shape
    groups = lax.axis_size("user")
    parts = lax.axis_size("item")
    width = user_hidden.shape[1] // parts
    lines = parts // CORES
    me = lax.axis_index("user").astype(jnp.int32)
    part = lax.axis_index("item").astype(jnp.int32)
    others = me ^ jnp.arange(groups, dtype=jnp.int32)
    both = part ^ jnp.arange(CORES, dtype=jnp.int32)
    order = (both[:, None] ^ (CORES * jnp.arange(lines, dtype=jnp.int32))[None, :]).reshape(-1)
    first = (part * groups + others) * rows
    me = me.reshape(1)

    packed, targets = pack(user_emb, positive, user_expert, item_expert)
    users = lax.all_gather(packed, "item", axis=0)
    items = exchange([item_emb] * groups, "user")
    cols = lax.all_to_all(
        cut(user_hidden, item_hidden, parts, packed), "item", split_axis=0, concat_axis=0, tiled=True
    )

    gathered = exchange([stats(first, users, items, rows, packed)] * parts, "item")
    losses, user_part, item_parts = grads(first, users, items, gathered, rows, cols)
    row_loss = lax.dynamic_slice_in_dim(losses[0], part * rows, rows)
    user_grad = lax.psum_scatter(user_part, "item", scatter_dimension=0, tiled=True)
    item_pieces = exchange(item_parts, "user")

    item_routed = route(me, targets, item_pieces, 1, groups, packed)
    hidden_rows = exchange(slot_hidden(me, users, cols, groups, item_routed[0]), "user")
    item_sent = jnp.stack(exchange(item_routed, "user"))
    user_routed = route(me, targets, [user_grad], 0, groups, item_sent)
    user_sent = jnp.stack(exchange(user_routed, "user"))
    item_line = exchange([item_sent] * lines, "item", CORES)
    item_cross = item_line + [swap(piece, "item", 1) for piece in item_line]
    user_all = lax.all_gather(user_sent, "item", axis=0)
    item_weight_grad = outer(order, hidden_rows, item_cross, 1)
    user_weight_grad = outer(order, hidden_rows, [user_all], 0)
    return (row_loss, user_weight_grad, item_weight_grad)


def solution(mesh):
    placed = (
        P(("user", "item"), None),
        P(("item", "user"), None),
        P(("user", "item"), None),
        P(("item", "user"), None),
        P(("user", "item"), None),
        P(("item", "user"), None),
        P(("user", "item")),
    )
    return jax.shard_map(
        shards,
        mesh=mesh,
        in_specs=placed,
        out_specs=(P(("user", "item")), P("user", "item", None), P("user", "item", None)),
        check_vma=False,
    )
```

time: 209 us -> 208 us (level)
  the two profiles are of different devices: /device:TPU:0 before, /device:TPU:11 now
where the time goes in v7:
time: 208 us; the launch traced here: 207 us
  waiting for transfers between devices  106 us (51%)
  starting transfers between devices  38.6 us (19%)
  Pallas kernels  29.5 us (14%)
  local copies, waits for them, and re-layouts  15.6 us (8%)
  between operations  13.8 us (7%)
  other arithmetic  3.28 us (2%)
    ppermute x29, waiting for transfers between devices, swap(): return lax.ppermute(piece, axis, [(j, j ^ bits) for j in range(size)])  75.4 us
    ppermute x29, starting transfers between devices, swap(): return lax.ppermute(piece, axis, [(j, j ^ bits) for j in range(size)])  32.8 us
    all_gather x1, waiting for transfers between devices, shards(): users = lax.all_gather(packed, 'item', axis=0)  24.9 us
    unnamed x44, local copies, waits for them, and re-layouts  14.9 us
    pallas_call x1, Pallas kernels, grads(): pl.pallas_call(functools.partial(grad_kernel, rows=rows, chunk=64, count=...  7.02 us
    pallas_call x2, Pallas kernels, outer(): pl.pallas_call(functools.partial(outer_kernel, groups=len(hidden)), grid=...  6.1 us
    all_to_all x1, starting transfers between devices, shards(): lax.all_to_all(cut(user_hidden, item_hidden, parts, packed), 'item', spli...  5.77 us
    reduce_scatter x1, waiting for transfers between devices, shards(): lax.psum_scatter(user_part, 'item', scatter_dimension=0, tiled=True)  5.2 us
  transfers between devices with their start and end apart: 33, of which 20 were waited for; matrix products, arithmetic and copies ran while one was open for 1% of the time, Pallas kernels for 7%

profile of v7, /device:TPU:11, one launch (start us, length us, event | category | flops | bytes accessed | tf_op | source)
XLA Modules:
  0.0 207.1 jit_solution(14889662124559432392)
XLA Ops:
  7.2 1.7 shard_map.94
  12.3 1.5 shard_map.96
  13.8 5.8 %all-to-all-start = ((bf16[8,512,256]{2,1,0:T(8,128)(2,1)}), bf16[8,512,256]{2,1,0:T(8,128)(2,1)}, u32[]{:S(2)}, u32[]{:S(2)}) async-start(bf16[8,512,256]{2,1,0:T(8,128)(2,1)} %shard_map.96), calls=%async_computation | async-start | bytes 4194304 | tf_op jit(solution)/shard_map/all_to_all | solution.py:346
  23.0 2.2 %collective-permute-done.refs_1_.refs_9_ = bf16[256,256]{1,0:T(8,128)(2,1)S(1)} collective-permute-done((bf16[256,256]{1,0:T(8,128)(2,1)S(1)}, bf16[256,256]{1,0:T(8,128)(2,1)S(1)}, u32[]{:S(2)}, u32[]{:S(2)}) %collective-permute-start) | collective-permute-done | bytes 131104 | tf_op jit(solution)/shard_map/ppermute | solution.py:40
  25.2 3.7 %collective-permute-done.2.refs_3_.refs_11_ = bf16[256,256]{1,0:T(8,128)(2,1)S(1)} collective-permute-done((bf16[256,256]{1,0:T(8,128)(2,1)S(1)}, bf16[256,256]{1,0:T(8,128)(2,1)S(1)}, u32[]{:S(2)}, u32[]{:S(2)}) %collective-permute-start.2) | collective-permute-done | bytes 131104 | tf_op jit(solution)/shard_map/ppermute | solution.py:40
  28.9 24.9 %all-gather.5.cloned.1.call-done = bf16[2176,256]{1,0:T(8,128)(2,1)} async-done(((bf16[272,256]{1,0:T(8,128)(2,1)}), bf16[2176,256]{1,0:T(8,128)(2,1)}) %all-gather.5.cloned.1.call-update) | async-done | bytes 1114128 | tf_op jit(solution)/shard_map/all_gather | solution.py:344
  55.0 4.1 %shard_map.95.refs_0_ = f32[3,2048]{1,0:T(4,128)S(1)} custom-call(s32[4]{0:T(128)S(1)} %add_multiply_fusion.first_ref, bf16[8,272,256]{2,1,0:T(8,128)(2,1)S(1)} %bitcast.16, bf16[256,256]{1,0:T(8,128)(2,1)S(1)} %copy-done.13, bf16[256,256]{1,0:T(8,128)(2,1)S(1)} %collective-permute-done.refs_1_.refs_9_, ...), custom_call_target="tpu_custom_call" | custom-call | flops 1024 | bytes 1024 | tf_op jit(solution)/shard_map/pallas_call | solution.py:117
  59.9 1.5 collective-permute-start.5
  61.4 2.7 %collective-permute-start.6 = (f32[3,2048]{1,0:T(4,128)S(1)}, f32[3,2048]{1,0:T(4,128)S(1)}, u32[]{:S(2)}, u32[]{:S(2)}) collective-permute-start(f32[3,2048]{1,0:T(4,128)S(1)} %shard_map.95.refs_0_), channel_id=1, source_target_pairs={{0,4},{1,5},{2,6},{3,7},{4,0},{5,1},{6,2},{7,3},{8,12},{9,13},{10,... | collective-permute-start | bytes 73736 | tf_op jit(solution)/shard_map/ppermute | solution.py:40
  64.1 1.5 collective-permute-start.8
  65.6 1.9 collective-permute-start.9
  67.5 9.9 %collective-permute-done.6.refs_4_ = f32[3,2048]{1,0:T(4,128)S(1)} collective-permute-done((f32[3,2048]{1,0:T(4,128)S(1)}, f32[3,2048]{1,0:T(4,128)S(1)}, u32[]{:S(2)}, u32[]{:S(2)}) %collective-permute-start.6) | collective-permute-done | bytes 24608 | tf_op jit(solution)/shard_map/ppermute | solution.py:40
  78.1 2.1 %collective-permute-done.8.refs_6_ = f32[3,2048]{1,0:T(4,128)S(1)} collective-permute-done((f32[3,2048]{1,0:T(4,128)S(1)}, f32[3,2048]{1,0:T(4,128)S(1)}, u32[]{:S(2)}, u32[]{:S(2)}) %collective-permute-start.8) | collective-permute-done | bytes 24608 | tf_op jit(solution)/shard_map/ppermute | solution.py:40
  81.4 7.0 %shard_map.97 = (f32[1,2048]{1,0:T(1,128)S(1)}, f32[2048,256]{1,0:T(8,128)}, f32[256,256]{1,0:T(8,128)S(1)}, f32[256,256]{1,0:T(8,128)S(1)}, f32[256,256]{1,0:T(8,128)S(1)}, /*index=5*/f32[256,256]{1,0:T(8,128)S(1)}) custom-call(s32[4]{0:T(128)S(1)} %add_multiply_fusion.first_ref, bf16[8,272,256]{2,1,0:T(8,128)(2,1)S(1)} %bitcast.17, ...), custom_call_target="tpu_custom_call" | custom-call | flops 1024 | bytes 1024 | tf_op jit(solution)/shard_map/pallas_call | solution.py:180
  91.9 5.0 %collective-permute-done.10.refs_1_ = f32[256,256]{1,0:T(8,128)S(1)} collective-permute-done((f32[256,256]{1,0:T(8,128)S(1)}, f32[256,256]{1,0:T(8,128)S(1)}, u32[]{:S(2)}, u32[]{:S(2)}) %collective-permute-start.10) | collective-permute-done | bytes 262176 | tf_op jit(solution)/shard_map/ppermute | solution.py:40
  96.9 6.5 %collective-permute-done.12.refs_3_ = f32[256,256]{1,0:T(8,128)S(1)} collective-permute-done((f32[256,256]{1,0:T(8,128)S(1)}, f32[256,256]{1,0:T(8,128)S(1)}, u32[]{:S(2)}, u32[]{:S(2)}) %collective-permute-start.12) | collective-permute-done | bytes 262176 | tf_op jit(solution)/shard_map/ppermute | solution.py:40
  104.1 2.1 %shard_map.98 = (bf16[128,256]{1,0:T(8,128)(2,1)}, bf16[128,256]{1,0:T(8,128)(2,1)}, bf16[128,256]{1,0:T(8,128)(2,1)}, bf16[128,256]{1,0:T(8,128)(2,1)}) custom-call(s32[1]{0:T(128)} %bitcast.5.me_ref, s32[2,256]{1,0:T(2,128)} %get-tuple-element.25.target_ref, f32[256,256]{1,0:T(8,128)} %copy-done.18, f32[256,256]{1,0:T(8,128)} %copy-done.19, ...), custom_call_target="tpu_custom_call" | custom-call | flops 1024 | bytes 1024 | tf_op jit(solution)/shard_map/pallas_call | solution.py:286
  108.8 1.6 collective-permute-done.18
  111.7 1.6 pad_maximum_fusion.refs_1_.refs_4_
  113.3 5.2 %reduce-scatter.2.cloned.1.call-done.refs_0_ = f32[256,256]{1,0:T(8,128)} async-done(((f32[2048,256]{1,0:T(8,128)}), f32[256,256]{1,0:T(8,128)}) %reduce-scatter.2.cloned.1.call-update) | async-done | bytes 262160 | tf_op jit(solution)/shard_map/reduce_scatter | solution.py:353
  118.5 1.9 shard_map.100
  123.0 1.6 collective-permute-done.21
  125.9 1.6 pad_maximum_fusion.1
  127.5 2.4 %collective-permute-start.22 = (bf16[4,128,256]{2,1,0:T(8,128)(2,1)}, bf16[4,128,256]{2,1,0:T(8,128)(2,1)}, u32[]{:S(2)}, u32[]{:S(2)}) collective-permute-start(bf16[4,128,256]{2,1,0:T(8,128)(2,1)} %pad_maximum_fusion.refs_1_.refs_4_), channel_id=1, source_target_pairs={{0,2},{1,3},{2,0},{3,1},{4,6},{5,7},{6,4},{7,5},{8,10},{9,11},{10,... | collective-permute-start | bytes 786440 | tf_op jit(solution)/shard_map/ppermute | solution.py:40
  129.9 5.0 %shard_map.99 = (bf16[2,8,128,256]{3,2,1,0:T(8,128)(2,1)}, bf16[2,8,128,256]{3,2,1,0:T(8,128)(2,1)}, bf16[2,8,128,256]{3,2,1,0:T(8,128)(2,1)}, bf16[2,8,128,256]{3,2,1,0:T(8,128)(2,1)}) custom-call(s32[1]{0:T(128)} %bitcast.5.me_ref, bf16[8,272,256]{2,1,0:T(8,128)(2,1)} %bitcast.15, bf16[8,512,256]{2,1,0:T(8,128)(2,1)} %all-to-all-done.refs_12_.hidden_ref, ...), custom_call_target="tpu_custom_call" | custom-call | flops 1024 | bytes 1024 | tf_op jit(solution)/shard_map/pallas_call | solution.py:255
  137.6 3.6 %collective-permute-start.23 = (bf16[4,128,256]{2,1,0:T(8,128)(2,1)S(1)}, bf16[4,128,256]{2,1,0:T(8,128)(2,1)S(1)}, u32[]{:S(2)}, u32[]{:S(2)}) collective-permute-start(bf16[4,128,256]{2,1,0:T(8,128)(2,1)S(1)} %copy-done.7), channel_id=1, source_target_pairs={{0,4},{1,5},{2,6},{3,7},{4,0},{5,1},{6,2},{7,3},{8,12},{9,13},{10,... | collective-permute-start | bytes 786440 | tf_op jit(solution)/shard_map/ppermute | solution.py:40
  141.5 27.4 %collective-permute-done.23.refs_6_ = bf16[4,128,256]{2,1,0:T(8,128)(2,1)S(1)} collective-permute-done((bf16[4,128,256]{2,1,0:T(8,128)(2,1)S(1)}, bf16[4,128,256]{2,1,0:T(8,128)(2,1)S(1)}, u32[]{:S(2)}, u32[]{:S(2)}) %collective-permute-start.23) | collective-permute-done | bytes 262176 | tf_op jit(solution)/shard_map/ppermute | solution.py:40
  168.9 3.6 %collective-permute-start.25 = (bf16[4,128,256]{2,1,0:T(8,128)(2,1)S(1)}, bf16[4,128,256]{2,1,0:T(8,128)(2,1)}, u32[]{:S(2)}, u32[]{:S(2)}) collective-permute-start(bf16[4,128,256]{2,1,0:T(8,128)(2,1)S(1)} %copy-done.7), channel_id=1, source_target_pairs={{0,1},{1,0},{2,3},{3,2},{4,5},{5,4},{6,7},{7,6},{8,9},{9,8},{10,11... | collective-permute-start | bytes 786440 | tf_op jit(solution)/shard_map/ppermute | solution.py:40
  172.5 9.0 %collective-permute-done.24.refs_7_ = bf16[4,128,256]{2,1,0:T(8,128)(2,1)S(1)} collective-permute-done((bf16[4,128,256]{2,1,0:T(8,128)(2,1)S(1)}, bf16[4,128,256]{2,1,0:T(8,128)(2,1)S(1)}, u32[]{:S(2)}, u32[]{:S(2)}) %collective-permute-start.24) | collective-permute-done | bytes 262176 | tf_op jit(solution)/shard_map/ppermute | solution.py:40
  191.7 3.5 %shard_map.102 = f32[8,256,256]{2,1,0:T(8,128)} custom-call(s32[8]{0:T(128)S(1)} %xor.40.order_ref, bf16[2,8,128,256]{3,2,1,0:T(8,128)(2,1)S(1)} %copy-done.2, bf16[2,8,128,256]{3,2,1,0:T(8,128)(2,1)S(1)} %collective-permute-done.13.refs_1_, bf16[2,8,128,256]{3,2,1,0:T(8,128)(2,1)S(1)} %collective-permute-done.14.refs_2_, ...), custom_call_target="tpu_custom_call" | custom-call | flops 1024 | bytes 1024 | tf_op jit(solution)/shard_map/pallas_call | solution.py:316
  196.3 1.6 copy-done.10
  197.9 2.6 %shard_map.101 = f32[8,256,256]{2,1,0:T(8,128)} custom-call(s32[8]{0:T(128)S(1)} %xor.40.order_ref, bf16[2,8,128,256]{3,2,1,0:T(8,128)(2,1)S(1)} %copy-done.3, bf16[2,8,128,256]{3,2,1,0:T(8,128)(2,1)S(1)} %collective-permute-done.13.refs_1_, bf16[2,8,128,256]{3,2,1,0:T(8,128)(2,1)S(1)} %collective-permute-done.14.refs_2_, ...), custom_call_target="tpu_custom_call" | custom-call | flops 1024 | bytes 1024 | tf_op jit(solution)/shard_map/pallas_call | solution.py:316
  (98 shorter events, 37.0 us)
Async XLA Ops:
  13.8 67.6 %all-to-all-start = ((bf16[8,512,256]{2,1,0:T(8,128)(2,1)}), bf16[8,512,256]{2,1,0:T(8,128)(2,1)}, u32[]{:S(2)}, u32[]{:S(2)}) async-start(bf16[8,512,256]{2,1,0:T(8,128)(2,1)} %shard_map.96), calls=%async_computation | async-start | bytes 4194304 | tf_op jit(solution)/shard_map/all_to_all | solution.py:346
  19.5 34.3 %all-gather.5.cloned.1.call-start = ((), (), s32[]{:S(2)}) async-start(), calls=%async_computation.3 | async-start | bytes 1253376 | tf_op jit(solution)/shard_map/all_gather | solution.py:344
  20.2 98.2 %reduce-scatter.2.cloned.1.call-start = ((), (), s32[]{:S(2)}) async-start(), calls=%async_computation.2 | async-start | bytes 2359296 | tf_op jit(solution)/shard_map/reduce_scatter | solution.py:353
  20.3 4.9 %collective-permute-start = (bf16[256,256]{1,0:T(8,128)(2,1)S(1)}, bf16[256,256]{1,0:T(8,128)(2,1)S(1)}, u32[]{:S(2)}, u32[]{:S(2)}) collective-permute-start(bf16[256,256]{1,0:T(8,128)(2,1)S(1)} %copy-done.13), channel_id=1, source_target_pairs={{0,8},{8,0},{16,24},{24,16},{1,9},{9,1},{17,25},{25,17},{2,10},{10... | collective-permute-start | bytes 393224 | tf_op jit(solution)/shard_map/ppermute | solution.py:40
  20.6 4.6 %collective-permute-start.1 = (bf16[256,256]{1,0:T(8,128)(2,1)S(1)}, bf16[256,256]{1,0:T(8,128)(2,1)S(1)}, u32[]{:S(2)}, u32[]{:S(2)}) collective-permute-start(bf16[256,256]{1,0:T(8,128)(2,1)S(1)} %copy-done.13), channel_id=1, source_target_pairs={{0,16},{8,24},{16,0},{24,8},{1,17},{9,25},{17,1},{25,9},{2,18},{10... | collective-permute-start | bytes 393224 | tf_op jit(solution)/shard_map/ppermute | solution.py:40
  21.9 7.0 %collective-permute-start.2 = (bf16[256,256]{1,0:T(8,128)(2,1)S(1)}, bf16[256,256]{1,0:T(8,128)(2,1)S(1)}, u32[]{:S(2)}, u32[]{:S(2)}) collective-permute-start(bf16[256,256]{1,0:T(8,128)(2,1)S(1)} %copy-done.13), channel_id=1, source_target_pairs={{0,24},{8,16},{16,8},{24,0},{1,25},{9,17},{17,9},{25,1},{2,26},{10... | collective-permute-start | bytes 393224 | tf_op jit(solution)/shard_map/ppermute | solution.py:40
  59.2 4.9 %collective-permute-start.3 = (f32[3,2048]{1,0:T(4,128)S(1)}, f32[3,2048]{1,0:T(4,128)S(1)}, u32[]{:S(2)}, u32[]{:S(2)}) collective-permute-start(f32[3,2048]{1,0:T(4,128)S(1)} %shard_map.95.refs_0_), channel_id=1, source_target_pairs={{0,1},{1,0},{2,3},{3,2},{4,5},{5,4},{6,7},{7,6},{8,9},{9,8},{10,11... | collective-permute-start | bytes 73736 | tf_op jit(solution)/shard_map/ppermute | solution.py:40
  59.5 6.1 %collective-permute-start.4 = (f32[3,2048]{1,0:T(4,128)S(1)}, f32[3,2048]{1,0:T(4,128)S(1)}, u32[]{:S(2)}, u32[]{:S(2)}) collective-permute-start(f32[3,2048]{1,0:T(4,128)S(1)} %shard_map.95.refs_0_), channel_id=1, source_target_pairs={{0,2},{1,3},{2,0},{3,1},{4,6},{5,7},{6,4},{7,5},{8,10},{9,11},{10,... | collective-permute-start | bytes 73736 | tf_op jit(solution)/shard_map/ppermute | solution.py:40
  59.9 7.6 %collective-permute-start.5 = (f32[3,2048]{1,0:T(4,128)S(1)}, f32[3,2048]{1,0:T(4,128)S(1)}, u32[]{:S(2)}, u32[]{:S(2)}) collective-permute-start(f32[3,2048]{1,0:T(4,128)S(1)} %shard_map.95.refs_0_), channel_id=1, source_target_pairs={{0,3},{1,2},{2,1},{3,0},{4,7},{5,6},{6,5},{7,4},{8,11},{9,10},{10,... | collective-permute-start | bytes 73736 | tf_op jit(solution)/shard_map/ppermute | solution.py:40
  61.4 16.0 %collective-permute-start.6 = (f32[3,2048]{1,0:T(4,128)S(1)}, f32[3,2048]{1,0:T(4,128)S(1)}, u32[]{:S(2)}, u32[]{:S(2)}) collective-permute-start(f32[3,2048]{1,0:T(4,128)S(1)} %shard_map.95.refs_0_), channel_id=1, source_target_pairs={{0,4},{1,5},{2,6},{3,7},{4,0},{5,1},{6,2},{7,3},{8,12},{9,13},{10,... | collective-permute-start | bytes 73736 | tf_op jit(solution)/shard_map/ppermute | solution.py:40
  64.1 14.0 %collective-permute-start.7 = (f32[3,2048]{1,0:T(4,128)S(1)}, f32[3,2048]{1,0:T(4,128)S(1)}, u32[]{:S(2)}, u32[]{:S(2)}) collective-permute-start(f32[3,2048]{1,0:T(4,128)S(1)} %shard_map.95.refs_0_), channel_id=1, source_target_pairs={{0,5},{1,4},{2,7},{3,6},{4,1},{5,0},{6,3},{7,2},{8,13},{9,12},{10,... | collective-permute-start | bytes 73736 | tf_op jit(solution)/shard_map/ppermute | solution.py:40
  64.1 16.1 %collective-permute-start.8 = (f32[3,2048]{1,0:T(4,128)S(1)}, f32[3,2048]{1,0:T(4,128)S(1)}, u32[]{:S(2)}, u32[]{:S(2)}) collective-permute-start(f32[3,2048]{1,0:T(4,128)S(1)} %shard_map.95.refs_0_), channel_id=1, source_target_pairs={{0,6},{1,7},{2,4},{3,5},{4,2},{5,3},{6,0},{7,1},{8,14},{9,15},{10,... | collective-permute-start | bytes 73736 | tf_op jit(solution)/shard_map/ppermute | solution.py:40
  65.6 15.8 %collective-permute-start.9 = (f32[3,2048]{1,0:T(4,128)S(1)}, f32[3,2048]{1,0:T(4,128)S(1)}, u32[]{:S(2)}, u32[]{:S(2)}) collective-permute-start(f32[3,2048]{1,0:T(4,128)S(1)} %shard_map.95.refs_0_), channel_id=1, source_target_pairs={{0,7},{1,6},{2,5},{3,4},{4,3},{5,2},{6,1},{7,0},{8,15},{9,14},{10,... | collective-permute-start | bytes 73736 | tf_op jit(solution)/shard_map/ppermute | solution.py:40
  89.1 106.0 %all-gather.7.cloned.1.call-start = ((), (), s32[]{:S(2)}) async-start(), calls=%async_computation.4 | async-start | bytes 2359296 | tf_op jit(solution)/shard_map/all_gather | solution.py:363
  89.2 7.7 %collective-permute-start.10 = (f32[256,256]{1,0:T(8,128)S(1)}, f32[256,256]{1,0:T(8,128)S(1)}, u32[]{:S(2)}, u32[]{:S(2)}) collective-permute-start(f32[256,256]{1,0:T(8,128)S(1)} %get-tuple-element.27), channel_id=1, source_target_pairs={{0,8},{8,0},{16,24},{24,16},{1,9},{9,1},{17,25},{25,17},{2,10},{10... | collective-permute-start | bytes 786440 | tf_op jit(solution)/shard_map/ppermute | solution.py:40
  89.5 7.4 %collective-permute-start.11 = (f32[256,256]{1,0:T(8,128)S(1)}, f32[256,256]{1,0:T(8,128)S(1)}, u32[]{:S(2)}, u32[]{:S(2)}) collective-permute-start(f32[256,256]{1,0:T(8,128)S(1)} %get-tuple-element.28), channel_id=1, source_target_pairs={{0,16},{8,24},{16,0},{24,8},{1,17},{9,25},{17,1},{25,9},{2,18},{10... | collective-permute-start | bytes 786440 | tf_op jit(solution)/shard_map/ppermute | solution.py:40
  90.7 12.6 %collective-permute-start.12 = (f32[256,256]{1,0:T(8,128)S(1)}, f32[256,256]{1,0:T(8,128)S(1)}, u32[]{:S(2)}, u32[]{:S(2)}) collective-permute-start(f32[256,256]{1,0:T(8,128)S(1)} %get-tuple-element.29), channel_id=1, source_target_pairs={{0,24},{8,16},{16,8},{24,0},{1,25},{9,17},{17,9},{25,1},{2,26},{10... | collective-permute-start | bytes 786440 | tf_op jit(solution)/shard_map/ppermute | solution.py:40
  106.2 4.2 %collective-permute-start.18 = (bf16[128,256]{1,0:T(8,128)(2,1)}, bf16[128,256]{1,0:T(8,128)(2,1)S(1)}, u32[]{:S(2)}, u32[]{:S(2)}) collective-permute-start(bf16[128,256]{1,0:T(8,128)(2,1)} %get-tuple-element.38), channel_id=1, source_target_pairs={{0,24},{8,16},{16,8},{24,0},{1,25},{9,17},{17,9},{25,1},{2,26},{10... | collective-permute-start | bytes 196616 | tf_op jit(solution)/shard_map/ppermute | solution.py:40
  107.6 4.0 %collective-permute-start.17 = (bf16[128,256]{1,0:T(8,128)(2,1)}, bf16[128,256]{1,0:T(8,128)(2,1)S(1)}, u32[]{:S(2)}, u32[]{:S(2)}) collective-permute-start(bf16[128,256]{1,0:T(8,128)(2,1)} %get-tuple-element.37), channel_id=1, source_target_pairs={{0,16},{8,24},{16,0},{24,8},{1,17},{9,25},{17,1},{25,9},{2,18},{10... | collective-permute-start | bytes 196616 | tf_op jit(solution)/shard_map/ppermute | solution.py:40
  107.7 4.0 %collective-permute-start.16 = (bf16[128,256]{1,0:T(8,128)(2,1)}, bf16[128,256]{1,0:T(8,128)(2,1)S(1)}, u32[]{:S(2)}, u32[]{:S(2)}) collective-permute-start(bf16[128,256]{1,0:T(8,128)(2,1)} %get-tuple-element.36), channel_id=1, source_target_pairs={{0,8},{8,0},{16,24},{24,16},{1,9},{9,1},{17,25},{25,17},{2,10},{10... | collective-permute-start | bytes 196616 | tf_op jit(solution)/shard_map/ppermute | solution.py:40
  120.3 4.3 %collective-permute-start.21 = (bf16[128,256]{1,0:T(8,128)(2,1)}, bf16[128,256]{1,0:T(8,128)(2,1)S(1)}, u32[]{:S(2)}, u32[]{:S(2)}) collective-permute-start(bf16[128,256]{1,0:T(8,128)(2,1)} %get-tuple-element.42), channel_id=1, source_target_pairs={{0,24},{8,16},{16,8},{24,0},{1,25},{9,17},{17,9},{25,1},{2,26},{10... | collective-permute-start | bytes 196616 | tf_op jit(solution)/shard_map/ppermute | solution.py:40
  121.5 3.7 %collective-permute-start.20 = (bf16[128,256]{1,0:T(8,128)(2,1)}, bf16[128,256]{1,0:T(8,128)(2,1)S(1)}, u32[]{:S(2)}, u32[]{:S(2)}) collective-permute-start(bf16[128,256]{1,0:T(8,128)(2,1)} %get-tuple-element.41), channel_id=1, source_target_pairs={{0,16},{8,24},{16,0},{24,8},{1,17},{9,25},{17,1},{25,9},{2,18},{10... | collective-permute-start | bytes 196616 | tf_op jit(solution)/shard_map/ppermute | solution.py:40
  122.5 3.3 %collective-permute-start.19 = (bf16[128,256]{1,0:T(8,128)(2,1)}, bf16[128,256]{1,0:T(8,128)(2,1)S(1)}, u32[]{:S(2)}, u32[]{:S(2)}) collective-permute-start(bf16[128,256]{1,0:T(8,128)(2,1)} %get-tuple-element.40), channel_id=1, source_target_pairs={{0,8},{8,0},{16,24},{24,16},{1,9},{9,1},{17,25},{25,17},{2,10},{10... | collective-permute-start | bytes 196616 | tf_op jit(solution)/shard_map/ppermute | solution.py:40
  127.5 13.7 %collective-permute-start.22 = (bf16[4,128,256]{2,1,0:T(8,128)(2,1)}, bf16[4,128,256]{2,1,0:T(8,128)(2,1)}, u32[]{:S(2)}, u32[]{:S(2)}) collective-permute-start(bf16[4,128,256]{2,1,0:T(8,128)(2,1)} %pad_maximum_fusion.refs_1_.refs_4_), channel_id=1, source_target_pairs={{0,2},{1,3},{2,0},{3,1},{4,6},{5,7},{6,4},{7,5},{8,10},{9,11},{10,... | collective-permute-start | bytes 786440 | tf_op jit(solution)/shard_map/ppermute | solution.py:40
  134.9 51.4 %collective-permute-start.13 = (bf16[2,8,128,256]{3,2,1,0:T(8,128)(2,1)}, bf16[2,8,128,256]{3,2,1,0:T(8,128)(2,1)S(1)}, u32[]{:S(2)}, u32[]{:S(2)}) collective-permute-start(bf16[2,8,128,256]{3,2,1,0:T(8,128)(2,1)} %get-tuple-element.32), channel_id=1, source_target_pairs={{0,8},{8,0},{16,24},{24,16},{1,9},{9,1},{17,25},{25,17},{2,10},{10... | collective-permute-start | bytes 3145736 | tf_op jit(solution)/shard_map/ppermute | solution.py:40
  136.0 50.3 %collective-permute-start.14 = (bf16[2,8,128,256]{3,2,1,0:T(8,128)(2,1)}, bf16[2,8,128,256]{3,2,1,0:T(8,128)(2,1)S(1)}, u32[]{:S(2)}, u32[]{:S(2)}) collective-permute-start(bf16[2,8,128,256]{3,2,1,0:T(8,128)(2,1)} %get-tuple-element.33), channel_id=1, source_target_pairs={{0,16},{8,24},{16,0},{24,8},{1,17},{9,25},{17,1},{25,9},{2,18},{10... | collective-permute-start | bytes 3145736 | tf_op jit(solution)/shard_map/ppermute | solution.py:40
  137.1 49.1 %collective-permute-start.15 = (bf16[2,8,128,256]{3,2,1,0:T(8,128)(2,1)}, bf16[2,8,128,256]{3,2,1,0:T(8,128)(2,1)S(1)}, u32[]{:S(2)}, u32[]{:S(2)}) collective-permute-start(bf16[2,8,128,256]{3,2,1,0:T(8,128)(2,1)} %get-tuple-element.34), channel_id=1, source_target_pairs={{0,24},{8,16},{16,8},{24,0},{1,25},{9,17},{17,9},{25,1},{2,26},{10... | collective-permute-start | bytes 3145736 | tf_op jit(solution)/shard_map/ppermute | solution.py:40
  137.6 31.3 %collective-permute-start.23 = (bf16[4,128,256]{2,1,0:T(8,128)(2,1)S(1)}, bf16[4,128,256]{2,1,0:T(8,128)(2,1)S(1)}, u32[]{:S(2)}, u32[]{:S(2)}) collective-permute-start(bf16[4,128,256]{2,1,0:T(8,128)(2,1)S(1)} %copy-done.7), channel_id=1, source_target_pairs={{0,4},{1,5},{2,6},{3,7},{4,0},{5,1},{6,2},{7,3},{8,12},{9,13},{10,... | collective-permute-start | bytes 786440 | tf_op jit(solution)/shard_map/ppermute | solution.py:40
  141.2 40.3 %collective-permute-start.24 = (bf16[4,128,256]{2,1,0:T(8,128)(2,1)S(1)}, bf16[4,128,256]{2,1,0:T(8,128)(2,1)S(1)}, u32[]{:S(2)}, u32[]{:S(2)}) collective-permute-start(bf16[4,128,256]{2,1,0:T(8,128)(2,1)S(1)} %copy-done.7), channel_id=1, source_target_pairs={{0,6},{1,7},{2,4},{3,5},{4,2},{5,3},{6,0},{7,1},{8,14},{9,15},{10,... | collective-permute-start | bytes 786440 | tf_op jit(solution)/shard_map/ppermute | solution.py:40
  168.9 14.0 %collective-permute-start.25 = (bf16[4,128,256]{2,1,0:T(8,128)(2,1)S(1)}, bf16[4,128,256]{2,1,0:T(8,128)(2,1)}, u32[]{:S(2)}, u32[]{:S(2)}) collective-permute-start(bf16[4,128,256]{2,1,0:T(8,128)(2,1)S(1)} %copy-done.7), channel_id=1, source_target_pairs={{0,1},{1,0},{2,3},{3,2},{4,5},{5,4},{6,7},{7,6},{8,9},{9,8},{10,11... | collective-permute-start | bytes 786440 | tf_op jit(solution)/shard_map/ppermute | solution.py:40
  182.2 2.1 %collective-permute-start.26 = (bf16[4,128,256]{2,1,0:T(8,128)(2,1)}, bf16[4,128,256]{2,1,0:T(8,128)(2,1)}, u32[]{:S(2)}, u32[]{:S(2)}) collective-permute-start(bf16[4,128,256]{2,1,0:T(8,128)(2,1)} %collective-permute-done.22.refs_5_), channel_id=1, source_target_pairs={{0,1},{1,0},{2,3},{3,2},{4,5},{5,4},{6,7},{7,6},{8,9},{9,8},{10,11... | collective-permute-start | bytes 786440 | tf_op jit(solution)/shard_map/ppermute | solution.py:40
  182.9 2.6 %collective-permute-start.27 = (bf16[4,128,256]{2,1,0:T(8,128)(2,1)}, bf16[4,128,256]{2,1,0:T(8,128)(2,1)}, u32[]{:S(2)}, u32[]{:S(2)}) collective-permute-start(bf16[4,128,256]{2,1,0:T(8,128)(2,1)} %copy-done.14), channel_id=1, source_target_pairs={{0,1},{1,0},{2,3},{3,2},{4,5},{5,4},{6,7},{7,6},{8,9},{9,8},{10,11... | collective-permute-start | bytes 786440 | tf_op jit(solution)/shard_map/ppermute | solution.py:40
  (23 other events, 136.0 us)
Sparse Core Ops, SparseCore 0:
  22.0 31.7 all-gather.4
  89.3 29.1 reduce-scatter.1
  127.6 50.7 all-gather.6

commit v8 on v7

--- a/solution.py
+++ b/solution.py
@@ -267,12 +267,12 @@
     )(me, users, hidden, after)
 
 
-def route_kernel(me_ref, target_ref, *refs, tower, count):
+def route_kernel(me_ref, target_ref, *refs, tower, count, order):
     total = refs[0][...]
     for ref in refs[1:count]:
         total = total + ref[...]
     low = total.astype(BF16)
-    out_refs = refs[count + 1 :]
+    out_refs = refs[count + order :]
     span = out_refs[0].shape[0]
     onehot = onehot_of(target_ref[tower : tower + 1, :], me_ref[0], len(out_refs))
     moved = mm(onehot, low, 1, 0).astype(BF16)
@@ -284,12 +284,27 @@
     rows, emb = pieces[0].shape
     span = EXPERTS * CAP // groups
     return pl.pallas_call(
-        functools.partial(route_kernel, tower=tower, count=len(pieces)),
-        in_specs=[SCALARS] + [WHOLE] * (1 + len(pieces)) + [ANYWHERE],
+        functools.partial(route_kernel, tower=tower, count=len(pieces), order=len(after)),
+        in_specs=[SCALARS] + [WHOLE] * (1 + len(pieces)) + [ANYWHERE] * len(after),
         out_specs=[WHOLE] * groups,
         out_shape=[jax.ShapeDtypeStruct((span, emb), BF16)] * groups,
         cost_estimate=SMALL,
-    )(me, targets, *pieces, after)
+    )(me, targets, *pieces, *after)
+
+
+def stack_kernel(*refs, count):
+    for k in range(count):
+        refs[-1][k] = refs[k][...]
+
+
+def stack(pieces, after=()):
+    return pl.pallas_call(
+        functools.partial(stack_kernel, count=len(pieces)),
+        in_specs=[WHOLE] * len(pieces) + [ANYWHERE] * len(after),
+        out_specs=WHOLE,
+        out_shape=jax.ShapeDtypeStruct((len(pieces),) + pieces[0].shape, pieces[0].dtype),
+        cost_estimate=SMALL,
+    )(*pieces, *after)
 
 
 def outer_kernel(order_ref, *refs, groups):
@@ -353,12 +368,13 @@
     user_grad = lax.psum_scatter(user_part, "item", scatter_dimension=0, tiled=True)
     item_pieces = exchange(item_parts, "user")
 
-    item_routed = route(me, targets, item_pieces, 1, groups, packed)
-    hidden_rows = exchange(slot_hidden(me, users, cols, groups, item_routed[0]), "user")
-    item_sent = jnp.stack(exchange(item_routed, "user"))
-    user_routed = route(me, targets, [user_grad], 0, groups, item_sent)
-    user_sent = jnp.stack(exchange(user_routed, "user"))
+    hidden_slots = slot_hidden(me, users, cols, groups, item_parts[0])
+    hidden_rows = exchange(hidden_slots, "user")
+    item_routed = route(me, targets, item_pieces, 1, groups, hidden_slots[:1])
+    item_sent = stack(exchange(item_routed, "user"))
     item_line = exchange([item_sent] * lines, "item", CORES)
+    user_routed = route(me, targets, [user_grad], 0, groups, [item_sent] + hidden_rows[1:3])
+    user_sent = stack(exchange(user_routed, "user"), item_line[1:3])
     item_cross = item_line + [swap(piece, "item", 1) for piece in item_line]
     user_all = lax.all_gather(user_sent, "item", axis=0)
     item_weight_grad = outer(order, hidden_rows, item_cross, 1)

time: 208 us -> 215 us (1.034)
  waiting for transfers between devices: 106 us -> 84.6 us
  starting transfers between devices: 38.6 us -> 59.5 us
  local copies, waits for them, and re-layouts: 15.6 us -> 23.3 us
  Pallas kernels: 29.5 us -> 32.8 us
  other arithmetic: 3.28 us -> 0.08 us
    ppermute x29, starting transfers between devices: 32.8 us -> 53.6 us  [swap(): return lax.ppermute(piece, axis, [(j, j ^ bits) for j in range(size)])]
    ppermute x29, waiting for transfers between devices: 75.4 us -> 59.8 us  [swap(): return lax.ppermute(piece, axis, [(j, j ^ bits) for j in range(size)])]
    unnamed x44 -> x78, local copies, waits for them, and re-layouts: 14.9 us -> 22.7 us
    reduce_scatter x1, waiting for transfers between devices: 5.2 us -> 0.02 us  [shards(): lax.psum_scatter(user_part, 'item', scatter_dimension=0, tiled=True)]
    pallas_call x0 -> x2, Pallas kernels: none -> 3.34 us  [stack(): pl.pallas_call(functools.partial(stack_kernel, count=len(pieces)), in_spe...]
    another operation x2 -> x0, other arithmetic: 3.19 us -> none  [the longest x1 1.6 us: shards(): item_sent = jnp.stack(exchange(item_routed, 'user'))]
  transfers between devices with their start and end apart: 33 -> 33, of which waited for: 20 -> 13; matrix products, arithmetic and copies ran while one was open for 1% -> 0% of each run, Pallas kernels for 7% -> 9%
where the time goes in v8:
time: 215 us; the launch traced here: 214 us
  waiting for transfers between devices  84.6 us (39%)
  starting transfers between devices  59.5 us (28%)
  Pallas kernels  32.8 us (15%)
  local copies, waits for them, and re-layouts  23.3 us (11%)
  between operations  13.9 us (6%)
    ppermute x29, waiting for transfers between devices, swap(): return lax.ppermute(piece, axis, [(j, j ^ bits) for j in range(size)])  59.8 us
    ppermute x29, starting transfers between devices, swap(): return lax.ppermute(piece, axis, [(j, j ^ bits) for j in range(size)])  53.6 us
    all_gather x1, waiting for transfers between devices, shards(): users = lax.all_gather(packed, 'item', axis=0)  24 us
    unnamed x78, local copies, waits for them, and re-layouts  22.7 us
    pallas_call x1, Pallas kernels, grads(): pl.pallas_call(functools.partial(grad_kernel, rows=rows, chunk=64, count=...  7.02 us
    pallas_call x2, Pallas kernels, outer(): pl.pallas_call(functools.partial(outer_kernel, groups=len(hidden)), grid=...  5.97 us
    all_to_all x1, starting transfers between devices, shards(): lax.all_to_all(cut(user_hidden, item_hidden, parts, packed), 'item', spli...  5.77 us
    pallas_call x1, Pallas kernels, slot_hidden(): pl.pallas_call(hidden_kernel, grid=(blocks // pair,), in_specs=[SCALARS,...  5.09 us
  transfers between devices with their start and end apart: 33, of which 13 were waited for; matrix products, arithmetic and copies ran while one was open for 0% of the time, Pallas kernels for 9%

profile of v8, /device:TPU:11, one launch (start us, length us, event | category | flops | bytes accessed | tf_op | source)
XLA Modules:
  0.0 214.1 jit_solution(13515706812573991343)
XLA Ops:
  7.2 1.7 shard_map.94
  12.3 1.5 shard_map.96
  13.8 5.8 %all-to-all-start = ((bf16[8,512,256]{2,1,0:T(8,128)(2,1)}), bf16[8,512,256]{2,1,0:T(8,128)(2,1)}, u32[]{:S(2)}, u32[]{:S(2)}) async-start(bf16[8,512,256]{2,1,0:T(8,128)(2,1)} %shard_map.96), calls=%async_computation | async-start | bytes 4194304 | tf_op jit(solution)/shard_map/all_to_all | solution.py:361
  20.3 1.3 collective-permute-start.2
  23.0 3.1 %collective-permute-done.2.refs_3_.refs_11_ = bf16[256,256]{1,0:T(8,128)(2,1)S(1)} collective-permute-done((bf16[256,256]{1,0:T(8,128)(2,1)S(1)}, bf16[256,256]{1,0:T(8,128)(2,1)S(1)}, u32[]{:S(2)}, u32[]{:S(2)}) %collective-permute-start.2) | collective-permute-done | bytes 131104 | tf_op jit(solution)/shard_map/ppermute | solution.py:40
  26.1 3.4 %collective-permute-done.1.refs_2_.refs_10_ = bf16[256,256]{1,0:T(8,128)(2,1)S(1)} collective-permute-done((bf16[256,256]{1,0:T(8,128)(2,1)S(1)}, bf16[256,256]{1,0:T(8,128)(2,1)S(1)}, u32[]{:S(2)}, u32[]{:S(2)}) %collective-permute-start.1) | collective-permute-done | bytes 131104 | tf_op jit(solution)/shard_map/ppermute | solution.py:40
  29.5 24.0 %all-gather.5.cloned.1.call-done = bf16[2176,256]{1,0:T(8,128)(2,1)} async-done(((bf16[272,256]{1,0:T(8,128)(2,1)}), bf16[2176,256]{1,0:T(8,128)(2,1)}) %all-gather.5.cloned.1.call-update) | async-done | bytes 1114128 | tf_op jit(solution)/shard_map/all_gather | solution.py:359
  53.5 1.2 copy-done
  54.8 4.1 %shard_map.95.refs_0_ = f32[3,2048]{1,0:T(4,128)S(1)} custom-call(s32[4]{0:T(128)S(1)} %add_multiply_fusion.first_ref, bf16[8,272,256]{2,1,0:T(8,128)(2,1)S(1)} %bitcast.8, bf16[256,256]{1,0:T(8,128)(2,1)S(1)} %copy-done.19, bf16[256,256]{1,0:T(8,128)(2,1)S(1)} %collective-permute-done.refs_1_.refs_9_, ...), custom_call_target="tpu_custom_call" | custom-call | flops 1024 | bytes 1024 | tf_op jit(solution)/shard_map/pallas_call | solution.py:117
  60.6 5.4 %collective-permute-start.7 = (f32[3,2048]{1,0:T(4,128)S(1)}, f32[3,2048]{1,0:T(4,128)S(1)}, u32[]{:S(2)}, u32[]{:S(2)}) collective-permute-start(f32[3,2048]{1,0:T(4,128)S(1)} %shard_map.95.refs_0_), channel_id=1, source_target_pairs={{0,5},{1,4},{2,7},{3,6},{4,1},{5,0},{6,3},{7,2},{8,13},{9,12},{10,... | collective-permute-start | bytes 73736 | tf_op jit(solution)/shard_map/ppermute | solution.py:40
  66.6 13.1 %collective-permute-done.9.refs_7_ = f32[3,2048]{1,0:T(4,128)S(1)} collective-permute-done((f32[3,2048]{1,0:T(4,128)S(1)}, f32[3,2048]{1,0:T(4,128)S(1)}, u32[]{:S(2)}, u32[]{:S(2)}) %collective-permute-start.9) | collective-permute-done | bytes 24608 | tf_op jit(solution)/shard_map/ppermute | solution.py:40
  79.8 1.4 collective-permute-start.3
  81.1 1.8 collective-permute-done.4.refs_2_
  83.0 7.0 %shard_map.97 = (f32[1,2048]{1,0:T(1,128)S(1)}, f32[2048,256]{1,0:T(8,128)}, f32[256,256]{1,0:T(8,128)S(1)}, f32[256,256]{1,0:T(8,128)S(1)}, f32[256,256]{1,0:T(8,128)S(1)}, /*index=5*/f32[256,256]{1,0:T(8,128)S(1)}) custom-call(s32[4]{0:T(128)S(1)} %add_multiply_fusion.first_ref, bf16[8,272,256]{2,1,0:T(8,128)(2,1)S(1)} %bitcast.9, ...), custom_call_target="tpu_custom_call" | custom-call | flops 1024 | bytes 1024 | tf_op jit(solution)/shard_map/pallas_call | solution.py:180
  90.8 5.1 %shard_map.98 = (bf16[2,8,128,256]{3,2,1,0:T(8,128)(2,1)}, bf16[2,8,128,256]{3,2,1,0:T(8,128)(2,1)}, bf16[2,8,128,256]{3,2,1,0:T(8,128)(2,1)}, bf16[2,8,128,256]{3,2,1,0:T(8,128)(2,1)}) custom-call(s32[1]{0:T(128)} %bitcast.5.me_ref, bf16[8,272,256]{2,1,0:T(8,128)(2,1)} %bitcast.7, bf16[8,512,256]{2,1,0:T(8,128)(2,1)} %all-to-all-done.refs_12_.hidden_ref, ...), custom_call_target="tpu_custom_call" | custom-call | flops 1024 | bytes 1024 | tf_op jit(solution)/shard_map/pallas_call | solution.py:255
  96.2 1.2 collective-permute-start.11
  100.1 25.8 %collective-permute-done.13.refs_1_ = f32[256,256]{1,0:T(8,128)S(1)} collective-permute-done((f32[256,256]{1,0:T(8,128)}, f32[256,256]{1,0:T(8,128)S(1)}, u32[]{:S(2)}, u32[]{:S(2)}) %collective-permute-start.13) | collective-permute-done | bytes 262176 | tf_op jit(solution)/shard_map/ppermute | solution.py:40
  125.9 6.6 %collective-permute-done.15.refs_3_ = f32[256,256]{1,0:T(8,128)S(1)} collective-permute-done((f32[256,256]{1,0:T(8,128)S(1)}, f32[256,256]{1,0:T(8,128)S(1)}, u32[]{:S(2)}, u32[]{:S(2)}) %collective-permute-start.15) | collective-permute-done | bytes 262176 | tf_op jit(solution)/shard_map/ppermute | solution.py:40
  133.2 2.1 shard_map.99
  135.8 2.1 collective-permute-start.18
  140.7 1.7 shard_map.100.refs_1_.refs_4_
  142.9 1.7 collective-permute-start.22
  146.0 1.9 shard_map.101
  147.9 1.4 collective-permute-start.20
  151.4 2.9 %collective-permute-done.22.refs_4_.refs_5_ = bf16[4,128,256]{2,1,0:T(8,128)(2,1)} collective-permute-done((bf16[4,128,256]{2,1,0:T(8,128)(2,1)}, bf16[4,128,256]{2,1,0:T(8,128)(2,1)}, u32[]{:S(2)}, u32[]{:S(2)}) %collective-permute-start.22) | collective-permute-done | bytes 262176 | tf_op jit(solution)/shard_map/ppermute | solution.py:40
  155.0 1.7 shard_map.102
  156.7 3.2 %collective-permute-start.12 = (bf16[2,8,128,256]{3,2,1,0:T(8,128)(2,1)}, bf16[2,8,128,256]{3,2,1,0:T(8,128)(2,1)S(1)}, u32[]{:S(2)}, u32[]{:S(2)}) collective-permute-start(bf16[2,8,128,256]{3,2,1,0:T(8,128)(2,1)} %get-tuple-element.29), channel_id=1, source_target_pairs={{0,24},{8,16},{16,8},{24,0},{1,25},{9,17},{17,9},{25,1},{2,26},{10... | collective-permute-start | bytes 3145736 | tf_op jit(solution)/shard_map/ppermute | solution.py:40
  160.7 4.1 %collective-permute-start.25 = (bf16[4,128,256]{2,1,0:T(8,128)(2,1)S(1)}, bf16[4,128,256]{2,1,0:T(8,128)(2,1)S(1)}, u32[]{:S(2)}, u32[]{:S(2)}) collective-permute-start(bf16[4,128,256]{2,1,0:T(8,128)(2,1)S(1)} %copy-done.12), channel_id=1, source_target_pairs={{0,1},{1,0},{2,3},{3,2},{4,5},{5,4},{6,7},{7,6},{8,9},{9,8},{10,11... | collective-permute-start | bytes 786440 | tf_op jit(solution)/shard_map/ppermute | solution.py:40
  165.4 21.4 %collective-permute-start.28 = (bf16[4,128,256]{2,1,0:T(8,128)(2,1)S(1)}, bf16[4,128,256]{2,1,0:T(8,128)(2,1)}, u32[]{:S(2)}, u32[]{:S(2)}) collective-permute-start(bf16[4,128,256]{2,1,0:T(8,128)(2,1)S(1)} %collective-permute-done.24.refs_7_), channel_id=1, source_target_pairs={{0,1},{1,0},{2,3},{3,2},{4,5},{5,4},{6,7},{7,6},{8,9},{9,8},{10,11... | collective-permute-start | bytes 786440 | tf_op jit(solution)/shard_map/ppermute | solution.py:40
  198.8 3.3 %shard_map.104 = f32[8,256,256]{2,1,0:T(8,128)} custom-call(s32[8]{0:T(128)S(1)} %xor.40.order_ref, bf16[2,8,128,256]{3,2,1,0:T(8,128)(2,1)S(1)} %copy-done.2, bf16[2,8,128,256]{3,2,1,0:T(8,128)(2,1)S(1)} %copy-done.4, bf16[2,8,128,256]{3,2,1,0:T(8,128)(2,1)S(1)} %copy-done.7, bf16[2,8,128,256]{3,2,1,0:T(8,128)(2,1)S(1)} %copy-done.10, ...), custom_call_target="tpu_custom_call" | custom-call | flops 1024 | bytes 1024 | tf_op jit(solution)/shard_map/pallas_call | solution.py:331
  203.4 1.6 copy-done.13
  205.0 2.6 %shard_map.103 = f32[8,256,256]{2,1,0:T(8,128)} custom-call(s32[8]{0:T(128)S(1)} %xor.40.order_ref, bf16[2,8,128,256]{3,2,1,0:T(8,128)(2,1)S(1)} %copy-done.2, bf16[2,8,128,256]{3,2,1,0:T(8,128)(2,1)S(1)} %copy-done.5, bf16[2,8,128,256]{3,2,1,0:T(8,128)(2,1)S(1)} %copy-done.8, bf16[2,8,128,256]{3,2,1,0:T(8,128)(2,1)S(1)} %copy-done.11, ...), custom_call_target="tpu_custom_call" | custom-call | flops 1024 | bytes 1024 | tf_op jit(solution)/shard_map/pallas_call | solution.py:331
  (132 shorter events, 34.9 us)
Async XLA Ops:
  13.8 69.2 %all-to-all-start = ((bf16[8,512,256]{2,1,0:T(8,128)(2,1)}), bf16[8,512,256]{2,1,0:T(8,128)(2,1)}, u32[]{:S(2)}, u32[]{:S(2)}) async-start(bf16[8,512,256]{2,1,0:T(8,128)(2,1)} %shard_map.96), calls=%async_computation | async-start | bytes 4194304 | tf_op jit(solution)/shard_map/all_to_all | solution.py:361
  19.5 34.0 %all-gather.5.cloned.1.call-start = ((), (), s32[]{:S(2)}) async-start(), calls=%async_computation.3 | async-start | bytes 1253376 | tf_op jit(solution)/shard_map/all_gather | solution.py:359
  20.2 124.5 %reduce-scatter.2.cloned.1.call-start = ((), (), s32[]{:S(2)}) async-start(), calls=%async_computation.2 | async-start | bytes 2359296 | tf_op jit(solution)/shard_map/reduce_scatter | solution.py:368
  20.3 5.8 %collective-permute-start.2 = (bf16[256,256]{1,0:T(8,128)(2,1)S(1)}, bf16[256,256]{1,0:T(8,128)(2,1)S(1)}, u32[]{:S(2)}, u32[]{:S(2)}) collective-permute-start(bf16[256,256]{1,0:T(8,128)(2,1)S(1)} %copy-done.19), channel_id=1, source_target_pairs={{0,24},{8,16},{16,8},{24,0},{1,25},{9,17},{17,9},{25,1},{2,26},{10... | collective-permute-start | bytes 393224 | tf_op jit(solution)/shard_map/ppermute | solution.py:40
  21.6 7.9 %collective-permute-start.1 = (bf16[256,256]{1,0:T(8,128)(2,1)S(1)}, bf16[256,256]{1,0:T(8,128)(2,1)S(1)}, u32[]{:S(2)}, u32[]{:S(2)}) collective-permute-start(bf16[256,256]{1,0:T(8,128)(2,1)S(1)} %copy-done.19), channel_id=1, source_target_pairs={{0,16},{8,24},{16,0},{24,8},{1,17},{9,25},{17,1},{25,9},{2,18},{10... | collective-permute-start | bytes 393224 | tf_op jit(solution)/shard_map/ppermute | solution.py:40
  21.8 7.7 %collective-permute-start = (bf16[256,256]{1,0:T(8,128)(2,1)S(1)}, bf16[256,256]{1,0:T(8,128)(2,1)S(1)}, u32[]{:S(2)}, u32[]{:S(2)}) collective-permute-start(bf16[256,256]{1,0:T(8,128)(2,1)S(1)} %copy-done.19), channel_id=1, source_target_pairs={{0,8},{8,0},{16,24},{24,16},{1,9},{9,1},{17,25},{25,17},{2,10},{10... | collective-permute-start | bytes 393224 | tf_op jit(solution)/shard_map/ppermute | solution.py:40
  58.9 20.8 %collective-permute-start.9 = (f32[3,2048]{1,0:T(4,128)S(1)}, f32[3,2048]{1,0:T(4,128)S(1)}, u32[]{:S(2)}, u32[]{:S(2)}) collective-permute-start(f32[3,2048]{1,0:T(4,128)S(1)} %shard_map.95.refs_0_), channel_id=1, source_target_pairs={{0,7},{1,6},{2,5},{3,4},{4,3},{5,2},{6,1},{7,0},{8,15},{9,14},{10,... | collective-permute-start | bytes 73736 | tf_op jit(solution)/shard_map/ppermute | solution.py:40
  60.2 19.6 %collective-permute-start.8 = (f32[3,2048]{1,0:T(4,128)S(1)}, f32[3,2048]{1,0:T(4,128)S(1)}, u32[]{:S(2)}, u32[]{:S(2)}) collective-permute-start(f32[3,2048]{1,0:T(4,128)S(1)} %shard_map.95.refs_0_), channel_id=1, source_target_pairs={{0,6},{1,7},{2,4},{3,5},{4,2},{5,3},{6,0},{7,1},{8,14},{9,15},{10,... | collective-permute-start | bytes 73736 | tf_op jit(solution)/shard_map/ppermute | solution.py:40
  60.6 20.5 %collective-permute-start.7 = (f32[3,2048]{1,0:T(4,128)S(1)}, f32[3,2048]{1,0:T(4,128)S(1)}, u32[]{:S(2)}, u32[]{:S(2)}) collective-permute-start(f32[3,2048]{1,0:T(4,128)S(1)} %shard_map.95.refs_0_), channel_id=1, source_target_pairs={{0,5},{1,4},{2,7},{3,6},{4,1},{5,0},{6,3},{7,2},{8,13},{9,12},{10,... | collective-permute-start | bytes 73736 | tf_op jit(solution)/shard_map/ppermute | solution.py:40
  66.0 15.1 %collective-permute-start.6 = (f32[3,2048]{1,0:T(4,128)S(1)}, f32[3,2048]{1,0:T(4,128)S(1)}, u32[]{:S(2)}, u32[]{:S(2)}) collective-permute-start(f32[3,2048]{1,0:T(4,128)S(1)} %shard_map.95.refs_0_), channel_id=1, source_target_pairs={{0,4},{1,5},{2,6},{3,7},{4,0},{5,1},{6,2},{7,3},{8,12},{9,13},{10,... | collective-permute-start | bytes 73736 | tf_op jit(solution)/shard_map/ppermute | solution.py:40
  66.0 15.1 %collective-permute-start.5 = (f32[3,2048]{1,0:T(4,128)S(1)}, f32[3,2048]{1,0:T(4,128)S(1)}, u32[]{:S(2)}, u32[]{:S(2)}) collective-permute-start(f32[3,2048]{1,0:T(4,128)S(1)} %shard_map.95.refs_0_), channel_id=1, source_target_pairs={{0,3},{1,2},{2,1},{3,0},{4,7},{5,6},{6,5},{7,4},{8,11},{9,10},{10,... | collective-permute-start | bytes 73736 | tf_op jit(solution)/shard_map/ppermute | solution.py:40
  79.7 3.2 %collective-permute-start.4 = (f32[3,2048]{1,0:T(4,128)S(1)}, f32[3,2048]{1,0:T(4,128)S(1)}, u32[]{:S(2)}, u32[]{:S(2)}) collective-permute-start(f32[3,2048]{1,0:T(4,128)S(1)} %shard_map.95.refs_0_), channel_id=1, source_target_pairs={{0,2},{1,3},{2,0},{3,1},{4,6},{5,7},{6,4},{7,5},{8,10},{9,11},{10,... | collective-permute-start | bytes 73736 | tf_op jit(solution)/shard_map/ppermute | solution.py:40
  90.7 111.4 %all-gather.7.cloned.1.call-start = ((), (), s32[]{:S(2)}) async-start(), calls=%async_computation.4 | async-start | bytes 2359296 | tf_op jit(solution)/shard_map/all_gather | solution.py:379
  95.9 48.8 %collective-permute-start.10 = (bf16[2,8,128,256]{3,2,1,0:T(8,128)(2,1)}, bf16[2,8,128,256]{3,2,1,0:T(8,128)(2,1)S(1)}, u32[]{:S(2)}, u32[]{:S(2)}) collective-permute-start(bf16[2,8,128,256]{3,2,1,0:T(8,128)(2,1)} %get-tuple-element.27), channel_id=1, source_target_pairs={{0,8},{8,0},{16,24},{24,16},{1,9},{9,1},{17,25},{25,17},{2,10},{10... | collective-permute-start | bytes 3145736 | tf_op jit(solution)/shard_map/ppermute | solution.py:40
  96.2 48.5 %collective-permute-start.11 = (bf16[2,8,128,256]{3,2,1,0:T(8,128)(2,1)}, bf16[2,8,128,256]{3,2,1,0:T(8,128)(2,1)S(1)}, u32[]{:S(2)}, u32[]{:S(2)}) collective-permute-start(bf16[2,8,128,256]{3,2,1,0:T(8,128)(2,1)} %get-tuple-element.28), channel_id=1, source_target_pairs={{0,16},{8,24},{16,0},{24,8},{1,17},{9,25},{17,1},{25,9},{2,18},{10... | collective-permute-start | bytes 3145736 | tf_op jit(solution)/shard_map/ppermute | solution.py:40
  97.4 28.4 %collective-permute-start.13 = (f32[256,256]{1,0:T(8,128)}, f32[256,256]{1,0:T(8,128)S(1)}, u32[]{:S(2)}, u32[]{:S(2)}) collective-permute-start(f32[256,256]{1,0:T(8,128)} %copy-done.29), channel_id=1, source_target_pairs={{0,8},{8,0},{16,24},{24,16},{1,9},{9,1},{17,25},{25,17},{2,10},{10... | collective-permute-start | bytes 786440 | tf_op jit(solution)/shard_map/ppermute | solution.py:40
  98.6 27.2 %collective-permute-start.14 = (f32[256,256]{1,0:T(8,128)}, f32[256,256]{1,0:T(8,128)S(1)}, u32[]{:S(2)}, u32[]{:S(2)}) collective-permute-start(f32[256,256]{1,0:T(8,128)} %copy-done.28), channel_id=1, source_target_pairs={{0,16},{8,24},{16,0},{24,8},{1,17},{9,25},{17,1},{25,9},{2,18},{10... | collective-permute-start | bytes 786440 | tf_op jit(solution)/shard_map/ppermute | solution.py:40
  98.9 33.6 %collective-permute-start.15 = (f32[256,256]{1,0:T(8,128)S(1)}, f32[256,256]{1,0:T(8,128)S(1)}, u32[]{:S(2)}, u32[]{:S(2)}) collective-permute-start(f32[256,256]{1,0:T(8,128)S(1)} %get-tuple-element.34), channel_id=1, source_target_pairs={{0,24},{8,16},{16,8},{24,0},{1,25},{9,17},{17,9},{25,1},{2,26},{10... | collective-permute-start | bytes 786440 | tf_op jit(solution)/shard_map/ppermute | solution.py:40
  135.3 3.3 %collective-permute-start.16 = (bf16[128,256]{1,0:T(8,128)(2,1)}, bf16[128,256]{1,0:T(8,128)(2,1)S(1)}, u32[]{:S(2)}, u32[]{:S(2)}) collective-permute-start(bf16[128,256]{1,0:T(8,128)(2,1)} %get-tuple-element.36), channel_id=1, source_target_pairs={{0,8},{8,0},{16,24},{24,16},{1,9},{9,1},{17,25},{25,17},{2,10},{10... | collective-permute-start | bytes 196616 | tf_op jit(solution)/shard_map/ppermute | solution.py:40
  135.6 3.3 %collective-permute-start.17 = (bf16[128,256]{1,0:T(8,128)(2,1)}, bf16[128,256]{1,0:T(8,128)(2,1)S(1)}, u32[]{:S(2)}, u32[]{:S(2)}) collective-permute-start(bf16[128,256]{1,0:T(8,128)(2,1)} %get-tuple-element.37), channel_id=1, source_target_pairs={{0,16},{8,24},{16,0},{24,8},{1,17},{9,25},{17,1},{25,9},{2,18},{10... | collective-permute-start | bytes 196616 | tf_op jit(solution)/shard_map/ppermute | solution.py:40
  135.8 4.2 %collective-permute-start.18 = (bf16[128,256]{1,0:T(8,128)(2,1)}, bf16[128,256]{1,0:T(8,128)(2,1)S(1)}, u32[]{:S(2)}, u32[]{:S(2)}) collective-permute-start(bf16[128,256]{1,0:T(8,128)(2,1)} %get-tuple-element.38), channel_id=1, source_target_pairs={{0,24},{8,16},{16,8},{24,0},{1,25},{9,17},{17,9},{25,1},{2,26},{10... | collective-permute-start | bytes 196616 | tf_op jit(solution)/shard_map/ppermute | solution.py:40
  142.4 9.0 %collective-permute-start.23 = (bf16[4,128,256]{2,1,0:T(8,128)(2,1)}, bf16[4,128,256]{2,1,0:T(8,128)(2,1)}, u32[]{:S(2)}, u32[]{:S(2)}) collective-permute-start(bf16[4,128,256]{2,1,0:T(8,128)(2,1)} %shard_map.100.refs_1_.refs_4_), channel_id=1, source_target_pairs={{0,4},{1,5},{2,6},{3,7},{4,0},{5,1},{6,2},{7,3},{8,12},{9,13},{10,... | collective-permute-start | bytes 786440 | tf_op jit(solution)/shard_map/ppermute | solution.py:40
  142.9 11.4 %collective-permute-start.22 = (bf16[4,128,256]{2,1,0:T(8,128)(2,1)}, bf16[4,128,256]{2,1,0:T(8,128)(2,1)}, u32[]{:S(2)}, u32[]{:S(2)}) collective-permute-start(bf16[4,128,256]{2,1,0:T(8,128)(2,1)} %shard_map.100.refs_1_.refs_4_), channel_id=1, source_target_pairs={{0,2},{1,3},{2,0},{3,1},{4,6},{5,7},{6,4},{7,5},{8,10},{9,11},{10,... | collective-permute-start | bytes 786440 | tf_op jit(solution)/shard_map/ppermute | solution.py:40
  147.9 6.4 %collective-permute-start.19 = (bf16[128,256]{1,0:T(8,128)(2,1)}, bf16[128,256]{1,0:T(8,128)(2,1)S(1)}, u32[]{:S(2)}, u32[]{:S(2)}) collective-permute-start(bf16[128,256]{1,0:T(8,128)(2,1)} %get-tuple-element.40), channel_id=1, source_target_pairs={{0,8},{8,0},{16,24},{24,16},{1,9},{9,1},{17,25},{25,17},{2,10},{10... | collective-permute-start | bytes 196616 | tf_op jit(solution)/shard_map/ppermute | solution.py:40
  147.9 6.4 %collective-permute-start.20 = (bf16[128,256]{1,0:T(8,128)(2,1)}, bf16[128,256]{1,0:T(8,128)(2,1)S(1)}, u32[]{:S(2)}, u32[]{:S(2)}) collective-permute-start(bf16[128,256]{1,0:T(8,128)(2,1)} %get-tuple-element.41), channel_id=1, source_target_pairs={{0,16},{8,24},{16,0},{24,8},{1,17},{9,25},{17,1},{25,9},{2,18},{10... | collective-permute-start | bytes 196616 | tf_op jit(solution)/shard_map/ppermute | solution.py:40
  149.3 5.0 %collective-permute-start.21 = (bf16[128,256]{1,0:T(8,128)(2,1)}, bf16[128,256]{1,0:T(8,128)(2,1)S(1)}, u32[]{:S(2)}, u32[]{:S(2)}) collective-permute-start(bf16[128,256]{1,0:T(8,128)(2,1)} %get-tuple-element.42), channel_id=1, source_target_pairs={{0,24},{8,16},{16,8},{24,0},{1,25},{9,17},{17,9},{25,1},{2,26},{10... | collective-permute-start | bytes 196616 | tf_op jit(solution)/shard_map/ppermute | solution.py:40
  156.7 33.7 %collective-permute-start.12 = (bf16[2,8,128,256]{3,2,1,0:T(8,128)(2,1)}, bf16[2,8,128,256]{3,2,1,0:T(8,128)(2,1)S(1)}, u32[]{:S(2)}, u32[]{:S(2)}) collective-permute-start(bf16[2,8,128,256]{3,2,1,0:T(8,128)(2,1)} %get-tuple-element.29), channel_id=1, source_target_pairs={{0,24},{8,16},{16,8},{24,0},{1,25},{9,17},{17,9},{25,1},{2,26},{10... | collective-permute-start | bytes 3145736 | tf_op jit(solution)/shard_map/ppermute | solution.py:40
  159.9 5.5 %collective-permute-start.24 = (bf16[4,128,256]{2,1,0:T(8,128)(2,1)S(1)}, bf16[4,128,256]{2,1,0:T(8,128)(2,1)S(1)}, u32[]{:S(2)}, u32[]{:S(2)}) collective-permute-start(bf16[4,128,256]{2,1,0:T(8,128)(2,1)S(1)} %copy-done.12), channel_id=1, source_target_pairs={{0,6},{1,7},{2,4},{3,5},{4,2},{5,3},{6,0},{7,1},{8,14},{9,15},{10,... | collective-permute-start | bytes 786440 | tf_op jit(solution)/shard_map/ppermute | solution.py:40
  160.7 27.5 %collective-permute-start.25 = (bf16[4,128,256]{2,1,0:T(8,128)(2,1)S(1)}, bf16[4,128,256]{2,1,0:T(8,128)(2,1)S(1)}, u32[]{:S(2)}, u32[]{:S(2)}) collective-permute-start(bf16[4,128,256]{2,1,0:T(8,128)(2,1)S(1)} %copy-done.12), channel_id=1, source_target_pairs={{0,1},{1,0},{2,3},{3,2},{4,5},{5,4},{6,7},{7,6},{8,9},{9,8},{10,11... | collective-permute-start | bytes 786440 | tf_op jit(solution)/shard_map/ppermute | solution.py:40
  164.8 24.1 %collective-permute-start.27 = (bf16[4,128,256]{2,1,0:T(8,128)(2,1)}, bf16[4,128,256]{2,1,0:T(8,128)(2,1)S(1)}, u32[]{:S(2)}, u32[]{:S(2)}) collective-permute-start(bf16[4,128,256]{2,1,0:T(8,128)(2,1)} %collective-permute-done.23.refs_5_.refs_6_), channel_id=1, source_target_pairs={{0,1},{1,0},{2,3},{3,2},{4,5},{5,4},{6,7},{7,6},{8,9},{9,8},{10,11... | collective-permute-start | bytes 786440 | tf_op jit(solution)/shard_map/ppermute | solution.py:40
  164.8 24.8 %collective-permute-start.26 = (bf16[4,128,256]{2,1,0:T(8,128)(2,1)}, bf16[4,128,256]{2,1,0:T(8,128)(2,1)S(1)}, u32[]{:S(2)}, u32[]{:S(2)}) collective-permute-start(bf16[4,128,256]{2,1,0:T(8,128)(2,1)} %collective-permute-done.22.refs_4_.refs_5_), channel_id=1, source_target_pairs={{0,1},{1,0},{2,3},{3,2},{4,5},{5,4},{6,7},{7,6},{8,9},{9,8},{10,11... | collective-permute-start | bytes 786440 | tf_op jit(solution)/shard_map/ppermute | solution.py:40
  165.4 23.5 %collective-permute-start.28 = (bf16[4,128,256]{2,1,0:T(8,128)(2,1)S(1)}, bf16[4,128,256]{2,1,0:T(8,128)(2,1)}, u32[]{:S(2)}, u32[]{:S(2)}) collective-permute-start(bf16[4,128,256]{2,1,0:T(8,128)(2,1)S(1)} %collective-permute-done.24.refs_7_), channel_id=1, source_target_pairs={{0,1},{1,0},{2,3},{3,2},{4,5},{5,4},{6,7},{7,6},{8,9},{9,8},{10,11... | collective-permute-start | bytes 786440 | tf_op jit(solution)/shard_map/ppermute | solution.py:40
  (40 other events, 201.9 us)
Sparse Core Ops, SparseCore 0:
  22.6 30.9 all-gather.4
  90.8 29.3 reduce-scatter.1
  156.8 35.5 all-gather.6

commit v9 on v8

--- a/solution.py
+++ b/solution.py
@@ -208,24 +208,22 @@
     return results[0], results[1], results[2:]
 
 
-def cut_kernel(user_ref, item_ref, _, out_ref):
-    rows = user_ref.shape[0]
+def cut_kernel(in_ref, _, out_ref):
     width = out_ref.shape[2]
     for k in range(out_ref.shape[0]):
-        out_ref[k, :rows, :] = user_ref[:, k * width : (k + 1) * width]
-        out_ref[k, rows:, :] = item_ref[:, k * width : (k + 1) * width]
-
-
-def cut(user_hidden, item_hidden, parts, after):
-    rows, total = user_hidden.shape
+        out_ref[k] = in_ref[:, k * width : (k + 1) * width]
+
+
+def cut(hidden, parts, after):
+    rows, total = hidden.shape
     return pl.pallas_call(
         cut_kernel,
-        in_specs=[WHOLE] * 2 + [ANYWHERE],
+        in_specs=[WHOLE, ANYWHERE],
         out_specs=WHOLE,
-        out_shape=jax.ShapeDtypeStruct((parts, 2 * rows, total // parts), BF16),
+        out_shape=jax.ShapeDtypeStruct((parts, rows, total // parts), BF16),
         compiler_params=pltpu.CompilerParams(vmem_limit_bytes=24 * MIB),
         cost_estimate=SMALL,
-    )(user_hidden, item_hidden, after)
+    )(hidden, after)
 
 
 def onehot_of(target, me, groups):
@@ -235,36 +233,34 @@
     return (place == target).astype(F32).astype(BF16)
 
 
-def hidden_kernel(me_ref, users_ref, hidden_ref, _, *out_refs):
-    rows = users_ref.shape[2]
-    _, pair, span, _ = out_refs[0].shape
+def hidden_kernel(users_ref, user_ref, item_ref, _, out_ref):
+    groups, _, pair, span, _ = out_ref.shape
     for half in range(pair):
-        for tower in range(2):
-            onehot = onehot_of(number(users_ref[half], 1 + tower), me_ref[0], len(out_refs))
-            values = hidden_ref[half, tower * rows : (tower + 1) * rows, :]
-            moved = mm(onehot, values, 1, 0).astype(BF16)
-            for k, out_ref in enumerate(out_refs):
-                out_ref[tower, half] = moved[k * span : (k + 1) * span, :]
-
-
-def slot_hidden(me, users, hidden, groups, after):
-    blocks, height, rows = users.shape
-    width = hidden.shape[2]
+        for tower, hidden_ref in enumerate((user_ref, item_ref)):
+            onehot = onehot_of(number(users_ref[half], 1 + tower), 0, groups)
+            moved = mm(onehot, hidden_ref[half], 1, 0).astype(BF16)
+            for k in range(groups):
+                out_ref[k, tower, half] = moved[k * span : (k + 1) * span, :]
+
+
+def slot_hidden(users, user_hidden, item_hidden, groups, after):
+    blocks, rows, width = user_hidden.shape
     span = EXPERTS * CAP // groups
     pair = 2
+    half = pl.BlockSpec((pair, rows, width), lambda b: (b, 0, 0))
     return pl.pallas_call(
         hidden_kernel,
         grid=(blocks // pair,),
         in_specs=[
-            SCALARS,
             pl.BlockSpec((pair, EXTRA, rows), lambda b: (b, rows // EXTRA, 0)),
-            pl.BlockSpec((pair, 2 * rows, width), lambda b: (b, 0, 0)),
+            half,
+            half,
             ANYWHERE,
         ],
-        out_specs=[pl.BlockSpec((2, pair, span, width), lambda b: (0, b, 0, 0))] * groups,
-        out_shape=[jax.ShapeDtypeStruct((2, blocks, span, width), BF16)] * groups,
-        cost_estimate=SMALL,
-    )(me, users, hidden, after)
+        out_specs=pl.BlockSpec((groups, 2, pair, span, width), lambda b: (0, 0, b, 0, 0)),
+        out_shape=jax.ShapeDtypeStruct((groups, 2, blocks, span, width), BF16),
+        cost_estimate=SMALL,
+    )(users, user_hidden, item_hidden, after)
 
 
 def route_kernel(me_ref, target_ref, *refs, tower, count, order):
@@ -307,38 +303,38 @@
     )(*pieces, *after)
 
 
-def outer_kernel(order_ref, *refs, groups):
-    hidden_refs, grad_refs, out_ref = refs[:groups], refs[groups:-1], refs[-1]
-    _, blocks, span, width = hidden_refs[0].shape
+def outer_kernel(order_ref, me_ref, hidden_ref, *refs):
+    grad_refs, out_ref = refs[:-1], refs[-1]
+    groups, _, blocks, span, _ = hidden_ref.shape
     for e in range(span // CAP):
         here = slice(e * CAP, (e + 1) * CAP)
         left, right = [], []
         for j in range(blocks):
-            for k, hidden_ref in enumerate(hidden_refs):
+            for k in range(groups):
                 if len(grad_refs) == 1:
-                    left.append(hidden_ref[0, j, here, :])
+                    left.append(hidden_ref[me_ref[0] ^ k, 0, j, here, :])
                     right.append(grad_refs[0][j, k, here, :])
                 else:
-                    left.append(hidden_ref[0, order_ref[j], here, :])
+                    left.append(hidden_ref[me_ref[0] ^ k, 0, order_ref[j], here, :])
                     right.append(grad_refs[j][k, here, :])
         out_ref[e] = mm(jnp.concatenate(left), jnp.concatenate(right), 0, 0)
 
 
-def outer(order, hidden, grads, tower):
-    _, blocks, span, width = hidden[0].shape
+def outer(order, me, hidden, grads, tower):
+    groups, _, blocks, span, width = hidden.shape
     emb = grads[0].shape[-1]
     own = span // CAP
     return pl.pallas_call(
-        functools.partial(outer_kernel, groups=len(hidden)),
+        outer_kernel,
         grid=(1,),
-        in_specs=[SCALARS]
-        + [pl.BlockSpec((1, blocks, span, width), lambda _: (tower, 0, 0, 0))] * len(hidden)
+        in_specs=[SCALARS, SCALARS]
+        + [pl.BlockSpec((groups, 1, blocks, span, width), lambda _: (0, tower, 0, 0, 0))]
         + [pl.BlockSpec(g.shape, lambda _, d=g.ndim: (0,) * d) for g in grads],
         out_specs=pl.BlockSpec((own, width, emb), lambda _: (0, 0, 0)),
         out_shape=jax.ShapeDtypeStruct((own, width, emb), F32),
-        compiler_params=pltpu.CompilerParams(vmem_limit_bytes=40 * MIB),
-        cost_estimate=SMALL,
-    )(order, *hidden, *grads)
+        compiler_params=pltpu.CompilerParams(vmem_limit_bytes=56 * MIB),
+        cost_estimate=SMALL,
+    )(order, me, hidden, *grads)
 
 
 def shards(user_emb, item_emb, user_hidden, item_hidden, user_expert, item_expert, positive):
@@ -358,27 +354,30 @@
     packed, targets = pack(user_emb, positive, user_expert, item_expert)
     users = lax.all_gather(packed, "item", axis=0)
     items = exchange([item_emb] * groups, "user")
-    cols = lax.all_to_all(
-        cut(user_hidden, item_hidden, parts, packed), "item", split_axis=0, concat_axis=0, tiled=True
-    )
-
-    gathered = exchange([stats(first, users, items, rows, packed)] * parts, "item")
-    losses, user_part, item_parts = grads(first, users, items, gathered, rows, cols)
+
+    def scatter(pieces, axis):
+        return lax.all_to_all(pieces, axis, split_axis=0, concat_axis=0, tiled=True)
+
+    user_cols = scatter(cut(user_hidden, parts, items[1]), "item")
+    found = stats(first, users, items, rows, packed)
+    item_cols = scatter(cut(item_hidden, parts, found), "item")
+    gathered = exchange([found] * parts, "item")
+    losses, user_part, item_parts = grads(first, users, items, gathered, rows, user_cols)
     row_loss = lax.dynamic_slice_in_dim(losses[0], part * rows, rows)
     user_grad = lax.psum_scatter(user_part, "item", scatter_dimension=0, tiled=True)
     item_pieces = exchange(item_parts, "user")
 
-    hidden_slots = slot_hidden(me, users, cols, groups, item_parts[0])
-    hidden_rows = exchange(hidden_slots, "user")
-    item_routed = route(me, targets, item_pieces, 1, groups, hidden_slots[:1])
+    item_routed = route(me, targets, item_pieces, 1, groups, [])
     item_sent = stack(exchange(item_routed, "user"))
     item_line = exchange([item_sent] * lines, "item", CORES)
-    user_routed = route(me, targets, [user_grad], 0, groups, [item_sent] + hidden_rows[1:3])
-    user_sent = stack(exchange(user_routed, "user"), item_line[1:3])
+    hidden_slots = slot_hidden(users, user_cols, item_cols, groups, item_sent)
+    hidden_rows = scatter(hidden_slots, "user")
+    user_routed = route(me, targets, [user_grad], 0, groups, [hidden_slots])
+    user_sent = stack(exchange(user_routed, "user"))
     item_cross = item_line + [swap(piece, "item", 1) for piece in item_line]
     user_all = lax.all_gather(user_sent, "item", axis=0)
-    item_weight_grad = outer(order, hidden_rows, item_cross, 1)
-    user_weight_grad = outer(order, hidden_rows, [user_all], 0)
+    item_weight_grad = outer(order, me, hidden_rows, item_cross, 1)
+    user_weight_grad = outer(order, me, hidden_rows, [user_all], 0)
     return (row_loss, user_weight_grad, item_weight_grad)
 
 

time: 215 us -> 208 us (0.967)
  starting transfers between devices: 59.5 us -> 42.2 us
  waiting for transfers between devices: 84.6 us -> 99.4 us
  local copies, waits for them, and re-layouts: 23.3 us -> 15.3 us
  Pallas kernels: 32.8 us -> 35.2 us
    ppermute x29 -> x26, starting transfers between devices: 53.6 us -> 24.3 us  [swap(): return lax.ppermute(piece, axis, [(j, j ^ bits) for j in range(size)])]
    all_to_all x1 -> x3, waiting for transfers between devices: 0.01 us -> 19.3 us  [scatter(): return lax.all_to_all(pieces, axis, split_axis=0, concat_axis=0, tiled=True)]
    all_gather x1, waiting for transfers between devices: 24 us -> 6.67 us  [shards(): users = lax.all_gather(packed, 'item', axis=0)]
    all_to_all x1 -> x3, starting transfers between devices: 5.77 us -> 17.9 us  [scatter(): return lax.all_to_all(pieces, axis, split_axis=0, concat_axis=0, tiled=True)]
    ppermute x29 -> x26, waiting for transfers between devices: 59.8 us -> 69 us  [swap(): return lax.ppermute(piece, axis, [(j, j ^ bits) for j in range(size)])]
    unnamed x78, local copies, waits for them, and re-layouts: 22.7 us -> 14.1 us
    reduce_scatter x1, waiting for transfers between devices: 0.02 us -> 4.34 us  [shards(): lax.psum_scatter(user_part, 'item', scatter_dimension=0, tiled=True)]
    pallas_call x4 -> x5, Pallas kernels: 12.5 us -> 15.7 us  [the longest x2 8.56 us: outer(): pl.pallas_call(outer_kernel, grid=(1,), in_specs=[SCALARS, SCALARS] + [pl...]
  transfers between devices with their start and end apart: 33 -> 32, of which waited for: 13 -> 22; matrix products, arithmetic and copies ran while one was open for 0% -> 1% of each run, Pallas kernels for 9% -> 9%
where the time goes in v9:
time: 208 us; the launch traced here: 206 us
  waiting for transfers between devices  99.4 us (48%)
  starting transfers between devices  42.2 us (20%)
  Pallas kernels  35.2 us (17%)
  local copies, waits for them, and re-layouts  15.3 us (7%)
  between operations  14 us (7%)
    ppermute x26, waiting for transfers between devices, swap(): return lax.ppermute(piece, axis, [(j, j ^ bits) for j in range(size)])  69 us
    ppermute x26, starting transfers between devices, swap(): return lax.ppermute(piece, axis, [(j, j ^ bits) for j in range(size)])  24.3 us
    all_to_all x3, waiting for transfers between devices, scatter(): return lax.all_to_all(pieces, axis, split_axis=0, concat_axis=0, tiled=True)  19.3 us
    all_to_all x3, starting transfers between devices, scatter(): return lax.all_to_all(pieces, axis, split_axis=0, concat_axis=0, tiled=True)  17.9 us
    unnamed x78, local copies, waits for them, and re-layouts  14.1 us
    pallas_call x2, Pallas kernels, outer(): pl.pallas_call(outer_kernel, grid=(1,), in_specs=[SCALARS, SCALARS] + [pl...  8.56 us
    all_gather x1, waiting for transfers between devices, shards(): users = lax.all_gather(packed, 'item', axis=0)  6.67 us
    pallas_call x1, Pallas kernels, grads(): pl.pallas_call(functools.partial(grad_kernel, rows=rows, chunk=64, count=...  6.37 us
  transfers between devices with their start and end apart: 32, of which 22 were waited for; matrix products, arithmetic and copies ran while one was open for 1% of the time, Pallas kernels for 9%

profile of v9, /device:TPU:11, one launch (start us, length us, event | category | flops | bytes accessed | tf_op | source)
XLA Modules:
  0.0 206.2 jit_solution(3942232467069284252)
XLA Ops:
  7.2 1.7 shard_map.94
  9.3 4.3 %collective-permute-done.refs_1_._.refs_9_ = bf16[256,256]{1,0:T(8,128)(2,1)S(1)} collective-permute-done((bf16[256,256]{1,0:T(8,128)(2,1)}, bf16[256,256]{1,0:T(8,128)(2,1)S(1)}, u32[]{:S(2)}, u32[]{:S(2)}) %collective-permute-start) | collective-permute-done | bytes 131104 | tf_op jit(solution)/shard_map/ppermute | solution.py:40
  15.9 6.5 %all-to-all-start = ((bf16[8,256,256]{2,1,0:T(8,128)(2,1)}), bf16[8,256,256]{2,1,0:T(8,128)(2,1)S(1)}, u32[]{:S(2)}, u32[]{:S(2)}) async-start(bf16[8,256,256]{2,1,0:T(8,128)(2,1)} %shard_map.96), calls=%async_computation | async-start | bytes 2097152 | tf_op jit(solution)/shard_map/all_to_all | solution.py:359
  23.9 4.2 %collective-permute-done.2.refs_3_.refs_11_ = bf16[256,256]{1,0:T(8,128)(2,1)S(1)} collective-permute-done((bf16[256,256]{1,0:T(8,128)(2,1)S(1)}, bf16[256,256]{1,0:T(8,128)(2,1)S(1)}, u32[]{:S(2)}, u32[]{:S(2)}) %collective-permute-start.2) | collective-permute-done | bytes 131104 | tf_op jit(solution)/shard_map/ppermute | solution.py:40
  28.1 3.5 %collective-permute-done.1.refs_2_.refs_10_ = bf16[256,256]{1,0:T(8,128)(2,1)S(1)} collective-permute-done((bf16[256,256]{1,0:T(8,128)(2,1)S(1)}, bf16[256,256]{1,0:T(8,128)(2,1)S(1)}, u32[]{:S(2)}, u32[]{:S(2)}) %collective-permute-start.1) | collective-permute-done | bytes 131104 | tf_op jit(solution)/shard_map/ppermute | solution.py:40
  31.6 6.7 %all-gather.5.cloned.1.call-done = bf16[2176,256]{1,0:T(8,128)(2,1)} async-done(((bf16[272,256]{1,0:T(8,128)(2,1)}), bf16[2176,256]{1,0:T(8,128)(2,1)}) %all-gather.5.cloned.1.call-update) | async-done | bytes 1114128 | tf_op jit(solution)/shard_map/all_gather | solution.py:355
  39.5 4.1 %shard_map.95.refs_0_._ = f32[3,2048]{1,0:T(4,128)S(1)} custom-call(s32[4]{0:T(128)S(1)} %add_multiply_fusion.first_ref, bf16[8,272,256]{2,1,0:T(8,128)(2,1)S(1)} %bitcast.8, bf16[256,256]{1,0:T(8,128)(2,1)S(1)} %copy-done.7, bf16[256,256]{1,0:T(8,128)(2,1)S(1)} %collective-permute-done.refs_1_._.refs_9_, ...), custom_call_target="tpu_custom_call" | custom-call | flops 1024 | bytes 1024 | tf_op jit(solution)/shard_map/pallas_call | solution.py:117
  46.6 6.5 %collective-permute-start.7 = (f32[3,2048]{1,0:T(4,128)S(1)}, f32[3,2048]{1,0:T(4,128)}, u32[]{:S(2)}, u32[]{:S(2)}) collective-permute-start(f32[3,2048]{1,0:T(4,128)S(1)} %shard_map.95.refs_0_._), channel_id=1, source_target_pairs={{0,5},{1,4},{2,7},{3,6},{4,1},{5,0},{6,3},{7,2},{8,13},{9,12},{10,... | collective-permute-start | bytes 73736 | tf_op jit(solution)/shard_map/ppermute | solution.py:40
  53.5 3.0 %collective-permute-done.9.refs_7_ = f32[3,2048]{1,0:T(4,128)S(1)} collective-permute-done((f32[3,2048]{1,0:T(4,128)S(1)}, f32[3,2048]{1,0:T(4,128)S(1)}, u32[]{:S(2)}, u32[]{:S(2)}) %collective-permute-start.9) | collective-permute-done | bytes 24608 | tf_op jit(solution)/shard_map/ppermute | solution.py:40
  56.6 1.3 collective-permute-done.8.refs_6_
  62.4 6.4 %shard_map.97 = (f32[1,2048]{1,0:T(1,128)S(1)}, f32[2048,256]{1,0:T(8,128)S(1)}, f32[256,256]{1,0:T(8,128)S(1)}, f32[256,256]{1,0:T(8,128)S(1)}, f32[256,256]{1,0:T(8,128)S(1)}, /*index=5*/f32[256,256]{1,0:T(8,128)S(1)}) custom-call(s32[4]{0:T(128)S(1)} %add_multiply_fusion.first_ref, bf16[8,272,256]{2,1,0:T(8,128)(2,1)S(1)} %bitcast.9, ...), custom_call_target="tpu_custom_call" | custom-call | flops 1024 | bytes 1024 | tf_op jit(solution)/shard_map/pallas_call | solution.py:180
  68.8 1.3 copy-done.3
  74.1 5.2 %all-to-all-start.1 = ((bf16[8,256,256]{2,1,0:T(8,128)(2,1)}), bf16[8,256,256]{2,1,0:T(8,128)(2,1)S(1)}, u32[]{:S(2)}, u32[]{:S(2)}) async-start(bf16[8,256,256]{2,1,0:T(8,128)(2,1)} %shard_map.98), calls=%async_computation.1 | async-start | bytes 2097152 | tf_op jit(solution)/shard_map/all_to_all | solution.py:359
  82.0 5.0 %collective-permute-done.10.refs_1_ = f32[256,256]{1,0:T(8,128)S(1)} collective-permute-done((f32[256,256]{1,0:T(8,128)S(1)}, f32[256,256]{1,0:T(8,128)S(1)}, u32[]{:S(2)}, u32[]{:S(2)}) %collective-permute-start.10) | collective-permute-done | bytes 262176 | tf_op jit(solution)/shard_map/ppermute | solution.py:40
  87.0 6.4 %collective-permute-done.12.refs_3_ = f32[256,256]{1,0:T(8,128)S(1)} collective-permute-done((f32[256,256]{1,0:T(8,128)S(1)}, f32[256,256]{1,0:T(8,128)S(1)}, u32[]{:S(2)}, u32[]{:S(2)}) %collective-permute-start.12) | collective-permute-done | bytes 262176 | tf_op jit(solution)/shard_map/ppermute | solution.py:40
  94.1 2.1 %shard_map.99 = (bf16[128,256]{1,0:T(8,128)(2,1)}, bf16[128,256]{1,0:T(8,128)(2,1)}, bf16[128,256]{1,0:T(8,128)(2,1)}, bf16[128,256]{1,0:T(8,128)(2,1)}) custom-call(s32[1]{0:T(128)} %bitcast.5.me_ref, s32[2,256]{1,0:T(2,128)} %get-tuple-element.21.target_ref, f32[256,256]{1,0:T(8,128)} %copy-done.12, f32[256,256]{1,0:T(8,128)} %copy-done.30, ...), custom_call_target="tpu_custom_call" | custom-call | flops 1024 | bytes 1024 | tf_op jit(solution)/shard_map/pallas_call | solution.py:282
  96.8 2.0 collective-permute-start.15
  101.9 1.6 shard_map.100._.refs_0_
  103.6 13.4 %all-to-all-done.1.item_ref = bf16[8,256,256]{2,1,0:T(8,128)(2,1)S(1)} async-done(((bf16[8,256,256]{2,1,0:T(8,128)(2,1)}), bf16[8,256,256]{2,1,0:T(8,128)(2,1)S(1)}, u32[]{:S(2)}, u32[]{:S(2)}) %all-to-all-start.1) | async-done | bytes 1048608 | tf_op jit(solution)/shard_map/all_to_all | solution.py:359
  118.0 5.0 %shard_map.101.refs_1_ = bf16[4,2,8,128,256]{4,3,2,1,0:T(8,128)(2,1)} custom-call(bf16[8,272,256]{2,1,0:T(8,128)(2,1)} %bitcast.7, bf16[8,256,256]{2,1,0:T(8,128)(2,1)} %copy-done.2, bf16[8,256,256]{2,1,0:T(8,128)(2,1)} %copy-done.21, bf16[4,128,256]{2,1,0:T(8,128)(2,1)} %shard_map.100._.refs_0_), custom_call_target="tpu_custom_call" | custom-call | flops 1024 | bytes 1024 | tf_op jit(solution)/shard_map/pallas_call | solution.py:251
  123.0 4.3 %reduce-scatter.2.cloned.1.call-done.refs_0_ = f32[256,256]{1,0:T(8,128)} async-done(((f32[2048,256]{1,0:T(8,128)}), f32[256,256]{1,0:T(8,128)}) %reduce-scatter.2.cloned.1.call-update) | async-done | bytes 262160 | tf_op jit(solution)/shard_map/reduce_scatter | solution.py:367
  127.4 1.9 shard_map.102
  133.4 2.4 %collective-permute-done.18.refs_3_ = bf16[128,256]{1,0:T(8,128)(2,1)S(1)} collective-permute-done((bf16[128,256]{1,0:T(8,128)(2,1)}, bf16[128,256]{1,0:T(8,128)(2,1)S(1)}, u32[]{:S(2)}, u32[]{:S(2)}) %collective-permute-start.18) | collective-permute-done | bytes 65568 | tf_op jit(solution)/shard_map/ppermute | solution.py:40
  136.5 1.7 shard_map.103
  138.2 6.2 %all-to-all-start.2 = ((bf16[4,2,8,128,256]{4,3,2,1,0:T(8,128)(2,1)}), bf16[4,2,8,128,256]{4,3,2,1,0:T(8,128)(2,1)}, u32[]{:S(2)}, u32[]{:S(2)}) async-start(bf16[4,2,8,128,256]{4,3,2,1,0:T(8,128)(2,1)} %shard_map.101.refs_1_), calls=%async_computation.2 | async-start | bytes 8388608 | tf_op jit(solution)/shard_map/all_to_all | solution.py:359
  144.7 2.3 %collective-permute-start.19 = (bf16[4,128,256]{2,1,0:T(8,128)(2,1)S(1)}, bf16[4,128,256]{2,1,0:T(8,128)(2,1)S(1)}, u32[]{:S(2)}, u32[]{:S(2)}) collective-permute-start(bf16[4,128,256]{2,1,0:T(8,128)(2,1)S(1)} %copy-done.22), channel_id=1, source_target_pairs={{0,2},{1,3},{2,0},{3,1},{4,6},{5,7},{6,4},{7,5},{8,10},{9,11},{10,... | collective-permute-start | bytes 786440 | tf_op jit(solution)/shard_map/ppermute | solution.py:40
  147.0 1.6 collective-permute-start.22
  148.6 26.6 %collective-permute-done.21.refs_3_ = bf16[4,128,256]{2,1,0:T(8,128)(2,1)S(1)} collective-permute-done((bf16[4,128,256]{2,1,0:T(8,128)(2,1)S(1)}, bf16[4,128,256]{2,1,0:T(8,128)(2,1)S(1)}, u32[]{:S(2)}, u32[]{:S(2)}) %collective-permute-start.21) | collective-permute-done | bytes 262176 | tf_op jit(solution)/shard_map/ppermute | solution.py:40
  176.0 7.2 %collective-permute-done.20.refs_2_ = bf16[4,128,256]{2,1,0:T(8,128)(2,1)S(1)} collective-permute-done((bf16[4,128,256]{2,1,0:T(8,128)(2,1)S(1)}, bf16[4,128,256]{2,1,0:T(8,128)(2,1)S(1)}, u32[]{:S(2)}, u32[]{:S(2)}) %collective-permute-start.20) | collective-permute-done | bytes 262176 | tf_op jit(solution)/shard_map/ppermute | solution.py:40
  185.2 5.9 %all-to-all-done.2.hidden_ref = bf16[4,2,8,128,256]{4,3,2,1,0:T(8,128)(2,1)} async-done(((bf16[4,2,8,128,256]{4,3,2,1,0:T(8,128)(2,1)}), bf16[4,2,8,128,256]{4,3,2,1,0:T(8,128)(2,1)}, u32[]{:S(2)}, u32[]{:S(2)}) %all-to-all-start.2) | async-done | bytes 4194336 | tf_op jit(solution)/shard_map/all_to_all | solution.py:359
  191.1 4.2 %shard_map.105 = f32[8,256,256]{2,1,0:T(8,128)} custom-call(s32[8]{0:T(128)} %xor.40.order_ref, s32[1]{0:T(128)} %bitcast.5.me_ref, bf16[4,2,8,128,256]{4,3,2,1,0:T(8,128)(2,1)} %all-to-all-done.2.hidden_ref, bf16[4,128,256]{2,1,0:T(8,128)(2,1)} %shard_map.100._.refs_0_, bf16[4,128,256]{2,1,0:T(8,128)(2,1)} %copy-done.25, bf16[4,128,256]{2,1,0:T(8,128)(2,1)} %copy-done.24, ...), custom_call_target="tpu_custom_call" | custom-call | flops 1024 | bytes 1024 | tf_op jit(solution)/shard_map/pallas_call | solution.py:327
  195.4 4.3 %shard_map.104 = f32[8,256,256]{2,1,0:T(8,128)} custom-call(s32[8]{0:T(128)} %xor.40.order_ref, s32[1]{0:T(128)} %bitcast.5.me_ref, bf16[4,2,8,128,256]{4,3,2,1,0:T(8,128)(2,1)} %all-to-all-done.2.hidden_ref, bf16[8,4,128,256]{3,2,1,0:T(8,128)(2,1)} %bitcast.10), custom_call_target="tpu_custom_call" | custom-call | flops 1024 | bytes 1024 | tf_op jit(solution)/shard_map/pallas_call | solution.py:327
  (131 shorter events, 33.1 us)
Async XLA Ops:
  7.2 31.1 %all-gather.5.cloned.1.call-start = ((), (), s32[]{:S(2)}) async-start(), calls=%async_computation.5 | async-start | bytes 1253376 | tf_op jit(solution)/shard_map/all_gather | solution.py:355
  9.0 4.6 %collective-permute-start = (bf16[256,256]{1,0:T(8,128)(2,1)}, bf16[256,256]{1,0:T(8,128)(2,1)S(1)}, u32[]{:S(2)}, u32[]{:S(2)}) collective-permute-start(bf16[256,256]{1,0:T(8,128)(2,1)} %refs_8_.1), channel_id=1, source_target_pairs={{0,8},{8,0},{16,24},{24,16},{1,9},{9,1},{17,25},{25,17},{2,10},{10... | collective-permute-start | bytes 393224 | tf_op jit(solution)/shard_map/ppermute | solution.py:40
  15.9 43.0 %all-to-all-start = ((bf16[8,256,256]{2,1,0:T(8,128)(2,1)}), bf16[8,256,256]{2,1,0:T(8,128)(2,1)S(1)}, u32[]{:S(2)}, u32[]{:S(2)}) async-start(bf16[8,256,256]{2,1,0:T(8,128)(2,1)} %shard_map.96), calls=%async_computation | async-start | bytes 2097152 | tf_op jit(solution)/shard_map/all_to_all | solution.py:359
  22.4 105.0 %reduce-scatter.2.cloned.1.call-start = ((), (), s32[]{:S(2)}) async-start(), calls=%async_computation.4 | async-start | bytes 2359296 | tf_op jit(solution)/shard_map/reduce_scatter | solution.py:367
  22.4 5.7 %collective-permute-start.2 = (bf16[256,256]{1,0:T(8,128)(2,1)S(1)}, bf16[256,256]{1,0:T(8,128)(2,1)S(1)}, u32[]{:S(2)}, u32[]{:S(2)}) collective-permute-start(bf16[256,256]{1,0:T(8,128)(2,1)S(1)} %copy-done.7), channel_id=1, source_target_pairs={{0,24},{8,16},{16,8},{24,0},{1,25},{9,17},{17,9},{25,1},{2,26},{10... | collective-permute-start | bytes 393224 | tf_op jit(solution)/shard_map/ppermute | solution.py:40
  23.7 7.9 %collective-permute-start.1 = (bf16[256,256]{1,0:T(8,128)(2,1)S(1)}, bf16[256,256]{1,0:T(8,128)(2,1)S(1)}, u32[]{:S(2)}, u32[]{:S(2)}) collective-permute-start(bf16[256,256]{1,0:T(8,128)(2,1)S(1)} %copy-done.7), channel_id=1, source_target_pairs={{0,16},{8,24},{16,0},{24,8},{1,17},{9,25},{17,1},{25,9},{2,18},{10... | collective-permute-start | bytes 393224 | tf_op jit(solution)/shard_map/ppermute | solution.py:40
  45.0 11.6 %collective-permute-start.9 = (f32[3,2048]{1,0:T(4,128)S(1)}, f32[3,2048]{1,0:T(4,128)S(1)}, u32[]{:S(2)}, u32[]{:S(2)}) collective-permute-start(f32[3,2048]{1,0:T(4,128)S(1)} %shard_map.95.refs_0_._), channel_id=1, source_target_pairs={{0,7},{1,6},{2,5},{3,4},{4,3},{5,2},{6,1},{7,0},{8,15},{9,14},{10,... | collective-permute-start | bytes 73736 | tf_op jit(solution)/shard_map/ppermute | solution.py:40
  46.3 11.6 %collective-permute-start.8 = (f32[3,2048]{1,0:T(4,128)S(1)}, f32[3,2048]{1,0:T(4,128)S(1)}, u32[]{:S(2)}, u32[]{:S(2)}) collective-permute-start(f32[3,2048]{1,0:T(4,128)S(1)} %shard_map.95.refs_0_._), channel_id=1, source_target_pairs={{0,6},{1,7},{2,4},{3,5},{4,2},{5,3},{6,0},{7,1},{8,14},{9,15},{10,... | collective-permute-start | bytes 73736 | tf_op jit(solution)/shard_map/ppermute | solution.py:40
  46.6 12.3 %collective-permute-start.7 = (f32[3,2048]{1,0:T(4,128)S(1)}, f32[3,2048]{1,0:T(4,128)}, u32[]{:S(2)}, u32[]{:S(2)}) collective-permute-start(f32[3,2048]{1,0:T(4,128)S(1)} %shard_map.95.refs_0_._), channel_id=1, source_target_pairs={{0,5},{1,4},{2,7},{3,6},{4,1},{5,0},{6,3},{7,2},{8,13},{9,12},{10,... | collective-permute-start | bytes 73736 | tf_op jit(solution)/shard_map/ppermute | solution.py:40
  53.1 5.8 %collective-permute-start.6 = (f32[3,2048]{1,0:T(4,128)S(1)}, f32[3,2048]{1,0:T(4,128)}, u32[]{:S(2)}, u32[]{:S(2)}) collective-permute-start(f32[3,2048]{1,0:T(4,128)S(1)} %shard_map.95.refs_0_._), channel_id=1, source_target_pairs={{0,4},{1,5},{2,6},{3,7},{4,0},{5,1},{6,2},{7,3},{8,12},{9,13},{10,... | collective-permute-start | bytes 73736 | tf_op jit(solution)/shard_map/ppermute | solution.py:40
  53.1 5.8 %collective-permute-start.5 = (f32[3,2048]{1,0:T(4,128)S(1)}, f32[3,2048]{1,0:T(4,128)}, u32[]{:S(2)}, u32[]{:S(2)}) collective-permute-start(f32[3,2048]{1,0:T(4,128)S(1)} %shard_map.95.refs_0_._), channel_id=1, source_target_pairs={{0,3},{1,2},{2,1},{3,0},{4,7},{5,6},{6,5},{7,4},{8,11},{9,10},{10,... | collective-permute-start | bytes 73736 | tf_op jit(solution)/shard_map/ppermute | solution.py:40
  56.6 2.9 %collective-permute-start.4 = (f32[3,2048]{1,0:T(4,128)S(1)}, f32[3,2048]{1,0:T(4,128)}, u32[]{:S(2)}, u32[]{:S(2)}) collective-permute-start(f32[3,2048]{1,0:T(4,128)S(1)} %shard_map.95.refs_0_._), channel_id=1, source_target_pairs={{0,2},{1,3},{2,0},{3,1},{4,6},{5,7},{6,4},{7,5},{8,10},{9,11},{10,... | collective-permute-start | bytes 73736 | tf_op jit(solution)/shard_map/ppermute | solution.py:40
  58.5 1.4 collective-permute-start.3
  74.1 42.9 %all-to-all-start.1 = ((bf16[8,256,256]{2,1,0:T(8,128)(2,1)}), bf16[8,256,256]{2,1,0:T(8,128)(2,1)S(1)}, u32[]{:S(2)}, u32[]{:S(2)}) async-start(bf16[8,256,256]{2,1,0:T(8,128)(2,1)} %shard_map.98), calls=%async_computation.1 | async-start | bytes 2097152 | tf_op jit(solution)/shard_map/all_to_all | solution.py:359
  79.3 116.1 %all-gather.7.cloned.1.call-start = ((), (), s32[]{:S(2)}) async-start(), calls=%async_computation.6 | async-start | bytes 2359296 | tf_op jit(solution)/shard_map/all_gather | solution.py:378
  79.3 7.7 %collective-permute-start.10 = (f32[256,256]{1,0:T(8,128)S(1)}, f32[256,256]{1,0:T(8,128)S(1)}, u32[]{:S(2)}, u32[]{:S(2)}) collective-permute-start(f32[256,256]{1,0:T(8,128)S(1)} %copy-done.20), channel_id=1, source_target_pairs={{0,8},{8,0},{16,24},{24,16},{1,9},{9,1},{17,25},{25,17},{2,10},{10... | collective-permute-start | bytes 786440 | tf_op jit(solution)/shard_map/ppermute | solution.py:40
  79.6 7.4 %collective-permute-start.11 = (f32[256,256]{1,0:T(8,128)S(1)}, f32[256,256]{1,0:T(8,128)S(1)}, u32[]{:S(2)}, u32[]{:S(2)}) collective-permute-start(f32[256,256]{1,0:T(8,128)S(1)} %copy-done.18), channel_id=1, source_target_pairs={{0,16},{8,24},{16,0},{24,8},{1,17},{9,25},{17,1},{25,9},{2,18},{10... | collective-permute-start | bytes 786440 | tf_op jit(solution)/shard_map/ppermute | solution.py:40
  80.8 12.6 %collective-permute-start.12 = (f32[256,256]{1,0:T(8,128)S(1)}, f32[256,256]{1,0:T(8,128)S(1)}, u32[]{:S(2)}, u32[]{:S(2)}) collective-permute-start(f32[256,256]{1,0:T(8,128)S(1)} %copy-done.16), channel_id=1, source_target_pairs={{0,24},{8,16},{16,8},{24,0},{1,25},{9,17},{17,9},{25,1},{2,26},{10... | collective-permute-start | bytes 786440 | tf_op jit(solution)/shard_map/ppermute | solution.py:40
  96.2 3.7 %collective-permute-start.13 = (bf16[128,256]{1,0:T(8,128)(2,1)}, bf16[128,256]{1,0:T(8,128)(2,1)S(1)}, u32[]{:S(2)}, u32[]{:S(2)}) collective-permute-start(bf16[128,256]{1,0:T(8,128)(2,1)} %get-tuple-element.27), channel_id=1, source_target_pairs={{0,8},{8,0},{16,24},{24,16},{1,9},{9,1},{17,25},{25,17},{2,10},{10... | collective-permute-start | bytes 196616 | tf_op jit(solution)/shard_map/ppermute | solution.py:40
  96.6 3.7 %collective-permute-start.14 = (bf16[128,256]{1,0:T(8,128)(2,1)}, bf16[128,256]{1,0:T(8,128)(2,1)S(1)}, u32[]{:S(2)}, u32[]{:S(2)}) collective-permute-start(bf16[128,256]{1,0:T(8,128)(2,1)} %get-tuple-element.28), channel_id=1, source_target_pairs={{0,16},{8,24},{16,0},{24,8},{1,17},{9,25},{17,1},{25,9},{2,18},{10... | collective-permute-start | bytes 196616 | tf_op jit(solution)/shard_map/ppermute | solution.py:40
  96.8 4.5 %collective-permute-start.15 = (bf16[128,256]{1,0:T(8,128)(2,1)}, bf16[128,256]{1,0:T(8,128)(2,1)S(1)}, u32[]{:S(2)}, u32[]{:S(2)}) collective-permute-start(bf16[128,256]{1,0:T(8,128)(2,1)} %get-tuple-element.29), channel_id=1, source_target_pairs={{0,24},{8,16},{16,8},{24,0},{1,25},{9,17},{17,9},{25,1},{2,26},{10... | collective-permute-start | bytes 196616 | tf_op jit(solution)/shard_map/ppermute | solution.py:40
  129.2 3.9 %collective-permute-start.16 = (bf16[128,256]{1,0:T(8,128)(2,1)}, bf16[128,256]{1,0:T(8,128)(2,1)S(1)}, u32[]{:S(2)}, u32[]{:S(2)}) collective-permute-start(bf16[128,256]{1,0:T(8,128)(2,1)} %get-tuple-element.32), channel_id=1, source_target_pairs={{0,8},{8,0},{16,24},{24,16},{1,9},{9,1},{17,25},{25,17},{2,10},{10... | collective-permute-start | bytes 196616 | tf_op jit(solution)/shard_map/ppermute | solution.py:40
  129.5 3.9 %collective-permute-start.17 = (bf16[128,256]{1,0:T(8,128)(2,1)}, bf16[128,256]{1,0:T(8,128)(2,1)S(1)}, u32[]{:S(2)}, u32[]{:S(2)}) collective-permute-start(bf16[128,256]{1,0:T(8,128)(2,1)} %get-tuple-element.33), channel_id=1, source_target_pairs={{0,16},{8,24},{16,0},{24,8},{1,17},{9,25},{17,1},{25,9},{2,18},{10... | collective-permute-start | bytes 196616 | tf_op jit(solution)/shard_map/ppermute | solution.py:40
  130.7 5.1 %collective-permute-start.18 = (bf16[128,256]{1,0:T(8,128)(2,1)}, bf16[128,256]{1,0:T(8,128)(2,1)S(1)}, u32[]{:S(2)}, u32[]{:S(2)}) collective-permute-start(bf16[128,256]{1,0:T(8,128)(2,1)} %get-tuple-element.34), channel_id=1, source_target_pairs={{0,24},{8,16},{16,8},{24,0},{1,25},{9,17},{17,9},{25,1},{2,26},{10... | collective-permute-start | bytes 196616 | tf_op jit(solution)/shard_map/ppermute | solution.py:40
  138.2 52.9 %all-to-all-start.2 = ((bf16[4,2,8,128,256]{4,3,2,1,0:T(8,128)(2,1)}), bf16[4,2,8,128,256]{4,3,2,1,0:T(8,128)(2,1)}, u32[]{:S(2)}, u32[]{:S(2)}) async-start(bf16[4,2,8,128,256]{4,3,2,1,0:T(8,128)(2,1)} %shard_map.101.refs_1_), calls=%async_computation.2 | async-start | bytes 8388608 | tf_op jit(solution)/shard_map/all_to_all | solution.py:359
  144.3 30.9 %collective-permute-start.21 = (bf16[4,128,256]{2,1,0:T(8,128)(2,1)S(1)}, bf16[4,128,256]{2,1,0:T(8,128)(2,1)S(1)}, u32[]{:S(2)}, u32[]{:S(2)}) collective-permute-start(bf16[4,128,256]{2,1,0:T(8,128)(2,1)S(1)} %copy-done.22), channel_id=1, source_target_pairs={{0,6},{1,7},{2,4},{3,5},{4,2},{5,3},{6,0},{7,1},{8,14},{9,15},{10,... | collective-permute-start | bytes 786440 | tf_op jit(solution)/shard_map/ppermute | solution.py:40
  144.3 38.8 %collective-permute-start.20 = (bf16[4,128,256]{2,1,0:T(8,128)(2,1)S(1)}, bf16[4,128,256]{2,1,0:T(8,128)(2,1)S(1)}, u32[]{:S(2)}, u32[]{:S(2)}) collective-permute-start(bf16[4,128,256]{2,1,0:T(8,128)(2,1)S(1)} %copy-done.22), channel_id=1, source_target_pairs={{0,4},{1,5},{2,6},{3,7},{4,0},{5,1},{6,2},{7,3},{8,12},{9,13},{10,... | collective-permute-start | bytes 786440 | tf_op jit(solution)/shard_map/ppermute | solution.py:40
  144.7 39.0 %collective-permute-start.19 = (bf16[4,128,256]{2,1,0:T(8,128)(2,1)S(1)}, bf16[4,128,256]{2,1,0:T(8,128)(2,1)S(1)}, u32[]{:S(2)}, u32[]{:S(2)}) collective-permute-start(bf16[4,128,256]{2,1,0:T(8,128)(2,1)S(1)} %copy-done.22), channel_id=1, source_target_pairs={{0,2},{1,3},{2,0},{3,1},{4,6},{5,7},{6,4},{7,5},{8,10},{9,11},{10,... | collective-permute-start | bytes 786440 | tf_op jit(solution)/shard_map/ppermute | solution.py:40
  147.0 38.0 %collective-permute-start.22 = (bf16[4,128,256]{2,1,0:T(8,128)(2,1)S(1)}, bf16[4,128,256]{2,1,0:T(8,128)(2,1)S(1)}, u32[]{:S(2)}, u32[]{:S(2)}) collective-permute-start(bf16[4,128,256]{2,1,0:T(8,128)(2,1)S(1)} %copy-done.22), channel_id=1, source_target_pairs={{0,1},{1,0},{2,3},{3,2},{4,5},{5,4},{6,7},{7,6},{8,9},{9,8},{10,11... | collective-permute-start | bytes 786440 | tf_op jit(solution)/shard_map/ppermute | solution.py:40
  175.2 9.8 %collective-permute-start.25 = (bf16[4,128,256]{2,1,0:T(8,128)(2,1)S(1)}, bf16[4,128,256]{2,1,0:T(8,128)(2,1)S(1)}, u32[]{:S(2)}, u32[]{:S(2)}) collective-permute-start(bf16[4,128,256]{2,1,0:T(8,128)(2,1)S(1)} %collective-permute-done.21.refs_3_), channel_id=1, source_target_pairs={{0,1},{1,0},{2,3},{3,2},{4,5},{5,4},{6,7},{7,6},{8,9},{9,8},{10,11... | collective-permute-start | bytes 786440 | tf_op jit(solution)/shard_map/ppermute | solution.py:40
  183.2 1.9 collective-permute-start.24
  183.7 1.5 collective-permute-start.23
  (39 other events, 216.0 us)
Sparse Core Ops, SparseCore 0:
  10.2 28.0 all-gather.4
  73.1 54.2 reduce-scatter.1
  138.3 42.6 all-gather.6

commit v10 on v9

--- a/solution.py
+++ b/solution.py
@@ -22,6 +22,8 @@
 SCALARS = pl.BlockSpec(memory_space=pltpu.SMEM)
 WHOLE = pl.BlockSpec(memory_space=pltpu.VMEM)
 ANYWHERE = pl.BlockSpec(memory_space=pl.ANY)
+VMEM = 60 * MIB
+LARGE = pl.CostEstimate(flops=1 << 36, bytes_accessed=1 << 28, transcendentals=0)
 SMALL = pl.CostEstimate(flops=1024, bytes_accessed=1024, transcendentals=0)
 
 
@@ -75,6 +77,7 @@
             jax.ShapeDtypeStruct((rows + EXTRA, width), BF16),
             jax.ShapeDtypeStruct((2, rows), jnp.int32),
         ],
+        compiler_params=pltpu.CompilerParams(vmem_limit_bytes=VMEM),
         cost_estimate=SMALL,
     )(emb, positive.reshape(1, rows), user_expert.reshape(1, rows), item_expert.reshape(1, rows))
 
@@ -123,7 +126,7 @@
         out_specs=pl.BlockSpec((3, pair * rows), lambda b: (0, b)),
         out_shape=jax.ShapeDtypeStruct((3, blocks * rows), F32),
         scratch_shapes=[pltpu.VMEM((pair, n_cols, rows), F32)],
-        compiler_params=pltpu.CompilerParams(vmem_limit_bytes=40 * MIB),
+        compiler_params=pltpu.CompilerParams(vmem_limit_bytes=VMEM),
         cost_estimate=SMALL,
     )(first, users, *items, after)
 
@@ -202,7 +205,7 @@
             pltpu.VMEM((pair, n_cols, rows), BF16),
             pltpu.VMEM((emb, n_cols), BF16),
         ],
-        compiler_params=pltpu.CompilerParams(vmem_limit_bytes=48 * MIB),
+        compiler_params=pltpu.CompilerParams(vmem_limit_bytes=VMEM),
         cost_estimate=SMALL,
     )(first, users, *gathered, *items, after)
     return results[0], results[1], results[2:]
@@ -221,7 +224,7 @@
         in_specs=[WHOLE, ANYWHERE],
         out_specs=WHOLE,
         out_shape=jax.ShapeDtypeStruct((parts, rows, total // parts), BF16),
-        compiler_params=pltpu.CompilerParams(vmem_limit_bytes=24 * MIB),
+        compiler_params=pltpu.CompilerParams(vmem_limit_bytes=VMEM),
         cost_estimate=SMALL,
     )(hidden, after)
 
@@ -233,34 +236,45 @@
     return (place == target).astype(F32).astype(BF16)
 
 
-def hidden_kernel(users_ref, user_ref, item_ref, _, out_ref):
-    groups, _, pair, span, _ = out_ref.shape
+def hidden_kernel(me_ref, users_ref, hidden_ref, _, *out_refs, tower):
+    count, (pair, span, _) = len(out_refs), out_refs[0].shape[-3:]
+    groups = out_refs[0].shape[0] if count == 1 else count
+    me = 0 if count == 1 else me_ref[0]
     for half in range(pair):
-        for tower, hidden_ref in enumerate((user_ref, item_ref)):
-            onehot = onehot_of(number(users_ref[half], 1 + tower), 0, groups)
-            moved = mm(onehot, hidden_ref[half], 1, 0).astype(BF16)
-            for k in range(groups):
-                out_ref[k, tower, half] = moved[k * span : (k + 1) * span, :]
-
-
-def slot_hidden(users, user_hidden, item_hidden, groups, after):
-    blocks, rows, width = user_hidden.shape
+        onehot = onehot_of(number(users_ref[half], 1 + tower), me, groups)
+        moved = mm(onehot, hidden_ref[half], 1, 0).astype(BF16)
+        for k in range(groups):
+            part = moved[k * span : (k + 1) * span, :]
+            if count == 1:
+                out_refs[0][k, half] = part
+            else:
+                out_refs[k][half] = part
+
+
+def slot_hidden(me, users, hidden, groups, tower, apart, after):
+    blocks, rows, width = hidden.shape
     span = EXPERTS * CAP // groups
     pair = 2
-    half = pl.BlockSpec((pair, rows, width), lambda b: (b, 0, 0))
-    return pl.pallas_call(
-        hidden_kernel,
+    if apart:
+        out_specs = [pl.BlockSpec((pair, span, width), lambda b: (b, 0, 0))] * groups
+        out_shape = [jax.ShapeDtypeStruct((blocks, span, width), BF16)] * groups
+    else:
+        out_specs = [pl.BlockSpec((groups, pair, span, width), lambda b: (0, b, 0, 0))]
+        out_shape = [jax.ShapeDtypeStruct((groups, blocks, span, width), BF16)]
+    return pl.pallas_call(
+        functools.partial(hidden_kernel, tower=tower),
         grid=(blocks // pair,),
         in_specs=[
+            SCALARS,
             pl.BlockSpec((pair, EXTRA, rows), lambda b: (b, rows // EXTRA, 0)),
-            half,
-            half,
+            pl.BlockSpec((pair, rows, width), lambda b: (b, 0, 0)),
             ANYWHERE,
         ],
-        out_specs=pl.BlockSpec((groups, 2, pair, span, width), lambda b: (0, 0, b, 0, 0)),
-        out_shape=jax.ShapeDtypeStruct((groups, 2, blocks, span, width), BF16),
-        cost_estimate=SMALL,
-    )(users, user_hidden, item_hidden, after)
+        out_specs=out_specs,
+        out_shape=out_shape,
+        compiler_params=pltpu.CompilerParams(vmem_limit_bytes=VMEM),
+        cost_estimate=SMALL,
+    )(me, users, hidden, after)
 
 
 def route_kernel(me_ref, target_ref, *refs, tower, count, order):
@@ -284,6 +298,7 @@
         in_specs=[SCALARS] + [WHOLE] * (1 + len(pieces)) + [ANYWHERE] * len(after),
         out_specs=[WHOLE] * groups,
         out_shape=[jax.ShapeDtypeStruct((span, emb), BF16)] * groups,
+        compiler_params=pltpu.CompilerParams(vmem_limit_bytes=VMEM),
         cost_estimate=SMALL,
     )(me, targets, *pieces, *after)
 
@@ -299,42 +314,46 @@
         in_specs=[WHOLE] * len(pieces) + [ANYWHERE] * len(after),
         out_specs=WHOLE,
         out_shape=jax.ShapeDtypeStruct((len(pieces),) + pieces[0].shape, pieces[0].dtype),
+        compiler_params=pltpu.CompilerParams(vmem_limit_bytes=VMEM),
         cost_estimate=SMALL,
     )(*pieces, *after)
 
 
-def outer_kernel(order_ref, me_ref, hidden_ref, *refs):
-    grad_refs, out_ref = refs[:-1], refs[-1]
-    groups, _, blocks, span, _ = hidden_ref.shape
+def outer_kernel(order_ref, me_ref, *refs, count):
+    hidden_refs, grad_refs, out_ref = refs[:count], refs[count:-1], refs[-1]
+    blocks, span, _ = hidden_refs[0].shape[-3:]
+    groups = hidden_refs[0].shape[0] if count == 1 else count
     for e in range(span // CAP):
         here = slice(e * CAP, (e + 1) * CAP)
         left, right = [], []
         for j in range(blocks):
+            block = j if len(grad_refs) == 1 else order_ref[j]
             for k in range(groups):
+                if count == 1:
+                    left.append(hidden_refs[0][me_ref[0] ^ k, block, here, :])
+                else:
+                    left.append(hidden_refs[k][block, here, :])
                 if len(grad_refs) == 1:
-                    left.append(hidden_ref[me_ref[0] ^ k, 0, j, here, :])
                     right.append(grad_refs[0][j, k, here, :])
                 else:
-                    left.append(hidden_ref[me_ref[0] ^ k, 0, order_ref[j], here, :])
                     right.append(grad_refs[j][k, here, :])
         out_ref[e] = mm(jnp.concatenate(left), jnp.concatenate(right), 0, 0)
 
 
-def outer(order, me, hidden, grads, tower):
-    groups, _, blocks, span, width = hidden.shape
+def outer(order, me, hidden, grads, cost):
+    span, width = hidden[0].shape[-2:]
     emb = grads[0].shape[-1]
     own = span // CAP
     return pl.pallas_call(
-        outer_kernel,
+        functools.partial(outer_kernel, count=len(hidden)),
         grid=(1,),
         in_specs=[SCALARS, SCALARS]
-        + [pl.BlockSpec((groups, 1, blocks, span, width), lambda _: (0, tower, 0, 0, 0))]
-        + [pl.BlockSpec(g.shape, lambda _, d=g.ndim: (0,) * d) for g in grads],
+        + [pl.BlockSpec(g.shape, lambda _, d=g.ndim: (0,) * d) for g in hidden + grads],
         out_specs=pl.BlockSpec((own, width, emb), lambda _: (0, 0, 0)),
         out_shape=jax.ShapeDtypeStruct((own, width, emb), F32),
-        compiler_params=pltpu.CompilerParams(vmem_limit_bytes=56 * MIB),
-        cost_estimate=SMALL,
-    )(order, me, hidden, *grads)
+        compiler_params=pltpu.CompilerParams(vmem_limit_bytes=VMEM),
+        cost_estimate=cost,
+    )(order, me, *hidden, *grads)
 
 
 def shards(user_emb, item_emb, user_hidden, item_hidden, user_expert, item_expert, positive):
@@ -370,14 +389,16 @@
     item_routed = route(me, targets, item_pieces, 1, groups, [])
     item_sent = stack(exchange(item_routed, "user"))
     item_line = exchange([item_sent] * lines, "item", CORES)
-    hidden_slots = slot_hidden(users, user_cols, item_cols, groups, item_sent)
-    hidden_rows = scatter(hidden_slots, "user")
-    user_routed = route(me, targets, [user_grad], 0, groups, [hidden_slots])
+    user_slots = slot_hidden(me, users, user_cols, groups, 0, True, item_routed[0])
+    user_rows = exchange(user_slots, "user")
+    item_slots = slot_hidden(me, users, item_cols, groups, 1, False, item_sent)
+    item_rows = [scatter(item_slots[0], "user")]
+    user_routed = route(me, targets, [user_grad], 0, groups, [item_slots[0]] + user_rows[1:])
     user_sent = stack(exchange(user_routed, "user"))
     item_cross = item_line + [swap(piece, "item", 1) for piece in item_line]
     user_all = lax.all_gather(user_sent, "item", axis=0)
-    item_weight_grad = outer(order, me, hidden_rows, item_cross, 1)
-    user_weight_grad = outer(order, me, hidden_rows, [user_all], 0)
+    item_weight_grad = outer(order, me, item_rows, item_cross, LARGE)
+    user_weight_grad = outer(order, me, user_rows, [user_all], SMALL)
     return (row_loss, user_weight_grad, item_weight_grad)
 
 

time: 208 us -> 231 us (1.11)
  waiting for transfers between devices: 99.4 us -> 120 us
  Pallas kernels: 35.2 us -> 44.1 us
  local copies, waits for them, and re-layouts: 15.3 us -> 8.21 us
    all_gather x1, waiting for transfers between devices: 0.01 us -> 28.9 us  [shards(): user_all = lax.all_gather(user_sent, 'item', axis=0)]
    unnamed x78 -> x64, local copies, waits for them, and re-layouts: 14.1 us -> 6.39 us
    all_to_all x3, waiting for transfers between devices: 19.3 us -> 13.9 us  [scatter(): return lax.all_to_all(pieces, axis, split_axis=0, concat_axis=0, tiled=True)]
    reduce_scatter x1, waiting for transfers between devices: 4.34 us -> 0.01 us  [shards(): lax.psum_scatter(user_part, 'item', scatter_dimension=0, tiled=True)]
    ppermute x26 -> x29, starting transfers between devices: 24.3 us -> 28.1 us  [swap(): return lax.ppermute(piece, axis, [(j, j ^ bits) for j in range(size)])]
    all_to_all x3, starting transfers between devices: 17.9 us -> 14.3 us  [scatter(): return lax.all_to_all(pieces, axis, split_axis=0, concat_axis=0, tiled=True)]
    pallas_call x3 -> x4, Pallas kernels: 13.6 us -> 16.8 us  [the longest x2 8.56 us: outer(): pl.pallas_call(functools.partial(outer_kernel, count=len(hidden)), grid=(...]
    all_gather x1, waiting for transfers between devices: 6.67 us -> 9.51 us  [shards(): users = lax.all_gather(packed, 'item', axis=0)]
  transfers between devices with their start and end apart: 32 -> 35, of which waited for: 22 -> 21; matrix products, arithmetic and copies ran while one was open for 1% -> 1% of each run, Pallas kernels for 9% -> 13%
where the time goes in v10:
time: 231 us; the launch traced here: 230 us
  waiting for transfers between devices  120 us (52%)
  Pallas kernels  44.1 us (19%)
  starting transfers between devices  42.5 us (18%)
  between operations  14 us (6%)
  local copies, waits for them, and re-layouts  8.21 us (4%)
    ppermute x29, waiting for transfers between devices, swap(): return lax.ppermute(piece, axis, [(j, j ^ bits) for j in range(size)])  68 us
    all_gather x1, waiting for transfers between devices, shards(): user_all = lax.all_gather(user_sent, 'item', axis=0)  28.9 us
    ppermute x29, starting transfers between devices, swap(): return lax.ppermute(piece, axis, [(j, j ^ bits) for j in range(size)])  28.1 us
    all_to_all x3, starting transfers between devices, scatter(): return lax.all_to_all(pieces, axis, split_axis=0, concat_axis=0, tiled=True)  14.3 us
    all_to_all x3, waiting for transfers between devices, scatter(): return lax.all_to_all(pieces, axis, split_axis=0, concat_axis=0, tiled=True)  13.9 us
    all_gather x1, waiting for transfers between devices, shards(): users = lax.all_gather(packed, 'item', axis=0)  9.51 us
    pallas_call x2, Pallas kernels, outer(): pl.pallas_call(functools.partial(outer_kernel, count=len(hidden)), grid=(...  8.56 us
    pallas_call x2, Pallas kernels, slot_hidden(): pl.pallas_call(functools.partial(hidden_kernel, tower=tower), grid=(block...  8.22 us
  transfers between devices with their start and end apart: 35, of which 21 were waited for; matrix products, arithmetic and copies ran while one was open for 1% of the time, Pallas kernels for 13%

profile of v10, /device:TPU:11, one launch (start us, length us, event | category | flops | bytes accessed | tf_op | source)
XLA Modules:
  0.0 229.5 jit_solution(18378852874984955670)
XLA Ops:
  7.2 1.7 shard_map.94
  9.3 4.3 %collective-permute-done.refs_1_._.refs_9_ = bf16[256,256]{1,0:T(8,128)(2,1)S(1)} collective-permute-done((bf16[256,256]{1,0:T(8,128)(2,1)}, bf16[256,256]{1,0:T(8,128)(2,1)S(1)}, u32[]{:S(2)}, u32[]{:S(2)}) %collective-permute-start) | collective-permute-done | bytes 131104 | tf_op jit(solution)/shard_map/ppermute | solution.py:42
  14.3 2.3 shard_map.96
  16.6 6.5 %all-to-all-start = ((bf16[8,256,256]{2,1,0:T(8,128)(2,1)}), bf16[8,256,256]{2,1,0:T(8,128)(2,1)S(1)}, u32[]{:S(2)}, u32[]{:S(2)}) async-start(bf16[8,256,256]{2,1,0:T(8,128)(2,1)} %shard_map.96), calls=%async_computation | async-start | bytes 2097152 | tf_op jit(solution)/shard_map/all_to_all | solution.py:378
  25.1 4.5 %collective-permute-done.1.refs_2_.refs_10_ = bf16[256,256]{1,0:T(8,128)(2,1)S(1)} collective-permute-done((bf16[256,256]{1,0:T(8,128)(2,1)S(1)}, bf16[256,256]{1,0:T(8,128)(2,1)S(1)}, u32[]{:S(2)}, u32[]{:S(2)}) %collective-permute-start.1) | collective-permute-done | bytes 131104 | tf_op jit(solution)/shard_map/ppermute | solution.py:42
  29.9 9.5 %all-gather.5.cloned.1.call-done = bf16[2176,256]{1,0:T(8,128)(2,1)} async-done(((bf16[272,256]{1,0:T(8,128)(2,1)}), bf16[2176,256]{1,0:T(8,128)(2,1)}) %all-gather.5.cloned.1.call-update) | async-done | bytes 1114128 | tf_op jit(solution)/shard_map/all_gather | solution.py:374
  39.4 5.4 %shard_map.95.refs_0_._ = f32[3,2048]{1,0:T(4,128)} custom-call(s32[4]{0:T(128)} %add_multiply_fusion.first_ref, bf16[8,272,256]{2,1,0:T(8,128)(2,1)} %bitcast.7, bf16[256,256]{1,0:T(8,128)(2,1)} %refs_8_.1, bf16[256,256]{1,0:T(8,128)(2,1)} %copy-done.5, bf16[256,256]{1,0:T(8,128)(2,1)} %copy-done.8, bf16[256,256]{1,0:T(8,128)(2,1)} %copy-done.9, ...), custom_call_target="tpu_custom_call" | custom-call | flops 1024 | bytes 1024 | tf_op jit(solution)/shard_map/pallas_call | solution.py:120
  47.0 3.4 %collective-permute-start.6 = (f32[3,2048]{1,0:T(4,128)}, f32[3,2048]{1,0:T(4,128)S(1)}, u32[]{:S(2)}, u32[]{:S(2)}) collective-permute-start(f32[3,2048]{1,0:T(4,128)} %shard_map.95.refs_0_._), channel_id=1, source_target_pairs={{0,4},{1,5},{2,6},{3,7},{4,0},{5,1},{6,2},{7,3},{8,12},{9,13},{10,... | collective-permute-start | bytes 73736 | tf_op jit(solution)/shard_map/ppermute | solution.py:42
  55.2 2.8 %collective-permute-done.8.refs_6_ = f32[3,2048]{1,0:T(4,128)S(1)} collective-permute-done((f32[3,2048]{1,0:T(4,128)}, f32[3,2048]{1,0:T(4,128)S(1)}, u32[]{:S(2)}, u32[]{:S(2)}) %collective-permute-start.8) | collective-permute-done | bytes 24608 | tf_op jit(solution)/shard_map/ppermute | solution.py:42
  60.1 8.2 %shard_map.97 = (f32[1,2048]{1,0:T(1,128)}, f32[2048,256]{1,0:T(8,128)}, f32[256,256]{1,0:T(8,128)}, f32[256,256]{1,0:T(8,128)}, f32[256,256]{1,0:T(8,128)}, /*index=5*/f32[256,256]{1,0:T(8,128)}) custom-call(s32[4]{0:T(128)} %add_multiply_fusion.first_ref, bf16[8,272,256]{2,1,0:T(8,128)(2,1)} %bitcast.8, f32[3,2048]{1,0:T(4,128)} %shard_map.95.refs_0_._, ...), custom_call_target="tpu_custom_call" | custom-call | flops 1024 | bytes 1024 | tf_op jit(solution)/shard_map/pallas_call | solution.py:183
  68.3 2.3 %shard_map.100 = bf16[8,256,256]{2,1,0:T(8,128)(2,1)} custom-call(bf16[256,2048]{1,0:T(8,128)(2,1)} %in_ref.3, f32[3,2048]{1,0:T(4,128)} %shard_map.95.refs_0_._), custom_call_target="tpu_custom_call" | custom-call | flops 1024 | bytes 1024 | tf_op jit(solution)/shard_map/pallas_call | solution.py:222
  70.7 4.2 %all-to-all-start.1 = ((bf16[8,256,256]{2,1,0:T(8,128)(2,1)}), bf16[8,256,256]{2,1,0:T(8,128)(2,1)S(1)}, u32[]{:S(2)}, u32[]{:S(2)}) async-start(bf16[8,256,256]{2,1,0:T(8,128)(2,1)} %shard_map.100), calls=%async_computation.2 | async-start | bytes 2097152 | tf_op jit(solution)/shard_map/all_to_all | solution.py:378
  77.5 5.0 %collective-permute-done.10.refs_1_ = f32[256,256]{1,0:T(8,128)S(1)} collective-permute-done((f32[256,256]{1,0:T(8,128)S(1)}, f32[256,256]{1,0:T(8,128)S(1)}, u32[]{:S(2)}, u32[]{:S(2)}) %collective-permute-start.10) | collective-permute-done | bytes 262176 | tf_op jit(solution)/shard_map/ppermute | solution.py:42
  82.6 6.3 %collective-permute-done.12.refs_3_ = f32[256,256]{1,0:T(8,128)S(1)} collective-permute-done((f32[256,256]{1,0:T(8,128)S(1)}, f32[256,256]{1,0:T(8,128)S(1)}, u32[]{:S(2)}, u32[]{:S(2)}) %collective-permute-start.12) | collective-permute-done | bytes 262176 | tf_op jit(solution)/shard_map/ppermute | solution.py:42
  89.6 2.1 shard_map.98
  92.5 1.9 collective-permute-start.18
  97.7 1.7 shard_map.101._.refs_1_
  99.3 13.3 %all-to-all-done.1.hidden_ref = bf16[8,256,256]{2,1,0:T(8,128)(2,1)S(1)} async-done(((bf16[8,256,256]{2,1,0:T(8,128)(2,1)}), bf16[8,256,256]{2,1,0:T(8,128)(2,1)S(1)}, u32[]{:S(2)}, u32[]{:S(2)}) %all-to-all-start.1) | async-done | bytes 1048608 | tf_op jit(solution)/shard_map/all_to_all | solution.py:378
  113.6 4.2 %shard_map.102.refs_1_ = bf16[4,8,128,256]{3,2,1,0:T(8,128)(2,1)} custom-call(s32[1]{0:T(128)} %bitcast.5.me_ref, bf16[8,272,256]{2,1,0:T(8,128)(2,1)} %bitcast.9, bf16[8,256,256]{2,1,0:T(8,128)(2,1)} %copy-done.1, bf16[4,128,256]{2,1,0:T(8,128)(2,1)} %shard_map.101._.refs_1_), custom_call_target="tpu_custom_call" | custom-call | flops 1024 | bytes 1024 | tf_op jit(solution)/shard_map/pallas_call | solution.py:264
  117.8 3.6 %all-to-all-start.2 = ((bf16[4,8,128,256]{3,2,1,0:T(8,128)(2,1)}), bf16[4,8,128,256]{3,2,1,0:T(8,128)(2,1)S(1)}, u32[]{:S(2)}, u32[]{:S(2)}) async-start(bf16[4,8,128,256]{3,2,1,0:T(8,128)(2,1)} %shard_map.102.refs_1_), calls=%async_computation.3 | async-start | bytes 4194304 | tf_op jit(solution)/shard_map/all_to_all | solution.py:378
  121.5 4.1 %shard_map.99 = (bf16[8,128,256]{2,1,0:T(8,128)(2,1)}, bf16[8,128,256]{2,1,0:T(8,128)(2,1)}, bf16[8,128,256]{2,1,0:T(8,128)(2,1)}, bf16[8,128,256]{2,1,0:T(8,128)(2,1)}) custom-call(s32[1]{0:T(128)} %bitcast.5.me_ref, bf16[8,272,256]{2,1,0:T(8,128)(2,1)} %bitcast.10, bf16[8,256,256]{2,1,0:T(8,128)(2,1)} %copy-done, bf16[128,256]{1,0:T(8,128)(2,1)} %get-tuple-element.30._.refs_0_), custom_call_target="tpu_custom_call" | custom-call | flops 1024 | bytes 1024 | tf_op jit(solution)/shard_map/pallas_call | solution.py:264
  128.2 3.5 %collective-permute-start.22 = (bf16[4,128,256]{2,1,0:T(8,128)(2,1)S(1)}, bf16[4,128,256]{2,1,0:T(8,128)(2,1)}, u32[]{:S(2)}, u32[]{:S(2)}) collective-permute-start(bf16[4,128,256]{2,1,0:T(8,128)(2,1)S(1)} %copy-done.6), channel_id=1, source_target_pairs={{0,2},{1,3},{2,0},{3,1},{4,6},{5,7},{6,4},{7,5},{8,10},{9,11},{10,... | collective-permute-start | bytes 786440 | tf_op jit(solution)/shard_map/ppermute | solution.py:42
  131.7 24.0 %collective-permute-done.13.refs_2_.refs_1_ = bf16[8,128,256]{2,1,0:T(8,128)(2,1)S(1)} collective-permute-done((bf16[8,128,256]{2,1,0:T(8,128)(2,1)}, bf16[8,128,256]{2,1,0:T(8,128)(2,1)S(1)}, u32[]{:S(2)}, u32[]{:S(2)}) %collective-permute-start.13) | collective-permute-done | bytes 524320 | tf_op jit(solution)/shard_map/ppermute | solution.py:42
  155.7 1.9 collective-permute-start.24
  157.6 10.3 %collective-permute-done.15.refs_4_.refs_3_ = bf16[8,128,256]{2,1,0:T(8,128)(2,1)} collective-permute-done((bf16[8,128,256]{2,1,0:T(8,128)(2,1)}, bf16[8,128,256]{2,1,0:T(8,128)(2,1)}, u32[]{:S(2)}, u32[]{:S(2)}) %collective-permute-start.15) | collective-permute-done | bytes 524320 | tf_op jit(solution)/shard_map/ppermute | solution.py:42
  167.9 1.9 shard_map.103
  171.0 1.9 collective-permute-start.25
  174.5 2.3 %collective-permute-done.20.refs_2_ = bf16[128,256]{1,0:T(8,128)(2,1)S(1)} collective-permute-done((bf16[128,256]{1,0:T(8,128)(2,1)}, bf16[128,256]{1,0:T(8,128)(2,1)S(1)}, u32[]{:S(2)}, u32[]{:S(2)}) %collective-permute-start.20) | collective-permute-done | bytes 65568 | tf_op jit(solution)/shard_map/ppermute | solution.py:42
  178.9 2.1 collective-permute-done.21.refs_3_
  185.6 4.2 %shard_map.106 = f32[8,256,256]{2,1,0:T(8,128)} custom-call(s32[8]{0:T(128)} %xor.40.order_ref, s32[1]{0:T(128)} %bitcast.5.me_ref, bf16[4,8,128,256]{3,2,1,0:T(8,128)(2,1)} %copy-done.2, bf16[4,128,256]{2,1,0:T(8,128)(2,1)} %shard_map.101._.refs_1_, bf16[4,128,256]{2,1,0:T(8,128)(2,1)} %collective-permute-done.22.refs_2_, ...), custom_call_target="tpu_custom_call" | custom-call | flops 68719476736 | bytes 268435456 | tf_op jit(solution)/shard_map/pallas_call | solution.py:347
  189.8 28.9 %all-gather.7.cloned.1.call-done = bf16[32,128,256]{2,1,0:T(8,128)(2,1)} async-done(((bf16[4,128,256]{2,1,0:T(8,128)(2,1)}), bf16[32,128,256]{2,1,0:T(8,128)(2,1)}) %all-gather.7.cloned.1.call-update) | async-done | bytes 2097168 | tf_op jit(solution)/shard_map/all_gather | solution.py:399
  218.7 4.3 %shard_map.105 = f32[8,256,256]{2,1,0:T(8,128)} custom-call(s32[8]{0:T(128)} %xor.40.order_ref, s32[1]{0:T(128)} %bitcast.5.me_ref, bf16[8,128,256]{2,1,0:T(8,128)(2,1)} %get-tuple-element.31.refs_0_, bf16[8,128,256]{2,1,0:T(8,128)(2,1)} %copy-done.3, bf16[8,128,256]{2,1,0:T(8,128)(2,1)} %copy-done.4, ...), custom_call_target="tpu_custom_call" | custom-call | flops 1024 | bytes 1024 | tf_op jit(solution)/shard_map/pallas_call | solution.py:347
  (124 shorter events, 32.9 us)
Async XLA Ops:
  7.2 32.2 %all-gather.5.cloned.1.call-start = ((), (), s32[]{:S(2)}) async-start(), calls=%async_computation.5 | async-start | bytes 1253376 | tf_op jit(solution)/shard_map/all_gather | solution.py:374
  9.0 4.6 %collective-permute-start = (bf16[256,256]{1,0:T(8,128)(2,1)}, bf16[256,256]{1,0:T(8,128)(2,1)S(1)}, u32[]{:S(2)}, u32[]{:S(2)}) collective-permute-start(bf16[256,256]{1,0:T(8,128)(2,1)} %refs_8_.1), channel_id=1, source_target_pairs={{0,8},{8,0},{16,24},{24,16},{1,9},{9,1},{17,25},{25,17},{2,10},{10... | collective-permute-start | bytes 393224 | tf_op jit(solution)/shard_map/ppermute | solution.py:42
  16.6 36.8 %all-to-all-start = ((bf16[8,256,256]{2,1,0:T(8,128)(2,1)}), bf16[8,256,256]{2,1,0:T(8,128)(2,1)S(1)}, u32[]{:S(2)}, u32[]{:S(2)}) async-start(bf16[8,256,256]{2,1,0:T(8,128)(2,1)} %shard_map.96), calls=%async_computation | async-start | bytes 2097152 | tf_op jit(solution)/shard_map/all_to_all | solution.py:378
  23.1 144.8 %reduce-scatter.2.cloned.1.call-start = ((), (), s32[]{:S(2)}) async-start(), calls=%async_computation.4 | async-start | bytes 2359296 | tf_op jit(solution)/shard_map/reduce_scatter | solution.py:386
  23.1 6.5 %collective-permute-start.1 = (bf16[256,256]{1,0:T(8,128)(2,1)S(1)}, bf16[256,256]{1,0:T(8,128)(2,1)S(1)}, u32[]{:S(2)}, u32[]{:S(2)}) collective-permute-start(bf16[256,256]{1,0:T(8,128)(2,1)S(1)} %copy-done.7), channel_id=1, source_target_pairs={{0,16},{8,24},{16,0},{24,8},{1,17},{9,25},{17,1},{25,9},{2,18},{10... | collective-permute-start | bytes 393224 | tf_op jit(solution)/shard_map/ppermute | solution.py:42
  24.4 5.5 %collective-permute-start.2 = (bf16[256,256]{1,0:T(8,128)(2,1)S(1)}, bf16[256,256]{1,0:T(8,128)(2,1)S(1)}, u32[]{:S(2)}, u32[]{:S(2)}) collective-permute-start(bf16[256,256]{1,0:T(8,128)(2,1)S(1)} %copy-done.7), channel_id=1, source_target_pairs={{0,24},{8,16},{16,8},{24,0},{1,25},{9,17},{17,9},{25,1},{2,26},{10... | collective-permute-start | bytes 393224 | tf_op jit(solution)/shard_map/ppermute | solution.py:42
  44.8 5.6 %collective-permute-start.3 = (f32[3,2048]{1,0:T(4,128)}, f32[3,2048]{1,0:T(4,128)S(1)}, u32[]{:S(2)}, u32[]{:S(2)}) collective-permute-start(f32[3,2048]{1,0:T(4,128)} %shard_map.95.refs_0_._), channel_id=1, source_target_pairs={{0,1},{1,0},{2,3},{3,2},{4,5},{5,4},{6,7},{7,6},{8,9},{9,8},{10,11... | collective-permute-start | bytes 73736 | tf_op jit(solution)/shard_map/ppermute | solution.py:42
  45.1 6.8 %collective-permute-start.4 = (f32[3,2048]{1,0:T(4,128)}, f32[3,2048]{1,0:T(4,128)S(1)}, u32[]{:S(2)}, u32[]{:S(2)}) collective-permute-start(f32[3,2048]{1,0:T(4,128)} %shard_map.95.refs_0_._), channel_id=1, source_target_pairs={{0,2},{1,3},{2,0},{3,1},{4,6},{5,7},{6,4},{7,5},{8,10},{9,11},{10,... | collective-permute-start | bytes 73736 | tf_op jit(solution)/shard_map/ppermute | solution.py:42
  45.9 7.5 %collective-permute-start.5 = (f32[3,2048]{1,0:T(4,128)}, f32[3,2048]{1,0:T(4,128)S(1)}, u32[]{:S(2)}, u32[]{:S(2)}) collective-permute-start(f32[3,2048]{1,0:T(4,128)} %shard_map.95.refs_0_._), channel_id=1, source_target_pairs={{0,3},{1,2},{2,1},{3,0},{4,7},{5,6},{6,5},{7,4},{8,11},{9,10},{10,... | collective-permute-start | bytes 73736 | tf_op jit(solution)/shard_map/ppermute | solution.py:42
  47.0 7.1 %collective-permute-start.6 = (f32[3,2048]{1,0:T(4,128)}, f32[3,2048]{1,0:T(4,128)S(1)}, u32[]{:S(2)}, u32[]{:S(2)}) collective-permute-start(f32[3,2048]{1,0:T(4,128)} %shard_map.95.refs_0_._), channel_id=1, source_target_pairs={{0,4},{1,5},{2,6},{3,7},{4,0},{5,1},{6,2},{7,3},{8,12},{9,13},{10,... | collective-permute-start | bytes 73736 | tf_op jit(solution)/shard_map/ppermute | solution.py:42
  50.4 4.8 %collective-permute-start.7 = (f32[3,2048]{1,0:T(4,128)}, f32[3,2048]{1,0:T(4,128)S(1)}, u32[]{:S(2)}, u32[]{:S(2)}) collective-permute-start(f32[3,2048]{1,0:T(4,128)} %shard_map.95.refs_0_._), channel_id=1, source_target_pairs={{0,5},{1,4},{2,7},{3,6},{4,1},{5,0},{6,3},{7,2},{8,13},{9,12},{10,... | collective-permute-start | bytes 73736 | tf_op jit(solution)/shard_map/ppermute | solution.py:42
  50.4 7.6 %collective-permute-start.8 = (f32[3,2048]{1,0:T(4,128)}, f32[3,2048]{1,0:T(4,128)S(1)}, u32[]{:S(2)}, u32[]{:S(2)}) collective-permute-start(f32[3,2048]{1,0:T(4,128)} %shard_map.95.refs_0_._), channel_id=1, source_target_pairs={{0,6},{1,7},{2,4},{3,5},{4,2},{5,3},{6,0},{7,1},{8,14},{9,15},{10,... | collective-permute-start | bytes 73736 | tf_op jit(solution)/shard_map/ppermute | solution.py:42
  51.9 7.5 %collective-permute-start.9 = (f32[3,2048]{1,0:T(4,128)}, f32[3,2048]{1,0:T(4,128)S(1)}, u32[]{:S(2)}, u32[]{:S(2)}) collective-permute-start(f32[3,2048]{1,0:T(4,128)} %shard_map.95.refs_0_._), channel_id=1, source_target_pairs={{0,7},{1,6},{2,5},{3,4},{4,3},{5,2},{6,1},{7,0},{8,15},{9,14},{10,... | collective-permute-start | bytes 73736 | tf_op jit(solution)/shard_map/ppermute | solution.py:42
  70.7 42.0 %all-to-all-start.1 = ((bf16[8,256,256]{2,1,0:T(8,128)(2,1)}), bf16[8,256,256]{2,1,0:T(8,128)(2,1)S(1)}, u32[]{:S(2)}, u32[]{:S(2)}) async-start(bf16[8,256,256]{2,1,0:T(8,128)(2,1)} %shard_map.100), calls=%async_computation.2 | async-start | bytes 2097152 | tf_op jit(solution)/shard_map/all_to_all | solution.py:378
  74.9 7.6 %collective-permute-start.10 = (f32[256,256]{1,0:T(8,128)S(1)}, f32[256,256]{1,0:T(8,128)S(1)}, u32[]{:S(2)}, u32[]{:S(2)}) collective-permute-start(f32[256,256]{1,0:T(8,128)S(1)} %copy-done.31), channel_id=1, source_target_pairs={{0,8},{8,0},{16,24},{24,16},{1,9},{9,1},{17,25},{25,17},{2,10},{10... | collective-permute-start | bytes 786440 | tf_op jit(solution)/shard_map/ppermute | solution.py:42
  75.3 7.3 %collective-permute-start.11 = (f32[256,256]{1,0:T(8,128)S(1)}, f32[256,256]{1,0:T(8,128)S(1)}, u32[]{:S(2)}, u32[]{:S(2)}) collective-permute-start(f32[256,256]{1,0:T(8,128)S(1)} %copy-done.30), channel_id=1, source_target_pairs={{0,16},{8,24},{16,0},{24,8},{1,17},{9,25},{17,1},{25,9},{2,18},{10... | collective-permute-start | bytes 786440 | tf_op jit(solution)/shard_map/ppermute | solution.py:42
  76.4 12.5 %collective-permute-start.12 = (f32[256,256]{1,0:T(8,128)S(1)}, f32[256,256]{1,0:T(8,128)S(1)}, u32[]{:S(2)}, u32[]{:S(2)}) collective-permute-start(f32[256,256]{1,0:T(8,128)S(1)} %copy-done.29), channel_id=1, source_target_pairs={{0,24},{8,16},{16,8},{24,0},{1,25},{9,17},{17,9},{25,1},{2,26},{10... | collective-permute-start | bytes 786440 | tf_op jit(solution)/shard_map/ppermute | solution.py:42
  92.5 4.6 %collective-permute-start.18 = (bf16[128,256]{1,0:T(8,128)(2,1)}, bf16[128,256]{1,0:T(8,128)(2,1)S(1)}, u32[]{:S(2)}, u32[]{:S(2)}) collective-permute-start(bf16[128,256]{1,0:T(8,128)(2,1)} %get-tuple-element.38), channel_id=1, source_target_pairs={{0,24},{8,16},{16,8},{24,0},{1,25},{9,17},{17,9},{25,1},{2,26},{10... | collective-permute-start | bytes 196616 | tf_op jit(solution)/shard_map/ppermute | solution.py:42
  117.8 65.7 %all-to-all-start.2 = ((bf16[4,8,128,256]{3,2,1,0:T(8,128)(2,1)}), bf16[4,8,128,256]{3,2,1,0:T(8,128)(2,1)S(1)}, u32[]{:S(2)}, u32[]{:S(2)}) async-start(bf16[4,8,128,256]{3,2,1,0:T(8,128)(2,1)} %shard_map.102.refs_1_), calls=%async_computation.3 | async-start | bytes 4194304 | tf_op jit(solution)/shard_map/all_to_all | solution.py:378
  121.4 97.2 %all-gather.7.cloned.1.call-start = ((), (), s32[]{:S(2)}) async-start(), calls=%async_computation.6 | async-start | bytes 2359296 | tf_op jit(solution)/shard_map/all_gather | solution.py:399
  125.5 30.1 %collective-permute-start.13 = (bf16[8,128,256]{2,1,0:T(8,128)(2,1)}, bf16[8,128,256]{2,1,0:T(8,128)(2,1)S(1)}, u32[]{:S(2)}, u32[]{:S(2)}) collective-permute-start(bf16[8,128,256]{2,1,0:T(8,128)(2,1)} %get-tuple-element.32), channel_id=1, source_target_pairs={{0,8},{8,0},{16,24},{24,16},{1,9},{9,1},{17,25},{25,17},{2,10},{10... | collective-permute-start | bytes 1572872 | tf_op jit(solution)/shard_map/ppermute | solution.py:42
  125.5 32.0 %collective-permute-start.14 = (bf16[8,128,256]{2,1,0:T(8,128)(2,1)}, bf16[8,128,256]{2,1,0:T(8,128)(2,1)S(1)}, u32[]{:S(2)}, u32[]{:S(2)}) collective-permute-start(bf16[8,128,256]{2,1,0:T(8,128)(2,1)} %get-tuple-element.33), channel_id=1, source_target_pairs={{0,16},{8,24},{16,0},{24,8},{1,17},{9,25},{17,1},{25,9},{2,18},{10... | collective-permute-start | bytes 1572872 | tf_op jit(solution)/shard_map/ppermute | solution.py:42
  127.0 40.9 %collective-permute-start.15 = (bf16[8,128,256]{2,1,0:T(8,128)(2,1)}, bf16[8,128,256]{2,1,0:T(8,128)(2,1)}, u32[]{:S(2)}, u32[]{:S(2)}) collective-permute-start(bf16[8,128,256]{2,1,0:T(8,128)(2,1)} %get-tuple-element.34), channel_id=1, source_target_pairs={{0,24},{8,16},{16,8},{24,0},{1,25},{9,17},{17,9},{25,1},{2,26},{10... | collective-permute-start | bytes 1572872 | tf_op jit(solution)/shard_map/ppermute | solution.py:42
  128.2 44.7 %collective-permute-start.22 = (bf16[4,128,256]{2,1,0:T(8,128)(2,1)S(1)}, bf16[4,128,256]{2,1,0:T(8,128)(2,1)}, u32[]{:S(2)}, u32[]{:S(2)}) collective-permute-start(bf16[4,128,256]{2,1,0:T(8,128)(2,1)S(1)} %copy-done.6), channel_id=1, source_target_pairs={{0,2},{1,3},{2,0},{3,1},{4,6},{5,7},{6,4},{7,5},{8,10},{9,11},{10,... | collective-permute-start | bytes 786440 | tf_op jit(solution)/shard_map/ppermute | solution.py:42
  131.7 41.3 %collective-permute-start.23 = (bf16[4,128,256]{2,1,0:T(8,128)(2,1)S(1)}, bf16[4,128,256]{2,1,0:T(8,128)(2,1)}, u32[]{:S(2)}, u32[]{:S(2)}) collective-permute-start(bf16[4,128,256]{2,1,0:T(8,128)(2,1)S(1)} %copy-done.6), channel_id=1, source_target_pairs={{0,4},{1,5},{2,6},{3,7},{4,0},{5,1},{6,2},{7,3},{8,12},{9,13},{10,... | collective-permute-start | bytes 786440 | tf_op jit(solution)/shard_map/ppermute | solution.py:42
  155.7 17.7 %collective-permute-start.24 = (bf16[4,128,256]{2,1,0:T(8,128)(2,1)S(1)}, bf16[4,128,256]{2,1,0:T(8,128)(2,1)}, u32[]{:S(2)}, u32[]{:S(2)}) collective-permute-start(bf16[4,128,256]{2,1,0:T(8,128)(2,1)S(1)} %copy-done.6), channel_id=1, source_target_pairs={{0,6},{1,7},{2,4},{3,5},{4,2},{5,3},{6,0},{7,1},{8,14},{9,15},{10,... | collective-permute-start | bytes 786440 | tf_op jit(solution)/shard_map/ppermute | solution.py:42
  169.7 3.7 %collective-permute-start.19 = (bf16[128,256]{1,0:T(8,128)(2,1)}, bf16[128,256]{1,0:T(8,128)(2,1)S(1)}, u32[]{:S(2)}, u32[]{:S(2)}) collective-permute-start(bf16[128,256]{1,0:T(8,128)(2,1)} %get-tuple-element.40), channel_id=1, source_target_pairs={{0,8},{8,0},{16,24},{24,16},{1,9},{9,1},{17,25},{25,17},{2,10},{10... | collective-permute-start | bytes 196616 | tf_op jit(solution)/shard_map/ppermute | solution.py:42
  171.0 12.4 %collective-permute-start.25 = (bf16[4,128,256]{2,1,0:T(8,128)(2,1)S(1)}, bf16[4,128,256]{2,1,0:T(8,128)(2,1)S(1)}, u32[]{:S(2)}, u32[]{:S(2)}) collective-permute-start(bf16[4,128,256]{2,1,0:T(8,128)(2,1)S(1)} %copy-done.6), channel_id=1, source_target_pairs={{0,1},{1,0},{2,3},{3,2},{4,5},{5,4},{6,7},{7,6},{8,9},{9,8},{10,11... | collective-permute-start | bytes 786440 | tf_op jit(solution)/shard_map/ppermute | solution.py:42
  172.9 10.5 %collective-permute-start.26 = (bf16[4,128,256]{2,1,0:T(8,128)(2,1)}, bf16[4,128,256]{2,1,0:T(8,128)(2,1)S(1)}, u32[]{:S(2)}, u32[]{:S(2)}) collective-permute-start(bf16[4,128,256]{2,1,0:T(8,128)(2,1)} %collective-permute-done.22.refs_2_), channel_id=1, source_target_pairs={{0,1},{1,0},{2,3},{3,2},{4,5},{5,4},{6,7},{7,6},{8,9},{9,8},{10,11... | collective-permute-start | bytes 786440 | tf_op jit(solution)/shard_map/ppermute | solution.py:42
  173.0 10.5 %collective-permute-start.27 = (bf16[4,128,256]{2,1,0:T(8,128)(2,1)}, bf16[4,128,256]{2,1,0:T(8,128)(2,1)S(1)}, u32[]{:S(2)}, u32[]{:S(2)}) collective-permute-start(bf16[4,128,256]{2,1,0:T(8,128)(2,1)} %collective-permute-done.23.refs_3_), channel_id=1, source_target_pairs={{0,1},{1,0},{2,3},{3,2},{4,5},{5,4},{6,7},{7,6},{8,9},{9,8},{10,11... | collective-permute-start | bytes 786440 | tf_op jit(solution)/shard_map/ppermute | solution.py:42
  173.4 10.0 %collective-permute-start.28 = (bf16[4,128,256]{2,1,0:T(8,128)(2,1)}, bf16[4,128,256]{2,1,0:T(8,128)(2,1)}, u32[]{:S(2)}, u32[]{:S(2)}) collective-permute-start(bf16[4,128,256]{2,1,0:T(8,128)(2,1)} %collective-permute-done.24.refs_4_), channel_id=1, source_target_pairs={{0,1},{1,0},{2,3},{3,2},{4,5},{5,4},{6,7},{7,6},{8,9},{9,8},{10,11... | collective-permute-start | bytes 786440 | tf_op jit(solution)/shard_map/ppermute | solution.py:42
  176.8 4.2 %collective-permute-start.21 = (bf16[128,256]{1,0:T(8,128)(2,1)}, bf16[128,256]{1,0:T(8,128)(2,1)S(1)}, u32[]{:S(2)}, u32[]{:S(2)}) collective-permute-start(bf16[128,256]{1,0:T(8,128)(2,1)} %get-tuple-element.42), channel_id=1, source_target_pairs={{0,24},{8,16},{16,8},{24,0},{1,25},{9,17},{17,9},{25,1},{2,26},{10... | collective-permute-start | bytes 196616 | tf_op jit(solution)/shard_map/ppermute | solution.py:42
  (35 other events, 170.0 us)
Sparse Core Ops, SparseCore 0:
  10.2 29.1 all-gather.4
  68.4 53.1 reduce-scatter.1
  183.5 35.1 all-gather.6

commit v11 on v10

--- a/solution.py
+++ b/solution.py
@@ -23,7 +23,6 @@
 WHOLE = pl.BlockSpec(memory_space=pltpu.VMEM)
 ANYWHERE = pl.BlockSpec(memory_space=pl.ANY)
 VMEM = 60 * MIB
-LARGE = pl.CostEstimate(flops=1 << 36, bytes_accessed=1 << 28, transcendentals=0)
 SMALL = pl.CostEstimate(flops=1024, bytes_accessed=1024, transcendentals=0)
 
 
@@ -387,17 +386,17 @@
     item_pieces = exchange(item_parts, "user")
 
     item_routed = route(me, targets, item_pieces, 1, groups, [])
-    item_sent = stack(exchange(item_routed, "user"))
+    user_slots = slot_hidden(me, users, user_cols, groups, 0, True, item_routed[0])
+    item_sent = stack(exchange(item_routed, "user"), user_slots[:1])
     item_line = exchange([item_sent] * lines, "item", CORES)
-    user_slots = slot_hidden(me, users, user_cols, groups, 0, True, item_routed[0])
     user_rows = exchange(user_slots, "user")
-    item_slots = slot_hidden(me, users, item_cols, groups, 1, False, item_sent)
+    user_routed = route(me, targets, [user_grad], 0, groups, [item_sent] + user_rows[1:])
+    item_slots = slot_hidden(me, users, item_cols, groups, 1, False, user_routed[0])
+    user_sent = stack(exchange(user_routed, "user"), item_line[1:3] + [item_slots[0]])
     item_rows = [scatter(item_slots[0], "user")]
-    user_routed = route(me, targets, [user_grad], 0, groups, [item_slots[0]] + user_rows[1:])
-    user_sent = stack(exchange(user_routed, "user"))
     item_cross = item_line + [swap(piece, "item", 1) for piece in item_line]
     user_all = lax.all_gather(user_sent, "item", axis=0)
-    item_weight_grad = outer(order, me, item_rows, item_cross, LARGE)
+    item_weight_grad = outer(order, me, item_rows, item_cross, SMALL)
     user_weight_grad = outer(order, me, user_rows, [user_all], SMALL)
     return (row_loss, user_weight_grad, item_weight_grad)
 

time: 231 us -> 193 us (0.84)
  waiting for transfers between devices: 120 us -> 64.5 us
  starting transfers between devices: 42.5 us -> 57.4 us
    all_gather x1, waiting for transfers between devices: 28.9 us -> 0.01 us  [shards(): user_all = lax.all_gather(user_sent, 'item', axis=0)]
    ppermute x29, starting transfers between devices: 28.1 us -> 42.8 us  [swap(): return lax.ppermute(piece, axis, [(j, j ^ bits) for j in range(size)])]
    ppermute x29, waiting for transfers between devices: 68 us -> 54.3 us  [swap(): return lax.ppermute(piece, axis, [(j, j ^ bits) for j in range(size)])]
    all_to_all x3, waiting for transfers between devices: 13.9 us -> 0.57 us  [scatter(): return lax.all_to_all(pieces, axis, split_axis=0, concat_axis=0, tiled=True)]
    unnamed x64 -> x78, local copies, waits for them, and re-layouts: 6.39 us -> 8.06 us
  transfers between devices with their start and end apart: 35 -> 35, of which waited for: 21 -> 15; matrix products, arithmetic and copies ran while one was open for 1% -> 1% of each run, Pallas kernels for 13% -> 15%
where the time goes in v11:
time: 193 us; the launch traced here: 190 us
  waiting for transfers between devices  64.5 us (33%)
  starting transfers between devices  57.4 us (30%)
  Pallas kernels  44 us (23%)
  between operations  14 us (7%)
  local copies, waits for them, and re-layouts  9.89 us (5%)
    ppermute x29, waiting for transfers between devices, swap(): return lax.ppermute(piece, axis, [(j, j ^ bits) for j in range(size)])  54.3 us
    ppermute x29, starting transfers between devices, swap(): return lax.ppermute(piece, axis, [(j, j ^ bits) for j in range(size)])  42.8 us
    all_to_all x3, starting transfers between devices, scatter(): return lax.all_to_all(pieces, axis, split_axis=0, concat_axis=0, tiled=True)  14.5 us
    all_gather x1, waiting for transfers between devices, shards(): users = lax.all_gather(packed, 'item', axis=0)  9.51 us
    pallas_call x2, Pallas kernels, outer(): pl.pallas_call(functools.partial(outer_kernel, count=len(hidden)), grid=(...  8.58 us
    pallas_call x2, Pallas kernels, slot_hidden(): pl.pallas_call(functools.partial(hidden_kernel, tower=tower), grid=(block...  8.22 us
    pallas_call x1, Pallas kernels, grads(): pl.pallas_call(functools.partial(grad_kernel, rows=rows, chunk=64, count=...  8.18 us
    unnamed x78, local copies, waits for them, and re-layouts  8.06 us
  transfers between devices with their start and end apart: 35, of which 15 were waited for; matrix products, arithmetic and copies ran while one was open for 1% of the time, Pallas kernels for 15%

profile of v11, /device:TPU:11, one launch (start us, length us, event | category | flops | bytes accessed | tf_op | source)
XLA Modules:
  0.0 190.4 jit_solution(3846305484946585716)
XLA Ops:
  7.2 1.7 shard_map.94
  9.3 4.3 %collective-permute-done.refs_1_._.refs_9_ = bf16[256,256]{1,0:T(8,128)(2,1)S(1)} collective-permute-done((bf16[256,256]{1,0:T(8,128)(2,1)}, bf16[256,256]{1,0:T(8,128)(2,1)S(1)}, u32[]{:S(2)}, u32[]{:S(2)}) %collective-permute-start) | collective-permute-done | bytes 131104 | tf_op jit(solution)/shard_map/ppermute | solution.py:41
  14.3 2.3 %shard_map.96 = bf16[8,256,256]{2,1,0:T(8,128)(2,1)} custom-call(bf16[256,2048]{1,0:T(8,128)(2,1)} %in_ref.2, bf16[256,256]{1,0:T(8,128)(2,1)} %copy-done.7), custom_call_target="tpu_custom_call" | custom-call | flops 1024 | bytes 1024 | tf_op jit(solution)/shard_map/pallas_call | solution.py:221
  16.6 6.5 %all-to-all-start = ((bf16[8,256,256]{2,1,0:T(8,128)(2,1)}), bf16[8,256,256]{2,1,0:T(8,128)(2,1)S(1)}, u32[]{:S(2)}, u32[]{:S(2)}) async-start(bf16[8,256,256]{2,1,0:T(8,128)(2,1)} %shard_map.96), calls=%async_computation | async-start | bytes 2097152 | tf_op jit(solution)/shard_map/all_to_all | solution.py:377
  25.1 4.5 %collective-permute-done.1.refs_2_.refs_10_ = bf16[256,256]{1,0:T(8,128)(2,1)S(1)} collective-permute-done((bf16[256,256]{1,0:T(8,128)(2,1)S(1)}, bf16[256,256]{1,0:T(8,128)(2,1)S(1)}, u32[]{:S(2)}, u32[]{:S(2)}) %collective-permute-start.1) | collective-permute-done | bytes 131104 | tf_op jit(solution)/shard_map/ppermute | solution.py:41
  29.9 9.5 %all-gather.5.cloned.1.call-done = bf16[2176,256]{1,0:T(8,128)(2,1)} async-done(((bf16[272,256]{1,0:T(8,128)(2,1)}), bf16[2176,256]{1,0:T(8,128)(2,1)}) %all-gather.5.cloned.1.call-update) | async-done | bytes 1114128 | tf_op jit(solution)/shard_map/all_gather | solution.py:373
  39.4 5.4 %shard_map.95.refs_0_._ = f32[3,2048]{1,0:T(4,128)} custom-call(s32[4]{0:T(128)} %add_multiply_fusion.first_ref, bf16[8,272,256]{2,1,0:T(8,128)(2,1)} %bitcast.7, bf16[256,256]{1,0:T(8,128)(2,1)} %refs_8_.1, bf16[256,256]{1,0:T(8,128)(2,1)} %copy-done.7, bf16[256,256]{1,0:T(8,128)(2,1)} %copy-done.13, bf16[256,256]{1,0:T(8,128)(2,1)} %copy-done.14, ...), custom_call_target="tpu_custom_call" | custom-call | flops 1024 | bytes 1024 | tf_op jit(solution)/shard_map/pallas_call | solution.py:119
  47.0 3.4 %collective-permute-start.6 = (f32[3,2048]{1,0:T(4,128)}, f32[3,2048]{1,0:T(4,128)S(1)}, u32[]{:S(2)}, u32[]{:S(2)}) collective-permute-start(f32[3,2048]{1,0:T(4,128)} %shard_map.95.refs_0_._), channel_id=1, source_target_pairs={{0,4},{1,5},{2,6},{3,7},{4,0},{5,1},{6,2},{7,3},{8,12},{9,13},{10,... | collective-permute-start | bytes 73736 | tf_op jit(solution)/shard_map/ppermute | solution.py:41
  50.4 1.5 collective-permute-start.8
  55.2 2.8 %collective-permute-done.8.refs_6_ = f32[3,2048]{1,0:T(4,128)S(1)} collective-permute-done((f32[3,2048]{1,0:T(4,128)}, f32[3,2048]{1,0:T(4,128)S(1)}, u32[]{:S(2)}, u32[]{:S(2)}) %collective-permute-start.8) | collective-permute-done | bytes 24608 | tf_op jit(solution)/shard_map/ppermute | solution.py:41
  60.1 8.2 %shard_map.97 = (f32[1,2048]{1,0:T(1,128)}, f32[2048,256]{1,0:T(8,128)}, f32[256,256]{1,0:T(8,128)}, f32[256,256]{1,0:T(8,128)}, f32[256,256]{1,0:T(8,128)}, /*index=5*/f32[256,256]{1,0:T(8,128)}) custom-call(s32[4]{0:T(128)} %add_multiply_fusion.first_ref, bf16[8,272,256]{2,1,0:T(8,128)(2,1)} %bitcast.8, f32[3,2048]{1,0:T(4,128)} %shard_map.95.refs_0_._, ...), custom_call_target="tpu_custom_call" | custom-call | flops 1024 | bytes 1024 | tf_op jit(solution)/shard_map/pallas_call | solution.py:182
  68.3 2.4 %shard_map.102 = bf16[8,256,256]{2,1,0:T(8,128)(2,1)} custom-call(bf16[256,2048]{1,0:T(8,128)(2,1)} %in_ref.3, f32[3,2048]{1,0:T(4,128)} %shard_map.95.refs_0_._), custom_call_target="tpu_custom_call" | custom-call | flops 1024 | bytes 1024 | tf_op jit(solution)/shard_map/pallas_call | solution.py:221
  70.7 4.2 %all-to-all-start.1 = ((bf16[8,256,256]{2,1,0:T(8,128)(2,1)}), bf16[8,256,256]{2,1,0:T(8,128)(2,1)S(1)}, u32[]{:S(2)}, u32[]{:S(2)}) async-start(bf16[8,256,256]{2,1,0:T(8,128)(2,1)} %shard_map.102), calls=%async_computation.2 | async-start | bytes 2097152 | tf_op jit(solution)/shard_map/all_to_all | solution.py:377
  77.6 5.0 %collective-permute-done.10.refs_1_ = f32[256,256]{1,0:T(8,128)S(1)} collective-permute-done((f32[256,256]{1,0:T(8,128)S(1)}, f32[256,256]{1,0:T(8,128)S(1)}, u32[]{:S(2)}, u32[]{:S(2)}) %collective-permute-start.10) | collective-permute-done | bytes 262176 | tf_op jit(solution)/shard_map/ppermute | solution.py:41
  82.7 6.3 %collective-permute-done.12.refs_3_ = f32[256,256]{1,0:T(8,128)S(1)} collective-permute-done((f32[256,256]{1,0:T(8,128)S(1)}, f32[256,256]{1,0:T(8,128)S(1)}, u32[]{:S(2)}, u32[]{:S(2)}) %collective-permute-start.12) | collective-permute-done | bytes 262176 | tf_op jit(solution)/shard_map/ppermute | solution.py:41
  89.7 2.1 %shard_map.98 = (bf16[128,256]{1,0:T(8,128)(2,1)}, bf16[128,256]{1,0:T(8,128)(2,1)}, bf16[128,256]{1,0:T(8,128)(2,1)}, bf16[128,256]{1,0:T(8,128)(2,1)}) custom-call(s32[1]{0:T(128)} %bitcast.5.me_ref, s32[2,256]{1,0:T(2,128)} %get-tuple-element.25.target_ref, f32[256,256]{1,0:T(8,128)} %get-tuple-element.26.refs_0_, f32[256,256]{1,0:T(8,128)} %copy-done.15, ...), custom_call_target="tpu_custom_call" | custom-call | flops 1024 | bytes 1024 | tf_op jit(solution)/shard_map/pallas_call | solution.py:295
  91.8 4.1 %shard_map.99 = (bf16[8,128,256]{2,1,0:T(8,128)(2,1)}, bf16[8,128,256]{2,1,0:T(8,128)(2,1)}, bf16[8,128,256]{2,1,0:T(8,128)(2,1)}, bf16[8,128,256]{2,1,0:T(8,128)(2,1)}) custom-call(s32[1]{0:T(128)} %bitcast.5.me_ref, bf16[8,272,256]{2,1,0:T(8,128)(2,1)} %bitcast.9, bf16[8,256,256]{2,1,0:T(8,128)(2,1)} %copy-done, bf16[128,256]{1,0:T(8,128)(2,1)} %get-tuple-element.30._.refs_0_), custom_call_target="tpu_custom_call" | custom-call | flops 1024 | bytes 1024 | tf_op jit(solution)/shard_map/pallas_call | solution.py:263
  96.6 1.9 %collective-permute-start.15 = (bf16[8,128,256]{2,1,0:T(8,128)(2,1)}, bf16[8,128,256]{2,1,0:T(8,128)(2,1)S(1)}, u32[]{:S(2)}, u32[]{:S(2)}) collective-permute-start(bf16[8,128,256]{2,1,0:T(8,128)(2,1)} %get-tuple-element.34), channel_id=1, source_target_pairs={{0,24},{8,16},{16,8},{24,0},{1,25},{9,17},{17,9},{25,1},{2,26},{10... | collective-permute-start | bytes 1572872 | tf_op jit(solution)/shard_map/ppermute | solution.py:41
  99.3 21.7 %collective-permute-done.16.refs_1_ = bf16[128,256]{1,0:T(8,128)(2,1)S(1)} collective-permute-done((bf16[128,256]{1,0:T(8,128)(2,1)S(1)}, bf16[128,256]{1,0:T(8,128)(2,1)S(1)}, u32[]{:S(2)}, u32[]{:S(2)}) %collective-permute-start.16) | collective-permute-done | bytes 65568 | tf_op jit(solution)/shard_map/ppermute | solution.py:41
  121.0 4.0 %collective-permute-done.18.refs_3_ = bf16[128,256]{1,0:T(8,128)(2,1)S(1)} collective-permute-done((bf16[128,256]{1,0:T(8,128)(2,1)S(1)}, bf16[128,256]{1,0:T(8,128)(2,1)S(1)}, u32[]{:S(2)}, u32[]{:S(2)}) %collective-permute-start.18) | collective-permute-done | bytes 65568 | tf_op jit(solution)/shard_map/ppermute | solution.py:41
  125.6 1.7 shard_map.100.refs_1_
  128.1 1.6 collective-permute-start.23
  130.9 1.9 shard_map.101
  133.0 2.4 %collective-permute-start.21 = (bf16[128,256]{1,0:T(8,128)(2,1)}, bf16[128,256]{1,0:T(8,128)(2,1)S(1)}, u32[]{:S(2)}, u32[]{:S(2)}) collective-permute-start(bf16[128,256]{1,0:T(8,128)(2,1)} %get-tuple-element.42), channel_id=1, source_target_pairs={{0,24},{8,16},{16,8},{24,0},{1,25},{9,17},{17,9},{25,1},{2,26},{10... | collective-permute-start | bytes 196616 | tf_op jit(solution)/shard_map/ppermute | solution.py:41
  136.3 4.1 %shard_map.103.refs_6_ = bf16[4,8,128,256]{3,2,1,0:T(8,128)(2,1)} custom-call(s32[1]{0:T(128)} %bitcast.5.me_ref, bf16[8,272,256]{2,1,0:T(8,128)(2,1)} %bitcast.10, bf16[8,256,256]{2,1,0:T(8,128)(2,1)} %copy-done.2, bf16[128,256]{1,0:T(8,128)(2,1)} %get-tuple-element.39._.refs_0_), custom_call_target="tpu_custom_call" | custom-call | flops 1024 | bytes 1024 | tf_op jit(solution)/shard_map/pallas_call | solution.py:263
  141.9 1.6 shard_map.104
  143.6 3.8 %all-to-all-start.2 = ((bf16[4,8,128,256]{3,2,1,0:T(8,128)(2,1)}), bf16[4,8,128,256]{3,2,1,0:T(8,128)(2,1)S(1)}, u32[]{:S(2)}, u32[]{:S(2)}) async-start(bf16[4,8,128,256]{3,2,1,0:T(8,128)(2,1)} %shard_map.103.refs_6_), calls=%async_computation.3 | async-start | bytes 4194304 | tf_op jit(solution)/shard_map/all_to_all | solution.py:377
  147.7 5.5 %collective-permute-start.25 = (bf16[4,128,256]{2,1,0:T(8,128)(2,1)S(1)}, bf16[4,128,256]{2,1,0:T(8,128)(2,1)S(1)}, u32[]{:S(2)}, u32[]{:S(2)}) collective-permute-start(bf16[4,128,256]{2,1,0:T(8,128)(2,1)S(1)} %copy-done.3), channel_id=1, source_target_pairs={{0,1},{1,0},{2,3},{3,2},{4,5},{5,4},{6,7},{7,6},{8,9},{9,8},{10,11... | collective-permute-start | bytes 786440 | tf_op jit(solution)/shard_map/ppermute | solution.py:41
  153.7 2.0 %collective-permute-done.24.refs_4_ = bf16[4,128,256]{2,1,0:T(8,128)(2,1)S(1)} collective-permute-done((bf16[4,128,256]{2,1,0:T(8,128)(2,1)S(1)}, bf16[4,128,256]{2,1,0:T(8,128)(2,1)S(1)}, u32[]{:S(2)}, u32[]{:S(2)}) %collective-permute-start.24) | collective-permute-done | bytes 262176 | tf_op jit(solution)/shard_map/ppermute | solution.py:41
  155.8 15.6 %collective-permute-start.28 = (bf16[4,128,256]{2,1,0:T(8,128)(2,1)S(1)}, bf16[4,128,256]{2,1,0:T(8,128)(2,1)}, u32[]{:S(2)}, u32[]{:S(2)}) collective-permute-start(bf16[4,128,256]{2,1,0:T(8,128)(2,1)S(1)} %collective-permute-done.24.refs_4_), channel_id=1, source_target_pairs={{0,1},{1,0},{2,3},{3,2},{4,5},{5,4},{6,7},{7,6},{8,9},{9,8},{10,11... | collective-permute-start | bytes 786440 | tf_op jit(solution)/shard_map/ppermute | solution.py:41
  175.3 4.3 %shard_map.106 = f32[8,256,256]{2,1,0:T(8,128)} custom-call(s32[8]{0:T(128)} %xor.40.order_ref, s32[1]{0:T(128)} %bitcast.5.me_ref, bf16[4,8,128,256]{3,2,1,0:T(8,128)(2,1)} %copy-done.1, bf16[4,128,256]{2,1,0:T(8,128)(2,1)} %shard_map.100.refs_1_, bf16[4,128,256]{2,1,0:T(8,128)(2,1)} %copy-done.8, bf16[4,128,256]{2,1,0:T(8,128)(2,1)} %copy-done.10, ...), custom_call_target="tpu_custom_call" | custom-call | flops 1024 | bytes 1024 | tf_op jit(solution)/shard_map/pallas_call | solution.py:346
  179.6 4.3 %shard_map.105 = f32[8,256,256]{2,1,0:T(8,128)} custom-call(s32[8]{0:T(128)} %xor.40.order_ref, s32[1]{0:T(128)} %bitcast.5.me_ref, bf16[8,128,256]{2,1,0:T(8,128)(2,1)} %get-tuple-element.31.refs_4_.refs_0_, bf16[8,128,256]{2,1,0:T(8,128)(2,1)} %copy-done.4, bf16[8,128,256]{2,1,0:T(8,128)(2,1)} %copy-done.5, bf16[8,128,256]{2,1,0:T(8,128)(2,1)} %copy-done.6, ...), custom_call_target="tpu_custom_call" | custom-call | flops 1024 | bytes 1024 | tf_op jit(solution)/shard_map/pallas_call | solution.py:346
  (138 shorter events, 25.8 us)
Async XLA Ops:
  7.2 32.2 %all-gather.5.cloned.1.call-start = ((), (), s32[]{:S(2)}) async-start(), calls=%async_computation.5 | async-start | bytes 1253376 | tf_op jit(solution)/shard_map/all_gather | solution.py:373
  16.6 36.8 %all-to-all-start = ((bf16[8,256,256]{2,1,0:T(8,128)(2,1)}), bf16[8,256,256]{2,1,0:T(8,128)(2,1)S(1)}, u32[]{:S(2)}, u32[]{:S(2)}) async-start(bf16[8,256,256]{2,1,0:T(8,128)(2,1)} %shard_map.96), calls=%async_computation | async-start | bytes 2097152 | tf_op jit(solution)/shard_map/all_to_all | solution.py:377
  23.1 106.7 %reduce-scatter.2.cloned.1.call-start = ((), (), s32[]{:S(2)}) async-start(), calls=%async_computation.4 | async-start | bytes 2359296 | tf_op jit(solution)/shard_map/reduce_scatter | solution.py:385
  23.1 6.5 %collective-permute-start.1 = (bf16[256,256]{1,0:T(8,128)(2,1)S(1)}, bf16[256,256]{1,0:T(8,128)(2,1)S(1)}, u32[]{:S(2)}, u32[]{:S(2)}) collective-permute-start(bf16[256,256]{1,0:T(8,128)(2,1)S(1)} %copy-done.12), channel_id=1, source_target_pairs={{0,16},{8,24},{16,0},{24,8},{1,17},{9,25},{17,1},{25,9},{2,18},{10... | collective-permute-start | bytes 393224 | tf_op jit(solution)/shard_map/ppermute | solution.py:41
  24.4 5.5 %collective-permute-start.2 = (bf16[256,256]{1,0:T(8,128)(2,1)S(1)}, bf16[256,256]{1,0:T(8,128)(2,1)S(1)}, u32[]{:S(2)}, u32[]{:S(2)}) collective-permute-start(bf16[256,256]{1,0:T(8,128)(2,1)S(1)} %copy-done.12), channel_id=1, source_target_pairs={{0,24},{8,16},{16,8},{24,0},{1,25},{9,17},{17,9},{25,1},{2,26},{10... | collective-permute-start | bytes 393224 | tf_op jit(solution)/shard_map/ppermute | solution.py:41
  44.8 5.6 %collective-permute-start.3 = (f32[3,2048]{1,0:T(4,128)}, f32[3,2048]{1,0:T(4,128)S(1)}, u32[]{:S(2)}, u32[]{:S(2)}) collective-permute-start(f32[3,2048]{1,0:T(4,128)} %shard_map.95.refs_0_._), channel_id=1, source_target_pairs={{0,1},{1,0},{2,3},{3,2},{4,5},{5,4},{6,7},{7,6},{8,9},{9,8},{10,11... | collective-permute-start | bytes 73736 | tf_op jit(solution)/shard_map/ppermute | solution.py:41
  45.1 6.8 %collective-permute-start.4 = (f32[3,2048]{1,0:T(4,128)}, f32[3,2048]{1,0:T(4,128)S(1)}, u32[]{:S(2)}, u32[]{:S(2)}) collective-permute-start(f32[3,2048]{1,0:T(4,128)} %shard_map.95.refs_0_._), channel_id=1, source_target_pairs={{0,2},{1,3},{2,0},{3,1},{4,6},{5,7},{6,4},{7,5},{8,10},{9,11},{10,... | collective-permute-start | bytes 73736 | tf_op jit(solution)/shard_map/ppermute | solution.py:41
  45.9 7.5 %collective-permute-start.5 = (f32[3,2048]{1,0:T(4,128)}, f32[3,2048]{1,0:T(4,128)S(1)}, u32[]{:S(2)}, u32[]{:S(2)}) collective-permute-start(f32[3,2048]{1,0:T(4,128)} %shard_map.95.refs_0_._), channel_id=1, source_target_pairs={{0,3},{1,2},{2,1},{3,0},{4,7},{5,6},{6,5},{7,4},{8,11},{9,10},{10,... | collective-permute-start | bytes 73736 | tf_op jit(solution)/shard_map/ppermute | solution.py:41
  47.0 7.1 %collective-permute-start.6 = (f32[3,2048]{1,0:T(4,128)}, f32[3,2048]{1,0:T(4,128)S(1)}, u32[]{:S(2)}, u32[]{:S(2)}) collective-permute-start(f32[3,2048]{1,0:T(4,128)} %shard_map.95.refs_0_._), channel_id=1, source_target_pairs={{0,4},{1,5},{2,6},{3,7},{4,0},{5,1},{6,2},{7,3},{8,12},{9,13},{10,... | collective-permute-start | bytes 73736 | tf_op jit(solution)/shard_map/ppermute | solution.py:41
  50.4 7.6 %collective-permute-start.8 = (f32[3,2048]{1,0:T(4,128)}, f32[3,2048]{1,0:T(4,128)S(1)}, u32[]{:S(2)}, u32[]{:S(2)}) collective-permute-start(f32[3,2048]{1,0:T(4,128)} %shard_map.95.refs_0_._), channel_id=1, source_target_pairs={{0,6},{1,7},{2,4},{3,5},{4,2},{5,3},{6,0},{7,1},{8,14},{9,15},{10,... | collective-permute-start | bytes 73736 | tf_op jit(solution)/shard_map/ppermute | solution.py:41
  51.9 7.5 %collective-permute-start.9 = (f32[3,2048]{1,0:T(4,128)}, f32[3,2048]{1,0:T(4,128)S(1)}, u32[]{:S(2)}, u32[]{:S(2)}) collective-permute-start(f32[3,2048]{1,0:T(4,128)} %shard_map.95.refs_0_._), channel_id=1, source_target_pairs={{0,7},{1,6},{2,5},{3,4},{4,3},{5,2},{6,1},{7,0},{8,15},{9,14},{10,... | collective-permute-start | bytes 73736 | tf_op jit(solution)/shard_map/ppermute | solution.py:41
  70.7 64.7 %all-to-all-start.1 = ((bf16[8,256,256]{2,1,0:T(8,128)(2,1)}), bf16[8,256,256]{2,1,0:T(8,128)(2,1)S(1)}, u32[]{:S(2)}, u32[]{:S(2)}) async-start(bf16[8,256,256]{2,1,0:T(8,128)(2,1)} %shard_map.102), calls=%async_computation.2 | async-start | bytes 2097152 | tf_op jit(solution)/shard_map/all_to_all | solution.py:377
  74.9 104.7 %all-gather.7.cloned.1.call-start = ((), (), s32[]{:S(2)}) async-start(), calls=%async_computation.6 | async-start | bytes 2359296 | tf_op jit(solution)/shard_map/all_gather | solution.py:398
  74.9 7.7 %collective-permute-start.10 = (f32[256,256]{1,0:T(8,128)S(1)}, f32[256,256]{1,0:T(8,128)S(1)}, u32[]{:S(2)}, u32[]{:S(2)}) collective-permute-start(f32[256,256]{1,0:T(8,128)S(1)} %copy-done.35), channel_id=1, source_target_pairs={{0,8},{8,0},{16,24},{24,16},{1,9},{9,1},{17,25},{25,17},{2,10},{10... | collective-permute-start | bytes 786440 | tf_op jit(solution)/shard_map/ppermute | solution.py:41
  75.4 7.3 %collective-permute-start.11 = (f32[256,256]{1,0:T(8,128)S(1)}, f32[256,256]{1,0:T(8,128)S(1)}, u32[]{:S(2)}, u32[]{:S(2)}) collective-permute-start(f32[256,256]{1,0:T(8,128)S(1)} %copy-done.34), channel_id=1, source_target_pairs={{0,16},{8,24},{16,0},{24,8},{1,17},{9,25},{17,1},{25,9},{2,18},{10... | collective-permute-start | bytes 786440 | tf_op jit(solution)/shard_map/ppermute | solution.py:41
  76.5 12.5 %collective-permute-start.12 = (f32[256,256]{1,0:T(8,128)S(1)}, f32[256,256]{1,0:T(8,128)S(1)}, u32[]{:S(2)}, u32[]{:S(2)}) collective-permute-start(f32[256,256]{1,0:T(8,128)S(1)} %copy-done.33), channel_id=1, source_target_pairs={{0,24},{8,16},{16,8},{24,0},{1,25},{9,17},{17,9},{25,1},{2,26},{10... | collective-permute-start | bytes 786440 | tf_op jit(solution)/shard_map/ppermute | solution.py:41
  95.9 33.8 %collective-permute-start.13 = (bf16[8,128,256]{2,1,0:T(8,128)(2,1)}, bf16[8,128,256]{2,1,0:T(8,128)(2,1)S(1)}, u32[]{:S(2)}, u32[]{:S(2)}) collective-permute-start(bf16[8,128,256]{2,1,0:T(8,128)(2,1)} %get-tuple-element.32), channel_id=1, source_target_pairs={{0,8},{8,0},{16,24},{24,16},{1,9},{9,1},{17,25},{25,17},{2,10},{10... | collective-permute-start | bytes 1572872 | tf_op jit(solution)/shard_map/ppermute | solution.py:41
  96.3 33.4 %collective-permute-start.14 = (bf16[8,128,256]{2,1,0:T(8,128)(2,1)}, bf16[8,128,256]{2,1,0:T(8,128)(2,1)S(1)}, u32[]{:S(2)}, u32[]{:S(2)}) collective-permute-start(bf16[8,128,256]{2,1,0:T(8,128)(2,1)} %get-tuple-element.33), channel_id=1, source_target_pairs={{0,16},{8,24},{16,0},{24,8},{1,17},{9,25},{17,1},{25,9},{2,18},{10... | collective-permute-start | bytes 1572872 | tf_op jit(solution)/shard_map/ppermute | solution.py:41
  96.6 33.1 %collective-permute-start.15 = (bf16[8,128,256]{2,1,0:T(8,128)(2,1)}, bf16[8,128,256]{2,1,0:T(8,128)(2,1)S(1)}, u32[]{:S(2)}, u32[]{:S(2)}) collective-permute-start(bf16[8,128,256]{2,1,0:T(8,128)(2,1)} %get-tuple-element.34), channel_id=1, source_target_pairs={{0,24},{8,16},{16,8},{24,0},{1,25},{9,17},{17,9},{25,1},{2,26},{10... | collective-permute-start | bytes 1572872 | tf_op jit(solution)/shard_map/ppermute | solution.py:41
  98.5 22.5 %collective-permute-start.16 = (bf16[128,256]{1,0:T(8,128)(2,1)S(1)}, bf16[128,256]{1,0:T(8,128)(2,1)S(1)}, u32[]{:S(2)}, u32[]{:S(2)}) collective-permute-start(bf16[128,256]{1,0:T(8,128)(2,1)S(1)} %copy-done.38), channel_id=1, source_target_pairs={{0,8},{8,0},{16,24},{24,16},{1,9},{9,1},{17,25},{25,17},{2,10},{10... | collective-permute-start | bytes 196616 | tf_op jit(solution)/shard_map/ppermute | solution.py:41
  98.9 22.1 %collective-permute-start.17 = (bf16[128,256]{1,0:T(8,128)(2,1)S(1)}, bf16[128,256]{1,0:T(8,128)(2,1)S(1)}, u32[]{:S(2)}, u32[]{:S(2)}) collective-permute-start(bf16[128,256]{1,0:T(8,128)(2,1)S(1)} %copy-done.37), channel_id=1, source_target_pairs={{0,16},{8,24},{16,0},{24,8},{1,17},{9,25},{17,1},{25,9},{2,18},{10... | collective-permute-start | bytes 196616 | tf_op jit(solution)/shard_map/ppermute | solution.py:41
  127.3 13.2 %collective-permute-start.22 = (bf16[4,128,256]{2,1,0:T(8,128)(2,1)}, bf16[4,128,256]{2,1,0:T(8,128)(2,1)S(1)}, u32[]{:S(2)}, u32[]{:S(2)}) collective-permute-start(bf16[4,128,256]{2,1,0:T(8,128)(2,1)} %shard_map.100.refs_1_), channel_id=1, source_target_pairs={{0,2},{1,3},{2,0},{3,1},{4,6},{5,7},{6,4},{7,5},{8,10},{9,11},{10,... | collective-permute-start | bytes 786440 | tf_op jit(solution)/shard_map/ppermute | solution.py:41
  128.1 12.4 %collective-permute-start.23 = (bf16[4,128,256]{2,1,0:T(8,128)(2,1)}, bf16[4,128,256]{2,1,0:T(8,128)(2,1)S(1)}, u32[]{:S(2)}, u32[]{:S(2)}) collective-permute-start(bf16[4,128,256]{2,1,0:T(8,128)(2,1)} %shard_map.100.refs_1_), channel_id=1, source_target_pairs={{0,4},{1,5},{2,6},{3,7},{4,0},{5,1},{6,2},{7,3},{8,12},{9,13},{10,... | collective-permute-start | bytes 786440 | tf_op jit(solution)/shard_map/ppermute | solution.py:41
  132.7 7.8 %collective-permute-start.19 = (bf16[128,256]{1,0:T(8,128)(2,1)}, bf16[128,256]{1,0:T(8,128)(2,1)S(1)}, u32[]{:S(2)}, u32[]{:S(2)}) collective-permute-start(bf16[128,256]{1,0:T(8,128)(2,1)} %get-tuple-element.40), channel_id=1, source_target_pairs={{0,8},{8,0},{16,24},{24,16},{1,9},{9,1},{17,25},{25,17},{2,10},{10... | collective-permute-start | bytes 196616 | tf_op jit(solution)/shard_map/ppermute | solution.py:41
  132.8 7.7 %collective-permute-start.20 = (bf16[128,256]{1,0:T(8,128)(2,1)}, bf16[128,256]{1,0:T(8,128)(2,1)S(1)}, u32[]{:S(2)}, u32[]{:S(2)}) collective-permute-start(bf16[128,256]{1,0:T(8,128)(2,1)} %get-tuple-element.41), channel_id=1, source_target_pairs={{0,16},{8,24},{16,0},{24,8},{1,17},{9,25},{17,1},{25,9},{2,18},{10... | collective-permute-start | bytes 196616 | tf_op jit(solution)/shard_map/ppermute | solution.py:41
  133.0 7.6 %collective-permute-start.21 = (bf16[128,256]{1,0:T(8,128)(2,1)}, bf16[128,256]{1,0:T(8,128)(2,1)S(1)}, u32[]{:S(2)}, u32[]{:S(2)}) collective-permute-start(bf16[128,256]{1,0:T(8,128)(2,1)} %get-tuple-element.42), channel_id=1, source_target_pairs={{0,24},{8,16},{16,8},{24,0},{1,25},{9,17},{17,9},{25,1},{2,26},{10... | collective-permute-start | bytes 196616 | tf_op jit(solution)/shard_map/ppermute | solution.py:41
  143.6 29.7 %all-to-all-start.2 = ((bf16[4,8,128,256]{3,2,1,0:T(8,128)(2,1)}), bf16[4,8,128,256]{3,2,1,0:T(8,128)(2,1)S(1)}, u32[]{:S(2)}, u32[]{:S(2)}) async-start(bf16[4,8,128,256]{3,2,1,0:T(8,128)(2,1)} %shard_map.103.refs_6_), calls=%async_computation.3 | async-start | bytes 4194304 | tf_op jit(solution)/shard_map/all_to_all | solution.py:377
  147.4 8.3 %collective-permute-start.24 = (bf16[4,128,256]{2,1,0:T(8,128)(2,1)S(1)}, bf16[4,128,256]{2,1,0:T(8,128)(2,1)S(1)}, u32[]{:S(2)}, u32[]{:S(2)}) collective-permute-start(bf16[4,128,256]{2,1,0:T(8,128)(2,1)S(1)} %copy-done.3), channel_id=1, source_target_pairs={{0,6},{1,7},{2,4},{3,5},{4,2},{5,3},{6,0},{7,1},{8,14},{9,15},{10,... | collective-permute-start | bytes 786440 | tf_op jit(solution)/shard_map/ppermute | solution.py:41
  147.7 25.6 %collective-permute-start.25 = (bf16[4,128,256]{2,1,0:T(8,128)(2,1)S(1)}, bf16[4,128,256]{2,1,0:T(8,128)(2,1)S(1)}, u32[]{:S(2)}, u32[]{:S(2)}) collective-permute-start(bf16[4,128,256]{2,1,0:T(8,128)(2,1)S(1)} %copy-done.3), channel_id=1, source_target_pairs={{0,1},{1,0},{2,3},{3,2},{4,5},{5,4},{6,7},{7,6},{8,9},{9,8},{10,11... | collective-permute-start | bytes 786440 | tf_op jit(solution)/shard_map/ppermute | solution.py:41
  153.2 20.1 %collective-permute-start.26 = (bf16[4,128,256]{2,1,0:T(8,128)(2,1)S(1)}, bf16[4,128,256]{2,1,0:T(8,128)(2,1)}, u32[]{:S(2)}, u32[]{:S(2)}) collective-permute-start(bf16[4,128,256]{2,1,0:T(8,128)(2,1)S(1)} %copy-done.9), channel_id=1, source_target_pairs={{0,1},{1,0},{2,3},{3,2},{4,5},{5,4},{6,7},{7,6},{8,9},{9,8},{10,11... | collective-permute-start | bytes 786440 | tf_op jit(solution)/shard_map/ppermute | solution.py:41
  153.3 20.0 %collective-permute-start.27 = (bf16[4,128,256]{2,1,0:T(8,128)(2,1)S(1)}, bf16[4,128,256]{2,1,0:T(8,128)(2,1)}, u32[]{:S(2)}, u32[]{:S(2)}) collective-permute-start(bf16[4,128,256]{2,1,0:T(8,128)(2,1)S(1)} %copy-done.11), channel_id=1, source_target_pairs={{0,1},{1,0},{2,3},{3,2},{4,5},{5,4},{6,7},{7,6},{8,9},{9,8},{10,11... | collective-permute-start | bytes 786440 | tf_op jit(solution)/shard_map/ppermute | solution.py:41
  155.8 17.5 %collective-permute-start.28 = (bf16[4,128,256]{2,1,0:T(8,128)(2,1)S(1)}, bf16[4,128,256]{2,1,0:T(8,128)(2,1)}, u32[]{:S(2)}, u32[]{:S(2)}) collective-permute-start(bf16[4,128,256]{2,1,0:T(8,128)(2,1)S(1)} %collective-permute-done.24.refs_4_), channel_id=1, source_target_pairs={{0,1},{1,0},{2,3},{3,2},{4,5},{5,4},{6,7},{7,6},{8,9},{9,8},{10,11... | collective-permute-start | bytes 786440 | tf_op jit(solution)/shard_map/ppermute | solution.py:41
  (42 other events, 225.2 us)
Sparse Core Ops, SparseCore 0:
  10.2 29.1 all-gather.4
  68.4 53.3 reduce-scatter.1
  143.7 35.6 all-gather.6

commit v12 on v11

--- a/solution.py
+++ b/solution.py
@@ -385,12 +385,12 @@
     user_grad = lax.psum_scatter(user_part, "item", scatter_dimension=0, tiled=True)
     item_pieces = exchange(item_parts, "user")
 
-    item_routed = route(me, targets, item_pieces, 1, groups, [])
-    user_slots = slot_hidden(me, users, user_cols, groups, 0, True, item_routed[0])
-    item_sent = stack(exchange(item_routed, "user"), user_slots[:1])
+    user_slots = slot_hidden(me, users, user_cols, groups, 0, True, item_parts[0])
+    user_rows = exchange(user_slots, "user")
+    item_routed = route(me, targets, item_pieces, 1, groups, user_slots[:1])
+    item_sent = stack(exchange(item_routed, "user"))
     item_line = exchange([item_sent] * lines, "item", CORES)
-    user_rows = exchange(user_slots, "user")
-    user_routed = route(me, targets, [user_grad], 0, groups, [item_sent] + user_rows[1:])
+    user_routed = route(me, targets, [user_grad], 0, groups, user_rows[1:])
     item_slots = slot_hidden(me, users, item_cols, groups, 1, False, user_routed[0])
     user_sent = stack(exchange(user_routed, "user"), item_line[1:3] + [item_slots[0]])
     item_rows = [scatter(item_slots[0], "user")]

time: 193 us -> 185 us (0.959)
  waiting for transfers between devices: 64.5 us -> 59.5 us
  starting transfers between devices: 57.4 us -> 54 us
    ppermute x29, waiting for transfers between devices: 54.3 us -> 48.9 us  [swap(): return lax.ppermute(piece, axis, [(j, j ^ bits) for j in range(size)])]
    ppermute x29, starting transfers between devices: 42.8 us -> 39.1 us  [swap(): return lax.ppermute(piece, axis, [(j, j ^ bits) for j in range(size)])]
    unnamed x78 -> x72, local copies, waits for them, and re-layouts: 8.06 us -> 7.88 us
  transfers between devices with their start and end apart: 35 -> 35, of which waited for: 15 -> 16; matrix products, arithmetic and copies ran while one was open for 1% -> 1% of each run, Pallas kernels for 15% -> 15%
where the time goes in v12:
time: 185 us; the launch traced here: 182 us
  waiting for transfers between devices  59.5 us (32%)
  starting transfers between devices  54 us (29%)
  Pallas kernels  44 us (24%)
  between operations  14 us (8%)
  local copies, waits for them, and re-layouts  9.76 us (5%)
    ppermute x29, waiting for transfers between devices, swap(): return lax.ppermute(piece, axis, [(j, j ^ bits) for j in range(size)])  48.9 us
    ppermute x29, starting transfers between devices, swap(): return lax.ppermute(piece, axis, [(j, j ^ bits) for j in range(size)])  39.1 us
    all_to_all x3, starting transfers between devices, scatter(): return lax.all_to_all(pieces, axis, split_axis=0, concat_axis=0, tiled=True)  14.8 us
    all_gather x1, waiting for transfers between devices, shards(): users = lax.all_gather(packed, 'item', axis=0)  9.52 us
    pallas_call x2, Pallas kernels, outer(): pl.pallas_call(functools.partial(outer_kernel, count=len(hidden)), grid=(...  8.58 us
    pallas_call x1, Pallas kernels, grads(): pl.pallas_call(functools.partial(grad_kernel, rows=rows, chunk=64, count=...  8.17 us
    pallas_call x2, Pallas kernels, slot_hidden(): pl.pallas_call(functools.partial(hidden_kernel, tower=tower), grid=(block...  8.13 us
    unnamed x72, local copies, waits for them, and re-layouts  7.88 us
  transfers between devices with their start and end apart: 35, of which 16 were waited for; matrix products, arithmetic and copies ran while one was open for 1% of the time, Pallas kernels for 15%

profile of v12, /device:TPU:11, one launch (start us, length us, event | category | flops | bytes accessed | tf_op | source)
XLA Modules:
  0.0 181.8 jit_solution(7971301353227185275)
XLA Ops:
  7.2 1.7 shard_map.94
  9.3 4.3 %collective-permute-done.refs_1_._.refs_9_ = bf16[256,256]{1,0:T(8,128)(2,1)S(1)} collective-permute-done((bf16[256,256]{1,0:T(8,128)(2,1)}, bf16[256,256]{1,0:T(8,128)(2,1)S(1)}, u32[]{:S(2)}, u32[]{:S(2)}) %collective-permute-start) | collective-permute-done | bytes 131104 | tf_op jit(solution)/shard_map/ppermute | solution.py:41
  14.3 2.3 %shard_map.96 = bf16[8,256,256]{2,1,0:T(8,128)(2,1)} custom-call(bf16[256,2048]{1,0:T(8,128)(2,1)} %in_ref.2, bf16[256,256]{1,0:T(8,128)(2,1)} %copy-done.6), custom_call_target="tpu_custom_call" | custom-call | flops 1024 | bytes 1024 | tf_op jit(solution)/shard_map/pallas_call | solution.py:221
  16.6 6.5 %all-to-all-start = ((bf16[8,256,256]{2,1,0:T(8,128)(2,1)}), bf16[8,256,256]{2,1,0:T(8,128)(2,1)S(1)}, u32[]{:S(2)}, u32[]{:S(2)}) async-start(bf16[8,256,256]{2,1,0:T(8,128)(2,1)} %shard_map.96), calls=%async_computation | async-start | bytes 2097152 | tf_op jit(solution)/shard_map/all_to_all | solution.py:377
  23.1 1.3 collective-permute-start.1
  25.1 4.5 %collective-permute-done.1.refs_2_.refs_10_ = bf16[256,256]{1,0:T(8,128)(2,1)S(1)} collective-permute-done((bf16[256,256]{1,0:T(8,128)(2,1)S(1)}, bf16[256,256]{1,0:T(8,128)(2,1)S(1)}, u32[]{:S(2)}, u32[]{:S(2)}) %collective-permute-start.1) | collective-permute-done | bytes 131104 | tf_op jit(solution)/shard_map/ppermute | solution.py:41
  29.9 9.5 %all-gather.5.cloned.1.call-done = bf16[2176,256]{1,0:T(8,128)(2,1)} async-done(((bf16[272,256]{1,0:T(8,128)(2,1)}), bf16[2176,256]{1,0:T(8,128)(2,1)}) %all-gather.5.cloned.1.call-update) | async-done | bytes 1114128 | tf_op jit(solution)/shard_map/all_gather | solution.py:373
  39.4 5.4 %shard_map.95.refs_0_._ = f32[3,2048]{1,0:T(4,128)} custom-call(s32[4]{0:T(128)} %add_multiply_fusion.first_ref, bf16[8,272,256]{2,1,0:T(8,128)(2,1)} %bitcast.7, bf16[256,256]{1,0:T(8,128)(2,1)} %refs_8_.1, bf16[256,256]{1,0:T(8,128)(2,1)} %copy-done.6, bf16[256,256]{1,0:T(8,128)(2,1)} %copy-done.13, bf16[256,256]{1,0:T(8,128)(2,1)} %copy-done.14, ...), custom_call_target="tpu_custom_call" | custom-call | flops 1024 | bytes 1024 | tf_op jit(solution)/shard_map/pallas_call | solution.py:119
  47.0 3.4 %collective-permute-start.6 = (f32[3,2048]{1,0:T(4,128)}, f32[3,2048]{1,0:T(4,128)S(1)}, u32[]{:S(2)}, u32[]{:S(2)}) collective-permute-start(f32[3,2048]{1,0:T(4,128)} %shard_map.95.refs_0_._), channel_id=1, source_target_pairs={{0,4},{1,5},{2,6},{3,7},{4,0},{5,1},{6,2},{7,3},{8,12},{9,13},{10,... | collective-permute-start | bytes 73736 | tf_op jit(solution)/shard_map/ppermute | solution.py:41
  50.4 1.5 collective-permute-start.8
  55.2 2.8 %collective-permute-done.8.refs_6_ = f32[3,2048]{1,0:T(4,128)S(1)} collective-permute-done((f32[3,2048]{1,0:T(4,128)}, f32[3,2048]{1,0:T(4,128)S(1)}, u32[]{:S(2)}, u32[]{:S(2)}) %collective-permute-start.8) | collective-permute-done | bytes 24608 | tf_op jit(solution)/shard_map/ppermute | solution.py:41
  58.0 1.4 collective-permute-done.9.refs_7_
  60.1 8.2 %shard_map.97 = (f32[1,2048]{1,0:T(1,128)}, f32[2048,256]{1,0:T(8,128)}, f32[256,256]{1,0:T(8,128)}, f32[256,256]{1,0:T(8,128)}, f32[256,256]{1,0:T(8,128)}, /*index=5*/f32[256,256]{1,0:T(8,128)}) custom-call(s32[4]{0:T(128)} %add_multiply_fusion.first_ref, bf16[8,272,256]{2,1,0:T(8,128)(2,1)} %bitcast.8, f32[3,2048]{1,0:T(4,128)} %shard_map.95.refs_0_._, ...), custom_call_target="tpu_custom_call" | custom-call | flops 1024 | bytes 1024 | tf_op jit(solution)/shard_map/pallas_call | solution.py:182
  68.3 2.4 %shard_map.102 = bf16[8,256,256]{2,1,0:T(8,128)(2,1)} custom-call(bf16[256,2048]{1,0:T(8,128)(2,1)} %in_ref.3, f32[3,2048]{1,0:T(4,128)} %shard_map.95.refs_0_._), custom_call_target="tpu_custom_call" | custom-call | flops 1024 | bytes 1024 | tf_op jit(solution)/shard_map/pallas_call | solution.py:221
  70.7 4.3 %all-to-all-start.1 = ((bf16[8,256,256]{2,1,0:T(8,128)(2,1)}), bf16[8,256,256]{2,1,0:T(8,128)(2,1)S(1)}, u32[]{:S(2)}, u32[]{:S(2)}) async-start(bf16[8,256,256]{2,1,0:T(8,128)(2,1)} %shard_map.102), calls=%async_computation.2 | async-start | bytes 2097152 | tf_op jit(solution)/shard_map/all_to_all | solution.py:377
  77.7 4.0 %shard_map.98 = (bf16[8,128,256]{2,1,0:T(8,128)(2,1)}, bf16[8,128,256]{2,1,0:T(8,128)(2,1)}, bf16[8,128,256]{2,1,0:T(8,128)(2,1)}, bf16[8,128,256]{2,1,0:T(8,128)(2,1)}) custom-call(s32[1]{0:T(128)} %bitcast.5.me_ref, bf16[8,272,256]{2,1,0:T(8,128)(2,1)} %bitcast.9, bf16[8,256,256]{2,1,0:T(8,128)(2,1)} %copy-done, f32[256,256]{1,0:T(8,128)} %get-tuple-element.25._.refs_0_), custom_call_target="tpu_custom_call" | custom-call | flops 1024 | bytes 1024 | tf_op jit(solution)/shard_map/pallas_call | solution.py:263
  84.3 4.9 %collective-permute-done.18.refs_3_ = f32[256,256]{1,0:T(8,128)S(1)} collective-permute-done((f32[256,256]{1,0:T(8,128)S(1)}, f32[256,256]{1,0:T(8,128)S(1)}, u32[]{:S(2)}, u32[]{:S(2)}) %collective-permute-start.18) | collective-permute-done | bytes 262176 | tf_op jit(solution)/shard_map/ppermute | solution.py:41
  89.9 2.1 %shard_map.100 = (bf16[128,256]{1,0:T(8,128)(2,1)}, bf16[128,256]{1,0:T(8,128)(2,1)}, bf16[128,256]{1,0:T(8,128)(2,1)}, bf16[128,256]{1,0:T(8,128)(2,1)}) custom-call(s32[1]{0:T(128)} %bitcast.5.me_ref, s32[2,256]{1,0:T(2,128)} %get-tuple-element.30.target_ref, f32[256,256]{1,0:T(8,128)} %get-tuple-element.25._.refs_0_, f32[256,256]{1,0:T(8,128)} %copy-done.15, ...), custom_call_target="tpu_custom_call" | custom-call | flops 1024 | bytes 1024 | tf_op jit(solution)/shard_map/pallas_call | solution.py:295
  92.8 19.4 %collective-permute-done.19.refs_1_ = bf16[128,256]{1,0:T(8,128)(2,1)S(1)} collective-permute-done((bf16[128,256]{1,0:T(8,128)(2,1)}, bf16[128,256]{1,0:T(8,128)(2,1)S(1)}, u32[]{:S(2)}, u32[]{:S(2)}) %collective-permute-start.19) | collective-permute-done | bytes 65568 | tf_op jit(solution)/shard_map/ppermute | solution.py:41
  113.5 2.9 %collective-permute-done.21.refs_3_ = bf16[128,256]{1,0:T(8,128)(2,1)S(1)} collective-permute-done((bf16[128,256]{1,0:T(8,128)(2,1)}, bf16[128,256]{1,0:T(8,128)(2,1)S(1)}, u32[]{:S(2)}, u32[]{:S(2)}) %collective-permute-start.21) | collective-permute-done | bytes 65568 | tf_op jit(solution)/shard_map/ppermute | solution.py:41
  117.0 1.7 shard_map.101.refs_1_
  119.0 2.1 %collective-permute-start.23 = (bf16[4,128,256]{2,1,0:T(8,128)(2,1)}, bf16[4,128,256]{2,1,0:T(8,128)(2,1)S(1)}, u32[]{:S(2)}, u32[]{:S(2)}) collective-permute-start(bf16[4,128,256]{2,1,0:T(8,128)(2,1)} %shard_map.101.refs_1_), channel_id=1, source_target_pairs={{0,4},{1,5},{2,6},{3,7},{4,0},{5,1},{6,2},{7,3},{8,12},{9,13},{10,... | collective-permute-start | bytes 786440 | tf_op jit(solution)/shard_map/ppermute | solution.py:41
  122.3 1.9 %shard_map.99 = (bf16[128,256]{1,0:T(8,128)(2,1)}, bf16[128,256]{1,0:T(8,128)(2,1)}, bf16[128,256]{1,0:T(8,128)(2,1)}, bf16[128,256]{1,0:T(8,128)(2,1)}) custom-call(s32[1]{0:T(128)} %bitcast.5.me_ref, s32[2,256]{1,0:T(2,128)} %get-tuple-element.30.target_ref, f32[256,256]{1,0:T(8,128)} %reduce-scatter.2.cloned.1.call-done.refs_0_, ...), custom_call_target="tpu_custom_call" | custom-call | flops 1024 | bytes 1024 | tf_op jit(solution)/shard_map/pallas_call | solution.py:295
  127.8 4.1 %shard_map.103.refs_6_ = bf16[4,8,128,256]{3,2,1,0:T(8,128)(2,1)} custom-call(s32[1]{0:T(128)} %bitcast.5.me_ref, bf16[8,272,256]{2,1,0:T(8,128)(2,1)} %bitcast.10, bf16[8,256,256]{2,1,0:T(8,128)(2,1)} %copy-done.2, bf16[128,256]{1,0:T(8,128)(2,1)} %get-tuple-element.32._.refs_0_), custom_call_target="tpu_custom_call" | custom-call | flops 1024 | bytes 1024 | tf_op jit(solution)/shard_map/pallas_call | solution.py:263
  133.4 1.6 shard_map.104
  135.1 4.0 %all-to-all-start.2 = ((bf16[4,8,128,256]{3,2,1,0:T(8,128)(2,1)}), bf16[4,8,128,256]{3,2,1,0:T(8,128)(2,1)S(1)}, u32[]{:S(2)}, u32[]{:S(2)}) async-start(bf16[4,8,128,256]{3,2,1,0:T(8,128)(2,1)} %shard_map.103.refs_6_), calls=%async_computation.3 | async-start | bytes 4194304 | tf_op jit(solution)/shard_map/all_to_all | solution.py:377
  139.4 4.3 %collective-permute-start.25 = (bf16[4,128,256]{2,1,0:T(8,128)(2,1)S(1)}, bf16[4,128,256]{2,1,0:T(8,128)(2,1)S(1)}, u32[]{:S(2)}, u32[]{:S(2)}) collective-permute-start(bf16[4,128,256]{2,1,0:T(8,128)(2,1)S(1)} %copy-done.11), channel_id=1, source_target_pairs={{0,1},{1,0},{2,3},{3,2},{4,5},{5,4},{6,7},{7,6},{8,9},{9,8},{10,11... | collective-permute-start | bytes 786440 | tf_op jit(solution)/shard_map/ppermute | solution.py:41
  144.2 6.5 %collective-permute-done.24.refs_4_ = bf16[4,128,256]{2,1,0:T(8,128)(2,1)S(1)} collective-permute-done((bf16[4,128,256]{2,1,0:T(8,128)(2,1)S(1)}, bf16[4,128,256]{2,1,0:T(8,128)(2,1)S(1)}, u32[]{:S(2)}, u32[]{:S(2)}) %collective-permute-start.24) | collective-permute-done | bytes 262176 | tf_op jit(solution)/shard_map/ppermute | solution.py:41
  150.7 11.8 %collective-permute-start.28 = (bf16[4,128,256]{2,1,0:T(8,128)(2,1)S(1)}, bf16[4,128,256]{2,1,0:T(8,128)(2,1)}, u32[]{:S(2)}, u32[]{:S(2)}) collective-permute-start(bf16[4,128,256]{2,1,0:T(8,128)(2,1)S(1)} %collective-permute-done.24.refs_4_), channel_id=1, source_target_pairs={{0,1},{1,0},{2,3},{3,2},{4,5},{5,4},{6,7},{7,6},{8,9},{9,8},{10,11... | collective-permute-start | bytes 786440 | tf_op jit(solution)/shard_map/ppermute | solution.py:41
  165.1 1.3 copy-done.1
  166.5 4.3 %shard_map.106 = f32[8,256,256]{2,1,0:T(8,128)} custom-call(s32[8]{0:T(128)} %xor.40.order_ref, s32[1]{0:T(128)} %bitcast.5.me_ref, bf16[4,8,128,256]{3,2,1,0:T(8,128)(2,1)} %copy-done.1, bf16[4,128,256]{2,1,0:T(8,128)(2,1)} %shard_map.101.refs_1_, bf16[4,128,256]{2,1,0:T(8,128)(2,1)} %copy-done.7, bf16[4,128,256]{2,1,0:T(8,128)(2,1)} %copy-done.9, ...), custom_call_target="tpu_custom_call" | custom-call | flops 1024 | bytes 1024 | tf_op jit(solution)/shard_map/pallas_call | solution.py:346
  170.9 4.3 %shard_map.105 = f32[8,256,256]{2,1,0:T(8,128)} custom-call(s32[8]{0:T(128)} %xor.40.order_ref, s32[1]{0:T(128)} %bitcast.5.me_ref, bf16[8,128,256]{2,1,0:T(8,128)(2,1)} %get-tuple-element.26.refs_4_.refs_0_, bf16[8,128,256]{2,1,0:T(8,128)(2,1)} %copy-done.3, bf16[8,128,256]{2,1,0:T(8,128)(2,1)} %copy-done.4, bf16[8,128,256]{2,1,0:T(8,128)(2,1)} %copy-done.5, ...), custom_call_target="tpu_custom_call" | custom-call | flops 1024 | bytes 1024 | tf_op jit(solution)/shard_map/pallas_call | solution.py:346
  (132 shorter events, 27.2 us)
Async XLA Ops:
  7.2 32.2 %all-gather.5.cloned.1.call-start = ((), (), s32[]{:S(2)}) async-start(), calls=%async_computation.5 | async-start | bytes 1253376 | tf_op jit(solution)/shard_map/all_gather | solution.py:373
  16.6 36.8 %all-to-all-start = ((bf16[8,256,256]{2,1,0:T(8,128)(2,1)}), bf16[8,256,256]{2,1,0:T(8,128)(2,1)S(1)}, u32[]{:S(2)}, u32[]{:S(2)}) async-start(bf16[8,256,256]{2,1,0:T(8,128)(2,1)} %shard_map.96), calls=%async_computation | async-start | bytes 2097152 | tf_op jit(solution)/shard_map/all_to_all | solution.py:377
  23.1 98.3 %reduce-scatter.2.cloned.1.call-start = ((), (), s32[]{:S(2)}) async-start(), calls=%async_computation.4 | async-start | bytes 2359296 | tf_op jit(solution)/shard_map/reduce_scatter | solution.py:385
  23.1 6.5 %collective-permute-start.1 = (bf16[256,256]{1,0:T(8,128)(2,1)S(1)}, bf16[256,256]{1,0:T(8,128)(2,1)S(1)}, u32[]{:S(2)}, u32[]{:S(2)}) collective-permute-start(bf16[256,256]{1,0:T(8,128)(2,1)S(1)} %copy-done.12), channel_id=1, source_target_pairs={{0,16},{8,24},{16,0},{24,8},{1,17},{9,25},{17,1},{25,9},{2,18},{10... | collective-permute-start | bytes 393224 | tf_op jit(solution)/shard_map/ppermute | solution.py:41
  24.4 5.5 %collective-permute-start.2 = (bf16[256,256]{1,0:T(8,128)(2,1)S(1)}, bf16[256,256]{1,0:T(8,128)(2,1)S(1)}, u32[]{:S(2)}, u32[]{:S(2)}) collective-permute-start(bf16[256,256]{1,0:T(8,128)(2,1)S(1)} %copy-done.12), channel_id=1, source_target_pairs={{0,24},{8,16},{16,8},{24,0},{1,25},{9,17},{17,9},{25,1},{2,26},{10... | collective-permute-start | bytes 393224 | tf_op jit(solution)/shard_map/ppermute | solution.py:41
  44.8 5.6 %collective-permute-start.3 = (f32[3,2048]{1,0:T(4,128)}, f32[3,2048]{1,0:T(4,128)S(1)}, u32[]{:S(2)}, u32[]{:S(2)}) collective-permute-start(f32[3,2048]{1,0:T(4,128)} %shard_map.95.refs_0_._), channel_id=1, source_target_pairs={{0,1},{1,0},{2,3},{3,2},{4,5},{5,4},{6,7},{7,6},{8,9},{9,8},{10,11... | collective-permute-start | bytes 73736 | tf_op jit(solution)/shard_map/ppermute | solution.py:41
  45.1 6.8 %collective-permute-start.4 = (f32[3,2048]{1,0:T(4,128)}, f32[3,2048]{1,0:T(4,128)S(1)}, u32[]{:S(2)}, u32[]{:S(2)}) collective-permute-start(f32[3,2048]{1,0:T(4,128)} %shard_map.95.refs_0_._), channel_id=1, source_target_pairs={{0,2},{1,3},{2,0},{3,1},{4,6},{5,7},{6,4},{7,5},{8,10},{9,11},{10,... | collective-permute-start | bytes 73736 | tf_op jit(solution)/shard_map/ppermute | solution.py:41
  45.9 7.4 %collective-permute-start.5 = (f32[3,2048]{1,0:T(4,128)}, f32[3,2048]{1,0:T(4,128)S(1)}, u32[]{:S(2)}, u32[]{:S(2)}) collective-permute-start(f32[3,2048]{1,0:T(4,128)} %shard_map.95.refs_0_._), channel_id=1, source_target_pairs={{0,3},{1,2},{2,1},{3,0},{4,7},{5,6},{6,5},{7,4},{8,11},{9,10},{10,... | collective-permute-start | bytes 73736 | tf_op jit(solution)/shard_map/ppermute | solution.py:41
  47.0 7.1 %collective-permute-start.6 = (f32[3,2048]{1,0:T(4,128)}, f32[3,2048]{1,0:T(4,128)S(1)}, u32[]{:S(2)}, u32[]{:S(2)}) collective-permute-start(f32[3,2048]{1,0:T(4,128)} %shard_map.95.refs_0_._), channel_id=1, source_target_pairs={{0,4},{1,5},{2,6},{3,7},{4,0},{5,1},{6,2},{7,3},{8,12},{9,13},{10,... | collective-permute-start | bytes 73736 | tf_op jit(solution)/shard_map/ppermute | solution.py:41
  50.4 7.6 %collective-permute-start.8 = (f32[3,2048]{1,0:T(4,128)}, f32[3,2048]{1,0:T(4,128)S(1)}, u32[]{:S(2)}, u32[]{:S(2)}) collective-permute-start(f32[3,2048]{1,0:T(4,128)} %shard_map.95.refs_0_._), channel_id=1, source_target_pairs={{0,6},{1,7},{2,4},{3,5},{4,2},{5,3},{6,0},{7,1},{8,14},{9,15},{10,... | collective-permute-start | bytes 73736 | tf_op jit(solution)/shard_map/ppermute | solution.py:41
  51.9 7.5 %collective-permute-start.9 = (f32[3,2048]{1,0:T(4,128)}, f32[3,2048]{1,0:T(4,128)S(1)}, u32[]{:S(2)}, u32[]{:S(2)}) collective-permute-start(f32[3,2048]{1,0:T(4,128)} %shard_map.95.refs_0_._), channel_id=1, source_target_pairs={{0,7},{1,6},{2,5},{3,4},{4,3},{5,2},{6,1},{7,0},{8,15},{9,14},{10,... | collective-permute-start | bytes 73736 | tf_op jit(solution)/shard_map/ppermute | solution.py:41
  70.7 56.1 %all-to-all-start.1 = ((bf16[8,256,256]{2,1,0:T(8,128)(2,1)}), bf16[8,256,256]{2,1,0:T(8,128)(2,1)S(1)}, u32[]{:S(2)}, u32[]{:S(2)}) async-start(bf16[8,256,256]{2,1,0:T(8,128)(2,1)} %shard_map.102), calls=%async_computation.2 | async-start | bytes 2097152 | tf_op jit(solution)/shard_map/all_to_all | solution.py:377
  74.9 96.0 %all-gather.7.cloned.1.call-start = ((), (), s32[]{:S(2)}) async-start(), calls=%async_computation.6 | async-start | bytes 2359296 | tf_op jit(solution)/shard_map/all_gather | solution.py:398
  74.9 8.2 %collective-permute-start.16 = (f32[256,256]{1,0:T(8,128)S(1)}, f32[256,256]{1,0:T(8,128)S(1)}, u32[]{:S(2)}, u32[]{:S(2)}) collective-permute-start(f32[256,256]{1,0:T(8,128)S(1)} %copy-done.35), channel_id=1, source_target_pairs={{0,8},{8,0},{16,24},{24,16},{1,9},{9,1},{17,25},{25,17},{2,10},{10... | collective-permute-start | bytes 786440 | tf_op jit(solution)/shard_map/ppermute | solution.py:41
  75.3 9.0 %collective-permute-start.17 = (f32[256,256]{1,0:T(8,128)S(1)}, f32[256,256]{1,0:T(8,128)S(1)}, u32[]{:S(2)}, u32[]{:S(2)}) collective-permute-start(f32[256,256]{1,0:T(8,128)S(1)} %copy-done.34), channel_id=1, source_target_pairs={{0,16},{8,24},{16,0},{24,8},{1,17},{9,25},{17,1},{25,9},{2,18},{10... | collective-permute-start | bytes 786440 | tf_op jit(solution)/shard_map/ppermute | solution.py:41
  76.5 12.7 %collective-permute-start.18 = (f32[256,256]{1,0:T(8,128)S(1)}, f32[256,256]{1,0:T(8,128)S(1)}, u32[]{:S(2)}, u32[]{:S(2)}) collective-permute-start(f32[256,256]{1,0:T(8,128)S(1)} %copy-done.33), channel_id=1, source_target_pairs={{0,24},{8,16},{16,8},{24,0},{1,25},{9,17},{17,9},{25,1},{2,26},{10... | collective-permute-start | bytes 786440 | tf_op jit(solution)/shard_map/ppermute | solution.py:41
  81.6 39.5 %collective-permute-start.10 = (bf16[8,128,256]{2,1,0:T(8,128)(2,1)}, bf16[8,128,256]{2,1,0:T(8,128)(2,1)S(1)}, u32[]{:S(2)}, u32[]{:S(2)}) collective-permute-start(bf16[8,128,256]{2,1,0:T(8,128)(2,1)} %get-tuple-element.27), channel_id=1, source_target_pairs={{0,8},{8,0},{16,24},{24,16},{1,9},{9,1},{17,25},{25,17},{2,10},{10... | collective-permute-start | bytes 1572872 | tf_op jit(solution)/shard_map/ppermute | solution.py:41
  81.9 39.2 %collective-permute-start.11 = (bf16[8,128,256]{2,1,0:T(8,128)(2,1)}, bf16[8,128,256]{2,1,0:T(8,128)(2,1)S(1)}, u32[]{:S(2)}, u32[]{:S(2)}) collective-permute-start(bf16[8,128,256]{2,1,0:T(8,128)(2,1)} %get-tuple-element.28), channel_id=1, source_target_pairs={{0,16},{8,24},{16,0},{24,8},{1,17},{9,25},{17,1},{25,9},{2,18},{10... | collective-permute-start | bytes 1572872 | tf_op jit(solution)/shard_map/ppermute | solution.py:41
  83.1 38.0 %collective-permute-start.12 = (bf16[8,128,256]{2,1,0:T(8,128)(2,1)}, bf16[8,128,256]{2,1,0:T(8,128)(2,1)S(1)}, u32[]{:S(2)}, u32[]{:S(2)}) collective-permute-start(bf16[8,128,256]{2,1,0:T(8,128)(2,1)} %get-tuple-element.29), channel_id=1, source_target_pairs={{0,24},{8,16},{16,8},{24,0},{1,25},{9,17},{17,9},{25,1},{2,26},{10... | collective-permute-start | bytes 1572872 | tf_op jit(solution)/shard_map/ppermute | solution.py:41
  92.0 20.1 %collective-permute-start.19 = (bf16[128,256]{1,0:T(8,128)(2,1)}, bf16[128,256]{1,0:T(8,128)(2,1)S(1)}, u32[]{:S(2)}, u32[]{:S(2)}) collective-permute-start(bf16[128,256]{1,0:T(8,128)(2,1)} %get-tuple-element.40), channel_id=1, source_target_pairs={{0,8},{8,0},{16,24},{24,16},{1,9},{9,1},{17,25},{25,17},{2,10},{10... | collective-permute-start | bytes 196616 | tf_op jit(solution)/shard_map/ppermute | solution.py:41
  92.2 21.2 %collective-permute-start.20 = (bf16[128,256]{1,0:T(8,128)(2,1)}, bf16[128,256]{1,0:T(8,128)(2,1)S(1)}, u32[]{:S(2)}, u32[]{:S(2)}) collective-permute-start(bf16[128,256]{1,0:T(8,128)(2,1)} %get-tuple-element.41), channel_id=1, source_target_pairs={{0,16},{8,24},{16,0},{24,8},{1,17},{9,25},{17,1},{25,9},{2,18},{10... | collective-permute-start | bytes 196616 | tf_op jit(solution)/shard_map/ppermute | solution.py:41
  118.6 13.3 %collective-permute-start.22 = (bf16[4,128,256]{2,1,0:T(8,128)(2,1)}, bf16[4,128,256]{2,1,0:T(8,128)(2,1)S(1)}, u32[]{:S(2)}, u32[]{:S(2)}) collective-permute-start(bf16[4,128,256]{2,1,0:T(8,128)(2,1)} %shard_map.101.refs_1_), channel_id=1, source_target_pairs={{0,2},{1,3},{2,0},{3,1},{4,6},{5,7},{6,4},{7,5},{8,10},{9,11},{10,... | collective-permute-start | bytes 786440 | tf_op jit(solution)/shard_map/ppermute | solution.py:41
  119.0 12.9 %collective-permute-start.23 = (bf16[4,128,256]{2,1,0:T(8,128)(2,1)}, bf16[4,128,256]{2,1,0:T(8,128)(2,1)S(1)}, u32[]{:S(2)}, u32[]{:S(2)}) collective-permute-start(bf16[4,128,256]{2,1,0:T(8,128)(2,1)} %shard_map.101.refs_1_), channel_id=1, source_target_pairs={{0,4},{1,5},{2,6},{3,7},{4,0},{5,1},{6,2},{7,3},{8,12},{9,13},{10,... | collective-permute-start | bytes 786440 | tf_op jit(solution)/shard_map/ppermute | solution.py:41
  124.2 7.8 %collective-permute-start.13 = (bf16[128,256]{1,0:T(8,128)(2,1)}, bf16[128,256]{1,0:T(8,128)(2,1)S(1)}, u32[]{:S(2)}, u32[]{:S(2)}) collective-permute-start(bf16[128,256]{1,0:T(8,128)(2,1)} %get-tuple-element.33), channel_id=1, source_target_pairs={{0,8},{8,0},{16,24},{24,16},{1,9},{9,1},{17,25},{25,17},{2,10},{10... | collective-permute-start | bytes 196616 | tf_op jit(solution)/shard_map/ppermute | solution.py:41
  124.5 7.5 %collective-permute-start.14 = (bf16[128,256]{1,0:T(8,128)(2,1)}, bf16[128,256]{1,0:T(8,128)(2,1)S(1)}, u32[]{:S(2)}, u32[]{:S(2)}) collective-permute-start(bf16[128,256]{1,0:T(8,128)(2,1)} %get-tuple-element.34), channel_id=1, source_target_pairs={{0,16},{8,24},{16,0},{24,8},{1,17},{9,25},{17,1},{25,9},{2,18},{10... | collective-permute-start | bytes 196616 | tf_op jit(solution)/shard_map/ppermute | solution.py:41
  125.6 6.4 %collective-permute-start.15 = (bf16[128,256]{1,0:T(8,128)(2,1)}, bf16[128,256]{1,0:T(8,128)(2,1)S(1)}, u32[]{:S(2)}, u32[]{:S(2)}) collective-permute-start(bf16[128,256]{1,0:T(8,128)(2,1)} %get-tuple-element.35), channel_id=1, source_target_pairs={{0,24},{8,16},{16,8},{24,0},{1,25},{9,17},{17,9},{25,1},{2,26},{10... | collective-permute-start | bytes 196616 | tf_op jit(solution)/shard_map/ppermute | solution.py:41
  135.1 29.4 %all-to-all-start.2 = ((bf16[4,8,128,256]{3,2,1,0:T(8,128)(2,1)}), bf16[4,8,128,256]{3,2,1,0:T(8,128)(2,1)S(1)}, u32[]{:S(2)}, u32[]{:S(2)}) async-start(bf16[4,8,128,256]{3,2,1,0:T(8,128)(2,1)} %shard_map.103.refs_6_), calls=%async_computation.3 | async-start | bytes 4194304 | tf_op jit(solution)/shard_map/all_to_all | solution.py:377
  139.1 11.6 %collective-permute-start.24 = (bf16[4,128,256]{2,1,0:T(8,128)(2,1)S(1)}, bf16[4,128,256]{2,1,0:T(8,128)(2,1)S(1)}, u32[]{:S(2)}, u32[]{:S(2)}) collective-permute-start(bf16[4,128,256]{2,1,0:T(8,128)(2,1)S(1)} %copy-done.11), channel_id=1, source_target_pairs={{0,6},{1,7},{2,4},{3,5},{4,2},{5,3},{6,0},{7,1},{8,14},{9,15},{10,... | collective-permute-start | bytes 786440 | tf_op jit(solution)/shard_map/ppermute | solution.py:41
  139.4 25.1 %collective-permute-start.25 = (bf16[4,128,256]{2,1,0:T(8,128)(2,1)S(1)}, bf16[4,128,256]{2,1,0:T(8,128)(2,1)S(1)}, u32[]{:S(2)}, u32[]{:S(2)}) collective-permute-start(bf16[4,128,256]{2,1,0:T(8,128)(2,1)S(1)} %copy-done.11), channel_id=1, source_target_pairs={{0,1},{1,0},{2,3},{3,2},{4,5},{5,4},{6,7},{7,6},{8,9},{9,8},{10,11... | collective-permute-start | bytes 786440 | tf_op jit(solution)/shard_map/ppermute | solution.py:41
  143.7 20.8 %collective-permute-start.26 = (bf16[4,128,256]{2,1,0:T(8,128)(2,1)S(1)}, bf16[4,128,256]{2,1,0:T(8,128)(2,1)}, u32[]{:S(2)}, u32[]{:S(2)}) collective-permute-start(bf16[4,128,256]{2,1,0:T(8,128)(2,1)S(1)} %copy-done.8), channel_id=1, source_target_pairs={{0,1},{1,0},{2,3},{3,2},{4,5},{5,4},{6,7},{7,6},{8,9},{9,8},{10,11... | collective-permute-start | bytes 786440 | tf_op jit(solution)/shard_map/ppermute | solution.py:41
  143.8 20.7 %collective-permute-start.27 = (bf16[4,128,256]{2,1,0:T(8,128)(2,1)S(1)}, bf16[4,128,256]{2,1,0:T(8,128)(2,1)}, u32[]{:S(2)}, u32[]{:S(2)}) collective-permute-start(bf16[4,128,256]{2,1,0:T(8,128)(2,1)S(1)} %copy-done.10), channel_id=1, source_target_pairs={{0,1},{1,0},{2,3},{3,2},{4,5},{5,4},{6,7},{7,6},{8,9},{9,8},{10,11... | collective-permute-start | bytes 786440 | tf_op jit(solution)/shard_map/ppermute | solution.py:41
  150.7 13.8 %collective-permute-start.28 = (bf16[4,128,256]{2,1,0:T(8,128)(2,1)S(1)}, bf16[4,128,256]{2,1,0:T(8,128)(2,1)}, u32[]{:S(2)}, u32[]{:S(2)}) collective-permute-start(bf16[4,128,256]{2,1,0:T(8,128)(2,1)S(1)} %collective-permute-done.24.refs_4_), channel_id=1, source_target_pairs={{0,1},{1,0},{2,3},{3,2},{4,5},{5,4},{6,7},{7,6},{8,9},{9,8},{10,11... | collective-permute-start | bytes 786440 | tf_op jit(solution)/shard_map/ppermute | solution.py:41
  (39 other events, 174.0 us)
Sparse Core Ops, SparseCore 0:
  10.2 29.1 all-gather.4
  68.4 52.9 reduce-scatter.1
  135.2 35.7 all-gather.6

commit v13 on v12

--- a/solution.py
+++ b/solution.py
@@ -388,11 +388,11 @@
     user_slots = slot_hidden(me, users, user_cols, groups, 0, True, item_parts[0])
     user_rows = exchange(user_slots, "user")
     item_routed = route(me, targets, item_pieces, 1, groups, user_slots[:1])
-    item_sent = stack(exchange(item_routed, "user"))
+    item_slots = slot_hidden(me, users, item_cols, groups, 1, False, item_routed[0])
+    user_routed = route(me, targets, [user_grad], 0, groups, [*item_slots, *user_rows[1:]])
+    item_sent = stack(exchange(item_routed, "user"), user_routed[:1])
     item_line = exchange([item_sent] * lines, "item", CORES)
-    user_routed = route(me, targets, [user_grad], 0, groups, user_rows[1:])
-    item_slots = slot_hidden(me, users, item_cols, groups, 1, False, user_routed[0])
-    user_sent = stack(exchange(user_routed, "user"), item_line[1:3] + [item_slots[0]])
+    user_sent = stack(exchange(user_routed, "user"), item_line[1:2])
     item_rows = [scatter(item_slots[0], "user")]
     item_cross = item_line + [swap(piece, "item", 1) for piece in item_line]
     user_all = lax.all_gather(user_sent, "item", axis=0)

time: 185 us -> 208 us (1.12); the launches traced: 182 us -> 207 us
  waiting for transfers between devices: 59.5 us -> 85.8 us
    ppermute x29, waiting for transfers between devices: 48.9 us -> 75.6 us  [swap(): return lax.ppermute(piece, axis, [(j, j ^ bits) for j in range(size)])]
    unnamed x72 -> x70, local copies, waits for them, and re-layouts: 7.88 us -> 7.32 us
  transfers between devices with their start and end apart: 35 -> 35, of which waited for: 16 -> 15; matrix products, arithmetic and copies ran while one was open for 1% -> 1% of each run, Pallas kernels for 15% -> 13%
where the time goes in v13:
time: 208 us; the launch traced here: 207 us
  waiting for transfers between devices  85.8 us (41%)
  starting transfers between devices  53.8 us (26%)
  Pallas kernels  44 us (21%)
  between operations  14 us (7%)
  local copies, waits for them, and re-layouts  9.2 us (4%)
    ppermute x29, waiting for transfers between devices, swap(): return lax.ppermute(piece, axis, [(j, j ^ bits) for j in range(size)])  75.6 us
    ppermute x29, starting transfers between devices, swap(): return lax.ppermute(piece, axis, [(j, j ^ bits) for j in range(size)])  38 us
    all_to_all x3, starting transfers between devices, scatter(): return lax.all_to_all(pieces, axis, split_axis=0, concat_axis=0, tiled=True)  15.8 us
    all_gather x1, waiting for transfers between devices, shards(): users = lax.all_gather(packed, 'item', axis=0)  9.54 us
    pallas_call x2, Pallas kernels, outer(): pl.pallas_call(functools.partial(outer_kernel, count=len(hidden)), grid=(...  8.56 us
    pallas_call x1, Pallas kernels, grads(): pl.pallas_call(functools.partial(grad_kernel, rows=rows, chunk=64, count=...  8.18 us
    pallas_call x2, Pallas kernels, slot_hidden(): pl.pallas_call(functools.partial(hidden_kernel, tower=tower), grid=(block...  8.15 us
    unnamed x70, local copies, waits for them, and re-layouts  7.32 us
  transfers between devices with their start and end apart: 35, of which 15 were waited for; matrix products, arithmetic and copies ran while one was open for 1% of the time, Pallas kernels for 13%

profile of v13, /device:TPU:11, one launch (start us, length us, event | category | flops | bytes accessed | tf_op | source)
XLA Modules:
  0.0 207.4 jit_solution(9947422019028929266)
XLA Ops:
  7.2 1.7 shard_map.94
  9.3 4.3 %collective-permute-done.refs_1_._.refs_9_ = bf16[256,256]{1,0:T(8,128)(2,1)S(1)} collective-permute-done((bf16[256,256]{1,0:T(8,128)(2,1)}, bf16[256,256]{1,0:T(8,128)(2,1)S(1)}, u32[]{:S(2)}, u32[]{:S(2)}) %collective-permute-start) | collective-permute-done | bytes 131104 | tf_op jit(solution)/shard_map/ppermute | solution.py:41
  14.3 2.3 %shard_map.96 = bf16[8,256,256]{2,1,0:T(8,128)(2,1)} custom-call(bf16[256,2048]{1,0:T(8,128)(2,1)} %in_ref.2, bf16[256,256]{1,0:T(8,128)(2,1)} %copy-done.6), custom_call_target="tpu_custom_call" | custom-call | flops 1024 | bytes 1024 | tf_op jit(solution)/shard_map/pallas_call | solution.py:221
  16.6 6.5 %all-to-all-start = ((bf16[8,256,256]{2,1,0:T(8,128)(2,1)}), bf16[8,256,256]{2,1,0:T(8,128)(2,1)S(1)}, u32[]{:S(2)}, u32[]{:S(2)}) async-start(bf16[8,256,256]{2,1,0:T(8,128)(2,1)} %shard_map.96), calls=%async_computation | async-start | bytes 2097152 | tf_op jit(solution)/shard_map/all_to_all | solution.py:377
  23.1 1.3 collective-permute-start.1
  25.1 4.5 %collective-permute-done.1.refs_2_.refs_10_ = bf16[256,256]{1,0:T(8,128)(2,1)S(1)} collective-permute-done((bf16[256,256]{1,0:T(8,128)(2,1)S(1)}, bf16[256,256]{1,0:T(8,128)(2,1)S(1)}, u32[]{:S(2)}, u32[]{:S(2)}) %collective-permute-start.1) | collective-permute-done | bytes 131104 | tf_op jit(solution)/shard_map/ppermute | solution.py:41
  29.9 9.5 %all-gather.5.cloned.1.call-done = bf16[2176,256]{1,0:T(8,128)(2,1)} async-done(((bf16[272,256]{1,0:T(8,128)(2,1)}), bf16[2176,256]{1,0:T(8,128)(2,1)}) %all-gather.5.cloned.1.call-update) | async-done | bytes 1114128 | tf_op jit(solution)/shard_map/all_gather | solution.py:373
  39.4 5.4 %shard_map.95.refs_0_._ = f32[3,2048]{1,0:T(4,128)} custom-call(s32[4]{0:T(128)} %add_multiply_fusion.first_ref, bf16[8,272,256]{2,1,0:T(8,128)(2,1)} %bitcast.7, bf16[256,256]{1,0:T(8,128)(2,1)} %refs_8_.1, bf16[256,256]{1,0:T(8,128)(2,1)} %copy-done.6, bf16[256,256]{1,0:T(8,128)(2,1)} %copy-done.11, bf16[256,256]{1,0:T(8,128)(2,1)} %copy-done.12, ...), custom_call_target="tpu_custom_call" | custom-call | flops 1024 | bytes 1024 | tf_op jit(solution)/shard_map/pallas_call | solution.py:119
  47.0 3.4 %collective-permute-start.6 = (f32[3,2048]{1,0:T(4,128)}, f32[3,2048]{1,0:T(4,128)S(1)}, u32[]{:S(2)}, u32[]{:S(2)}) collective-permute-start(f32[3,2048]{1,0:T(4,128)} %shard_map.95.refs_0_._), channel_id=1, source_target_pairs={{0,4},{1,5},{2,6},{3,7},{4,0},{5,1},{6,2},{7,3},{8,12},{9,13},{10,... | collective-permute-start | bytes 73736 | tf_op jit(solution)/shard_map/ppermute | solution.py:41
  50.4 1.5 collective-permute-start.8
  55.2 2.8 %collective-permute-done.8.refs_6_ = f32[3,2048]{1,0:T(4,128)S(1)} collective-permute-done((f32[3,2048]{1,0:T(4,128)}, f32[3,2048]{1,0:T(4,128)S(1)}, u32[]{:S(2)}, u32[]{:S(2)}) %collective-permute-start.8) | collective-permute-done | bytes 24608 | tf_op jit(solution)/shard_map/ppermute | solution.py:41
  58.0 1.4 collective-permute-done.9.refs_7_
  60.1 8.2 %shard_map.97 = (f32[1,2048]{1,0:T(1,128)}, f32[2048,256]{1,0:T(8,128)}, f32[256,256]{1,0:T(8,128)}, f32[256,256]{1,0:T(8,128)}, f32[256,256]{1,0:T(8,128)}, /*index=5*/f32[256,256]{1,0:T(8,128)}) custom-call(s32[4]{0:T(128)} %add_multiply_fusion.first_ref, bf16[8,272,256]{2,1,0:T(8,128)(2,1)} %bitcast.8, f32[3,2048]{1,0:T(4,128)} %shard_map.95.refs_0_._, ...), custom_call_target="tpu_custom_call" | custom-call | flops 1024 | bytes 1024 | tf_op jit(solution)/shard_map/pallas_call | solution.py:182
  68.3 2.4 %shard_map.99 = bf16[8,256,256]{2,1,0:T(8,128)(2,1)} custom-call(bf16[256,2048]{1,0:T(8,128)(2,1)} %in_ref.3, f32[3,2048]{1,0:T(4,128)} %shard_map.95.refs_0_._), custom_call_target="tpu_custom_call" | custom-call | flops 1024 | bytes 1024 | tf_op jit(solution)/shard_map/pallas_call | solution.py:221
  70.7 4.4 %all-to-all-start.1 = ((bf16[8,256,256]{2,1,0:T(8,128)(2,1)}), bf16[8,256,256]{2,1,0:T(8,128)(2,1)S(1)}, u32[]{:S(2)}, u32[]{:S(2)}) async-start(bf16[8,256,256]{2,1,0:T(8,128)(2,1)} %shard_map.99), calls=%async_computation.2 | async-start | bytes 2097152 | tf_op jit(solution)/shard_map/all_to_all | solution.py:377
  75.4 4.0 %shard_map.98 = (bf16[8,128,256]{2,1,0:T(8,128)(2,1)}, bf16[8,128,256]{2,1,0:T(8,128)(2,1)}, bf16[8,128,256]{2,1,0:T(8,128)(2,1)}, bf16[8,128,256]{2,1,0:T(8,128)(2,1)}) custom-call(s32[1]{0:T(128)} %bitcast.5.me_ref, bf16[8,272,256]{2,1,0:T(8,128)(2,1)} %bitcast.9, bf16[8,256,256]{2,1,0:T(8,128)(2,1)} %copy-done, f32[256,256]{1,0:T(8,128)} %get-tuple-element.25._.refs_0_), custom_call_target="tpu_custom_call" | custom-call | flops 1024 | bytes 1024 | tf_op jit(solution)/shard_map/pallas_call | solution.py:263
  83.3 1.3 collective-permute-start.15
  84.5 31.3 %collective-permute-done.14.refs_2_ = f32[256,256]{1,0:T(8,128)S(1)} collective-permute-done((f32[256,256]{1,0:T(8,128)S(1)}, f32[256,256]{1,0:T(8,128)S(1)}, u32[]{:S(2)}, u32[]{:S(2)}) %collective-permute-start.14) | collective-permute-done | bytes 262176 | tf_op jit(solution)/shard_map/ppermute | solution.py:41
  116.6 2.1 %shard_map.100 = (bf16[128,256]{1,0:T(8,128)(2,1)}, bf16[128,256]{1,0:T(8,128)(2,1)}, bf16[128,256]{1,0:T(8,128)(2,1)}, bf16[128,256]{1,0:T(8,128)(2,1)}) custom-call(s32[1]{0:T(128)} %bitcast.5.me_ref, s32[2,256]{1,0:T(2,128)} %get-tuple-element.30.target_ref, f32[256,256]{1,0:T(8,128)} %get-tuple-element.25._.refs_0_, f32[256,256]{1,0:T(8,128)} %copy-done.13, ...), custom_call_target="tpu_custom_call" | custom-call | flops 1024 | bytes 1024 | tf_op jit(solution)/shard_map/pallas_call | solution.py:295
  122.4 4.1 %shard_map.101.refs_1_ = bf16[4,8,128,256]{3,2,1,0:T(8,128)(2,1)} custom-call(s32[1]{0:T(128)} %bitcast.5.me_ref, bf16[8,272,256]{2,1,0:T(8,128)(2,1)} %bitcast.10, bf16[8,256,256]{2,1,0:T(8,128)(2,1)} %copy-done.2, bf16[128,256]{1,0:T(8,128)(2,1)} %get-tuple-element.35._.refs_0_), custom_call_target="tpu_custom_call" | custom-call | flops 1024 | bytes 1024 | tf_op jit(solution)/shard_map/pallas_call | solution.py:263
  127.5 1.9 shard_map.102
  130.1 1.7 shard_map.103.refs_1_
  135.7 2.0 collective-permute-done.18.refs_3_
  139.0 1.7 shard_map.104
  140.7 4.9 %all-to-all-start.2 = ((bf16[4,8,128,256]{3,2,1,0:T(8,128)(2,1)}), bf16[4,8,128,256]{3,2,1,0:T(8,128)(2,1)S(1)}, u32[]{:S(2)}, u32[]{:S(2)}) async-start(bf16[4,8,128,256]{3,2,1,0:T(8,128)(2,1)} %shard_map.101.refs_1_), calls=%async_computation.3 | async-start | bytes 4194304 | tf_op jit(solution)/shard_map/all_to_all | solution.py:377
  145.6 2.1 collective-permute-start.23
  148.0 5.5 %collective-permute-start.25 = (bf16[4,128,256]{2,1,0:T(8,128)(2,1)S(1)}, bf16[4,128,256]{2,1,0:T(8,128)(2,1)S(1)}, u32[]{:S(2)}, u32[]{:S(2)}) collective-permute-start(bf16[4,128,256]{2,1,0:T(8,128)(2,1)S(1)} %copy-done.9), channel_id=1, source_target_pairs={{0,1},{1,0},{2,3},{3,2},{4,5},{5,4},{6,7},{7,6},{8,9},{9,8},{10,11... | collective-permute-start | bytes 786440 | tf_op jit(solution)/shard_map/ppermute | solution.py:41
  153.5 18.1 %collective-permute-done.23.refs_3_ = bf16[4,128,256]{2,1,0:T(8,128)(2,1)S(1)} collective-permute-done((bf16[4,128,256]{2,1,0:T(8,128)(2,1)S(1)}, bf16[4,128,256]{2,1,0:T(8,128)(2,1)S(1)}, u32[]{:S(2)}, u32[]{:S(2)}) %collective-permute-start.23) | collective-permute-done | bytes 262176 | tf_op jit(solution)/shard_map/ppermute | solution.py:41
  171.6 8.6 %collective-permute-start.27 = (bf16[4,128,256]{2,1,0:T(8,128)(2,1)S(1)}, bf16[4,128,256]{2,1,0:T(8,128)(2,1)}, u32[]{:S(2)}, u32[]{:S(2)}) collective-permute-start(bf16[4,128,256]{2,1,0:T(8,128)(2,1)S(1)} %collective-permute-done.23.refs_3_), channel_id=1, source_target_pairs={{0,1},{1,0},{2,3},{3,2},{4,5},{5,4},{6,7},{7,6},{8,9},{9,8},{10,11... | collective-permute-start | bytes 786440 | tf_op jit(solution)/shard_map/ppermute | solution.py:41
  180.2 8.0 %collective-permute-done.24.refs_4_ = bf16[4,128,256]{2,1,0:T(8,128)(2,1)S(1)} collective-permute-done((bf16[4,128,256]{2,1,0:T(8,128)(2,1)S(1)}, bf16[4,128,256]{2,1,0:T(8,128)(2,1)S(1)}, u32[]{:S(2)}, u32[]{:S(2)}) %collective-permute-start.24) | collective-permute-done | bytes 262176 | tf_op jit(solution)/shard_map/ppermute | solution.py:41
  192.3 4.2 %shard_map.106 = f32[8,256,256]{2,1,0:T(8,128)} custom-call(s32[8]{0:T(128)} %xor.40.order_ref, s32[1]{0:T(128)} %bitcast.5.me_ref, bf16[4,8,128,256]{3,2,1,0:T(8,128)(2,1)} %copy-done.1, bf16[4,128,256]{2,1,0:T(8,128)(2,1)} %shard_map.103.refs_1_, bf16[4,128,256]{2,1,0:T(8,128)(2,1)} %copy-done.7, bf16[4,128,256]{2,1,0:T(8,128)(2,1)} %copy-done.16, ...), custom_call_target="tpu_custom_call" | custom-call | flops 1024 | bytes 1024 | tf_op jit(solution)/shard_map/pallas_call | solution.py:346
  196.5 4.3 %shard_map.105 = f32[8,256,256]{2,1,0:T(8,128)} custom-call(s32[8]{0:T(128)} %xor.40.order_ref, s32[1]{0:T(128)} %bitcast.5.me_ref, bf16[8,128,256]{2,1,0:T(8,128)(2,1)} %get-tuple-element.26.refs_4_.refs_0_, bf16[8,128,256]{2,1,0:T(8,128)(2,1)} %copy-done.3, bf16[8,128,256]{2,1,0:T(8,128)(2,1)} %copy-done.4, bf16[8,128,256]{2,1,0:T(8,128)(2,1)} %copy-done.5, ...), custom_call_target="tpu_custom_call" | custom-call | flops 1024 | bytes 1024 | tf_op jit(solution)/shard_map/pallas_call | solution.py:346
  (130 shorter events, 28.0 us)
Async XLA Ops:
  7.2 32.3 %all-gather.5.cloned.1.call-start = ((), (), s32[]{:S(2)}) async-start(), calls=%async_computation.5 | async-start | bytes 1253376 | tf_op jit(solution)/shard_map/all_gather | solution.py:373
  9.0 4.6 %collective-permute-start = (bf16[256,256]{1,0:T(8,128)(2,1)}, bf16[256,256]{1,0:T(8,128)(2,1)S(1)}, u32[]{:S(2)}, u32[]{:S(2)}) collective-permute-start(bf16[256,256]{1,0:T(8,128)(2,1)} %refs_8_.1), channel_id=1, source_target_pairs={{0,8},{8,0},{16,24},{24,16},{1,9},{9,1},{17,25},{25,17},{2,10},{10... | collective-permute-start | bytes 393224 | tf_op jit(solution)/shard_map/ppermute | solution.py:41
  16.6 36.8 %all-to-all-start = ((bf16[8,256,256]{2,1,0:T(8,128)(2,1)}), bf16[8,256,256]{2,1,0:T(8,128)(2,1)S(1)}, u32[]{:S(2)}, u32[]{:S(2)}) async-start(bf16[8,256,256]{2,1,0:T(8,128)(2,1)} %shard_map.96), calls=%async_computation | async-start | bytes 2097152 | tf_op jit(solution)/shard_map/all_to_all | solution.py:377
  23.1 103.5 %reduce-scatter.2.cloned.1.call-start = ((), (), s32[]{:S(2)}) async-start(), calls=%async_computation.4 | async-start | bytes 2359296 | tf_op jit(solution)/shard_map/reduce_scatter | solution.py:385
  23.1 6.5 %collective-permute-start.1 = (bf16[256,256]{1,0:T(8,128)(2,1)S(1)}, bf16[256,256]{1,0:T(8,128)(2,1)S(1)}, u32[]{:S(2)}, u32[]{:S(2)}) collective-permute-start(bf16[256,256]{1,0:T(8,128)(2,1)S(1)} %copy-done.10), channel_id=1, source_target_pairs={{0,16},{8,24},{16,0},{24,8},{1,17},{9,25},{17,1},{25,9},{2,18},{10... | collective-permute-start | bytes 393224 | tf_op jit(solution)/shard_map/ppermute | solution.py:41
  24.4 5.5 %collective-permute-start.2 = (bf16[256,256]{1,0:T(8,128)(2,1)S(1)}, bf16[256,256]{1,0:T(8,128)(2,1)S(1)}, u32[]{:S(2)}, u32[]{:S(2)}) collective-permute-start(bf16[256,256]{1,0:T(8,128)(2,1)S(1)} %copy-done.10), channel_id=1, source_target_pairs={{0,24},{8,16},{16,8},{24,0},{1,25},{9,17},{17,9},{25,1},{2,26},{10... | collective-permute-start | bytes 393224 | tf_op jit(solution)/shard_map/ppermute | solution.py:41
  44.8 5.6 %collective-permute-start.3 = (f32[3,2048]{1,0:T(4,128)}, f32[3,2048]{1,0:T(4,128)S(1)}, u32[]{:S(2)}, u32[]{:S(2)}) collective-permute-start(f32[3,2048]{1,0:T(4,128)} %shard_map.95.refs_0_._), channel_id=1, source_target_pairs={{0,1},{1,0},{2,3},{3,2},{4,5},{5,4},{6,7},{7,6},{8,9},{9,8},{10,11... | collective-permute-start | bytes 73736 | tf_op jit(solution)/shard_map/ppermute | solution.py:41
  45.1 6.8 %collective-permute-start.4 = (f32[3,2048]{1,0:T(4,128)}, f32[3,2048]{1,0:T(4,128)S(1)}, u32[]{:S(2)}, u32[]{:S(2)}) collective-permute-start(f32[3,2048]{1,0:T(4,128)} %shard_map.95.refs_0_._), channel_id=1, source_target_pairs={{0,2},{1,3},{2,0},{3,1},{4,6},{5,7},{6,4},{7,5},{8,10},{9,11},{10,... | collective-permute-start | bytes 73736 | tf_op jit(solution)/shard_map/ppermute | solution.py:41
  45.9 7.5 %collective-permute-start.5 = (f32[3,2048]{1,0:T(4,128)}, f32[3,2048]{1,0:T(4,128)S(1)}, u32[]{:S(2)}, u32[]{:S(2)}) collective-permute-start(f32[3,2048]{1,0:T(4,128)} %shard_map.95.refs_0_._), channel_id=1, source_target_pairs={{0,3},{1,2},{2,1},{3,0},{4,7},{5,6},{6,5},{7,4},{8,11},{9,10},{10,... | collective-permute-start | bytes 73736 | tf_op jit(solution)/shard_map/ppermute | solution.py:41
  47.0 7.1 %collective-permute-start.6 = (f32[3,2048]{1,0:T(4,128)}, f32[3,2048]{1,0:T(4,128)S(1)}, u32[]{:S(2)}, u32[]{:S(2)}) collective-permute-start(f32[3,2048]{1,0:T(4,128)} %shard_map.95.refs_0_._), channel_id=1, source_target_pairs={{0,4},{1,5},{2,6},{3,7},{4,0},{5,1},{6,2},{7,3},{8,12},{9,13},{10,... | collective-permute-start | bytes 73736 | tf_op jit(solution)/shard_map/ppermute | solution.py:41
  50.4 4.8 %collective-permute-start.7 = (f32[3,2048]{1,0:T(4,128)}, f32[3,2048]{1,0:T(4,128)S(1)}, u32[]{:S(2)}, u32[]{:S(2)}) collective-permute-start(f32[3,2048]{1,0:T(4,128)} %shard_map.95.refs_0_._), channel_id=1, source_target_pairs={{0,5},{1,4},{2,7},{3,6},{4,1},{5,0},{6,3},{7,2},{8,13},{9,12},{10,... | collective-permute-start | bytes 73736 | tf_op jit(solution)/shard_map/ppermute | solution.py:41
  50.4 7.6 %collective-permute-start.8 = (f32[3,2048]{1,0:T(4,128)}, f32[3,2048]{1,0:T(4,128)S(1)}, u32[]{:S(2)}, u32[]{:S(2)}) collective-permute-start(f32[3,2048]{1,0:T(4,128)} %shard_map.95.refs_0_._), channel_id=1, source_target_pairs={{0,6},{1,7},{2,4},{3,5},{4,2},{5,3},{6,0},{7,1},{8,14},{9,15},{10,... | collective-permute-start | bytes 73736 | tf_op jit(solution)/shard_map/ppermute | solution.py:41
  51.9 7.5 %collective-permute-start.9 = (f32[3,2048]{1,0:T(4,128)}, f32[3,2048]{1,0:T(4,128)S(1)}, u32[]{:S(2)}, u32[]{:S(2)}) collective-permute-start(f32[3,2048]{1,0:T(4,128)} %shard_map.95.refs_0_._), channel_id=1, source_target_pairs={{0,7},{1,6},{2,5},{3,4},{4,3},{5,2},{6,1},{7,0},{8,15},{9,14},{10,... | collective-permute-start | bytes 73736 | tf_op jit(solution)/shard_map/ppermute | solution.py:41
  70.7 50.7 %all-to-all-start.1 = ((bf16[8,256,256]{2,1,0:T(8,128)(2,1)}), bf16[8,256,256]{2,1,0:T(8,128)(2,1)S(1)}, u32[]{:S(2)}, u32[]{:S(2)}) async-start(bf16[8,256,256]{2,1,0:T(8,128)(2,1)} %shard_map.99), calls=%async_computation.2 | async-start | bytes 2097152 | tf_op jit(solution)/shard_map/all_to_all | solution.py:377
  75.1 121.5 %all-gather.7.cloned.1.call-start = ((), (), s32[]{:S(2)}) async-start(), calls=%async_computation.6 | async-start | bytes 2359296 | tf_op jit(solution)/shard_map/all_gather | solution.py:398
  75.1 8.2 %collective-permute-start.13 = (f32[256,256]{1,0:T(8,128)S(1)}, f32[256,256]{1,0:T(8,128)S(1)}, u32[]{:S(2)}, u32[]{:S(2)}) collective-permute-start(f32[256,256]{1,0:T(8,128)S(1)} %copy-done.34), channel_id=1, source_target_pairs={{0,8},{8,0},{16,24},{24,16},{1,9},{9,1},{17,25},{25,17},{2,10},{10... | collective-permute-start | bytes 786440 | tf_op jit(solution)/shard_map/ppermute | solution.py:41
  79.4 40.7 %collective-permute-start.10 = (bf16[8,128,256]{2,1,0:T(8,128)(2,1)}, bf16[8,128,256]{2,1,0:T(8,128)(2,1)S(1)}, u32[]{:S(2)}, u32[]{:S(2)}) collective-permute-start(bf16[8,128,256]{2,1,0:T(8,128)(2,1)} %get-tuple-element.27), channel_id=1, source_target_pairs={{0,8},{8,0},{16,24},{24,16},{1,9},{9,1},{17,25},{25,17},{2,10},{10... | collective-permute-start | bytes 1572872 | tf_op jit(solution)/shard_map/ppermute | solution.py:41
  80.6 45.9 %collective-permute-start.11 = (bf16[8,128,256]{2,1,0:T(8,128)(2,1)}, bf16[8,128,256]{2,1,0:T(8,128)(2,1)S(1)}, u32[]{:S(2)}, u32[]{:S(2)}) collective-permute-start(bf16[8,128,256]{2,1,0:T(8,128)(2,1)} %get-tuple-element.28), channel_id=1, source_target_pairs={{0,16},{8,24},{16,0},{24,8},{1,17},{9,25},{17,1},{25,9},{2,18},{10... | collective-permute-start | bytes 1572872 | tf_op jit(solution)/shard_map/ppermute | solution.py:41
  81.7 44.8 %collective-permute-start.12 = (bf16[8,128,256]{2,1,0:T(8,128)(2,1)}, bf16[8,128,256]{2,1,0:T(8,128)(2,1)S(1)}, u32[]{:S(2)}, u32[]{:S(2)}) collective-permute-start(bf16[8,128,256]{2,1,0:T(8,128)(2,1)} %get-tuple-element.29), channel_id=1, source_target_pairs={{0,24},{8,16},{16,8},{24,0},{1,25},{9,17},{17,9},{25,1},{2,26},{10... | collective-permute-start | bytes 1572872 | tf_op jit(solution)/shard_map/ppermute | solution.py:41
  82.1 33.7 %collective-permute-start.14 = (f32[256,256]{1,0:T(8,128)S(1)}, f32[256,256]{1,0:T(8,128)S(1)}, u32[]{:S(2)}, u32[]{:S(2)}) collective-permute-start(f32[256,256]{1,0:T(8,128)S(1)} %copy-done.33), channel_id=1, source_target_pairs={{0,16},{8,24},{16,0},{24,8},{1,17},{9,25},{17,1},{25,9},{2,18},{10... | collective-permute-start | bytes 786440 | tf_op jit(solution)/shard_map/ppermute | solution.py:41
  83.3 32.5 %collective-permute-start.15 = (f32[256,256]{1,0:T(8,128)S(1)}, f32[256,256]{1,0:T(8,128)S(1)}, u32[]{:S(2)}, u32[]{:S(2)}) collective-permute-start(f32[256,256]{1,0:T(8,128)S(1)} %copy-done.32), channel_id=1, source_target_pairs={{0,24},{8,16},{16,8},{24,0},{1,25},{9,17},{17,9},{25,1},{2,26},{10... | collective-permute-start | bytes 786440 | tf_op jit(solution)/shard_map/ppermute | solution.py:41
  118.7 10.7 %collective-permute-start.19 = (bf16[128,256]{1,0:T(8,128)(2,1)}, bf16[128,256]{1,0:T(8,128)(2,1)S(1)}, u32[]{:S(2)}, u32[]{:S(2)}) collective-permute-start(bf16[128,256]{1,0:T(8,128)(2,1)} %get-tuple-element.40), channel_id=1, source_target_pairs={{0,8},{8,0},{16,24},{24,16},{1,9},{9,1},{17,25},{25,17},{2,10},{10... | collective-permute-start | bytes 196616 | tf_op jit(solution)/shard_map/ppermute | solution.py:41
  119.0 10.4 %collective-permute-start.20 = (bf16[128,256]{1,0:T(8,128)(2,1)}, bf16[128,256]{1,0:T(8,128)(2,1)S(1)}, u32[]{:S(2)}, u32[]{:S(2)}) collective-permute-start(bf16[128,256]{1,0:T(8,128)(2,1)} %get-tuple-element.41), channel_id=1, source_target_pairs={{0,16},{8,24},{16,0},{24,8},{1,17},{9,25},{17,1},{25,9},{2,18},{10... | collective-permute-start | bytes 196616 | tf_op jit(solution)/shard_map/ppermute | solution.py:41
  120.2 9.2 %collective-permute-start.21 = (bf16[128,256]{1,0:T(8,128)(2,1)}, bf16[128,256]{1,0:T(8,128)(2,1)S(1)}, u32[]{:S(2)}, u32[]{:S(2)}) collective-permute-start(bf16[128,256]{1,0:T(8,128)(2,1)} %get-tuple-element.42), channel_id=1, source_target_pairs={{0,24},{8,16},{16,8},{24,0},{1,25},{9,17},{17,9},{25,1},{2,26},{10... | collective-permute-start | bytes 196616 | tf_op jit(solution)/shard_map/ppermute | solution.py:41
  131.7 6.0 %collective-permute-start.22 = (bf16[4,128,256]{2,1,0:T(8,128)(2,1)}, bf16[4,128,256]{2,1,0:T(8,128)(2,1)S(1)}, u32[]{:S(2)}, u32[]{:S(2)}) collective-permute-start(bf16[4,128,256]{2,1,0:T(8,128)(2,1)} %shard_map.103.refs_1_), channel_id=1, source_target_pairs={{0,2},{1,3},{2,0},{3,1},{4,6},{5,7},{6,4},{7,5},{8,10},{9,11},{10,... | collective-permute-start | bytes 786440 | tf_op jit(solution)/shard_map/ppermute | solution.py:41
  133.5 4.2 %collective-permute-start.18 = (bf16[128,256]{1,0:T(8,128)(2,1)}, bf16[128,256]{1,0:T(8,128)(2,1)S(1)}, u32[]{:S(2)}, u32[]{:S(2)}) collective-permute-start(bf16[128,256]{1,0:T(8,128)(2,1)} %get-tuple-element.39), channel_id=1, source_target_pairs={{0,24},{8,16},{16,8},{24,0},{1,25},{9,17},{17,9},{25,1},{2,26},{10... | collective-permute-start | bytes 196616 | tf_op jit(solution)/shard_map/ppermute | solution.py:41
  140.7 50.2 %all-to-all-start.2 = ((bf16[4,8,128,256]{3,2,1,0:T(8,128)(2,1)}), bf16[4,8,128,256]{3,2,1,0:T(8,128)(2,1)S(1)}, u32[]{:S(2)}, u32[]{:S(2)}) async-start(bf16[4,8,128,256]{3,2,1,0:T(8,128)(2,1)} %shard_map.101.refs_1_), calls=%async_computation.3 | async-start | bytes 4194304 | tf_op jit(solution)/shard_map/all_to_all | solution.py:377
  145.6 26.0 %collective-permute-start.23 = (bf16[4,128,256]{2,1,0:T(8,128)(2,1)S(1)}, bf16[4,128,256]{2,1,0:T(8,128)(2,1)S(1)}, u32[]{:S(2)}, u32[]{:S(2)}) collective-permute-start(bf16[4,128,256]{2,1,0:T(8,128)(2,1)S(1)} %copy-done.9), channel_id=1, source_target_pairs={{0,4},{1,5},{2,6},{3,7},{4,0},{5,1},{6,2},{7,3},{8,12},{9,13},{10,... | collective-permute-start | bytes 786440 | tf_op jit(solution)/shard_map/ppermute | solution.py:41
  147.7 40.6 %collective-permute-start.24 = (bf16[4,128,256]{2,1,0:T(8,128)(2,1)S(1)}, bf16[4,128,256]{2,1,0:T(8,128)(2,1)S(1)}, u32[]{:S(2)}, u32[]{:S(2)}) collective-permute-start(bf16[4,128,256]{2,1,0:T(8,128)(2,1)S(1)} %copy-done.9), channel_id=1, source_target_pairs={{0,6},{1,7},{2,4},{3,5},{4,2},{5,3},{6,0},{7,1},{8,14},{9,15},{10,... | collective-permute-start | bytes 786440 | tf_op jit(solution)/shard_map/ppermute | solution.py:41
  148.0 43.0 %collective-permute-start.25 = (bf16[4,128,256]{2,1,0:T(8,128)(2,1)S(1)}, bf16[4,128,256]{2,1,0:T(8,128)(2,1)S(1)}, u32[]{:S(2)}, u32[]{:S(2)}) collective-permute-start(bf16[4,128,256]{2,1,0:T(8,128)(2,1)S(1)} %copy-done.9), channel_id=1, source_target_pairs={{0,1},{1,0},{2,3},{3,2},{4,5},{5,4},{6,7},{7,6},{8,9},{9,8},{10,11... | collective-permute-start | bytes 786440 | tf_op jit(solution)/shard_map/ppermute | solution.py:41
  153.4 37.5 %collective-permute-start.26 = (bf16[4,128,256]{2,1,0:T(8,128)(2,1)S(1)}, bf16[4,128,256]{2,1,0:T(8,128)(2,1)}, u32[]{:S(2)}, u32[]{:S(2)}) collective-permute-start(bf16[4,128,256]{2,1,0:T(8,128)(2,1)S(1)} %copy-done.8), channel_id=1, source_target_pairs={{0,1},{1,0},{2,3},{3,2},{4,5},{5,4},{6,7},{7,6},{8,9},{9,8},{10,11... | collective-permute-start | bytes 786440 | tf_op jit(solution)/shard_map/ppermute | solution.py:41
  171.6 19.3 %collective-permute-start.27 = (bf16[4,128,256]{2,1,0:T(8,128)(2,1)S(1)}, bf16[4,128,256]{2,1,0:T(8,128)(2,1)}, u32[]{:S(2)}, u32[]{:S(2)}) collective-permute-start(bf16[4,128,256]{2,1,0:T(8,128)(2,1)S(1)} %collective-permute-done.23.refs_3_), channel_id=1, source_target_pairs={{0,1},{1,0},{2,3},{3,2},{4,5},{5,4},{6,7},{7,6},{8,9},{9,8},{10,11... | collective-permute-start | bytes 786440 | tf_op jit(solution)/shard_map/ppermute | solution.py:41
  (38 other events, 207.9 us)
Sparse Core Ops, SparseCore 0:
  10.2 29.1 all-gather.4
  68.4 53.2 reduce-scatter.1
  140.8 45.2 all-gather.6

commit v14 on v12

--- a/solution.py
+++ b/solution.py
@@ -343,12 +343,19 @@
     span, width = hidden[0].shape[-2:]
     emb = grads[0].shape[-1]
     own = span // CAP
+    steps = 2
+
+    def part(array):
+        front = array.shape[:-2]
+        return pl.BlockSpec(
+            front + (span // steps, array.shape[-1]), lambda e, d=len(front): (0,) * d + (e, 0)
+        )
+
     return pl.pallas_call(
         functools.partial(outer_kernel, count=len(hidden)),
-        grid=(1,),
-        in_specs=[SCALARS, SCALARS]
-        + [pl.BlockSpec(g.shape, lambda _, d=g.ndim: (0,) * d) for g in hidden + grads],
-        out_specs=pl.BlockSpec((own, width, emb), lambda _: (0, 0, 0)),
+        grid=(steps,),
+        in_specs=[SCALARS, SCALARS] + [part(array) for array in hidden + grads],
+        out_specs=pl.BlockSpec((own // steps, width, emb), lambda e: (e, 0, 0)),
         out_shape=jax.ShapeDtypeStruct((own, width, emb), F32),
         compiler_params=pltpu.CompilerParams(vmem_limit_bytes=VMEM),
         cost_estimate=cost,
@@ -377,8 +384,9 @@
         return lax.all_to_all(pieces, axis, split_axis=0, concat_axis=0, tiled=True)
 
     user_cols = scatter(cut(user_hidden, parts, items[1]), "item")
-    found = stats(first, users, items, rows, packed)
-    item_cols = scatter(cut(item_hidden, parts, found), "item")
+    item_blocks = cut(item_hidden, parts, items[1])
+    found = stats(first, users, items, rows, item_blocks)
+    item_cols = scatter(item_blocks, "item")
     gathered = exchange([found] * parts, "item")
     losses, user_part, item_parts = grads(first, users, items, gathered, rows, user_cols)
     row_loss = lax.dynamic_slice_in_dim(losses[0], part * rows, rows)

time: 185 us -> 183 us (0.989)
  waiting for transfers between devices: 59.5 us -> 68.2 us
  starting transfers between devices: 54 us -> 46 us
    ppermute x29, starting transfers between devices: 39.1 us -> 31 us  [swap(): return lax.ppermute(piece, axis, [(j, j ^ bits) for j in range(size)])]
    ppermute x29, waiting for transfers between devices: 48.9 us -> 55.6 us  [swap(): return lax.ppermute(piece, axis, [(j, j ^ bits) for j in range(size)])]
    reduce_scatter x1, waiting for transfers between devices: 0.22 us -> 2.12 us  [shards(): lax.psum_scatter(user_part, 'item', scatter_dimension=0, tiled=True)]
where the time goes in v14:
time: 183 us; the launch traced here: 180 us
  waiting for transfers between devices  68.2 us (37%)
  starting transfers between devices  46 us (25%)
  Pallas kernels  42.6 us (23%)
  between operations  14 us (8%)
  local copies, waits for them, and re-layouts  8.87 us (5%)
    ppermute x29, waiting for transfers between devices, swap(): return lax.ppermute(piece, axis, [(j, j ^ bits) for j in range(size)])  55.6 us
    ppermute x29, starting transfers between devices, swap(): return lax.ppermute(piece, axis, [(j, j ^ bits) for j in range(size)])  31 us
    all_to_all x3, starting transfers between devices, scatter(): return lax.all_to_all(pieces, axis, split_axis=0, concat_axis=0, tiled=True)  15 us
    all_gather x1, waiting for transfers between devices, shards(): users = lax.all_gather(packed, 'item', axis=0)  8.92 us
    pallas_call x1, Pallas kernels, grads(): pl.pallas_call(functools.partial(grad_kernel, rows=rows, chunk=64, count=...  8.17 us
    pallas_call x2, Pallas kernels, slot_hidden(): pl.pallas_call(functools.partial(hidden_kernel, tower=tower), grid=(block...  8.12 us
    pallas_call x2, Pallas kernels, outer(): pl.pallas_call(functools.partial(outer_kernel, count=len(hidden)), grid=(...  7.31 us
    unnamed x72, local copies, waits for them, and re-layouts  6.99 us
  transfers between devices with their start and end apart: 35, of which 16 were waited for; matrix products, arithmetic and copies ran while one was open for 1% of the time, Pallas kernels for 15%

profile of v14, /device:TPU:11, one launch (start us, length us, event | category | flops | bytes accessed | tf_op | source)
XLA Modules:
  0.0 180.3 jit_solution(15165691682429687839)
XLA Ops:
  7.2 1.7 shard_map.94
  9.3 4.3 %collective-permute-done._.refs_1_.refs_9_ = bf16[256,256]{1,0:T(8,128)(2,1)S(1)} collective-permute-done((bf16[256,256]{1,0:T(8,128)(2,1)}, bf16[256,256]{1,0:T(8,128)(2,1)S(1)}, u32[]{:S(2)}, u32[]{:S(2)}) %collective-permute-start) | collective-permute-done | bytes 131104 | tf_op jit(solution)/shard_map/ppermute | solution.py:41
  14.3 2.3 %shard_map.97 = bf16[8,256,256]{2,1,0:T(8,128)(2,1)} custom-call(bf16[256,2048]{1,0:T(8,128)(2,1)} %in_ref.3, bf16[256,256]{1,0:T(8,128)(2,1)} %copy-done.3), custom_call_target="tpu_custom_call" | custom-call | flops 1024 | bytes 1024 | tf_op jit(solution)/shard_map/pallas_call | solution.py:221
  16.6 6.5 %all-to-all-start = ((bf16[8,256,256]{2,1,0:T(8,128)(2,1)}), bf16[8,256,256]{2,1,0:T(8,128)(2,1)S(1)}, u32[]{:S(2)}, u32[]{:S(2)}) async-start(bf16[8,256,256]{2,1,0:T(8,128)(2,1)} %shard_map.97), calls=%async_computation | async-start | bytes 2097152 | tf_op jit(solution)/shard_map/all_to_all | solution.py:384
  25.1 2.3 %shard_map.95.refs_4_ = bf16[8,256,256]{2,1,0:T(8,128)(2,1)} custom-call(bf16[256,2048]{1,0:T(8,128)(2,1)} %in_ref.2, bf16[256,256]{1,0:T(8,128)(2,1)} %copy-done.3), custom_call_target="tpu_custom_call" | custom-call | flops 1024 | bytes 1024 | tf_op jit(solution)/shard_map/pallas_call | solution.py:221
  27.4 2.2 %collective-permute-done.1.refs_2_.refs_10_ = bf16[256,256]{1,0:T(8,128)(2,1)S(1)} collective-permute-done((bf16[256,256]{1,0:T(8,128)(2,1)S(1)}, bf16[256,256]{1,0:T(8,128)(2,1)S(1)}, u32[]{:S(2)}, u32[]{:S(2)}) %collective-permute-start.1) | collective-permute-done | bytes 131104 | tf_op jit(solution)/shard_map/ppermute | solution.py:41
  29.8 8.9 %all-gather.5.cloned.1.call-done = bf16[2176,256]{1,0:T(8,128)(2,1)} async-done(((bf16[272,256]{1,0:T(8,128)(2,1)}), bf16[2176,256]{1,0:T(8,128)(2,1)}) %all-gather.5.cloned.1.call-update) | async-done | bytes 1114128 | tf_op jit(solution)/shard_map/all_gather | solution.py:380
  38.7 5.4 %shard_map.96.refs_0_ = f32[3,2048]{1,0:T(4,128)} custom-call(s32[4]{0:T(128)} %add_multiply_fusion.first_ref, bf16[8,272,256]{2,1,0:T(8,128)(2,1)} %bitcast.7, bf16[256,256]{1,0:T(8,128)(2,1)} %refs_8_.1, bf16[256,256]{1,0:T(8,128)(2,1)} %copy-done.3, bf16[256,256]{1,0:T(8,128)(2,1)} %copy-done.13, bf16[256,256]{1,0:T(8,128)(2,1)} %copy-done.14, ...), custom_call_target="tpu_custom_call" | custom-call | flops 1024 | bytes 1024 | tf_op jit(solution)/shard_map/pallas_call | solution.py:119
  46.2 3.7 %collective-permute-start.6 = (f32[3,2048]{1,0:T(4,128)}, f32[3,2048]{1,0:T(4,128)S(1)}, u32[]{:S(2)}, u32[]{:S(2)}) collective-permute-start(f32[3,2048]{1,0:T(4,128)} %shard_map.96.refs_0_), channel_id=1, source_target_pairs={{0,4},{1,5},{2,6},{3,7},{4,0},{5,1},{6,2},{7,3},{8,12},{9,13},{10,... | collective-permute-start | bytes 73736 | tf_op jit(solution)/shard_map/ppermute | solution.py:41
  49.9 1.5 collective-permute-start.8
  54.8 2.8 %collective-permute-done.8.refs_6_ = f32[3,2048]{1,0:T(4,128)S(1)} collective-permute-done((f32[3,2048]{1,0:T(4,128)}, f32[3,2048]{1,0:T(4,128)S(1)}, u32[]{:S(2)}, u32[]{:S(2)}) %collective-permute-start.8) | collective-permute-done | bytes 24608 | tf_op jit(solution)/shard_map/ppermute | solution.py:41
  57.5 1.4 collective-permute-done.9.refs_7_
  59.6 8.2 %shard_map.98 = (f32[1,2048]{1,0:T(1,128)}, f32[2048,256]{1,0:T(8,128)}, f32[256,256]{1,0:T(8,128)}, f32[256,256]{1,0:T(8,128)}, f32[256,256]{1,0:T(8,128)}, /*index=5*/f32[256,256]{1,0:T(8,128)}) custom-call(s32[4]{0:T(128)} %add_multiply_fusion.first_ref, bf16[8,272,256]{2,1,0:T(8,128)(2,1)} %bitcast.8, f32[3,2048]{1,0:T(4,128)} %shard_map.96.refs_0_, ...), custom_call_target="tpu_custom_call" | custom-call | flops 1024 | bytes 1024 | tf_op jit(solution)/shard_map/pallas_call | solution.py:182
  67.8 4.4 %all-to-all-start.1 = ((bf16[8,256,256]{2,1,0:T(8,128)(2,1)}), bf16[8,256,256]{2,1,0:T(8,128)(2,1)S(1)}, u32[]{:S(2)}, u32[]{:S(2)}) async-start(bf16[8,256,256]{2,1,0:T(8,128)(2,1)} %shard_map.95.refs_4_), calls=%async_computation.2 | async-start | bytes 2097152 | tf_op jit(solution)/shard_map/all_to_all | solution.py:384
  75.0 4.0 %shard_map.99 = (bf16[8,128,256]{2,1,0:T(8,128)(2,1)}, bf16[8,128,256]{2,1,0:T(8,128)(2,1)}, bf16[8,128,256]{2,1,0:T(8,128)(2,1)}, bf16[8,128,256]{2,1,0:T(8,128)(2,1)}) custom-call(s32[1]{0:T(128)} %bitcast.5.me_ref, bf16[8,272,256]{2,1,0:T(8,128)(2,1)} %bitcast.9, bf16[8,256,256]{2,1,0:T(8,128)(2,1)} %copy-done, f32[256,256]{1,0:T(8,128)} %get-tuple-element.25._.refs_0_), custom_call_target="tpu_custom_call" | custom-call | flops 1024 | bytes 1024 | tf_op jit(solution)/shard_map/pallas_call | solution.py:263
  81.6 4.8 %collective-permute-done.18.refs_3_ = f32[256,256]{1,0:T(8,128)S(1)} collective-permute-done((f32[256,256]{1,0:T(8,128)S(1)}, f32[256,256]{1,0:T(8,128)S(1)}, u32[]{:S(2)}, u32[]{:S(2)}) %collective-permute-start.18) | collective-permute-done | bytes 262176 | tf_op jit(solution)/shard_map/ppermute | solution.py:41
  87.2 2.1 %shard_map.101 = (bf16[128,256]{1,0:T(8,128)(2,1)}, bf16[128,256]{1,0:T(8,128)(2,1)}, bf16[128,256]{1,0:T(8,128)(2,1)}, bf16[128,256]{1,0:T(8,128)(2,1)}) custom-call(s32[1]{0:T(128)} %bitcast.5.me_ref, s32[2,256]{1,0:T(2,128)} %get-tuple-element.30.target_ref, f32[256,256]{1,0:T(8,128)} %get-tuple-element.25._.refs_0_, f32[256,256]{1,0:T(8,128)} %copy-done.15, ...), custom_call_target="tpu_custom_call" | custom-call | flops 1024 | bytes 1024 | tf_op jit(solution)/shard_map/pallas_call | solution.py:295
  90.2 19.2 %collective-permute-done.19.refs_1_ = bf16[128,256]{1,0:T(8,128)(2,1)S(1)} collective-permute-done((bf16[128,256]{1,0:T(8,128)(2,1)}, bf16[128,256]{1,0:T(8,128)(2,1)S(1)}, u32[]{:S(2)}, u32[]{:S(2)}) %collective-permute-start.19) | collective-permute-done | bytes 65568 | tf_op jit(solution)/shard_map/ppermute | solution.py:41
  110.7 3.0 %collective-permute-done.21.refs_3_ = bf16[128,256]{1,0:T(8,128)(2,1)S(1)} collective-permute-done((bf16[128,256]{1,0:T(8,128)(2,1)}, bf16[128,256]{1,0:T(8,128)(2,1)S(1)}, u32[]{:S(2)}, u32[]{:S(2)}) %collective-permute-start.21) | collective-permute-done | bytes 65568 | tf_op jit(solution)/shard_map/ppermute | solution.py:41
  114.3 1.7 shard_map.102.refs_1_
  116.4 2.1 %collective-permute-start.23 = (bf16[4,128,256]{2,1,0:T(8,128)(2,1)}, bf16[4,128,256]{2,1,0:T(8,128)(2,1)S(1)}, u32[]{:S(2)}, u32[]{:S(2)}) collective-permute-start(bf16[4,128,256]{2,1,0:T(8,128)(2,1)} %shard_map.102.refs_1_), channel_id=1, source_target_pairs={{0,4},{1,5},{2,6},{3,7},{4,0},{5,1},{6,2},{7,3},{8,12},{9,13},{10,... | collective-permute-start | bytes 786440 | tf_op jit(solution)/shard_map/ppermute | solution.py:41
  118.5 2.1 %reduce-scatter.2.cloned.1.call-done.refs_0_ = f32[256,256]{1,0:T(8,128)} async-done(((f32[2048,256]{1,0:T(8,128)}), f32[256,256]{1,0:T(8,128)}) %reduce-scatter.2.cloned.1.call-update) | async-done | bytes 262160 | tf_op jit(solution)/shard_map/reduce_scatter | solution.py:393
  120.6 1.9 %shard_map.100 = (bf16[128,256]{1,0:T(8,128)(2,1)}, bf16[128,256]{1,0:T(8,128)(2,1)}, bf16[128,256]{1,0:T(8,128)(2,1)}, bf16[128,256]{1,0:T(8,128)(2,1)}) custom-call(s32[1]{0:T(128)} %bitcast.5.me_ref, s32[2,256]{1,0:T(2,128)} %get-tuple-element.30.target_ref, f32[256,256]{1,0:T(8,128)} %reduce-scatter.2.cloned.1.call-done.refs_0_, ...), custom_call_target="tpu_custom_call" | custom-call | flops 1024 | bytes 1024 | tf_op jit(solution)/shard_map/pallas_call | solution.py:295
  126.2 4.1 %shard_map.103.refs_6_ = bf16[4,8,128,256]{3,2,1,0:T(8,128)(2,1)} custom-call(s32[1]{0:T(128)} %bitcast.5.me_ref, bf16[8,272,256]{2,1,0:T(8,128)(2,1)} %bitcast.10, bf16[8,256,256]{2,1,0:T(8,128)(2,1)} %copy-done.2, bf16[128,256]{1,0:T(8,128)(2,1)} %get-tuple-element.32._.refs_0_), custom_call_target="tpu_custom_call" | custom-call | flops 1024 | bytes 1024 | tf_op jit(solution)/shard_map/pallas_call | solution.py:263
  131.8 1.6 shard_map.104
  133.5 4.1 %all-to-all-start.2 = ((bf16[4,8,128,256]{3,2,1,0:T(8,128)(2,1)}), bf16[4,8,128,256]{3,2,1,0:T(8,128)(2,1)S(1)}, u32[]{:S(2)}, u32[]{:S(2)}) async-start(bf16[4,8,128,256]{3,2,1,0:T(8,128)(2,1)} %shard_map.103.refs_6_), calls=%async_computation.3 | async-start | bytes 4194304 | tf_op jit(solution)/shard_map/all_to_all | solution.py:384
  137.6 3.4 %collective-permute-start.25 = (bf16[4,128,256]{2,1,0:T(8,128)(2,1)S(1)}, bf16[4,128,256]{2,1,0:T(8,128)(2,1)S(1)}, u32[]{:S(2)}, u32[]{:S(2)}) collective-permute-start(bf16[4,128,256]{2,1,0:T(8,128)(2,1)S(1)} %copy-done.11), channel_id=1, source_target_pairs={{0,1},{1,0},{2,3},{3,2},{4,5},{5,4},{6,7},{7,6},{8,9},{9,8},{10,11... | collective-permute-start | bytes 786440 | tf_op jit(solution)/shard_map/ppermute | solution.py:41
  141.5 15.7 %collective-permute-done.24.refs_4_ = bf16[4,128,256]{2,1,0:T(8,128)(2,1)S(1)} collective-permute-done((bf16[4,128,256]{2,1,0:T(8,128)(2,1)S(1)}, bf16[4,128,256]{2,1,0:T(8,128)(2,1)S(1)}, u32[]{:S(2)}, u32[]{:S(2)}) %collective-permute-start.24) | collective-permute-done | bytes 262176 | tf_op jit(solution)/shard_map/ppermute | solution.py:41
  157.2 4.4 %collective-permute-start.28 = (bf16[4,128,256]{2,1,0:T(8,128)(2,1)S(1)}, bf16[4,128,256]{2,1,0:T(8,128)(2,1)}, u32[]{:S(2)}, u32[]{:S(2)}) collective-permute-start(bf16[4,128,256]{2,1,0:T(8,128)(2,1)S(1)} %collective-permute-done.24.refs_4_), channel_id=1, source_target_pairs={{0,1},{1,0},{2,3},{3,2},{4,5},{5,4},{6,7},{7,6},{8,9},{9,8},{10,11... | collective-permute-start | bytes 786440 | tf_op jit(solution)/shard_map/ppermute | solution.py:41
  164.2 1.3 copy-done.1
  165.5 3.7 %shard_map.106 = f32[8,256,256]{2,1,0:T(8,128)} custom-call(s32[8]{0:T(128)} %xor.40.order_ref, s32[1]{0:T(128)} %bitcast.5.me_ref, bf16[4,8,128,256]{3,2,1,0:T(8,128)(2,1)} %copy-done.1, bf16[4,128,256]{2,1,0:T(8,128)(2,1)} %shard_map.102.refs_1_, bf16[4,128,256]{2,1,0:T(8,128)(2,1)} %copy-done.7, bf16[4,128,256]{2,1,0:T(8,128)(2,1)} %copy-done.9, ...), custom_call_target="tpu_custom_call" | custom-call | flops 1024 | bytes 1024 | tf_op jit(solution)/shard_map/pallas_call | solution.py:354
  170.1 3.7 %shard_map.105 = f32[8,256,256]{2,1,0:T(8,128)} custom-call(s32[8]{0:T(128)} %xor.40.order_ref, s32[1]{0:T(128)} %bitcast.5.me_ref, bf16[8,128,256]{2,1,0:T(8,128)(2,1)} %get-tuple-element.26.refs_4_.refs_0_, bf16[8,128,256]{2,1,0:T(8,128)(2,1)} %copy-done.4, bf16[8,128,256]{2,1,0:T(8,128)(2,1)} %copy-done.5, bf16[8,128,256]{2,1,0:T(8,128)(2,1)} %copy-done.6, ...), custom_call_target="tpu_custom_call" | custom-call | flops 1024 | bytes 1024 | tf_op jit(solution)/shard_map/pallas_call | solution.py:354
  (132 shorter events, 27.9 us)
Async XLA Ops:
  7.2 31.5 %all-gather.5.cloned.1.call-start = ((), (), s32[]{:S(2)}) async-start(), calls=%async_computation.5 | async-start | bytes 1253376 | tf_op jit(solution)/shard_map/all_gather | solution.py:380
  16.6 36.3 %all-to-all-start = ((bf16[8,256,256]{2,1,0:T(8,128)(2,1)}), bf16[8,256,256]{2,1,0:T(8,128)(2,1)S(1)}, u32[]{:S(2)}, u32[]{:S(2)}) async-start(bf16[8,256,256]{2,1,0:T(8,128)(2,1)} %shard_map.97), calls=%async_computation | async-start | bytes 2097152 | tf_op jit(solution)/shard_map/all_to_all | solution.py:384
  23.1 97.5 %reduce-scatter.2.cloned.1.call-start = ((), (), s32[]{:S(2)}) async-start(), calls=%async_computation.4 | async-start | bytes 2359296 | tf_op jit(solution)/shard_map/reduce_scatter | solution.py:393
  23.1 6.5 %collective-permute-start.1 = (bf16[256,256]{1,0:T(8,128)(2,1)S(1)}, bf16[256,256]{1,0:T(8,128)(2,1)S(1)}, u32[]{:S(2)}, u32[]{:S(2)}) collective-permute-start(bf16[256,256]{1,0:T(8,128)(2,1)S(1)} %copy-done.12), channel_id=1, source_target_pairs={{0,16},{8,24},{16,0},{24,8},{1,17},{9,25},{17,1},{25,9},{2,18},{10... | collective-permute-start | bytes 393224 | tf_op jit(solution)/shard_map/ppermute | solution.py:41
  24.4 5.4 %collective-permute-start.2 = (bf16[256,256]{1,0:T(8,128)(2,1)S(1)}, bf16[256,256]{1,0:T(8,128)(2,1)S(1)}, u32[]{:S(2)}, u32[]{:S(2)}) collective-permute-start(bf16[256,256]{1,0:T(8,128)(2,1)S(1)} %copy-done.12), channel_id=1, source_target_pairs={{0,24},{8,16},{16,8},{24,0},{1,25},{9,17},{17,9},{25,1},{2,26},{10... | collective-permute-start | bytes 393224 | tf_op jit(solution)/shard_map/ppermute | solution.py:41
  44.1 5.9 %collective-permute-start.3 = (f32[3,2048]{1,0:T(4,128)}, f32[3,2048]{1,0:T(4,128)S(1)}, u32[]{:S(2)}, u32[]{:S(2)}) collective-permute-start(f32[3,2048]{1,0:T(4,128)} %shard_map.96.refs_0_), channel_id=1, source_target_pairs={{0,1},{1,0},{2,3},{3,2},{4,5},{5,4},{6,7},{7,6},{8,9},{9,8},{10,11... | collective-permute-start | bytes 73736 | tf_op jit(solution)/shard_map/ppermute | solution.py:41
  44.3 7.1 %collective-permute-start.4 = (f32[3,2048]{1,0:T(4,128)}, f32[3,2048]{1,0:T(4,128)S(1)}, u32[]{:S(2)}, u32[]{:S(2)}) collective-permute-start(f32[3,2048]{1,0:T(4,128)} %shard_map.96.refs_0_), channel_id=1, source_target_pairs={{0,2},{1,3},{2,0},{3,1},{4,6},{5,7},{6,4},{7,5},{8,10},{9,11},{10,... | collective-permute-start | bytes 73736 | tf_op jit(solution)/shard_map/ppermute | solution.py:41
  45.3 7.5 %collective-permute-start.5 = (f32[3,2048]{1,0:T(4,128)}, f32[3,2048]{1,0:T(4,128)S(1)}, u32[]{:S(2)}, u32[]{:S(2)}) collective-permute-start(f32[3,2048]{1,0:T(4,128)} %shard_map.96.refs_0_), channel_id=1, source_target_pairs={{0,3},{1,2},{2,1},{3,0},{4,7},{5,6},{6,5},{7,4},{8,11},{9,10},{10,... | collective-permute-start | bytes 73736 | tf_op jit(solution)/shard_map/ppermute | solution.py:41
  46.2 7.3 %collective-permute-start.6 = (f32[3,2048]{1,0:T(4,128)}, f32[3,2048]{1,0:T(4,128)S(1)}, u32[]{:S(2)}, u32[]{:S(2)}) collective-permute-start(f32[3,2048]{1,0:T(4,128)} %shard_map.96.refs_0_), channel_id=1, source_target_pairs={{0,4},{1,5},{2,6},{3,7},{4,0},{5,1},{6,2},{7,3},{8,12},{9,13},{10,... | collective-permute-start | bytes 73736 | tf_op jit(solution)/shard_map/ppermute | solution.py:41
  49.9 7.6 %collective-permute-start.8 = (f32[3,2048]{1,0:T(4,128)}, f32[3,2048]{1,0:T(4,128)S(1)}, u32[]{:S(2)}, u32[]{:S(2)}) collective-permute-start(f32[3,2048]{1,0:T(4,128)} %shard_map.96.refs_0_), channel_id=1, source_target_pairs={{0,6},{1,7},{2,4},{3,5},{4,2},{5,3},{6,0},{7,1},{8,14},{9,15},{10,... | collective-permute-start | bytes 73736 | tf_op jit(solution)/shard_map/ppermute | solution.py:41
  51.4 7.5 %collective-permute-start.9 = (f32[3,2048]{1,0:T(4,128)}, f32[3,2048]{1,0:T(4,128)S(1)}, u32[]{:S(2)}, u32[]{:S(2)}) collective-permute-start(f32[3,2048]{1,0:T(4,128)} %shard_map.96.refs_0_), channel_id=1, source_target_pairs={{0,7},{1,6},{2,5},{3,4},{4,3},{5,2},{6,1},{7,0},{8,15},{9,14},{10,... | collective-permute-start | bytes 73736 | tf_op jit(solution)/shard_map/ppermute | solution.py:41
  67.8 57.4 %all-to-all-start.1 = ((bf16[8,256,256]{2,1,0:T(8,128)(2,1)}), bf16[8,256,256]{2,1,0:T(8,128)(2,1)S(1)}, u32[]{:S(2)}, u32[]{:S(2)}) async-start(bf16[8,256,256]{2,1,0:T(8,128)(2,1)} %shard_map.95.refs_4_), calls=%async_computation.2 | async-start | bytes 2097152 | tf_op jit(solution)/shard_map/all_to_all | solution.py:384
  72.3 97.8 %all-gather.7.cloned.1.call-start = ((), (), s32[]{:S(2)}) async-start(), calls=%async_computation.6 | async-start | bytes 2359296 | tf_op jit(solution)/shard_map/all_gather | solution.py:406
  72.3 8.1 %collective-permute-start.16 = (f32[256,256]{1,0:T(8,128)S(1)}, f32[256,256]{1,0:T(8,128)S(1)}, u32[]{:S(2)}, u32[]{:S(2)}) collective-permute-start(f32[256,256]{1,0:T(8,128)S(1)} %copy-done.35), channel_id=1, source_target_pairs={{0,8},{8,0},{16,24},{24,16},{1,9},{9,1},{17,25},{25,17},{2,10},{10... | collective-permute-start | bytes 786440 | tf_op jit(solution)/shard_map/ppermute | solution.py:41
  72.6 9.0 %collective-permute-start.17 = (f32[256,256]{1,0:T(8,128)S(1)}, f32[256,256]{1,0:T(8,128)S(1)}, u32[]{:S(2)}, u32[]{:S(2)}) collective-permute-start(f32[256,256]{1,0:T(8,128)S(1)} %copy-done.34), channel_id=1, source_target_pairs={{0,16},{8,24},{16,0},{24,8},{1,17},{9,25},{17,1},{25,9},{2,18},{10... | collective-permute-start | bytes 786440 | tf_op jit(solution)/shard_map/ppermute | solution.py:41
  73.8 12.7 %collective-permute-start.18 = (f32[256,256]{1,0:T(8,128)S(1)}, f32[256,256]{1,0:T(8,128)S(1)}, u32[]{:S(2)}, u32[]{:S(2)}) collective-permute-start(f32[256,256]{1,0:T(8,128)S(1)} %copy-done.33), channel_id=1, source_target_pairs={{0,24},{8,16},{16,8},{24,0},{1,25},{9,17},{17,9},{25,1},{2,26},{10... | collective-permute-start | bytes 786440 | tf_op jit(solution)/shard_map/ppermute | solution.py:41
  79.0 39.5 %collective-permute-start.10 = (bf16[8,128,256]{2,1,0:T(8,128)(2,1)}, bf16[8,128,256]{2,1,0:T(8,128)(2,1)S(1)}, u32[]{:S(2)}, u32[]{:S(2)}) collective-permute-start(bf16[8,128,256]{2,1,0:T(8,128)(2,1)} %get-tuple-element.27), channel_id=1, source_target_pairs={{0,8},{8,0},{16,24},{24,16},{1,9},{9,1},{17,25},{25,17},{2,10},{10... | collective-permute-start | bytes 1572872 | tf_op jit(solution)/shard_map/ppermute | solution.py:41
  79.2 39.2 %collective-permute-start.11 = (bf16[8,128,256]{2,1,0:T(8,128)(2,1)}, bf16[8,128,256]{2,1,0:T(8,128)(2,1)S(1)}, u32[]{:S(2)}, u32[]{:S(2)}) collective-permute-start(bf16[8,128,256]{2,1,0:T(8,128)(2,1)} %get-tuple-element.28), channel_id=1, source_target_pairs={{0,16},{8,24},{16,0},{24,8},{1,17},{9,25},{17,1},{25,9},{2,18},{10... | collective-permute-start | bytes 1572872 | tf_op jit(solution)/shard_map/ppermute | solution.py:41
  80.4 38.0 %collective-permute-start.12 = (bf16[8,128,256]{2,1,0:T(8,128)(2,1)}, bf16[8,128,256]{2,1,0:T(8,128)(2,1)S(1)}, u32[]{:S(2)}, u32[]{:S(2)}) collective-permute-start(bf16[8,128,256]{2,1,0:T(8,128)(2,1)} %get-tuple-element.29), channel_id=1, source_target_pairs={{0,24},{8,16},{16,8},{24,0},{1,25},{9,17},{17,9},{25,1},{2,26},{10... | collective-permute-start | bytes 1572872 | tf_op jit(solution)/shard_map/ppermute | solution.py:41
  89.3 20.1 %collective-permute-start.19 = (bf16[128,256]{1,0:T(8,128)(2,1)}, bf16[128,256]{1,0:T(8,128)(2,1)S(1)}, u32[]{:S(2)}, u32[]{:S(2)}) collective-permute-start(bf16[128,256]{1,0:T(8,128)(2,1)} %get-tuple-element.40), channel_id=1, source_target_pairs={{0,8},{8,0},{16,24},{24,16},{1,9},{9,1},{17,25},{25,17},{2,10},{10... | collective-permute-start | bytes 196616 | tf_op jit(solution)/shard_map/ppermute | solution.py:41
  89.5 21.2 %collective-permute-start.20 = (bf16[128,256]{1,0:T(8,128)(2,1)}, bf16[128,256]{1,0:T(8,128)(2,1)S(1)}, u32[]{:S(2)}, u32[]{:S(2)}) collective-permute-start(bf16[128,256]{1,0:T(8,128)(2,1)} %get-tuple-element.41), channel_id=1, source_target_pairs={{0,16},{8,24},{16,0},{24,8},{1,17},{9,25},{17,1},{25,9},{2,18},{10... | collective-permute-start | bytes 196616 | tf_op jit(solution)/shard_map/ppermute | solution.py:41
  116.0 14.4 %collective-permute-start.22 = (bf16[4,128,256]{2,1,0:T(8,128)(2,1)}, bf16[4,128,256]{2,1,0:T(8,128)(2,1)S(1)}, u32[]{:S(2)}, u32[]{:S(2)}) collective-permute-start(bf16[4,128,256]{2,1,0:T(8,128)(2,1)} %shard_map.102.refs_1_), channel_id=1, source_target_pairs={{0,2},{1,3},{2,0},{3,1},{4,6},{5,7},{6,4},{7,5},{8,10},{9,11},{10,... | collective-permute-start | bytes 786440 | tf_op jit(solution)/shard_map/ppermute | solution.py:41
  116.4 14.0 %collective-permute-start.23 = (bf16[4,128,256]{2,1,0:T(8,128)(2,1)}, bf16[4,128,256]{2,1,0:T(8,128)(2,1)S(1)}, u32[]{:S(2)}, u32[]{:S(2)}) collective-permute-start(bf16[4,128,256]{2,1,0:T(8,128)(2,1)} %shard_map.102.refs_1_), channel_id=1, source_target_pairs={{0,4},{1,5},{2,6},{3,7},{4,0},{5,1},{6,2},{7,3},{8,12},{9,13},{10,... | collective-permute-start | bytes 786440 | tf_op jit(solution)/shard_map/ppermute | solution.py:41
  122.5 7.9 %collective-permute-start.13 = (bf16[128,256]{1,0:T(8,128)(2,1)}, bf16[128,256]{1,0:T(8,128)(2,1)S(1)}, u32[]{:S(2)}, u32[]{:S(2)}) collective-permute-start(bf16[128,256]{1,0:T(8,128)(2,1)} %get-tuple-element.33), channel_id=1, source_target_pairs={{0,8},{8,0},{16,24},{24,16},{1,9},{9,1},{17,25},{25,17},{2,10},{10... | collective-permute-start | bytes 196616 | tf_op jit(solution)/shard_map/ppermute | solution.py:41
  122.8 7.6 %collective-permute-start.14 = (bf16[128,256]{1,0:T(8,128)(2,1)}, bf16[128,256]{1,0:T(8,128)(2,1)S(1)}, u32[]{:S(2)}, u32[]{:S(2)}) collective-permute-start(bf16[128,256]{1,0:T(8,128)(2,1)} %get-tuple-element.34), channel_id=1, source_target_pairs={{0,16},{8,24},{16,0},{24,8},{1,17},{9,25},{17,1},{25,9},{2,18},{10... | collective-permute-start | bytes 196616 | tf_op jit(solution)/shard_map/ppermute | solution.py:41
  124.0 6.4 %collective-permute-start.15 = (bf16[128,256]{1,0:T(8,128)(2,1)}, bf16[128,256]{1,0:T(8,128)(2,1)S(1)}, u32[]{:S(2)}, u32[]{:S(2)}) collective-permute-start(bf16[128,256]{1,0:T(8,128)(2,1)} %get-tuple-element.35), channel_id=1, source_target_pairs={{0,24},{8,16},{16,8},{24,0},{1,25},{9,17},{17,9},{25,1},{2,26},{10... | collective-permute-start | bytes 196616 | tf_op jit(solution)/shard_map/ppermute | solution.py:41
  133.5 30.0 %all-to-all-start.2 = ((bf16[4,8,128,256]{3,2,1,0:T(8,128)(2,1)}), bf16[4,8,128,256]{3,2,1,0:T(8,128)(2,1)S(1)}, u32[]{:S(2)}, u32[]{:S(2)}) async-start(bf16[4,8,128,256]{3,2,1,0:T(8,128)(2,1)} %shard_map.103.refs_6_), calls=%async_computation.3 | async-start | bytes 4194304 | tf_op jit(solution)/shard_map/all_to_all | solution.py:384
  137.5 19.6 %collective-permute-start.24 = (bf16[4,128,256]{2,1,0:T(8,128)(2,1)S(1)}, bf16[4,128,256]{2,1,0:T(8,128)(2,1)S(1)}, u32[]{:S(2)}, u32[]{:S(2)}) collective-permute-start(bf16[4,128,256]{2,1,0:T(8,128)(2,1)S(1)} %copy-done.11), channel_id=1, source_target_pairs={{0,6},{1,7},{2,4},{3,5},{4,2},{5,3},{6,0},{7,1},{8,14},{9,15},{10,... | collective-permute-start | bytes 786440 | tf_op jit(solution)/shard_map/ppermute | solution.py:41
  137.6 25.9 %collective-permute-start.25 = (bf16[4,128,256]{2,1,0:T(8,128)(2,1)S(1)}, bf16[4,128,256]{2,1,0:T(8,128)(2,1)S(1)}, u32[]{:S(2)}, u32[]{:S(2)}) collective-permute-start(bf16[4,128,256]{2,1,0:T(8,128)(2,1)S(1)} %copy-done.11), channel_id=1, source_target_pairs={{0,1},{1,0},{2,3},{3,2},{4,5},{5,4},{6,7},{7,6},{8,9},{9,8},{10,11... | collective-permute-start | bytes 786440 | tf_op jit(solution)/shard_map/ppermute | solution.py:41
  141.0 22.5 %collective-permute-start.26 = (bf16[4,128,256]{2,1,0:T(8,128)(2,1)S(1)}, bf16[4,128,256]{2,1,0:T(8,128)(2,1)}, u32[]{:S(2)}, u32[]{:S(2)}) collective-permute-start(bf16[4,128,256]{2,1,0:T(8,128)(2,1)S(1)} %copy-done.8), channel_id=1, source_target_pairs={{0,1},{1,0},{2,3},{3,2},{4,5},{5,4},{6,7},{7,6},{8,9},{9,8},{10,11... | collective-permute-start | bytes 786440 | tf_op jit(solution)/shard_map/ppermute | solution.py:41
  141.1 22.4 %collective-permute-start.27 = (bf16[4,128,256]{2,1,0:T(8,128)(2,1)S(1)}, bf16[4,128,256]{2,1,0:T(8,128)(2,1)}, u32[]{:S(2)}, u32[]{:S(2)}) collective-permute-start(bf16[4,128,256]{2,1,0:T(8,128)(2,1)S(1)} %copy-done.10), channel_id=1, source_target_pairs={{0,1},{1,0},{2,3},{3,2},{4,5},{5,4},{6,7},{7,6},{8,9},{9,8},{10,11... | collective-permute-start | bytes 786440 | tf_op jit(solution)/shard_map/ppermute | solution.py:41
  157.2 6.3 %collective-permute-start.28 = (bf16[4,128,256]{2,1,0:T(8,128)(2,1)S(1)}, bf16[4,128,256]{2,1,0:T(8,128)(2,1)}, u32[]{:S(2)}, u32[]{:S(2)}) collective-permute-start(bf16[4,128,256]{2,1,0:T(8,128)(2,1)S(1)} %collective-permute-done.24.refs_4_), channel_id=1, source_target_pairs={{0,1},{1,0},{2,3},{3,2},{4,5},{5,4},{6,7},{7,6},{8,9},{9,8},{10,11... | collective-permute-start | bytes 786440 | tf_op jit(solution)/shard_map/ppermute | solution.py:41
  (39 other events, 160.2 us)
Sparse Core Ops, SparseCore 0:
  9.6 29.0 all-gather.4
  67.9 52.6 reduce-scatter.1
  133.6 36.4 all-gather.6

commit v15 on v14

--- a/solution.py
+++ b/solution.py
@@ -235,7 +235,8 @@
     return (place == target).astype(F32).astype(BF16)
 
 
-def hidden_kernel(me_ref, users_ref, hidden_ref, _, *out_refs, tower):
+def hidden_kernel(me_ref, users_ref, hidden_ref, *refs, tower, order):
+    out_refs = refs[order:]
     count, (pair, span, _) = len(out_refs), out_refs[0].shape[-3:]
     groups = out_refs[0].shape[0] if count == 1 else count
     me = 0 if count == 1 else me_ref[0]
@@ -261,19 +262,19 @@
         out_specs = [pl.BlockSpec((groups, pair, span, width), lambda b: (0, b, 0, 0))]
         out_shape = [jax.ShapeDtypeStruct((groups, blocks, span, width), BF16)]
     return pl.pallas_call(
-        functools.partial(hidden_kernel, tower=tower),
+        functools.partial(hidden_kernel, tower=tower, order=len(after)),
         grid=(blocks // pair,),
         in_specs=[
             SCALARS,
             pl.BlockSpec((pair, EXTRA, rows), lambda b: (b, rows // EXTRA, 0)),
             pl.BlockSpec((pair, rows, width), lambda b: (b, 0, 0)),
-            ANYWHERE,
-        ],
+        ]
+        + [ANYWHERE] * len(after),
         out_specs=out_specs,
         out_shape=out_shape,
         compiler_params=pltpu.CompilerParams(vmem_limit_bytes=VMEM),
         cost_estimate=SMALL,
-    )(me, users, hidden, after)
+    )(me, users, hidden, *after)
 
 
 def route_kernel(me_ref, target_ref, *refs, tower, count, order):
@@ -393,19 +394,20 @@
     user_grad = lax.psum_scatter(user_part, "item", scatter_dimension=0, tiled=True)
     item_pieces = exchange(item_parts, "user")
 
-    user_slots = slot_hidden(me, users, user_cols, groups, 0, True, item_parts[0])
+    user_slots = slot_hidden(me, users, user_cols, groups, 0, True, item_pieces[1:])
     user_rows = exchange(user_slots, "user")
     item_routed = route(me, targets, item_pieces, 1, groups, user_slots[:1])
     item_sent = stack(exchange(item_routed, "user"))
     item_line = exchange([item_sent] * lines, "item", CORES)
-    user_routed = route(me, targets, [user_grad], 0, groups, user_rows[1:])
-    item_slots = slot_hidden(me, users, item_cols, groups, 1, False, user_routed[0])
-    user_sent = stack(exchange(user_routed, "user"), item_line[1:3] + [item_slots[0]])
+    user_routed = route(me, targets, [user_grad], 0, groups, [item_sent] + user_rows[1:])
+    user_sent = stack(exchange(user_routed, "user"), item_line[1:3])
+    item_slots = slot_hidden(me, users, item_cols, groups, 1, False, [user_sent])
     item_rows = [scatter(item_slots[0], "user")]
+    user_line = exchange([user_sent] * lines, "item", CORES)
+    user_cross = user_line + [swap(piece, "item", 1) for piece in user_line]
     item_cross = item_line + [swap(piece, "item", 1) for piece in item_line]
-    user_all = lax.all_gather(user_sent, "item", axis=0)
+    user_weight_grad = outer(order, me, user_rows, user_cross, SMALL)
     item_weight_grad = outer(order, me, item_rows, item_cross, SMALL)
-    user_weight_grad = outer(order, me, user_rows, [user_all], SMALL)
     return (row_loss, user_weight_grad, item_weight_grad)
 
 

time: 183 us -> 204 us (1.11)
  starting transfers between devices: 46 us -> 73.7 us
  waiting for transfers between devices: 68.2 us -> 61.7 us
    ppermute x29 -> x36, starting transfers between devices: 31 us -> 59 us  [swap(): return lax.ppermute(piece, axis, [(j, j ^ bits) for j in range(size)])]
    ppermute x29 -> x36, waiting for transfers between devices: 55.6 us -> 52.2 us  [swap(): return lax.ppermute(piece, axis, [(j, j ^ bits) for j in range(size)])]
    reduce_scatter x1, waiting for transfers between devices: 2.12 us -> 0.02 us  [shards(): lax.psum_scatter(user_part, 'item', scatter_dimension=0, tiled=True)]
    unnamed x72 -> x84, local copies, waits for them, and re-layouts: 6.99 us -> 8.13 us
  transfers between devices with their start and end apart: 35 -> 41, of which waited for: 16 -> 17; matrix products, arithmetic and copies ran while one was open for 1% -> 1% of each run, Pallas kernels for 15% -> 12%
where the time goes in v15:
time: 204 us; the launch traced here: 203 us
  starting transfers between devices  73.7 us (36%)
  waiting for transfers between devices  61.7 us (30%)
  Pallas kernels  42.6 us (21%)
  between operations  14.4 us (7%)
  local copies, waits for them, and re-layouts  9.96 us (5%)
    ppermute x36, starting transfers between devices, swap(): return lax.ppermute(piece, axis, [(j, j ^ bits) for j in range(size)])  59 us
    ppermute x36, waiting for transfers between devices, swap(): return lax.ppermute(piece, axis, [(j, j ^ bits) for j in range(size)])  52.2 us
    all_to_all x3, starting transfers between devices, scatter(): return lax.all_to_all(pieces, axis, split_axis=0, concat_axis=0, tiled=True)  14.7 us
    all_gather x1, waiting for transfers between devices, shards(): users = lax.all_gather(packed, 'item', axis=0)  8.92 us
    pallas_call x1, Pallas kernels, grads(): pl.pallas_call(functools.partial(grad_kernel, rows=rows, chunk=64, count=...  8.17 us
    unnamed x84, local copies, waits for them, and re-layouts  8.13 us
    pallas_call x2, Pallas kernels, slot_hidden(): pl.pallas_call(functools.partial(hidden_kernel, tower=tower, order=len(af...  8.1 us
    pallas_call x2, Pallas kernels, outer(): pl.pallas_call(functools.partial(outer_kernel, count=len(hidden)), grid=(...  7.3 us
  transfers between devices with their start and end apart: 41, of which 17 were waited for; matrix products, arithmetic and copies ran while one was open for 1% of the time, Pallas kernels for 12%

profile of v15, /device:TPU:11, one launch (start us, length us, event | category | flops | bytes accessed | tf_op | source)
XLA Modules:
  0.0 203.0 jit_solution(10152571782138389786)
XLA Ops:
  7.2 1.7 shard_map.94
  9.3 4.3 %collective-permute-done._.refs_1_.refs_9_ = bf16[256,256]{1,0:T(8,128)(2,1)S(1)} collective-permute-done((bf16[256,256]{1,0:T(8,128)(2,1)}, bf16[256,256]{1,0:T(8,128)(2,1)S(1)}, u32[]{:S(2)}, u32[]{:S(2)}) %collective-permute-start) | collective-permute-done | bytes 131104 | tf_op jit(solution)/shard_map/ppermute | solution.py:41
  14.3 2.3 %shard_map.97 = bf16[8,256,256]{2,1,0:T(8,128)(2,1)} custom-call(bf16[256,2048]{1,0:T(8,128)(2,1)} %in_ref.3, bf16[256,256]{1,0:T(8,128)(2,1)} %copy-done.5), custom_call_target="tpu_custom_call" | custom-call | flops 1024 | bytes 1024 | tf_op jit(solution)/shard_map/pallas_call | solution.py:221
  16.6 6.5 %all-to-all-start = ((bf16[8,256,256]{2,1,0:T(8,128)(2,1)}), bf16[8,256,256]{2,1,0:T(8,128)(2,1)S(1)}, u32[]{:S(2)}, u32[]{:S(2)}) async-start(bf16[8,256,256]{2,1,0:T(8,128)(2,1)} %shard_map.97), calls=%async_computation | async-start | bytes 2097152 | tf_op jit(solution)/shard_map/all_to_all | solution.py:385
  25.1 2.3 %shard_map.95.refs_4_ = bf16[8,256,256]{2,1,0:T(8,128)(2,1)} custom-call(bf16[256,2048]{1,0:T(8,128)(2,1)} %in_ref.2, bf16[256,256]{1,0:T(8,128)(2,1)} %copy-done.5), custom_call_target="tpu_custom_call" | custom-call | flops 1024 | bytes 1024 | tf_op jit(solution)/shard_map/pallas_call | solution.py:221
  27.4 2.2 %collective-permute-done.1.refs_2_.refs_10_ = bf16[256,256]{1,0:T(8,128)(2,1)S(1)} collective-permute-done((bf16[256,256]{1,0:T(8,128)(2,1)S(1)}, bf16[256,256]{1,0:T(8,128)(2,1)S(1)}, u32[]{:S(2)}, u32[]{:S(2)}) %collective-permute-start.1) | collective-permute-done | bytes 131104 | tf_op jit(solution)/shard_map/ppermute | solution.py:41
  29.8 8.9 %all-gather.3.cloned.1.call-done = bf16[2176,256]{1,0:T(8,128)(2,1)} async-done(((bf16[272,256]{1,0:T(8,128)(2,1)}), bf16[2176,256]{1,0:T(8,128)(2,1)}) %all-gather.3.cloned.1.call-update) | async-done | bytes 1114128 | tf_op jit(solution)/shard_map/all_gather | solution.py:381
  38.7 5.4 %shard_map.96.refs_0_ = f32[3,2048]{1,0:T(4,128)} custom-call(s32[4]{0:T(128)} %add_multiply_fusion.first_ref, bf16[8,272,256]{2,1,0:T(8,128)(2,1)} %bitcast.6, bf16[256,256]{1,0:T(8,128)(2,1)} %refs_8_.1, bf16[256,256]{1,0:T(8,128)(2,1)} %copy-done.5, bf16[256,256]{1,0:T(8,128)(2,1)} %copy-done.17, bf16[256,256]{1,0:T(8,128)(2,1)} %copy-done.18, ...), custom_call_target="tpu_custom_call" | custom-call | flops 1024 | bytes 1024 | tf_op jit(solution)/shard_map/pallas_call | solution.py:119
  46.2 3.7 %collective-permute-start.6 = (f32[3,2048]{1,0:T(4,128)}, f32[3,2048]{1,0:T(4,128)S(1)}, u32[]{:S(2)}, u32[]{:S(2)}) collective-permute-start(f32[3,2048]{1,0:T(4,128)} %shard_map.96.refs_0_), channel_id=1, source_target_pairs={{0,4},{1,5},{2,6},{3,7},{4,0},{5,1},{6,2},{7,3},{8,12},{9,13},{10,... | collective-permute-start | bytes 73736 | tf_op jit(solution)/shard_map/ppermute | solution.py:41
  54.8 2.7 %collective-permute-done.8.refs_6_ = f32[3,2048]{1,0:T(4,128)S(1)} collective-permute-done((f32[3,2048]{1,0:T(4,128)}, f32[3,2048]{1,0:T(4,128)S(1)}, u32[]{:S(2)}, u32[]{:S(2)}) %collective-permute-start.8) | collective-permute-done | bytes 24608 | tf_op jit(solution)/shard_map/ppermute | solution.py:41
  59.6 8.2 %shard_map.98 = (f32[1,2048]{1,0:T(1,128)}, f32[2048,256]{1,0:T(8,128)}, f32[256,256]{1,0:T(8,128)}, f32[256,256]{1,0:T(8,128)}, f32[256,256]{1,0:T(8,128)}, /*index=5*/f32[256,256]{1,0:T(8,128)}) custom-call(s32[4]{0:T(128)} %add_multiply_fusion.first_ref, bf16[8,272,256]{2,1,0:T(8,128)(2,1)} %bitcast.7, f32[3,2048]{1,0:T(4,128)} %shard_map.96.refs_0_, ...), custom_call_target="tpu_custom_call" | custom-call | flops 1024 | bytes 1024 | tf_op jit(solution)/shard_map/pallas_call | solution.py:182
  67.8 4.4 %all-to-all-start.1 = ((bf16[8,256,256]{2,1,0:T(8,128)(2,1)}), bf16[8,256,256]{2,1,0:T(8,128)(2,1)S(1)}, u32[]{:S(2)}, u32[]{:S(2)}) async-start(bf16[8,256,256]{2,1,0:T(8,128)(2,1)} %shard_map.95.refs_4_), calls=%async_computation.2 | async-start | bytes 2097152 | tf_op jit(solution)/shard_map/all_to_all | solution.py:385
  74.9 5.0 %collective-permute-done.10.refs_0_.refs_1_ = f32[256,256]{1,0:T(8,128)S(1)} collective-permute-done((f32[256,256]{1,0:T(8,128)S(1)}, f32[256,256]{1,0:T(8,128)S(1)}, u32[]{:S(2)}, u32[]{:S(2)}) %collective-permute-start.10) | collective-permute-done | bytes 262176 | tf_op jit(solution)/shard_map/ppermute | solution.py:41
  79.9 6.4 %collective-permute-done.12.refs_2_.refs_3_ = f32[256,256]{1,0:T(8,128)S(1)} collective-permute-done((f32[256,256]{1,0:T(8,128)S(1)}, f32[256,256]{1,0:T(8,128)S(1)}, u32[]{:S(2)}, u32[]{:S(2)}) %collective-permute-start.12) | collective-permute-done | bytes 262176 | tf_op jit(solution)/shard_map/ppermute | solution.py:41
  87.1 4.0 %shard_map.99 = (bf16[8,128,256]{2,1,0:T(8,128)(2,1)}, bf16[8,128,256]{2,1,0:T(8,128)(2,1)}, bf16[8,128,256]{2,1,0:T(8,128)(2,1)}, bf16[8,128,256]{2,1,0:T(8,128)(2,1)}) custom-call(s32[1]{0:T(128)} %bitcast.5.me_ref, bf16[8,272,256]{2,1,0:T(8,128)(2,1)} %bitcast.8, bf16[8,256,256]{2,1,0:T(8,128)(2,1)} %copy-done, f32[256,256]{1,0:T(8,128)} %copy-done.9, ...), custom_call_target="tpu_custom_call" | custom-call | flops 1024 | bytes 1024 | tf_op jit(solution)/shard_map/pallas_call | solution.py:264
  93.7 2.1 %shard_map.100 = (bf16[128,256]{1,0:T(8,128)(2,1)}, bf16[128,256]{1,0:T(8,128)(2,1)}, bf16[128,256]{1,0:T(8,128)(2,1)}, bf16[128,256]{1,0:T(8,128)(2,1)}) custom-call(s32[1]{0:T(128)} %bitcast.5.me_ref, s32[2,256]{1,0:T(2,128)} %get-tuple-element.32.target_ref, f32[256,256]{1,0:T(8,128)} %get-tuple-element.34.refs_0_, f32[256,256]{1,0:T(8,128)} %copy-done.9, ...), custom_call_target="tpu_custom_call" | custom-call | flops 1024 | bytes 1024 | tf_op jit(solution)/shard_map/pallas_call | solution.py:296
  97.3 18.8 %collective-permute-done.16.refs_1_ = bf16[128,256]{1,0:T(8,128)(2,1)S(1)} collective-permute-done((bf16[128,256]{1,0:T(8,128)(2,1)}, bf16[128,256]{1,0:T(8,128)(2,1)S(1)}, u32[]{:S(2)}, u32[]{:S(2)}) %collective-permute-start.16) | collective-permute-done | bytes 65568 | tf_op jit(solution)/shard_map/ppermute | solution.py:41
  117.1 3.3 %collective-permute-done.18.refs_3_ = bf16[128,256]{1,0:T(8,128)(2,1)S(1)} collective-permute-done((bf16[128,256]{1,0:T(8,128)(2,1)}, bf16[128,256]{1,0:T(8,128)(2,1)S(1)}, u32[]{:S(2)}, u32[]{:S(2)}) %collective-permute-start.18) | collective-permute-done | bytes 65568 | tf_op jit(solution)/shard_map/ppermute | solution.py:41
  121.0 1.7 shard_map.101.refs_1_
  123.4 1.8 collective-permute-start.23
  126.3 1.9 shard_map.102
  131.4 2.5 %collective-permute-done.23.refs_5_.refs_3_ = bf16[4,128,256]{2,1,0:T(8,128)(2,1)S(1)} collective-permute-done((bf16[4,128,256]{2,1,0:T(8,128)(2,1)}, bf16[4,128,256]{2,1,0:T(8,128)(2,1)S(1)}, u32[]{:S(2)}, u32[]{:S(2)}) %collective-permute-start.23) | collective-permute-done | bytes 262176 | tf_op jit(solution)/shard_map/ppermute | solution.py:41
  137.3 4.1 %shard_map.105 = bf16[4,8,128,256]{3,2,1,0:T(8,128)(2,1)} custom-call(s32[1]{0:T(128)} %bitcast.5.me_ref, bf16[8,272,256]{2,1,0:T(8,128)(2,1)} %bitcast.9, bf16[8,256,256]{2,1,0:T(8,128)(2,1)} %copy-done.2, bf16[4,128,256]{2,1,0:T(8,128)(2,1)} %shard_map.103.refs_4_.refs_0_), custom_call_target="tpu_custom_call" | custom-call | flops 1024 | bytes 1024 | tf_op jit(solution)/shard_map/pallas_call | solution.py:264
  141.4 3.7 %all-to-all-start.2 = ((bf16[4,8,128,256]{3,2,1,0:T(8,128)(2,1)}), bf16[4,8,128,256]{3,2,1,0:T(8,128)(2,1)S(1)}, u32[]{:S(2)}, u32[]{:S(2)}) async-start(bf16[4,8,128,256]{3,2,1,0:T(8,128)(2,1)} %shard_map.105), calls=%async_computation.3 | async-start | bytes 4194304 | tf_op jit(solution)/shard_map/all_to_all | solution.py:385
  148.1 6.9 %collective-permute-start.27 = (bf16[4,128,256]{2,1,0:T(8,128)(2,1)S(1)}, bf16[4,128,256]{2,1,0:T(8,128)(2,1)S(1)}, u32[]{:S(2)}, u32[]{:S(2)}) collective-permute-start(bf16[4,128,256]{2,1,0:T(8,128)(2,1)S(1)} %copy-done.3), channel_id=1, source_target_pairs={{0,1},{1,0},{2,3},{3,2},{4,5},{5,4},{6,7},{7,6},{8,9},{9,8},{10,11... | collective-permute-start | bytes 786440 | tf_op jit(solution)/shard_map/ppermute | solution.py:41
  155.1 8.6 %collective-permute-start.28 = (bf16[4,128,256]{2,1,0:T(8,128)(2,1)S(1)}, bf16[4,128,256]{2,1,0:T(8,128)(2,1)S(1)}, u32[]{:S(2)}, u32[]{:S(2)}) collective-permute-start(bf16[4,128,256]{2,1,0:T(8,128)(2,1)S(1)} %collective-permute-done.24.refs_5_), channel_id=1, source_target_pairs={{0,1},{1,0},{2,3},{3,2},{4,5},{5,4},{6,7},{7,6},{8,9},{9,8},{10,11... | collective-permute-start | bytes 786440 | tf_op jit(solution)/shard_map/ppermute | solution.py:41
  163.7 9.3 %collective-permute-start.29 = (bf16[4,128,256]{2,1,0:T(8,128)(2,1)S(1)}, bf16[4,128,256]{2,1,0:T(8,128)(2,1)S(1)}, u32[]{:S(2)}, u32[]{:S(2)}) collective-permute-start(bf16[4,128,256]{2,1,0:T(8,128)(2,1)S(1)} %collective-permute-done.25.refs_6_), channel_id=1, source_target_pairs={{0,1},{1,0},{2,3},{3,2},{4,5},{5,4},{6,7},{7,6},{8,9},{9,8},{10,11... | collective-permute-start | bytes 786440 | tf_op jit(solution)/shard_map/ppermute | solution.py:41
  173.0 2.1 %collective-permute-done.31.refs_4_ = bf16[4,128,256]{2,1,0:T(8,128)(2,1)S(1)} collective-permute-done((bf16[4,128,256]{2,1,0:T(8,128)(2,1)S(1)}, bf16[4,128,256]{2,1,0:T(8,128)(2,1)S(1)}, u32[]{:S(2)}, u32[]{:S(2)}) %collective-permute-start.31) | collective-permute-done | bytes 262176 | tf_op jit(solution)/shard_map/ppermute | solution.py:41
  175.1 4.9 %collective-permute-start.32 = (bf16[4,128,256]{2,1,0:T(8,128)(2,1)S(1)}, bf16[4,128,256]{2,1,0:T(8,128)(2,1)}, u32[]{:S(2)}, u32[]{:S(2)}) collective-permute-start(bf16[4,128,256]{2,1,0:T(8,128)(2,1)S(1)} %copy-done.4), channel_id=1, source_target_pairs={{0,1},{1,0},{2,3},{3,2},{4,5},{5,4},{6,7},{7,6},{8,9},{9,8},{10,11... | collective-permute-start | bytes 786440 | tf_op jit(solution)/shard_map/ppermute | solution.py:41
  180.8 2.7 %collective-permute-start.33 = (bf16[4,128,256]{2,1,0:T(8,128)(2,1)S(1)}, bf16[4,128,256]{2,1,0:T(8,128)(2,1)}, u32[]{:S(2)}, u32[]{:S(2)}) collective-permute-start(bf16[4,128,256]{2,1,0:T(8,128)(2,1)S(1)} %copy-done.13), channel_id=1, source_target_pairs={{0,1},{1,0},{2,3},{3,2},{4,5},{5,4},{6,7},{7,6},{8,9},{9,8},{10,11... | collective-permute-start | bytes 786440 | tf_op jit(solution)/shard_map/ppermute | solution.py:41
  186.8 3.7 %shard_map.104 = f32[8,256,256]{2,1,0:T(8,128)} custom-call(s32[8]{0:T(128)} %xor.40.order_ref, s32[1]{0:T(128)} %bitcast.5.me_ref, bf16[8,128,256]{2,1,0:T(8,128)(2,1)} %get-tuple-element.28.refs_4_.refs_0_, bf16[8,128,256]{2,1,0:T(8,128)(2,1)} %copy-done.6, bf16[8,128,256]{2,1,0:T(8,128)(2,1)} %copy-done.7, bf16[8,128,256]{2,1,0:T(8,128)(2,1)} %copy-done.8, ...), custom_call_target="tpu_custom_call" | custom-call | flops 1024 | bytes 1024 | tf_op jit(solution)/shard_map/pallas_call | solution.py:355
  192.5 3.6 %shard_map.106 = f32[8,256,256]{2,1,0:T(8,128)} custom-call(s32[8]{0:T(128)} %xor.40.order_ref, s32[1]{0:T(128)} %bitcast.5.me_ref, bf16[4,8,128,256]{3,2,1,0:T(8,128)(2,1)} %copy-done.1, bf16[4,128,256]{2,1,0:T(8,128)(2,1)} %shard_map.101.refs_1_, bf16[4,128,256]{2,1,0:T(8,128)(2,1)} %copy-done.12, bf16[4,128,256]{2,1,0:T(8,128)(2,1)} %copy-done.14, ...), custom_call_target="tpu_custom_call" | custom-call | flops 1024 | bytes 1024 | tf_op jit(solution)/shard_map/pallas_call | solution.py:355
  (155 shorter events, 38.8 us)
Async XLA Ops:
  7.2 31.5 %all-gather.3.cloned.1.call-start = ((), (), s32[]{:S(2)}) async-start(), calls=%async_computation.5 | async-start | bytes 1253376 | tf_op jit(solution)/shard_map/all_gather | solution.py:381
  16.6 36.3 %all-to-all-start = ((bf16[8,256,256]{2,1,0:T(8,128)(2,1)}), bf16[8,256,256]{2,1,0:T(8,128)(2,1)S(1)}, u32[]{:S(2)}, u32[]{:S(2)}) async-start(bf16[8,256,256]{2,1,0:T(8,128)(2,1)} %shard_map.97), calls=%async_computation | async-start | bytes 2097152 | tf_op jit(solution)/shard_map/all_to_all | solution.py:385
  23.1 102.2 %reduce-scatter.2.cloned.1.call-start = ((), (), s32[]{:S(2)}) async-start(), calls=%async_computation.4 | async-start | bytes 2359296 | tf_op jit(solution)/shard_map/reduce_scatter | solution.py:394
  23.1 6.5 %collective-permute-start.1 = (bf16[256,256]{1,0:T(8,128)(2,1)S(1)}, bf16[256,256]{1,0:T(8,128)(2,1)S(1)}, u32[]{:S(2)}, u32[]{:S(2)}) collective-permute-start(bf16[256,256]{1,0:T(8,128)(2,1)S(1)} %copy-done.16), channel_id=1, source_target_pairs={{0,16},{8,24},{16,0},{24,8},{1,17},{9,25},{17,1},{25,9},{2,18},{10... | collective-permute-start | bytes 393224 | tf_op jit(solution)/shard_map/ppermute | solution.py:41
  44.4 7.1 %collective-permute-start.4 = (f32[3,2048]{1,0:T(4,128)}, f32[3,2048]{1,0:T(4,128)S(1)}, u32[]{:S(2)}, u32[]{:S(2)}) collective-permute-start(f32[3,2048]{1,0:T(4,128)} %shard_map.96.refs_0_), channel_id=1, source_target_pairs={{0,2},{1,3},{2,0},{3,1},{4,6},{5,7},{6,4},{7,5},{8,10},{9,11},{10,... | collective-permute-start | bytes 73736 | tf_op jit(solution)/shard_map/ppermute | solution.py:41
  45.3 7.5 %collective-permute-start.5 = (f32[3,2048]{1,0:T(4,128)}, f32[3,2048]{1,0:T(4,128)S(1)}, u32[]{:S(2)}, u32[]{:S(2)}) collective-permute-start(f32[3,2048]{1,0:T(4,128)} %shard_map.96.refs_0_), channel_id=1, source_target_pairs={{0,3},{1,2},{2,1},{3,0},{4,7},{5,6},{6,5},{7,4},{8,11},{9,10},{10,... | collective-permute-start | bytes 73736 | tf_op jit(solution)/shard_map/ppermute | solution.py:41
  46.2 7.3 %collective-permute-start.6 = (f32[3,2048]{1,0:T(4,128)}, f32[3,2048]{1,0:T(4,128)S(1)}, u32[]{:S(2)}, u32[]{:S(2)}) collective-permute-start(f32[3,2048]{1,0:T(4,128)} %shard_map.96.refs_0_), channel_id=1, source_target_pairs={{0,4},{1,5},{2,6},{3,7},{4,0},{5,1},{6,2},{7,3},{8,12},{9,13},{10,... | collective-permute-start | bytes 73736 | tf_op jit(solution)/shard_map/ppermute | solution.py:41
  50.0 7.6 %collective-permute-start.8 = (f32[3,2048]{1,0:T(4,128)}, f32[3,2048]{1,0:T(4,128)S(1)}, u32[]{:S(2)}, u32[]{:S(2)}) collective-permute-start(f32[3,2048]{1,0:T(4,128)} %shard_map.96.refs_0_), channel_id=1, source_target_pairs={{0,6},{1,7},{2,4},{3,5},{4,2},{5,3},{6,0},{7,1},{8,14},{9,15},{10,... | collective-permute-start | bytes 73736 | tf_op jit(solution)/shard_map/ppermute | solution.py:41
  51.4 7.5 %collective-permute-start.9 = (f32[3,2048]{1,0:T(4,128)}, f32[3,2048]{1,0:T(4,128)S(1)}, u32[]{:S(2)}, u32[]{:S(2)}) collective-permute-start(f32[3,2048]{1,0:T(4,128)} %shard_map.96.refs_0_), channel_id=1, source_target_pairs={{0,7},{1,6},{2,5},{3,4},{4,3},{5,2},{6,1},{7,0},{8,15},{9,14},{10,... | collective-permute-start | bytes 73736 | tf_op jit(solution)/shard_map/ppermute | solution.py:41
  67.8 68.5 %all-to-all-start.1 = ((bf16[8,256,256]{2,1,0:T(8,128)(2,1)}), bf16[8,256,256]{2,1,0:T(8,128)(2,1)S(1)}, u32[]{:S(2)}, u32[]{:S(2)}) async-start(bf16[8,256,256]{2,1,0:T(8,128)(2,1)} %shard_map.95.refs_4_), calls=%async_computation.2 | async-start | bytes 2097152 | tf_op jit(solution)/shard_map/all_to_all | solution.py:385
  72.3 7.6 %collective-permute-start.10 = (f32[256,256]{1,0:T(8,128)S(1)}, f32[256,256]{1,0:T(8,128)S(1)}, u32[]{:S(2)}, u32[]{:S(2)}) collective-permute-start(f32[256,256]{1,0:T(8,128)S(1)} %copy-done.41), channel_id=1, source_target_pairs={{0,8},{8,0},{16,24},{24,16},{1,9},{9,1},{17,25},{25,17},{2,10},{10... | collective-permute-start | bytes 786440 | tf_op jit(solution)/shard_map/ppermute | solution.py:41
  72.5 7.4 %collective-permute-start.11 = (f32[256,256]{1,0:T(8,128)S(1)}, f32[256,256]{1,0:T(8,128)S(1)}, u32[]{:S(2)}, u32[]{:S(2)}) collective-permute-start(f32[256,256]{1,0:T(8,128)S(1)} %copy-done.40), channel_id=1, source_target_pairs={{0,16},{8,24},{16,0},{24,8},{1,17},{9,25},{17,1},{25,9},{2,18},{10... | collective-permute-start | bytes 786440 | tf_op jit(solution)/shard_map/ppermute | solution.py:41
  73.7 12.6 %collective-permute-start.12 = (f32[256,256]{1,0:T(8,128)S(1)}, f32[256,256]{1,0:T(8,128)S(1)}, u32[]{:S(2)}, u32[]{:S(2)}) collective-permute-start(f32[256,256]{1,0:T(8,128)S(1)} %copy-done.39), channel_id=1, source_target_pairs={{0,24},{8,16},{16,8},{24,0},{1,25},{9,17},{17,9},{25,1},{2,26},{10... | collective-permute-start | bytes 786440 | tf_op jit(solution)/shard_map/ppermute | solution.py:41
  91.0 34.1 %collective-permute-start.13 = (bf16[8,128,256]{2,1,0:T(8,128)(2,1)}, bf16[8,128,256]{2,1,0:T(8,128)(2,1)S(1)}, u32[]{:S(2)}, u32[]{:S(2)}) collective-permute-start(bf16[8,128,256]{2,1,0:T(8,128)(2,1)} %get-tuple-element.29), channel_id=1, source_target_pairs={{0,8},{8,0},{16,24},{24,16},{1,9},{9,1},{17,25},{25,17},{2,10},{10... | collective-permute-start | bytes 1572872 | tf_op jit(solution)/shard_map/ppermute | solution.py:41
  91.3 33.9 %collective-permute-start.14 = (bf16[8,128,256]{2,1,0:T(8,128)(2,1)}, bf16[8,128,256]{2,1,0:T(8,128)(2,1)S(1)}, u32[]{:S(2)}, u32[]{:S(2)}) collective-permute-start(bf16[8,128,256]{2,1,0:T(8,128)(2,1)} %get-tuple-element.30), channel_id=1, source_target_pairs={{0,16},{8,24},{16,0},{24,8},{1,17},{9,25},{17,1},{25,9},{2,18},{10... | collective-permute-start | bytes 1572872 | tf_op jit(solution)/shard_map/ppermute | solution.py:41
  92.5 32.6 %collective-permute-start.15 = (bf16[8,128,256]{2,1,0:T(8,128)(2,1)}, bf16[8,128,256]{2,1,0:T(8,128)(2,1)S(1)}, u32[]{:S(2)}, u32[]{:S(2)}) collective-permute-start(bf16[8,128,256]{2,1,0:T(8,128)(2,1)} %get-tuple-element.31), channel_id=1, source_target_pairs={{0,24},{8,16},{16,8},{24,0},{1,25},{9,17},{17,9},{25,1},{2,26},{10... | collective-permute-start | bytes 1572872 | tf_op jit(solution)/shard_map/ppermute | solution.py:41
  95.8 20.3 %collective-permute-start.16 = (bf16[128,256]{1,0:T(8,128)(2,1)}, bf16[128,256]{1,0:T(8,128)(2,1)S(1)}, u32[]{:S(2)}, u32[]{:S(2)}) collective-permute-start(bf16[128,256]{1,0:T(8,128)(2,1)} %get-tuple-element.36), channel_id=1, source_target_pairs={{0,8},{8,0},{16,24},{24,16},{1,9},{9,1},{17,25},{25,17},{2,10},{10... | collective-permute-start | bytes 196616 | tf_op jit(solution)/shard_map/ppermute | solution.py:41
  96.1 21.0 %collective-permute-start.17 = (bf16[128,256]{1,0:T(8,128)(2,1)}, bf16[128,256]{1,0:T(8,128)(2,1)S(1)}, u32[]{:S(2)}, u32[]{:S(2)}) collective-permute-start(bf16[128,256]{1,0:T(8,128)(2,1)} %get-tuple-element.37), channel_id=1, source_target_pairs={{0,16},{8,24},{16,0},{24,8},{1,17},{9,25},{17,1},{25,9},{2,18},{10... | collective-permute-start | bytes 196616 | tf_op jit(solution)/shard_map/ppermute | solution.py:41
  122.7 8.7 %collective-permute-start.22 = (bf16[4,128,256]{2,1,0:T(8,128)(2,1)}, bf16[4,128,256]{2,1,0:T(8,128)(2,1)S(1)}, u32[]{:S(2)}, u32[]{:S(2)}) collective-permute-start(bf16[4,128,256]{2,1,0:T(8,128)(2,1)} %shard_map.101.refs_1_), channel_id=1, source_target_pairs={{0,2},{1,3},{2,0},{3,1},{4,6},{5,7},{6,4},{7,5},{8,10},{9,11},{10,... | collective-permute-start | bytes 786440 | tf_op jit(solution)/shard_map/ppermute | solution.py:41
  123.4 10.5 %collective-permute-start.23 = (bf16[4,128,256]{2,1,0:T(8,128)(2,1)}, bf16[4,128,256]{2,1,0:T(8,128)(2,1)S(1)}, u32[]{:S(2)}, u32[]{:S(2)}) collective-permute-start(bf16[4,128,256]{2,1,0:T(8,128)(2,1)} %shard_map.101.refs_1_), channel_id=1, source_target_pairs={{0,4},{1,5},{2,6},{3,7},{4,0},{5,1},{6,2},{7,3},{8,12},{9,13},{10,... | collective-permute-start | bytes 786440 | tf_op jit(solution)/shard_map/ppermute | solution.py:41
  141.4 49.1 %all-to-all-start.2 = ((bf16[4,8,128,256]{3,2,1,0:T(8,128)(2,1)}), bf16[4,8,128,256]{3,2,1,0:T(8,128)(2,1)S(1)}, u32[]{:S(2)}, u32[]{:S(2)}) async-start(bf16[4,8,128,256]{3,2,1,0:T(8,128)(2,1)} %shard_map.105), calls=%async_computation.3 | async-start | bytes 4194304 | tf_op jit(solution)/shard_map/all_to_all | solution.py:385
  145.2 9.9 %collective-permute-start.24 = (bf16[4,128,256]{2,1,0:T(8,128)(2,1)S(1)}, bf16[4,128,256]{2,1,0:T(8,128)(2,1)S(1)}, u32[]{:S(2)}, u32[]{:S(2)}) collective-permute-start(bf16[4,128,256]{2,1,0:T(8,128)(2,1)S(1)} %copy-done.3), channel_id=1, source_target_pairs={{0,2},{1,3},{2,0},{3,1},{4,6},{5,7},{6,4},{7,5},{8,10},{9,11},{10,... | collective-permute-start | bytes 786440 | tf_op jit(solution)/shard_map/ppermute | solution.py:41
  146.5 17.2 %collective-permute-start.25 = (bf16[4,128,256]{2,1,0:T(8,128)(2,1)S(1)}, bf16[4,128,256]{2,1,0:T(8,128)(2,1)S(1)}, u32[]{:S(2)}, u32[]{:S(2)}) collective-permute-start(bf16[4,128,256]{2,1,0:T(8,128)(2,1)S(1)} %copy-done.3), channel_id=1, source_target_pairs={{0,4},{1,5},{2,6},{3,7},{4,0},{5,1},{6,2},{7,3},{8,12},{9,13},{10,... | collective-permute-start | bytes 786440 | tf_op jit(solution)/shard_map/ppermute | solution.py:41
  146.7 28.4 %collective-permute-start.31 = (bf16[4,128,256]{2,1,0:T(8,128)(2,1)S(1)}, bf16[4,128,256]{2,1,0:T(8,128)(2,1)S(1)}, u32[]{:S(2)}, u32[]{:S(2)}) collective-permute-start(bf16[4,128,256]{2,1,0:T(8,128)(2,1)S(1)} %copy-done.4), channel_id=1, source_target_pairs={{0,6},{1,7},{2,4},{3,5},{4,2},{5,3},{6,0},{7,1},{8,14},{9,15},{10,... | collective-permute-start | bytes 786440 | tf_op jit(solution)/shard_map/ppermute | solution.py:41
  147.9 32.9 %collective-permute-start.26 = (bf16[4,128,256]{2,1,0:T(8,128)(2,1)S(1)}, bf16[4,128,256]{2,1,0:T(8,128)(2,1)}, u32[]{:S(2)}, u32[]{:S(2)}) collective-permute-start(bf16[4,128,256]{2,1,0:T(8,128)(2,1)S(1)} %copy-done.3), channel_id=1, source_target_pairs={{0,6},{1,7},{2,4},{3,5},{4,2},{5,3},{6,0},{7,1},{8,14},{9,15},{10,... | collective-permute-start | bytes 786440 | tf_op jit(solution)/shard_map/ppermute | solution.py:41
  148.1 35.3 %collective-permute-start.27 = (bf16[4,128,256]{2,1,0:T(8,128)(2,1)S(1)}, bf16[4,128,256]{2,1,0:T(8,128)(2,1)S(1)}, u32[]{:S(2)}, u32[]{:S(2)}) collective-permute-start(bf16[4,128,256]{2,1,0:T(8,128)(2,1)S(1)} %copy-done.3), channel_id=1, source_target_pairs={{0,1},{1,0},{2,3},{3,2},{4,5},{5,4},{6,7},{7,6},{8,9},{9,8},{10,11... | collective-permute-start | bytes 786440 | tf_op jit(solution)/shard_map/ppermute | solution.py:41
  155.1 28.5 %collective-permute-start.28 = (bf16[4,128,256]{2,1,0:T(8,128)(2,1)S(1)}, bf16[4,128,256]{2,1,0:T(8,128)(2,1)S(1)}, u32[]{:S(2)}, u32[]{:S(2)}) collective-permute-start(bf16[4,128,256]{2,1,0:T(8,128)(2,1)S(1)} %collective-permute-done.24.refs_5_), channel_id=1, source_target_pairs={{0,1},{1,0},{2,3},{3,2},{4,5},{5,4},{6,7},{7,6},{8,9},{9,8},{10,11... | collective-permute-start | bytes 786440 | tf_op jit(solution)/shard_map/ppermute | solution.py:41
  163.7 20.5 %collective-permute-start.29 = (bf16[4,128,256]{2,1,0:T(8,128)(2,1)S(1)}, bf16[4,128,256]{2,1,0:T(8,128)(2,1)S(1)}, u32[]{:S(2)}, u32[]{:S(2)}) collective-permute-start(bf16[4,128,256]{2,1,0:T(8,128)(2,1)S(1)} %collective-permute-done.25.refs_6_), channel_id=1, source_target_pairs={{0,1},{1,0},{2,3},{3,2},{4,5},{5,4},{6,7},{7,6},{8,9},{9,8},{10,11... | collective-permute-start | bytes 786440 | tf_op jit(solution)/shard_map/ppermute | solution.py:41
  175.1 15.4 %collective-permute-start.32 = (bf16[4,128,256]{2,1,0:T(8,128)(2,1)S(1)}, bf16[4,128,256]{2,1,0:T(8,128)(2,1)}, u32[]{:S(2)}, u32[]{:S(2)}) collective-permute-start(bf16[4,128,256]{2,1,0:T(8,128)(2,1)S(1)} %copy-done.4), channel_id=1, source_target_pairs={{0,1},{1,0},{2,3},{3,2},{4,5},{5,4},{6,7},{7,6},{8,9},{9,8},{10,11... | collective-permute-start | bytes 786440 | tf_op jit(solution)/shard_map/ppermute | solution.py:41
  180.8 9.7 %collective-permute-start.33 = (bf16[4,128,256]{2,1,0:T(8,128)(2,1)S(1)}, bf16[4,128,256]{2,1,0:T(8,128)(2,1)}, u32[]{:S(2)}, u32[]{:S(2)}) collective-permute-start(bf16[4,128,256]{2,1,0:T(8,128)(2,1)S(1)} %copy-done.13), channel_id=1, source_target_pairs={{0,1},{1,0},{2,3},{3,2},{4,5},{5,4},{6,7},{7,6},{8,9},{9,8},{10,11... | collective-permute-start | bytes 786440 | tf_op jit(solution)/shard_map/ppermute | solution.py:41
  183.5 7.0 %collective-permute-start.34 = (bf16[4,128,256]{2,1,0:T(8,128)(2,1)S(1)}, bf16[4,128,256]{2,1,0:T(8,128)(2,1)S(1)}, u32[]{:S(2)}, u32[]{:S(2)}) collective-permute-start(bf16[4,128,256]{2,1,0:T(8,128)(2,1)S(1)} %copy-done.15), channel_id=1, source_target_pairs={{0,1},{1,0},{2,3},{3,2},{4,5},{5,4},{6,7},{7,6},{8,9},{9,8},{10,11... | collective-permute-start | bytes 786440 | tf_op jit(solution)/shard_map/ppermute | solution.py:41
  183.6 6.9 %collective-permute-start.35 = (bf16[4,128,256]{2,1,0:T(8,128)(2,1)S(1)}, bf16[4,128,256]{2,1,0:T(8,128)(2,1)}, u32[]{:S(2)}, u32[]{:S(2)}) collective-permute-start(bf16[4,128,256]{2,1,0:T(8,128)(2,1)S(1)} %collective-permute-done.31.refs_4_), channel_id=1, source_target_pairs={{0,1},{1,0},{2,3},{3,2},{4,5},{5,4},{6,7},{7,6},{8,9},{9,8},{10,11... | collective-permute-start | bytes 786440 | tf_op jit(solution)/shard_map/ppermute | solution.py:41
  (51 other events, 320.9 us)
Sparse Core Ops, SparseCore 0:
  9.6 29.0 all-gather.2
  67.9 52.7 reduce-scatter.1

commit v16 on v14

--- a/solution.py
+++ b/solution.py
@@ -400,7 +400,7 @@
     item_line = exchange([item_sent] * lines, "item", CORES)
     user_routed = route(me, targets, [user_grad], 0, groups, user_rows[1:])
     item_slots = slot_hidden(me, users, item_cols, groups, 1, False, user_routed[0])
-    user_sent = stack(exchange(user_routed, "user"), item_line[1:3] + [item_slots[0]])
+    user_sent = stack(exchange(user_routed, "user"), item_line[1:] + [item_slots[0]])
     item_rows = [scatter(item_slots[0], "user")]
     item_cross = item_line + [swap(piece, "item", 1) for piece in item_line]
     user_all = lax.all_gather(user_sent, "item", axis=0)

time: 183 us -> 189 us (1.033)
  waiting for transfers between devices: 68.2 us -> 79.8 us
  starting transfers between devices: 46 us -> 41.5 us
    all_to_all x3, waiting for transfers between devices: 0.49 us -> 15.7 us  [scatter(): return lax.all_to_all(pieces, axis, split_axis=0, concat_axis=0, tiled=True)]
    ppermute x29, starting transfers between devices: 31 us -> 26.2 us  [swap(): return lax.ppermute(piece, axis, [(j, j ^ bits) for j in range(size)])]
    ppermute x29, waiting for transfers between devices: 55.6 us -> 52.2 us  [swap(): return lax.ppermute(piece, axis, [(j, j ^ bits) for j in range(size)])]
    unnamed x72 -> x74, local copies, waits for them, and re-layouts: 6.99 us -> 6.26 us
  transfers between devices with their start and end apart: 35 -> 35, of which waited for: 16 -> 18; matrix products, arithmetic and copies ran while one was open for 1% -> 1% of each run, Pallas kernels for 15% -> 15%
where the time goes in v16:
time: 189 us; the launch traced here: 186 us
  waiting for transfers between devices  79.8 us (42%)
  Pallas kernels  42.6 us (23%)
  starting transfers between devices  41.5 us (22%)
  between operations  14 us (7%)
  local copies, waits for them, and re-layouts  8.01 us (4%)
    ppermute x29, waiting for transfers between devices, swap(): return lax.ppermute(piece, axis, [(j, j ^ bits) for j in range(size)])  52.2 us
    ppermute x29, starting transfers between devices, swap(): return lax.ppermute(piece, axis, [(j, j ^ bits) for j in range(size)])  26.2 us
    all_to_all x3, waiting for transfers between devices, scatter(): return lax.all_to_all(pieces, axis, split_axis=0, concat_axis=0, tiled=True)  15.7 us
    all_to_all x3, starting transfers between devices, scatter(): return lax.all_to_all(pieces, axis, split_axis=0, concat_axis=0, tiled=True)  15.2 us
    all_gather x1, waiting for transfers between devices, shards(): users = lax.all_gather(packed, 'item', axis=0)  8.91 us
    pallas_call x1, Pallas kernels, grads(): pl.pallas_call(functools.partial(grad_kernel, rows=rows, chunk=64, count=...  8.17 us
    pallas_call x2, Pallas kernels, slot_hidden(): pl.pallas_call(functools.partial(hidden_kernel, tower=tower), grid=(block...  8.12 us
    pallas_call x2, Pallas kernels, outer(): pl.pallas_call(functools.partial(outer_kernel, count=len(hidden)), grid=(...  7.32 us
  transfers between devices with their start and end apart: 35, of which 18 were waited for; matrix products, arithmetic and copies ran while one was open for 1% of the time, Pallas kernels for 15%

profile of v16, /device:TPU:11, one launch (start us, length us, event | category | flops | bytes accessed | tf_op | source)
XLA Modules:
  0.0 186.5 jit_solution(11745648862416578534)
XLA Ops:
  7.2 1.8 shard_map.94
  9.3 4.3 %collective-permute-done._.refs_1_.refs_9_ = bf16[256,256]{1,0:T(8,128)(2,1)S(1)} collective-permute-done((bf16[256,256]{1,0:T(8,128)(2,1)}, bf16[256,256]{1,0:T(8,128)(2,1)S(1)}, u32[]{:S(2)}, u32[]{:S(2)}) %collective-permute-start) | collective-permute-done | bytes 131104 | tf_op jit(solution)/shard_map/ppermute | solution.py:41
  14.3 2.3 %shard_map.97 = bf16[8,256,256]{2,1,0:T(8,128)(2,1)} custom-call(bf16[256,2048]{1,0:T(8,128)(2,1)} %in_ref.3, bf16[256,256]{1,0:T(8,128)(2,1)} %copy-done.3), custom_call_target="tpu_custom_call" | custom-call | flops 1024 | bytes 1024 | tf_op jit(solution)/shard_map/pallas_call | solution.py:221
  16.6 6.5 %all-to-all-start = ((bf16[8,256,256]{2,1,0:T(8,128)(2,1)}), bf16[8,256,256]{2,1,0:T(8,128)(2,1)S(1)}, u32[]{:S(2)}, u32[]{:S(2)}) async-start(bf16[8,256,256]{2,1,0:T(8,128)(2,1)} %shard_map.97), calls=%async_computation | async-start | bytes 2097152 | tf_op jit(solution)/shard_map/all_to_all | solution.py:384
  25.1 2.3 %shard_map.95.refs_4_ = bf16[8,256,256]{2,1,0:T(8,128)(2,1)} custom-call(bf16[256,2048]{1,0:T(8,128)(2,1)} %in_ref.2, bf16[256,256]{1,0:T(8,128)(2,1)} %copy-done.3), custom_call_target="tpu_custom_call" | custom-call | flops 1024 | bytes 1024 | tf_op jit(solution)/shard_map/pallas_call | solution.py:221
  27.4 2.2 %collective-permute-done.1.refs_2_.refs_10_ = bf16[256,256]{1,0:T(8,128)(2,1)S(1)} collective-permute-done((bf16[256,256]{1,0:T(8,128)(2,1)S(1)}, bf16[256,256]{1,0:T(8,128)(2,1)S(1)}, u32[]{:S(2)}, u32[]{:S(2)}) %collective-permute-start.1) | collective-permute-done | bytes 131104 | tf_op jit(solution)/shard_map/ppermute | solution.py:41
  29.8 8.9 %all-gather.5.cloned.1.call-done = bf16[2176,256]{1,0:T(8,128)(2,1)} async-done(((bf16[272,256]{1,0:T(8,128)(2,1)}), bf16[2176,256]{1,0:T(8,128)(2,1)}) %all-gather.5.cloned.1.call-update) | async-done | bytes 1114128 | tf_op jit(solution)/shard_map/all_gather | solution.py:380
  38.7 5.4 %shard_map.96.refs_0_ = f32[3,2048]{1,0:T(4,128)} custom-call(s32[4]{0:T(128)} %add_multiply_fusion.first_ref, bf16[8,272,256]{2,1,0:T(8,128)(2,1)} %bitcast.7, bf16[256,256]{1,0:T(8,128)(2,1)} %refs_8_.1, bf16[256,256]{1,0:T(8,128)(2,1)} %copy-done.3, bf16[256,256]{1,0:T(8,128)(2,1)} %copy-done.15, bf16[256,256]{1,0:T(8,128)(2,1)} %copy-done.16, ...), custom_call_target="tpu_custom_call" | custom-call | flops 1024 | bytes 1024 | tf_op jit(solution)/shard_map/pallas_call | solution.py:119
  46.2 3.7 %collective-permute-start.6 = (f32[3,2048]{1,0:T(4,128)}, f32[3,2048]{1,0:T(4,128)S(1)}, u32[]{:S(2)}, u32[]{:S(2)}) collective-permute-start(f32[3,2048]{1,0:T(4,128)} %shard_map.96.refs_0_), channel_id=1, source_target_pairs={{0,4},{1,5},{2,6},{3,7},{4,0},{5,1},{6,2},{7,3},{8,12},{9,13},{10,... | collective-permute-start | bytes 73736 | tf_op jit(solution)/shard_map/ppermute | solution.py:41
  50.0 1.5 collective-permute-start.8
  54.8 2.7 %collective-permute-done.8.refs_6_ = f32[3,2048]{1,0:T(4,128)S(1)} collective-permute-done((f32[3,2048]{1,0:T(4,128)}, f32[3,2048]{1,0:T(4,128)S(1)}, u32[]{:S(2)}, u32[]{:S(2)}) %collective-permute-start.8) | collective-permute-done | bytes 24608 | tf_op jit(solution)/shard_map/ppermute | solution.py:41
  57.5 1.4 collective-permute-done.9.refs_7_
  59.6 8.2 %shard_map.98 = (f32[1,2048]{1,0:T(1,128)}, f32[2048,256]{1,0:T(8,128)}, f32[256,256]{1,0:T(8,128)}, f32[256,256]{1,0:T(8,128)}, f32[256,256]{1,0:T(8,128)}, /*index=5*/f32[256,256]{1,0:T(8,128)}) custom-call(s32[4]{0:T(128)} %add_multiply_fusion.first_ref, bf16[8,272,256]{2,1,0:T(8,128)(2,1)} %bitcast.8, f32[3,2048]{1,0:T(4,128)} %shard_map.96.refs_0_, ...), custom_call_target="tpu_custom_call" | custom-call | flops 1024 | bytes 1024 | tf_op jit(solution)/shard_map/pallas_call | solution.py:182
  67.8 4.4 %all-to-all-start.1 = ((bf16[8,256,256]{2,1,0:T(8,128)(2,1)}), bf16[8,256,256]{2,1,0:T(8,128)(2,1)S(1)}, u32[]{:S(2)}, u32[]{:S(2)}) async-start(bf16[8,256,256]{2,1,0:T(8,128)(2,1)} %shard_map.95.refs_4_), calls=%async_computation.2 | async-start | bytes 2097152 | tf_op jit(solution)/shard_map/all_to_all | solution.py:384
  72.6 4.0 %shard_map.99 = (bf16[8,128,256]{2,1,0:T(8,128)(2,1)}, bf16[8,128,256]{2,1,0:T(8,128)(2,1)}, bf16[8,128,256]{2,1,0:T(8,128)(2,1)}, bf16[8,128,256]{2,1,0:T(8,128)(2,1)}) custom-call(s32[1]{0:T(128)} %bitcast.5.me_ref, bf16[8,272,256]{2,1,0:T(8,128)(2,1)} %bitcast.9, bf16[8,256,256]{2,1,0:T(8,128)(2,1)} %copy-done, f32[256,256]{1,0:T(8,128)} %get-tuple-element.25._.refs_0_), custom_call_target="tpu_custom_call" | custom-call | flops 1024 | bytes 1024 | tf_op jit(solution)/shard_map/pallas_call | solution.py:263
  81.6 3.2 %collective-permute-done.17.refs_2_ = f32[256,256]{1,0:T(8,128)S(1)} collective-permute-done((f32[256,256]{1,0:T(8,128)S(1)}, f32[256,256]{1,0:T(8,128)S(1)}, u32[]{:S(2)}, u32[]{:S(2)}) %collective-permute-start.17) | collective-permute-done | bytes 262176 | tf_op jit(solution)/shard_map/ppermute | solution.py:41
  84.8 12.9 %collective-permute-done.18.refs_3_ = f32[256,256]{1,0:T(8,128)S(1)} collective-permute-done((f32[256,256]{1,0:T(8,128)S(1)}, f32[256,256]{1,0:T(8,128)S(1)}, u32[]{:S(2)}, u32[]{:S(2)}) %collective-permute-start.18) | collective-permute-done | bytes 262176 | tf_op jit(solution)/shard_map/ppermute | solution.py:41
  98.4 2.1 %shard_map.101 = (bf16[128,256]{1,0:T(8,128)(2,1)}, bf16[128,256]{1,0:T(8,128)(2,1)}, bf16[128,256]{1,0:T(8,128)(2,1)}, bf16[128,256]{1,0:T(8,128)(2,1)}) custom-call(s32[1]{0:T(128)} %bitcast.5.me_ref, s32[2,256]{1,0:T(2,128)} %get-tuple-element.30.target_ref, f32[256,256]{1,0:T(8,128)} %get-tuple-element.25._.refs_0_, f32[256,256]{1,0:T(8,128)} %copy-done.17, ...), custom_call_target="tpu_custom_call" | custom-call | flops 1024 | bytes 1024 | tf_op jit(solution)/shard_map/pallas_call | solution.py:295
  100.9 8.5 %collective-permute-done.19.refs_1_ = bf16[128,256]{1,0:T(8,128)(2,1)S(1)} collective-permute-done((bf16[128,256]{1,0:T(8,128)(2,1)}, bf16[128,256]{1,0:T(8,128)(2,1)S(1)}, u32[]{:S(2)}, u32[]{:S(2)}) %collective-permute-start.19) | collective-permute-done | bytes 65568 | tf_op jit(solution)/shard_map/ppermute | solution.py:41
  110.4 4.5 %collective-permute-done.20.refs_2_ = bf16[128,256]{1,0:T(8,128)(2,1)S(1)} collective-permute-done((bf16[128,256]{1,0:T(8,128)(2,1)}, bf16[128,256]{1,0:T(8,128)(2,1)S(1)}, u32[]{:S(2)}, u32[]{:S(2)}) %collective-permute-start.20) | collective-permute-done | bytes 65568 | tf_op jit(solution)/shard_map/ppermute | solution.py:41
  115.5 1.6 shard_map.102.refs_1_
  120.8 1.9 %shard_map.100 = (bf16[128,256]{1,0:T(8,128)(2,1)}, bf16[128,256]{1,0:T(8,128)(2,1)}, bf16[128,256]{1,0:T(8,128)(2,1)}, bf16[128,256]{1,0:T(8,128)(2,1)}) custom-call(s32[1]{0:T(128)} %bitcast.5.me_ref, s32[2,256]{1,0:T(2,128)} %get-tuple-element.30.target_ref, f32[256,256]{1,0:T(8,128)} %reduce-scatter.2.cloned.1.call-done.refs_0_, ...), custom_call_target="tpu_custom_call" | custom-call | flops 1024 | bytes 1024 | tf_op jit(solution)/shard_map/pallas_call | solution.py:295
  124.2 2.4 %collective-permute-done.22.refs_4_.refs_2_ = bf16[4,128,256]{2,1,0:T(8,128)(2,1)S(1)} collective-permute-done((bf16[4,128,256]{2,1,0:T(8,128)(2,1)}, bf16[4,128,256]{2,1,0:T(8,128)(2,1)S(1)}, u32[]{:S(2)}, u32[]{:S(2)}) %collective-permute-start.22) | collective-permute-done | bytes 262176 | tf_op jit(solution)/shard_map/ppermute | solution.py:41
  128.6 4.1 %shard_map.103.refs_7_ = bf16[4,8,128,256]{3,2,1,0:T(8,128)(2,1)} custom-call(s32[1]{0:T(128)} %bitcast.5.me_ref, bf16[8,272,256]{2,1,0:T(8,128)(2,1)} %bitcast.10, bf16[8,256,256]{2,1,0:T(8,128)(2,1)} %copy-done.2, bf16[128,256]{1,0:T(8,128)(2,1)} %get-tuple-element.32._.refs_0_), custom_call_target="tpu_custom_call" | custom-call | flops 1024 | bytes 1024 | tf_op jit(solution)/shard_map/pallas_call | solution.py:263
  132.8 7.9 %collective-permute-done.24.refs_6_.refs_4_ = bf16[4,128,256]{2,1,0:T(8,128)(2,1)S(1)} collective-permute-done((bf16[4,128,256]{2,1,0:T(8,128)(2,1)}, bf16[4,128,256]{2,1,0:T(8,128)(2,1)S(1)}, u32[]{:S(2)}, u32[]{:S(2)}) %collective-permute-start.24) | collective-permute-done | bytes 262176 | tf_op jit(solution)/shard_map/ppermute | solution.py:41
  142.0 1.7 shard_map.104
  143.8 4.3 %all-to-all-start.2 = ((bf16[4,8,128,256]{3,2,1,0:T(8,128)(2,1)}), bf16[4,8,128,256]{3,2,1,0:T(8,128)(2,1)S(1)}, u32[]{:S(2)}, u32[]{:S(2)}) async-start(bf16[4,8,128,256]{3,2,1,0:T(8,128)(2,1)} %shard_map.103.refs_7_), calls=%async_computation.3 | async-start | bytes 4194304 | tf_op jit(solution)/shard_map/all_to_all | solution.py:384
  148.0 3.6 %collective-permute-start.25 = (bf16[4,128,256]{2,1,0:T(8,128)(2,1)S(1)}, bf16[4,128,256]{2,1,0:T(8,128)(2,1)S(1)}, u32[]{:S(2)}, u32[]{:S(2)}) collective-permute-start(bf16[4,128,256]{2,1,0:T(8,128)(2,1)S(1)} %copy-done.7), channel_id=1, source_target_pairs={{0,1},{1,0},{2,3},{3,2},{4,5},{5,4},{6,7},{7,6},{8,9},{9,8},{10,11... | collective-permute-start | bytes 786440 | tf_op jit(solution)/shard_map/ppermute | solution.py:41
  154.1 15.2 %all-to-all-done.2.refs_0_ = bf16[4,8,128,256]{3,2,1,0:T(8,128)(2,1)S(1)} async-done(((bf16[4,8,128,256]{3,2,1,0:T(8,128)(2,1)}), bf16[4,8,128,256]{3,2,1,0:T(8,128)(2,1)S(1)}, u32[]{:S(2)}, u32[]{:S(2)}) %all-to-all-start.2) | async-done | bytes 2097184 | tf_op jit(solution)/shard_map/all_to_all | solution.py:384
  170.7 3.7 %shard_map.106 = f32[8,256,256]{2,1,0:T(8,128)} custom-call(s32[8]{0:T(128)} %xor.40.order_ref, s32[1]{0:T(128)} %bitcast.5.me_ref, bf16[4,8,128,256]{3,2,1,0:T(8,128)(2,1)} %copy-done.1, bf16[4,128,256]{2,1,0:T(8,128)(2,1)} %shard_map.102.refs_1_, bf16[4,128,256]{2,1,0:T(8,128)(2,1)} %copy-done.8, bf16[4,128,256]{2,1,0:T(8,128)(2,1)} %copy-done.10, ...), custom_call_target="tpu_custom_call" | custom-call | flops 1024 | bytes 1024 | tf_op jit(solution)/shard_map/pallas_call | solution.py:354
  174.3 2.0 %all-gather.7.cloned.1.call-done = bf16[32,128,256]{2,1,0:T(8,128)(2,1)} async-done(((bf16[4,128,256]{2,1,0:T(8,128)(2,1)}), bf16[32,128,256]{2,1,0:T(8,128)(2,1)}) %all-gather.7.cloned.1.call-update) | async-done | bytes 2097168 | tf_op jit(solution)/shard_map/all_gather | solution.py:406
  176.3 3.7 %shard_map.105 = f32[8,256,256]{2,1,0:T(8,128)} custom-call(s32[8]{0:T(128)} %xor.40.order_ref, s32[1]{0:T(128)} %bitcast.5.me_ref, bf16[8,128,256]{2,1,0:T(8,128)(2,1)} %get-tuple-element.26.refs_4_.refs_0_, bf16[8,128,256]{2,1,0:T(8,128)(2,1)} %copy-done.4, bf16[8,128,256]{2,1,0:T(8,128)(2,1)} %copy-done.5, bf16[8,128,256]{2,1,0:T(8,128)(2,1)} %copy-done.6, ...), custom_call_target="tpu_custom_call" | custom-call | flops 1024 | bytes 1024 | tf_op jit(solution)/shard_map/pallas_call | solution.py:354
  (134 shorter events, 29.8 us)
Async XLA Ops:
  7.2 31.5 %all-gather.5.cloned.1.call-start = ((), (), s32[]{:S(2)}) async-start(), calls=%async_computation.5 | async-start | bytes 1253376 | tf_op jit(solution)/shard_map/all_gather | solution.py:380
  9.0 4.6 %collective-permute-start = (bf16[256,256]{1,0:T(8,128)(2,1)}, bf16[256,256]{1,0:T(8,128)(2,1)S(1)}, u32[]{:S(2)}, u32[]{:S(2)}) collective-permute-start(bf16[256,256]{1,0:T(8,128)(2,1)} %refs_8_.1), channel_id=1, source_target_pairs={{0,8},{8,0},{16,24},{24,16},{1,9},{9,1},{17,25},{25,17},{2,10},{10... | collective-permute-start | bytes 393224 | tf_op jit(solution)/shard_map/ppermute | solution.py:41
  16.6 36.3 %all-to-all-start = ((bf16[8,256,256]{2,1,0:T(8,128)(2,1)}), bf16[8,256,256]{2,1,0:T(8,128)(2,1)S(1)}, u32[]{:S(2)}, u32[]{:S(2)}) async-start(bf16[8,256,256]{2,1,0:T(8,128)(2,1)} %shard_map.97), calls=%async_computation | async-start | bytes 2097152 | tf_op jit(solution)/shard_map/all_to_all | solution.py:384
  23.1 97.7 %reduce-scatter.2.cloned.1.call-start = ((), (), s32[]{:S(2)}) async-start(), calls=%async_computation.4 | async-start | bytes 2359296 | tf_op jit(solution)/shard_map/reduce_scatter | solution.py:393
  23.1 6.5 %collective-permute-start.1 = (bf16[256,256]{1,0:T(8,128)(2,1)S(1)}, bf16[256,256]{1,0:T(8,128)(2,1)S(1)}, u32[]{:S(2)}, u32[]{:S(2)}) collective-permute-start(bf16[256,256]{1,0:T(8,128)(2,1)S(1)} %copy-done.14), channel_id=1, source_target_pairs={{0,16},{8,24},{16,0},{24,8},{1,17},{9,25},{17,1},{25,9},{2,18},{10... | collective-permute-start | bytes 393224 | tf_op jit(solution)/shard_map/ppermute | solution.py:41
  24.4 5.4 %collective-permute-start.2 = (bf16[256,256]{1,0:T(8,128)(2,1)S(1)}, bf16[256,256]{1,0:T(8,128)(2,1)S(1)}, u32[]{:S(2)}, u32[]{:S(2)}) collective-permute-start(bf16[256,256]{1,0:T(8,128)(2,1)S(1)} %copy-done.14), channel_id=1, source_target_pairs={{0,24},{8,16},{16,8},{24,0},{1,25},{9,17},{17,9},{25,1},{2,26},{10... | collective-permute-start | bytes 393224 | tf_op jit(solution)/shard_map/ppermute | solution.py:41
  44.1 5.9 %collective-permute-start.3 = (f32[3,2048]{1,0:T(4,128)}, f32[3,2048]{1,0:T(4,128)S(1)}, u32[]{:S(2)}, u32[]{:S(2)}) collective-permute-start(f32[3,2048]{1,0:T(4,128)} %shard_map.96.refs_0_), channel_id=1, source_target_pairs={{0,1},{1,0},{2,3},{3,2},{4,5},{5,4},{6,7},{7,6},{8,9},{9,8},{10,11... | collective-permute-start | bytes 73736 | tf_op jit(solution)/shard_map/ppermute | solution.py:41
  44.4 7.1 %collective-permute-start.4 = (f32[3,2048]{1,0:T(4,128)}, f32[3,2048]{1,0:T(4,128)S(1)}, u32[]{:S(2)}, u32[]{:S(2)}) collective-permute-start(f32[3,2048]{1,0:T(4,128)} %shard_map.96.refs_0_), channel_id=1, source_target_pairs={{0,2},{1,3},{2,0},{3,1},{4,6},{5,7},{6,4},{7,5},{8,10},{9,11},{10,... | collective-permute-start | bytes 73736 | tf_op jit(solution)/shard_map/ppermute | solution.py:41
  45.3 7.5 %collective-permute-start.5 = (f32[3,2048]{1,0:T(4,128)}, f32[3,2048]{1,0:T(4,128)S(1)}, u32[]{:S(2)}, u32[]{:S(2)}) collective-permute-start(f32[3,2048]{1,0:T(4,128)} %shard_map.96.refs_0_), channel_id=1, source_target_pairs={{0,3},{1,2},{2,1},{3,0},{4,7},{5,6},{6,5},{7,4},{8,11},{9,10},{10,... | collective-permute-start | bytes 73736 | tf_op jit(solution)/shard_map/ppermute | solution.py:41
  46.2 7.3 %collective-permute-start.6 = (f32[3,2048]{1,0:T(4,128)}, f32[3,2048]{1,0:T(4,128)S(1)}, u32[]{:S(2)}, u32[]{:S(2)}) collective-permute-start(f32[3,2048]{1,0:T(4,128)} %shard_map.96.refs_0_), channel_id=1, source_target_pairs={{0,4},{1,5},{2,6},{3,7},{4,0},{5,1},{6,2},{7,3},{8,12},{9,13},{10,... | collective-permute-start | bytes 73736 | tf_op jit(solution)/shard_map/ppermute | solution.py:41
  49.9 4.8 %collective-permute-start.7 = (f32[3,2048]{1,0:T(4,128)}, f32[3,2048]{1,0:T(4,128)S(1)}, u32[]{:S(2)}, u32[]{:S(2)}) collective-permute-start(f32[3,2048]{1,0:T(4,128)} %shard_map.96.refs_0_), channel_id=1, source_target_pairs={{0,5},{1,4},{2,7},{3,6},{4,1},{5,0},{6,3},{7,2},{8,13},{9,12},{10,... | collective-permute-start | bytes 73736 | tf_op jit(solution)/shard_map/ppermute | solution.py:41
  50.0 7.6 %collective-permute-start.8 = (f32[3,2048]{1,0:T(4,128)}, f32[3,2048]{1,0:T(4,128)S(1)}, u32[]{:S(2)}, u32[]{:S(2)}) collective-permute-start(f32[3,2048]{1,0:T(4,128)} %shard_map.96.refs_0_), channel_id=1, source_target_pairs={{0,6},{1,7},{2,4},{3,5},{4,2},{5,3},{6,0},{7,1},{8,14},{9,15},{10,... | collective-permute-start | bytes 73736 | tf_op jit(solution)/shard_map/ppermute | solution.py:41
  51.4 7.5 %collective-permute-start.9 = (f32[3,2048]{1,0:T(4,128)}, f32[3,2048]{1,0:T(4,128)S(1)}, u32[]{:S(2)}, u32[]{:S(2)}) collective-permute-start(f32[3,2048]{1,0:T(4,128)} %shard_map.96.refs_0_), channel_id=1, source_target_pairs={{0,7},{1,6},{2,5},{3,4},{4,3},{5,2},{6,1},{7,0},{8,15},{9,14},{10,... | collective-permute-start | bytes 73736 | tf_op jit(solution)/shard_map/ppermute | solution.py:41
  67.8 59.8 %all-to-all-start.1 = ((bf16[8,256,256]{2,1,0:T(8,128)(2,1)}), bf16[8,256,256]{2,1,0:T(8,128)(2,1)S(1)}, u32[]{:S(2)}, u32[]{:S(2)}) async-start(bf16[8,256,256]{2,1,0:T(8,128)(2,1)} %shard_map.95.refs_4_), calls=%async_computation.2 | async-start | bytes 2097152 | tf_op jit(solution)/shard_map/all_to_all | solution.py:384
  72.2 104.0 %all-gather.7.cloned.1.call-start = ((), (), s32[]{:S(2)}) async-start(), calls=%async_computation.6 | async-start | bytes 2359296 | tf_op jit(solution)/shard_map/all_gather | solution.py:406
  72.3 8.1 %collective-permute-start.16 = (f32[256,256]{1,0:T(8,128)S(1)}, f32[256,256]{1,0:T(8,128)S(1)}, u32[]{:S(2)}, u32[]{:S(2)}) collective-permute-start(f32[256,256]{1,0:T(8,128)S(1)} %copy-done.36), channel_id=1, source_target_pairs={{0,8},{8,0},{16,24},{24,16},{1,9},{9,1},{17,25},{25,17},{2,10},{10... | collective-permute-start | bytes 786440 | tf_op jit(solution)/shard_map/ppermute | solution.py:41
  76.5 43.1 %collective-permute-start.10 = (bf16[8,128,256]{2,1,0:T(8,128)(2,1)}, bf16[8,128,256]{2,1,0:T(8,128)(2,1)S(1)}, u32[]{:S(2)}, u32[]{:S(2)}) collective-permute-start(bf16[8,128,256]{2,1,0:T(8,128)(2,1)} %get-tuple-element.27), channel_id=1, source_target_pairs={{0,8},{8,0},{16,24},{24,16},{1,9},{9,1},{17,25},{25,17},{2,10},{10... | collective-permute-start | bytes 1572872 | tf_op jit(solution)/shard_map/ppermute | solution.py:41
  77.8 7.0 %collective-permute-start.17 = (f32[256,256]{1,0:T(8,128)S(1)}, f32[256,256]{1,0:T(8,128)S(1)}, u32[]{:S(2)}, u32[]{:S(2)}) collective-permute-start(f32[256,256]{1,0:T(8,128)S(1)} %copy-done.35), channel_id=1, source_target_pairs={{0,16},{8,24},{16,0},{24,8},{1,17},{9,25},{17,1},{25,9},{2,18},{10... | collective-permute-start | bytes 786440 | tf_op jit(solution)/shard_map/ppermute | solution.py:41
  79.0 18.7 %collective-permute-start.18 = (f32[256,256]{1,0:T(8,128)S(1)}, f32[256,256]{1,0:T(8,128)S(1)}, u32[]{:S(2)}, u32[]{:S(2)}) collective-permute-start(f32[256,256]{1,0:T(8,128)S(1)} %copy-done.34), channel_id=1, source_target_pairs={{0,24},{8,16},{16,8},{24,0},{1,25},{9,17},{17,9},{25,1},{2,26},{10... | collective-permute-start | bytes 786440 | tf_op jit(solution)/shard_map/ppermute | solution.py:41
  79.2 40.6 %collective-permute-start.11 = (bf16[8,128,256]{2,1,0:T(8,128)(2,1)}, bf16[8,128,256]{2,1,0:T(8,128)(2,1)S(1)}, u32[]{:S(2)}, u32[]{:S(2)}) collective-permute-start(bf16[8,128,256]{2,1,0:T(8,128)(2,1)} %get-tuple-element.28), channel_id=1, source_target_pairs={{0,16},{8,24},{16,0},{24,8},{1,17},{9,25},{17,1},{25,9},{2,18},{10... | collective-permute-start | bytes 1572872 | tf_op jit(solution)/shard_map/ppermute | solution.py:41
  80.4 39.4 %collective-permute-start.12 = (bf16[8,128,256]{2,1,0:T(8,128)(2,1)}, bf16[8,128,256]{2,1,0:T(8,128)(2,1)S(1)}, u32[]{:S(2)}, u32[]{:S(2)}) collective-permute-start(bf16[8,128,256]{2,1,0:T(8,128)(2,1)} %get-tuple-element.29), channel_id=1, source_target_pairs={{0,24},{8,16},{16,8},{24,0},{1,25},{9,17},{17,9},{25,1},{2,26},{10... | collective-permute-start | bytes 1572872 | tf_op jit(solution)/shard_map/ppermute | solution.py:41
  100.5 8.9 %collective-permute-start.19 = (bf16[128,256]{1,0:T(8,128)(2,1)}, bf16[128,256]{1,0:T(8,128)(2,1)S(1)}, u32[]{:S(2)}, u32[]{:S(2)}) collective-permute-start(bf16[128,256]{1,0:T(8,128)(2,1)} %get-tuple-element.40), channel_id=1, source_target_pairs={{0,8},{8,0},{16,24},{24,16},{1,9},{9,1},{17,25},{25,17},{2,10},{10... | collective-permute-start | bytes 196616 | tf_op jit(solution)/shard_map/ppermute | solution.py:41
  100.6 14.3 %collective-permute-start.20 = (bf16[128,256]{1,0:T(8,128)(2,1)}, bf16[128,256]{1,0:T(8,128)(2,1)S(1)}, u32[]{:S(2)}, u32[]{:S(2)}) collective-permute-start(bf16[128,256]{1,0:T(8,128)(2,1)} %get-tuple-element.41), channel_id=1, source_target_pairs={{0,16},{8,24},{16,0},{24,8},{1,17},{9,25},{17,1},{25,9},{2,18},{10... | collective-permute-start | bytes 196616 | tf_op jit(solution)/shard_map/ppermute | solution.py:41
  109.4 5.5 %collective-permute-start.21 = (bf16[128,256]{1,0:T(8,128)(2,1)}, bf16[128,256]{1,0:T(8,128)(2,1)S(1)}, u32[]{:S(2)}, u32[]{:S(2)}) collective-permute-start(bf16[128,256]{1,0:T(8,128)(2,1)} %get-tuple-element.42), channel_id=1, source_target_pairs={{0,24},{8,16},{16,8},{24,0},{1,25},{9,17},{17,9},{25,1},{2,26},{10... | collective-permute-start | bytes 196616 | tf_op jit(solution)/shard_map/ppermute | solution.py:41
  117.2 9.4 %collective-permute-start.22 = (bf16[4,128,256]{2,1,0:T(8,128)(2,1)}, bf16[4,128,256]{2,1,0:T(8,128)(2,1)S(1)}, u32[]{:S(2)}, u32[]{:S(2)}) collective-permute-start(bf16[4,128,256]{2,1,0:T(8,128)(2,1)} %shard_map.102.refs_1_), channel_id=1, source_target_pairs={{0,2},{1,3},{2,0},{3,1},{4,6},{5,7},{6,4},{7,5},{8,10},{9,11},{10,... | collective-permute-start | bytes 786440 | tf_op jit(solution)/shard_map/ppermute | solution.py:41
  118.2 14.5 %collective-permute-start.23 = (bf16[4,128,256]{2,1,0:T(8,128)(2,1)}, bf16[4,128,256]{2,1,0:T(8,128)(2,1)S(1)}, u32[]{:S(2)}, u32[]{:S(2)}) collective-permute-start(bf16[4,128,256]{2,1,0:T(8,128)(2,1)} %shard_map.102.refs_1_), channel_id=1, source_target_pairs={{0,4},{1,5},{2,6},{3,7},{4,0},{5,1},{6,2},{7,3},{8,12},{9,13},{10,... | collective-permute-start | bytes 786440 | tf_op jit(solution)/shard_map/ppermute | solution.py:41
  119.6 21.1 %collective-permute-start.24 = (bf16[4,128,256]{2,1,0:T(8,128)(2,1)}, bf16[4,128,256]{2,1,0:T(8,128)(2,1)S(1)}, u32[]{:S(2)}, u32[]{:S(2)}) collective-permute-start(bf16[4,128,256]{2,1,0:T(8,128)(2,1)} %shard_map.102.refs_1_), channel_id=1, source_target_pairs={{0,6},{1,7},{2,4},{3,5},{4,2},{5,3},{6,0},{7,1},{8,14},{9,15},{10,... | collective-permute-start | bytes 786440 | tf_op jit(solution)/shard_map/ppermute | solution.py:41
  122.7 18.0 %collective-permute-start.13 = (bf16[128,256]{1,0:T(8,128)(2,1)}, bf16[128,256]{1,0:T(8,128)(2,1)S(1)}, u32[]{:S(2)}, u32[]{:S(2)}) collective-permute-start(bf16[128,256]{1,0:T(8,128)(2,1)} %get-tuple-element.33), channel_id=1, source_target_pairs={{0,8},{8,0},{16,24},{24,16},{1,9},{9,1},{17,25},{25,17},{2,10},{10... | collective-permute-start | bytes 196616 | tf_op jit(solution)/shard_map/ppermute | solution.py:41
  122.9 17.8 %collective-permute-start.14 = (bf16[128,256]{1,0:T(8,128)(2,1)}, bf16[128,256]{1,0:T(8,128)(2,1)S(1)}, u32[]{:S(2)}, u32[]{:S(2)}) collective-permute-start(bf16[128,256]{1,0:T(8,128)(2,1)} %get-tuple-element.34), channel_id=1, source_target_pairs={{0,16},{8,24},{16,0},{24,8},{1,17},{9,25},{17,1},{25,9},{2,18},{10... | collective-permute-start | bytes 196616 | tf_op jit(solution)/shard_map/ppermute | solution.py:41
  126.5 14.2 %collective-permute-start.15 = (bf16[128,256]{1,0:T(8,128)(2,1)}, bf16[128,256]{1,0:T(8,128)(2,1)S(1)}, u32[]{:S(2)}, u32[]{:S(2)}) collective-permute-start(bf16[128,256]{1,0:T(8,128)(2,1)} %get-tuple-element.35), channel_id=1, source_target_pairs={{0,24},{8,16},{16,8},{24,0},{1,25},{9,17},{17,9},{25,1},{2,26},{10... | collective-permute-start | bytes 196616 | tf_op jit(solution)/shard_map/ppermute | solution.py:41
  143.8 25.6 %all-to-all-start.2 = ((bf16[4,8,128,256]{3,2,1,0:T(8,128)(2,1)}), bf16[4,8,128,256]{3,2,1,0:T(8,128)(2,1)S(1)}, u32[]{:S(2)}, u32[]{:S(2)}) async-start(bf16[4,8,128,256]{3,2,1,0:T(8,128)(2,1)} %shard_map.103.refs_7_), calls=%async_computation.3 | async-start | bytes 4194304 | tf_op jit(solution)/shard_map/all_to_all | solution.py:384
  148.0 6.1 %collective-permute-start.25 = (bf16[4,128,256]{2,1,0:T(8,128)(2,1)S(1)}, bf16[4,128,256]{2,1,0:T(8,128)(2,1)S(1)}, u32[]{:S(2)}, u32[]{:S(2)}) collective-permute-start(bf16[4,128,256]{2,1,0:T(8,128)(2,1)S(1)} %copy-done.7), channel_id=1, source_target_pairs={{0,1},{1,0},{2,3},{3,2},{4,5},{5,4},{6,7},{7,6},{8,9},{9,8},{10,11... | collective-permute-start | bytes 786440 | tf_op jit(solution)/shard_map/ppermute | solution.py:41
  (40 other events, 217.4 us)
Sparse Core Ops, SparseCore 0:
  9.6 29.0 all-gather.4
  67.9 52.8 reduce-scatter.1
  143.8 32.3 all-gather.6

commit v17 on v16

--- a/solution.py
+++ b/solution.py
@@ -400,7 +400,7 @@
     item_line = exchange([item_sent] * lines, "item", CORES)
     user_routed = route(me, targets, [user_grad], 0, groups, user_rows[1:])
     item_slots = slot_hidden(me, users, item_cols, groups, 1, False, user_routed[0])
-    user_sent = stack(exchange(user_routed, "user"), item_line[1:] + [item_slots[0]])
+    user_sent = stack(exchange(user_routed, "user"), item_line[1:2] + [item_slots[0]])
     item_rows = [scatter(item_slots[0], "user")]
     item_cross = item_line + [swap(piece, "item", 1) for piece in item_line]
     user_all = lax.all_gather(user_sent, "item", axis=0)

time: 189 us -> 197 us (1.042)
  waiting for transfers between devices: 79.8 us -> 87.3 us
    ppermute x29, waiting for transfers between devices: 52.2 us -> 73.5 us  [swap(): return lax.ppermute(piece, axis, [(j, j ^ bits) for j in range(size)])]
    all_to_all x3, waiting for transfers between devices: 15.7 us -> 0.5 us  [scatter(): return lax.all_to_all(pieces, axis, split_axis=0, concat_axis=0, tiled=True)]
    reduce_scatter x1, waiting for transfers between devices: 0.97 us -> 4.35 us  [shards(): lax.psum_scatter(user_part, 'item', scatter_dimension=0, tiled=True)]
    unnamed x74 -> x70, local copies, waits for them, and re-layouts: 6.26 us -> 6.86 us
  transfers between devices with their start and end apart: 35 -> 35, of which waited for: 18 -> 15; matrix products, arithmetic and copies ran while one was open for 1% -> 1% of each run, Pallas kernels for 15% -> 14%
where the time goes in v17:
time: 197 us; the launch traced here: 196 us
  waiting for transfers between devices  87.3 us (44%)
  starting transfers between devices  43 us (22%)
  Pallas kernels  42.6 us (22%)
  between operations  14 us (7%)
  local copies, waits for them, and re-layouts  8.75 us (4%)
    ppermute x29, waiting for transfers between devices, swap(): return lax.ppermute(piece, axis, [(j, j ^ bits) for j in range(size)])  73.5 us
    ppermute x29, starting transfers between devices, swap(): return lax.ppermute(piece, axis, [(j, j ^ bits) for j in range(size)])  28.2 us
    all_to_all x3, starting transfers between devices, scatter(): return lax.all_to_all(pieces, axis, split_axis=0, concat_axis=0, tiled=True)  14.7 us
    all_gather x1, waiting for transfers between devices, shards(): users = lax.all_gather(packed, 'item', axis=0)  8.92 us
    pallas_call x1, Pallas kernels, grads(): pl.pallas_call(functools.partial(grad_kernel, rows=rows, chunk=64, count=...  8.18 us
    pallas_call x2, Pallas kernels, slot_hidden(): pl.pallas_call(functools.partial(hidden_kernel, tower=tower), grid=(block...  8.1 us
    pallas_call x2, Pallas kernels, outer(): pl.pallas_call(functools.partial(outer_kernel, count=len(hidden)), grid=(...  7.33 us
    unnamed x70, local copies, waits for them, and re-layouts  6.86 us
  transfers between devices with their start and end apart: 35, of which 15 were waited for; matrix products, arithmetic and copies ran while one was open for 1% of the time, Pallas kernels for 14%

profile of v17, /device:TPU:11, one launch (start us, length us, event | category | flops | bytes accessed | tf_op | source)
XLA Modules:
  0.0 196.3 jit_solution(6481298363102230345)
XLA Ops:
  7.2 1.8 shard_map.94
  9.3 4.3 %collective-permute-done._.refs_1_.refs_9_ = bf16[256,256]{1,0:T(8,128)(2,1)S(1)} collective-permute-done((bf16[256,256]{1,0:T(8,128)(2,1)}, bf16[256,256]{1,0:T(8,128)(2,1)S(1)}, u32[]{:S(2)}, u32[]{:S(2)}) %collective-permute-start) | collective-permute-done | bytes 131104 | tf_op jit(solution)/shard_map/ppermute | solution.py:41
  14.3 2.3 %shard_map.97 = bf16[8,256,256]{2,1,0:T(8,128)(2,1)} custom-call(bf16[256,2048]{1,0:T(8,128)(2,1)} %in_ref.3, bf16[256,256]{1,0:T(8,128)(2,1)} %copy-done.3), custom_call_target="tpu_custom_call" | custom-call | flops 1024 | bytes 1024 | tf_op jit(solution)/shard_map/pallas_call | solution.py:221
  16.5 6.5 %all-to-all-start = ((bf16[8,256,256]{2,1,0:T(8,128)(2,1)}), bf16[8,256,256]{2,1,0:T(8,128)(2,1)S(1)}, u32[]{:S(2)}, u32[]{:S(2)}) async-start(bf16[8,256,256]{2,1,0:T(8,128)(2,1)} %shard_map.97), calls=%async_computation | async-start | bytes 2097152 | tf_op jit(solution)/shard_map/all_to_all | solution.py:384
  25.1 2.3 %shard_map.95.refs_4_ = bf16[8,256,256]{2,1,0:T(8,128)(2,1)} custom-call(bf16[256,2048]{1,0:T(8,128)(2,1)} %in_ref.2, bf16[256,256]{1,0:T(8,128)(2,1)} %copy-done.3), custom_call_target="tpu_custom_call" | custom-call | flops 1024 | bytes 1024 | tf_op jit(solution)/shard_map/pallas_call | solution.py:221
  27.4 2.2 %collective-permute-done.1.refs_2_.refs_10_ = bf16[256,256]{1,0:T(8,128)(2,1)S(1)} collective-permute-done((bf16[256,256]{1,0:T(8,128)(2,1)S(1)}, bf16[256,256]{1,0:T(8,128)(2,1)S(1)}, u32[]{:S(2)}, u32[]{:S(2)}) %collective-permute-start.1) | collective-permute-done | bytes 131104 | tf_op jit(solution)/shard_map/ppermute | solution.py:41
  29.8 8.9 %all-gather.5.cloned.1.call-done = bf16[2176,256]{1,0:T(8,128)(2,1)} async-done(((bf16[272,256]{1,0:T(8,128)(2,1)}), bf16[2176,256]{1,0:T(8,128)(2,1)}) %all-gather.5.cloned.1.call-update) | async-done | bytes 1114128 | tf_op jit(solution)/shard_map/all_gather | solution.py:380
  38.7 5.4 %shard_map.96.refs_0_ = f32[3,2048]{1,0:T(4,128)} custom-call(s32[4]{0:T(128)} %add_multiply_fusion.first_ref, bf16[8,272,256]{2,1,0:T(8,128)(2,1)} %bitcast.7, bf16[256,256]{1,0:T(8,128)(2,1)} %refs_8_.1, bf16[256,256]{1,0:T(8,128)(2,1)} %copy-done.3, bf16[256,256]{1,0:T(8,128)(2,1)} %copy-done.11, bf16[256,256]{1,0:T(8,128)(2,1)} %copy-done.12, ...), custom_call_target="tpu_custom_call" | custom-call | flops 1024 | bytes 1024 | tf_op jit(solution)/shard_map/pallas_call | solution.py:119
  46.2 3.7 %collective-permute-start.6 = (f32[3,2048]{1,0:T(4,128)}, f32[3,2048]{1,0:T(4,128)S(1)}, u32[]{:S(2)}, u32[]{:S(2)}) collective-permute-start(f32[3,2048]{1,0:T(4,128)} %shard_map.96.refs_0_), channel_id=1, source_target_pairs={{0,4},{1,5},{2,6},{3,7},{4,0},{5,1},{6,2},{7,3},{8,12},{9,13},{10,... | collective-permute-start | bytes 73736 | tf_op jit(solution)/shard_map/ppermute | solution.py:41
  49.9 1.5 collective-permute-start.8
  54.8 2.8 %collective-permute-done.8.refs_6_ = f32[3,2048]{1,0:T(4,128)S(1)} collective-permute-done((f32[3,2048]{1,0:T(4,128)}, f32[3,2048]{1,0:T(4,128)S(1)}, u32[]{:S(2)}, u32[]{:S(2)}) %collective-permute-start.8) | collective-permute-done | bytes 24608 | tf_op jit(solution)/shard_map/ppermute | solution.py:41
  59.6 8.2 %shard_map.98 = (f32[1,2048]{1,0:T(1,128)}, f32[2048,256]{1,0:T(8,128)}, f32[256,256]{1,0:T(8,128)}, f32[256,256]{1,0:T(8,128)}, f32[256,256]{1,0:T(8,128)}, /*index=5*/f32[256,256]{1,0:T(8,128)}) custom-call(s32[4]{0:T(128)} %add_multiply_fusion.first_ref, bf16[8,272,256]{2,1,0:T(8,128)(2,1)} %bitcast.8, f32[3,2048]{1,0:T(4,128)} %shard_map.96.refs_0_, ...), custom_call_target="tpu_custom_call" | custom-call | flops 1024 | bytes 1024 | tf_op jit(solution)/shard_map/pallas_call | solution.py:182
  67.8 4.4 %all-to-all-start.1 = ((bf16[8,256,256]{2,1,0:T(8,128)(2,1)}), bf16[8,256,256]{2,1,0:T(8,128)(2,1)S(1)}, u32[]{:S(2)}, u32[]{:S(2)}) async-start(bf16[8,256,256]{2,1,0:T(8,128)(2,1)} %shard_map.95.refs_4_), calls=%async_computation.2 | async-start | bytes 2097152 | tf_op jit(solution)/shard_map/all_to_all | solution.py:384
  75.0 4.0 %shard_map.99 = (bf16[8,128,256]{2,1,0:T(8,128)(2,1)}, bf16[8,128,256]{2,1,0:T(8,128)(2,1)}, bf16[8,128,256]{2,1,0:T(8,128)(2,1)}, bf16[8,128,256]{2,1,0:T(8,128)(2,1)}) custom-call(s32[1]{0:T(128)} %bitcast.5.me_ref, bf16[8,272,256]{2,1,0:T(8,128)(2,1)} %bitcast.9, bf16[8,256,256]{2,1,0:T(8,128)(2,1)} %copy-done, f32[256,256]{1,0:T(8,128)} %get-tuple-element.25._.refs_0_), custom_call_target="tpu_custom_call" | custom-call | flops 1024 | bytes 1024 | tf_op jit(solution)/shard_map/pallas_call | solution.py:263
  81.6 4.8 %collective-permute-done.18.refs_3_ = f32[256,256]{1,0:T(8,128)S(1)} collective-permute-done((f32[256,256]{1,0:T(8,128)S(1)}, f32[256,256]{1,0:T(8,128)S(1)}, u32[]{:S(2)}, u32[]{:S(2)}) %collective-permute-start.18) | collective-permute-done | bytes 262176 | tf_op jit(solution)/shard_map/ppermute | solution.py:41
  87.1 2.1 %shard_map.101 = (bf16[128,256]{1,0:T(8,128)(2,1)}, bf16[128,256]{1,0:T(8,128)(2,1)}, bf16[128,256]{1,0:T(8,128)(2,1)}, bf16[128,256]{1,0:T(8,128)(2,1)}) custom-call(s32[1]{0:T(128)} %bitcast.5.me_ref, s32[2,256]{1,0:T(2,128)} %get-tuple-element.30.target_ref, f32[256,256]{1,0:T(8,128)} %get-tuple-element.25._.refs_0_, f32[256,256]{1,0:T(8,128)} %copy-done.13, ...), custom_call_target="tpu_custom_call" | custom-call | flops 1024 | bytes 1024 | tf_op jit(solution)/shard_map/pallas_call | solution.py:295
  89.8 19.8 %collective-permute-done.19.refs_1_ = bf16[128,256]{1,0:T(8,128)(2,1)S(1)} collective-permute-done((bf16[128,256]{1,0:T(8,128)(2,1)}, bf16[128,256]{1,0:T(8,128)(2,1)S(1)}, u32[]{:S(2)}, u32[]{:S(2)}) %collective-permute-start.19) | collective-permute-done | bytes 65568 | tf_op jit(solution)/shard_map/ppermute | solution.py:41
  110.7 3.0 %collective-permute-done.21.refs_3_ = bf16[128,256]{1,0:T(8,128)(2,1)S(1)} collective-permute-done((bf16[128,256]{1,0:T(8,128)(2,1)}, bf16[128,256]{1,0:T(8,128)(2,1)S(1)}, u32[]{:S(2)}, u32[]{:S(2)}) %collective-permute-start.21) | collective-permute-done | bytes 65568 | tf_op jit(solution)/shard_map/ppermute | solution.py:41
  114.4 1.7 shard_map.102.refs_1_
  116.4 4.3 %reduce-scatter.2.cloned.1.call-done.refs_0_ = f32[256,256]{1,0:T(8,128)} async-done(((f32[2048,256]{1,0:T(8,128)}), f32[256,256]{1,0:T(8,128)}) %reduce-scatter.2.cloned.1.call-update) | async-done | bytes 262160 | tf_op jit(solution)/shard_map/reduce_scatter | solution.py:393
  120.7 1.9 shard_map.100
  122.7 1.4 collective-permute-start.14
  126.2 4.1 %shard_map.103.refs_5_ = bf16[4,8,128,256]{3,2,1,0:T(8,128)(2,1)} custom-call(s32[1]{0:T(128)} %bitcast.5.me_ref, bf16[8,272,256]{2,1,0:T(8,128)(2,1)} %bitcast.10, bf16[8,256,256]{2,1,0:T(8,128)(2,1)} %copy-done.2, bf16[128,256]{1,0:T(8,128)(2,1)} %get-tuple-element.32._.refs_0_), custom_call_target="tpu_custom_call" | custom-call | flops 1024 | bytes 1024 | tf_op jit(solution)/shard_map/pallas_call | solution.py:263
  131.7 1.7 shard_map.104
  133.4 3.8 %all-to-all-start.2 = ((bf16[4,8,128,256]{3,2,1,0:T(8,128)(2,1)}), bf16[4,8,128,256]{3,2,1,0:T(8,128)(2,1)S(1)}, u32[]{:S(2)}, u32[]{:S(2)}) async-start(bf16[4,8,128,256]{3,2,1,0:T(8,128)(2,1)} %shard_map.103.refs_5_), calls=%async_computation.3 | async-start | bytes 4194304 | tf_op jit(solution)/shard_map/all_to_all | solution.py:384
  137.5 3.3 %collective-permute-start.25 = (bf16[4,128,256]{2,1,0:T(8,128)(2,1)S(1)}, bf16[4,128,256]{2,1,0:T(8,128)(2,1)S(1)}, u32[]{:S(2)}, u32[]{:S(2)}) collective-permute-start(bf16[4,128,256]{2,1,0:T(8,128)(2,1)S(1)} %copy-done.7), channel_id=1, source_target_pairs={{0,1},{1,0},{2,3},{3,2},{4,5},{5,4},{6,7},{7,6},{8,9},{9,8},{10,11... | collective-permute-start | bytes 786440 | tf_op jit(solution)/shard_map/ppermute | solution.py:41
  140.8 22.9 %collective-permute-done.23.refs_3_ = bf16[4,128,256]{2,1,0:T(8,128)(2,1)S(1)} collective-permute-done((bf16[4,128,256]{2,1,0:T(8,128)(2,1)S(1)}, bf16[4,128,256]{2,1,0:T(8,128)(2,1)S(1)}, u32[]{:S(2)}, u32[]{:S(2)}) %collective-permute-start.23) | collective-permute-done | bytes 262176 | tf_op jit(solution)/shard_map/ppermute | solution.py:41
  163.7 2.9 %collective-permute-start.27 = (bf16[4,128,256]{2,1,0:T(8,128)(2,1)S(1)}, bf16[4,128,256]{2,1,0:T(8,128)(2,1)}, u32[]{:S(2)}, u32[]{:S(2)}) collective-permute-start(bf16[4,128,256]{2,1,0:T(8,128)(2,1)S(1)} %collective-permute-done.23.refs_3_), channel_id=1, source_target_pairs={{0,1},{1,0},{2,3},{3,2},{4,5},{5,4},{6,7},{7,6},{8,9},{9,8},{10,11... | collective-permute-start | bytes 786440 | tf_op jit(solution)/shard_map/ppermute | solution.py:41
  166.6 10.2 %collective-permute-done.24.refs_4_ = bf16[4,128,256]{2,1,0:T(8,128)(2,1)S(1)} collective-permute-done((bf16[4,128,256]{2,1,0:T(8,128)(2,1)S(1)}, bf16[4,128,256]{2,1,0:T(8,128)(2,1)S(1)}, u32[]{:S(2)}, u32[]{:S(2)}) %collective-permute-start.24) | collective-permute-done | bytes 262176 | tf_op jit(solution)/shard_map/ppermute | solution.py:41
  176.8 1.6 collective-permute-start.28
  182.4 3.6 %shard_map.106 = f32[8,256,256]{2,1,0:T(8,128)} custom-call(s32[8]{0:T(128)} %xor.40.order_ref, s32[1]{0:T(128)} %bitcast.5.me_ref, bf16[4,8,128,256]{3,2,1,0:T(8,128)(2,1)} %copy-done.1, bf16[4,128,256]{2,1,0:T(8,128)(2,1)} %shard_map.102.refs_1_, bf16[4,128,256]{2,1,0:T(8,128)(2,1)} %copy-done.8, bf16[4,128,256]{2,1,0:T(8,128)(2,1)} %copy-done.16, ...), custom_call_target="tpu_custom_call" | custom-call | flops 1024 | bytes 1024 | tf_op jit(solution)/shard_map/pallas_call | solution.py:354
  186.0 3.7 %shard_map.105 = f32[8,256,256]{2,1,0:T(8,128)} custom-call(s32[8]{0:T(128)} %xor.40.order_ref, s32[1]{0:T(128)} %bitcast.5.me_ref, bf16[8,128,256]{2,1,0:T(8,128)(2,1)} %get-tuple-element.26.refs_4_.refs_0_, bf16[8,128,256]{2,1,0:T(8,128)(2,1)} %copy-done.4, bf16[8,128,256]{2,1,0:T(8,128)(2,1)} %copy-done.5, bf16[8,128,256]{2,1,0:T(8,128)(2,1)} %copy-done.6, ...), custom_call_target="tpu_custom_call" | custom-call | flops 1024 | bytes 1024 | tf_op jit(solution)/shard_map/pallas_call | solution.py:354
  (130 shorter events, 27.3 us)
Async XLA Ops:
  7.2 31.5 %all-gather.5.cloned.1.call-start = ((), (), s32[]{:S(2)}) async-start(), calls=%async_computation.5 | async-start | bytes 1253376 | tf_op jit(solution)/shard_map/all_gather | solution.py:380
  16.5 36.3 %all-to-all-start = ((bf16[8,256,256]{2,1,0:T(8,128)(2,1)}), bf16[8,256,256]{2,1,0:T(8,128)(2,1)S(1)}, u32[]{:S(2)}, u32[]{:S(2)}) async-start(bf16[8,256,256]{2,1,0:T(8,128)(2,1)} %shard_map.97), calls=%async_computation | async-start | bytes 2097152 | tf_op jit(solution)/shard_map/all_to_all | solution.py:384
  23.1 97.7 %reduce-scatter.2.cloned.1.call-start = ((), (), s32[]{:S(2)}) async-start(), calls=%async_computation.4 | async-start | bytes 2359296 | tf_op jit(solution)/shard_map/reduce_scatter | solution.py:393
  23.1 6.5 %collective-permute-start.1 = (bf16[256,256]{1,0:T(8,128)(2,1)S(1)}, bf16[256,256]{1,0:T(8,128)(2,1)S(1)}, u32[]{:S(2)}, u32[]{:S(2)}) collective-permute-start(bf16[256,256]{1,0:T(8,128)(2,1)S(1)} %copy-done.10), channel_id=1, source_target_pairs={{0,16},{8,24},{16,0},{24,8},{1,17},{9,25},{17,1},{25,9},{2,18},{10... | collective-permute-start | bytes 393224 | tf_op jit(solution)/shard_map/ppermute | solution.py:41
  24.4 5.4 %collective-permute-start.2 = (bf16[256,256]{1,0:T(8,128)(2,1)S(1)}, bf16[256,256]{1,0:T(8,128)(2,1)S(1)}, u32[]{:S(2)}, u32[]{:S(2)}) collective-permute-start(bf16[256,256]{1,0:T(8,128)(2,1)S(1)} %copy-done.10), channel_id=1, source_target_pairs={{0,24},{8,16},{16,8},{24,0},{1,25},{9,17},{17,9},{25,1},{2,26},{10... | collective-permute-start | bytes 393224 | tf_op jit(solution)/shard_map/ppermute | solution.py:41
  44.1 5.8 %collective-permute-start.3 = (f32[3,2048]{1,0:T(4,128)}, f32[3,2048]{1,0:T(4,128)S(1)}, u32[]{:S(2)}, u32[]{:S(2)}) collective-permute-start(f32[3,2048]{1,0:T(4,128)} %shard_map.96.refs_0_), channel_id=1, source_target_pairs={{0,1},{1,0},{2,3},{3,2},{4,5},{5,4},{6,7},{7,6},{8,9},{9,8},{10,11... | collective-permute-start | bytes 73736 | tf_op jit(solution)/shard_map/ppermute | solution.py:41
  44.3 7.1 %collective-permute-start.4 = (f32[3,2048]{1,0:T(4,128)}, f32[3,2048]{1,0:T(4,128)S(1)}, u32[]{:S(2)}, u32[]{:S(2)}) collective-permute-start(f32[3,2048]{1,0:T(4,128)} %shard_map.96.refs_0_), channel_id=1, source_target_pairs={{0,2},{1,3},{2,0},{3,1},{4,6},{5,7},{6,4},{7,5},{8,10},{9,11},{10,... | collective-permute-start | bytes 73736 | tf_op jit(solution)/shard_map/ppermute | solution.py:41
  45.3 7.5 %collective-permute-start.5 = (f32[3,2048]{1,0:T(4,128)}, f32[3,2048]{1,0:T(4,128)S(1)}, u32[]{:S(2)}, u32[]{:S(2)}) collective-permute-start(f32[3,2048]{1,0:T(4,128)} %shard_map.96.refs_0_), channel_id=1, source_target_pairs={{0,3},{1,2},{2,1},{3,0},{4,7},{5,6},{6,5},{7,4},{8,11},{9,10},{10,... | collective-permute-start | bytes 73736 | tf_op jit(solution)/shard_map/ppermute | solution.py:41
  46.2 7.3 %collective-permute-start.6 = (f32[3,2048]{1,0:T(4,128)}, f32[3,2048]{1,0:T(4,128)S(1)}, u32[]{:S(2)}, u32[]{:S(2)}) collective-permute-start(f32[3,2048]{1,0:T(4,128)} %shard_map.96.refs_0_), channel_id=1, source_target_pairs={{0,4},{1,5},{2,6},{3,7},{4,0},{5,1},{6,2},{7,3},{8,12},{9,13},{10,... | collective-permute-start | bytes 73736 | tf_op jit(solution)/shard_map/ppermute | solution.py:41
  49.9 4.8 %collective-permute-start.7 = (f32[3,2048]{1,0:T(4,128)}, f32[3,2048]{1,0:T(4,128)S(1)}, u32[]{:S(2)}, u32[]{:S(2)}) collective-permute-start(f32[3,2048]{1,0:T(4,128)} %shard_map.96.refs_0_), channel_id=1, source_target_pairs={{0,5},{1,4},{2,7},{3,6},{4,1},{5,0},{6,3},{7,2},{8,13},{9,12},{10,... | collective-permute-start | bytes 73736 | tf_op jit(solution)/shard_map/ppermute | solution.py:41
  49.9 7.6 %collective-permute-start.8 = (f32[3,2048]{1,0:T(4,128)}, f32[3,2048]{1,0:T(4,128)S(1)}, u32[]{:S(2)}, u32[]{:S(2)}) collective-permute-start(f32[3,2048]{1,0:T(4,128)} %shard_map.96.refs_0_), channel_id=1, source_target_pairs={{0,6},{1,7},{2,4},{3,5},{4,2},{5,3},{6,0},{7,1},{8,14},{9,15},{10,... | collective-permute-start | bytes 73736 | tf_op jit(solution)/shard_map/ppermute | solution.py:41
  51.4 7.5 %collective-permute-start.9 = (f32[3,2048]{1,0:T(4,128)}, f32[3,2048]{1,0:T(4,128)S(1)}, u32[]{:S(2)}, u32[]{:S(2)}) collective-permute-start(f32[3,2048]{1,0:T(4,128)} %shard_map.96.refs_0_), channel_id=1, source_target_pairs={{0,7},{1,6},{2,5},{3,4},{4,3},{5,2},{6,1},{7,0},{8,15},{9,14},{10,... | collective-permute-start | bytes 73736 | tf_op jit(solution)/shard_map/ppermute | solution.py:41
  67.8 57.5 %all-to-all-start.1 = ((bf16[8,256,256]{2,1,0:T(8,128)(2,1)}), bf16[8,256,256]{2,1,0:T(8,128)(2,1)S(1)}, u32[]{:S(2)}, u32[]{:S(2)}) async-start(bf16[8,256,256]{2,1,0:T(8,128)(2,1)} %shard_map.95.refs_4_), calls=%async_computation.2 | async-start | bytes 2097152 | tf_op jit(solution)/shard_map/all_to_all | solution.py:384
  72.2 113.8 %all-gather.7.cloned.1.call-start = ((), (), s32[]{:S(2)}) async-start(), calls=%async_computation.6 | async-start | bytes 2359296 | tf_op jit(solution)/shard_map/all_gather | solution.py:406
  72.3 8.1 %collective-permute-start.16 = (f32[256,256]{1,0:T(8,128)S(1)}, f32[256,256]{1,0:T(8,128)S(1)}, u32[]{:S(2)}, u32[]{:S(2)}) collective-permute-start(f32[256,256]{1,0:T(8,128)S(1)} %copy-done.34), channel_id=1, source_target_pairs={{0,8},{8,0},{16,24},{24,16},{1,9},{9,1},{17,25},{25,17},{2,10},{10... | collective-permute-start | bytes 786440 | tf_op jit(solution)/shard_map/ppermute | solution.py:41
  72.6 9.0 %collective-permute-start.17 = (f32[256,256]{1,0:T(8,128)S(1)}, f32[256,256]{1,0:T(8,128)S(1)}, u32[]{:S(2)}, u32[]{:S(2)}) collective-permute-start(f32[256,256]{1,0:T(8,128)S(1)} %copy-done.33), channel_id=1, source_target_pairs={{0,16},{8,24},{16,0},{24,8},{1,17},{9,25},{17,1},{25,9},{2,18},{10... | collective-permute-start | bytes 786440 | tf_op jit(solution)/shard_map/ppermute | solution.py:41
  73.8 12.6 %collective-permute-start.18 = (f32[256,256]{1,0:T(8,128)S(1)}, f32[256,256]{1,0:T(8,128)S(1)}, u32[]{:S(2)}, u32[]{:S(2)}) collective-permute-start(f32[256,256]{1,0:T(8,128)S(1)} %copy-done.32), channel_id=1, source_target_pairs={{0,24},{8,16},{16,8},{24,0},{1,25},{9,17},{17,9},{25,1},{2,26},{10... | collective-permute-start | bytes 786440 | tf_op jit(solution)/shard_map/ppermute | solution.py:41
  78.9 37.4 %collective-permute-start.10 = (bf16[8,128,256]{2,1,0:T(8,128)(2,1)}, bf16[8,128,256]{2,1,0:T(8,128)(2,1)S(1)}, u32[]{:S(2)}, u32[]{:S(2)}) collective-permute-start(bf16[8,128,256]{2,1,0:T(8,128)(2,1)} %get-tuple-element.27), channel_id=1, source_target_pairs={{0,8},{8,0},{16,24},{24,16},{1,9},{9,1},{17,25},{25,17},{2,10},{10... | collective-permute-start | bytes 1572872 | tf_op jit(solution)/shard_map/ppermute | solution.py:41
  79.2 37.2 %collective-permute-start.11 = (bf16[8,128,256]{2,1,0:T(8,128)(2,1)}, bf16[8,128,256]{2,1,0:T(8,128)(2,1)S(1)}, u32[]{:S(2)}, u32[]{:S(2)}) collective-permute-start(bf16[8,128,256]{2,1,0:T(8,128)(2,1)} %get-tuple-element.28), channel_id=1, source_target_pairs={{0,16},{8,24},{16,0},{24,8},{1,17},{9,25},{17,1},{25,9},{2,18},{10... | collective-permute-start | bytes 1572872 | tf_op jit(solution)/shard_map/ppermute | solution.py:41
  80.4 36.0 %collective-permute-start.12 = (bf16[8,128,256]{2,1,0:T(8,128)(2,1)}, bf16[8,128,256]{2,1,0:T(8,128)(2,1)S(1)}, u32[]{:S(2)}, u32[]{:S(2)}) collective-permute-start(bf16[8,128,256]{2,1,0:T(8,128)(2,1)} %get-tuple-element.29), channel_id=1, source_target_pairs={{0,24},{8,16},{16,8},{24,0},{1,25},{9,17},{17,9},{25,1},{2,26},{10... | collective-permute-start | bytes 1572872 | tf_op jit(solution)/shard_map/ppermute | solution.py:41
  89.2 20.3 %collective-permute-start.19 = (bf16[128,256]{1,0:T(8,128)(2,1)}, bf16[128,256]{1,0:T(8,128)(2,1)S(1)}, u32[]{:S(2)}, u32[]{:S(2)}) collective-permute-start(bf16[128,256]{1,0:T(8,128)(2,1)} %get-tuple-element.40), channel_id=1, source_target_pairs={{0,8},{8,0},{16,24},{24,16},{1,9},{9,1},{17,25},{25,17},{2,10},{10... | collective-permute-start | bytes 196616 | tf_op jit(solution)/shard_map/ppermute | solution.py:41
  89.5 21.2 %collective-permute-start.20 = (bf16[128,256]{1,0:T(8,128)(2,1)}, bf16[128,256]{1,0:T(8,128)(2,1)S(1)}, u32[]{:S(2)}, u32[]{:S(2)}) collective-permute-start(bf16[128,256]{1,0:T(8,128)(2,1)} %get-tuple-element.41), channel_id=1, source_target_pairs={{0,16},{8,24},{16,0},{24,8},{1,17},{9,25},{17,1},{25,9},{2,18},{10... | collective-permute-start | bytes 196616 | tf_op jit(solution)/shard_map/ppermute | solution.py:41
  116.0 14.3 %collective-permute-start.22 = (bf16[4,128,256]{2,1,0:T(8,128)(2,1)}, bf16[4,128,256]{2,1,0:T(8,128)(2,1)S(1)}, u32[]{:S(2)}, u32[]{:S(2)}) collective-permute-start(bf16[4,128,256]{2,1,0:T(8,128)(2,1)} %shard_map.102.refs_1_), channel_id=1, source_target_pairs={{0,2},{1,3},{2,0},{3,1},{4,6},{5,7},{6,4},{7,5},{8,10},{9,11},{10,... | collective-permute-start | bytes 786440 | tf_op jit(solution)/shard_map/ppermute | solution.py:41
  122.6 7.8 %collective-permute-start.13 = (bf16[128,256]{1,0:T(8,128)(2,1)}, bf16[128,256]{1,0:T(8,128)(2,1)S(1)}, u32[]{:S(2)}, u32[]{:S(2)}) collective-permute-start(bf16[128,256]{1,0:T(8,128)(2,1)} %get-tuple-element.33), channel_id=1, source_target_pairs={{0,8},{8,0},{16,24},{24,16},{1,9},{9,1},{17,25},{25,17},{2,10},{10... | collective-permute-start | bytes 196616 | tf_op jit(solution)/shard_map/ppermute | solution.py:41
  122.7 7.7 %collective-permute-start.14 = (bf16[128,256]{1,0:T(8,128)(2,1)}, bf16[128,256]{1,0:T(8,128)(2,1)S(1)}, u32[]{:S(2)}, u32[]{:S(2)}) collective-permute-start(bf16[128,256]{1,0:T(8,128)(2,1)} %get-tuple-element.34), channel_id=1, source_target_pairs={{0,16},{8,24},{16,0},{24,8},{1,17},{9,25},{17,1},{25,9},{2,18},{10... | collective-permute-start | bytes 196616 | tf_op jit(solution)/shard_map/ppermute | solution.py:41
  124.1 6.3 %collective-permute-start.15 = (bf16[128,256]{1,0:T(8,128)(2,1)}, bf16[128,256]{1,0:T(8,128)(2,1)S(1)}, u32[]{:S(2)}, u32[]{:S(2)}) collective-permute-start(bf16[128,256]{1,0:T(8,128)(2,1)} %get-tuple-element.35), channel_id=1, source_target_pairs={{0,24},{8,16},{16,8},{24,0},{1,25},{9,17},{17,9},{25,1},{2,26},{10... | collective-permute-start | bytes 196616 | tf_op jit(solution)/shard_map/ppermute | solution.py:41
  133.4 47.0 %all-to-all-start.2 = ((bf16[4,8,128,256]{3,2,1,0:T(8,128)(2,1)}), bf16[4,8,128,256]{3,2,1,0:T(8,128)(2,1)S(1)}, u32[]{:S(2)}, u32[]{:S(2)}) async-start(bf16[4,8,128,256]{3,2,1,0:T(8,128)(2,1)} %shard_map.103.refs_5_), calls=%async_computation.3 | async-start | bytes 4194304 | tf_op jit(solution)/shard_map/all_to_all | solution.py:384
  137.2 26.5 %collective-permute-start.23 = (bf16[4,128,256]{2,1,0:T(8,128)(2,1)S(1)}, bf16[4,128,256]{2,1,0:T(8,128)(2,1)S(1)}, u32[]{:S(2)}, u32[]{:S(2)}) collective-permute-start(bf16[4,128,256]{2,1,0:T(8,128)(2,1)S(1)} %copy-done.7), channel_id=1, source_target_pairs={{0,4},{1,5},{2,6},{3,7},{4,0},{5,1},{6,2},{7,3},{8,12},{9,13},{10,... | collective-permute-start | bytes 786440 | tf_op jit(solution)/shard_map/ppermute | solution.py:41
  137.3 39.5 %collective-permute-start.24 = (bf16[4,128,256]{2,1,0:T(8,128)(2,1)S(1)}, bf16[4,128,256]{2,1,0:T(8,128)(2,1)S(1)}, u32[]{:S(2)}, u32[]{:S(2)}) collective-permute-start(bf16[4,128,256]{2,1,0:T(8,128)(2,1)S(1)} %copy-done.7), channel_id=1, source_target_pairs={{0,6},{1,7},{2,4},{3,5},{4,2},{5,3},{6,0},{7,1},{8,14},{9,15},{10,... | collective-permute-start | bytes 786440 | tf_op jit(solution)/shard_map/ppermute | solution.py:41
  137.5 42.9 %collective-permute-start.25 = (bf16[4,128,256]{2,1,0:T(8,128)(2,1)S(1)}, bf16[4,128,256]{2,1,0:T(8,128)(2,1)S(1)}, u32[]{:S(2)}, u32[]{:S(2)}) collective-permute-start(bf16[4,128,256]{2,1,0:T(8,128)(2,1)S(1)} %copy-done.7), channel_id=1, source_target_pairs={{0,1},{1,0},{2,3},{3,2},{4,5},{5,4},{6,7},{7,6},{8,9},{9,8},{10,11... | collective-permute-start | bytes 786440 | tf_op jit(solution)/shard_map/ppermute | solution.py:41
  140.8 39.6 %collective-permute-start.26 = (bf16[4,128,256]{2,1,0:T(8,128)(2,1)S(1)}, bf16[4,128,256]{2,1,0:T(8,128)(2,1)}, u32[]{:S(2)}, u32[]{:S(2)}) collective-permute-start(bf16[4,128,256]{2,1,0:T(8,128)(2,1)S(1)} %copy-done.9), channel_id=1, source_target_pairs={{0,1},{1,0},{2,3},{3,2},{4,5},{5,4},{6,7},{7,6},{8,9},{9,8},{10,11... | collective-permute-start | bytes 786440 | tf_op jit(solution)/shard_map/ppermute | solution.py:41
  163.7 16.6 %collective-permute-start.27 = (bf16[4,128,256]{2,1,0:T(8,128)(2,1)S(1)}, bf16[4,128,256]{2,1,0:T(8,128)(2,1)}, u32[]{:S(2)}, u32[]{:S(2)}) collective-permute-start(bf16[4,128,256]{2,1,0:T(8,128)(2,1)S(1)} %collective-permute-done.23.refs_3_), channel_id=1, source_target_pairs={{0,1},{1,0},{2,3},{3,2},{4,5},{5,4},{6,7},{7,6},{8,9},{9,8},{10,11... | collective-permute-start | bytes 786440 | tf_op jit(solution)/shard_map/ppermute | solution.py:41
  (38 other events, 170.5 us)
Sparse Core Ops, SparseCore 0:
  9.6 29.0 all-gather.4
  67.9 52.7 reduce-scatter.1
  133.5 43.6 all-gather.6
